TPU v7x, 32 devices: a whole 2x2x4 slice. The times are simulated.
32 devices in a mesh: dp: 2 (over x), ctx: 16 (over z, y, core).
Axes of the slice: x: 2, y: 2, z: 4, core: 2. Of those that a mesh axis runs over, the one named last changes fastest.
Arguments:
- query: bfloat16 [24576, 512], P(('dp', 'ctx')), parts along dimension 0, may hold values from -14 to 14
- key: bfloat16 [24576, 128], P(('dp', 'ctx')), parts along dimension 0, may hold values from -12 to 12
- value: bfloat16 [24576, 128], P(('dp', 'ctx')), parts along dimension 0, may hold values from -6 to 6
- d_out: bfloat16 [24576, 512], P(('dp', 'ctx')), parts along dimension 0, may hold values from -6 to 6
- doc_lengths: int32 [64], P('dp'), parts along dimension 0, may hold values from 1 to 768, 12288 in all
Outputs:
- attended: bfloat16 [24576, 512], P(('dp', 'ctx')), parts along dimension 0
- d_query: bfloat16 [24576, 512], P(('dp', 'ctx')), parts along dimension 0
- d_key: bfloat16 [24576, 128], P(('dp', 'ctx')), parts along dimension 0
- d_value: bfloat16 [24576, 128], P(('dp', 'ctx')), parts along dimension 0
There are 2 independent parts, one for each index of `dp`. A program takes and returns all parts, laid end to end along the dimension named above; each array names one. Nothing has to cross between parts.
Inputs may be any that keep to these rules, and one draw needn't show every extreme that they name: `doc_lengths`: the lengths of one session sum to 12288, and one of them is exactly 768.
All inputs are finite; a program needn't handle non-finite values.
Results may differ from a plain program's by a relative error of at most 0.035.
Values may be sent and summed in bfloat16 or wider, within the bound.
No kernel may reach another device: no remote copies, remote signals or barrier semaphores. Data moves between devices by JAX's collectives and lax.ppermute only.
A program may use at most 64 MiB of HBM per device.

v0:
```python
import math

import jax
import jax.numpy as jnp
from jax import lax
from jax.sharding import PartitionSpec as P

HD = 128
REACH = 2


masked_score = -1e30


def from_behind(value, axis, steps):
    count = lax.axis_size(axis)
    first, last = (max(0, -steps), min(count, count - steps))
    return lax.ppermute(value, axis, [(source, source + steps) for source in range(first, last)])


def doc_index(positions, doc_lengths):
    starts = jnp.cumsum(doc_lengths) - doc_lengths
    return jnp.sum((starts[None, :] <= positions[:, None]).astype(jnp.int32), axis=1) - 1


def score_block(query_heads, keys, allowed):
    scores = jnp.einsum("rhe,ke->hrk", query_heads, keys, preferred_element_type=jnp.float32) * (
        1.0 / math.sqrt(HD)
    )
    return jnp.where(allowed[None], scores, masked_score)


def row_delta(dout_heads, attended):
    summed = jnp.sum(dout_heads.astype(jnp.float32) * attended.astype(jnp.float32), axis=2)
    return jnp.transpose(summed)[:, :, None]


def backward_terms(query_heads, dout_heads, keys, values, weights, delta):
    scale = 1.0 / math.sqrt(HD)
    dprob = jnp.einsum("rhe,ke->hrk", dout_heads, values, preferred_element_type=jnp.float32)
    dscore = (weights.astype(jnp.float32) * (dprob - delta)).astype(jnp.bfloat16)
    grad_query = jnp.einsum("hrk,ke->rhe", dscore, keys, preferred_element_type=jnp.float32) * scale
    grad_key = (
        jnp.einsum("hrk,rhe->ke", dscore, query_heads, preferred_element_type=jnp.float32) * scale
    )
    grad_value = jnp.einsum("hrk,rhe->ke", weights, dout_heads, preferred_element_type=jnp.float32)
    return (grad_query, grad_key, grad_value)


def window_group(query_heads, dout_heads, keys, values, allowed):
    rows = query_heads.shape[0]
    scores = score_block(query_heads, keys, allowed)
    row_max = jnp.max(scores, axis=2, keepdims=True)
    log_total = row_max + jnp.log(jnp.sum(jnp.exp(scores - row_max), axis=2, keepdims=True))
    weights = jnp.where(allowed[None], jnp.exp(scores - log_total), 0.0).astype(jnp.bfloat16)
    attended = jnp.einsum(
        "hrk,ke->rhe", weights, values, preferred_element_type=jnp.float32
    ).astype(jnp.bfloat16)
    delta = row_delta(dout_heads, attended)
    grad_query, grad_key, grad_value = backward_terms(
        query_heads, dout_heads, keys, values, weights, delta
    )
    tiles = keys.shape[0] // rows
    key_parts = [grad_key[index * rows : (index + 1) * rows] for index in range(tiles)]
    value_parts = [grad_value[index * rows : (index + 1) * rows] for index in range(tiles)]
    return (attended, grad_query, key_parts, value_parts)


def body(query, key, value, d_out, doc_lengths):
    count = lax.axis_size("ctx")
    device = lax.axis_index("ctx")
    rows = query.shape[0] // 2
    heads = query.shape[1] // HD
    group_size = 2
    local = jnp.concatenate([key, value], axis=1)
    offsets = list(range(-REACH, 0)) + list(range(1, REACH + 1))
    pieces = {0: local}
    received = {}
    for offset in offsets:
        if offset == 1:
            both_blocks = from_behind(local, "ctx", -1)
            received[1] = both_blocks[rows:]
            folded = both_blocks[:rows]
        else:
            sent = local[:rows] if offset < 0 else local[rows:]
            received[offset] = from_behind(sent, "ctx", -offset)
    empty_half = jnp.zeros((rows, 2 * HD), local.dtype)
    for offset in offsets:
        if offset < 0:
            pieces[offset] = jnp.concatenate([received[offset], empty_half], axis=0)
        elif offset == 1:
            pieces[offset] = jnp.concatenate([folded, received[offset]], axis=0)
        else:
            pieces[offset] = jnp.concatenate([empty_half, received[offset]], axis=0)
    nearby = jnp.stack([pieces[offset] for offset in range(-REACH, REACH + 1)])
    grads = jnp.zeros((2 * REACH + 1, 2 * rows, 2 * HD), jnp.float32)
    line = jnp.arange(rows, dtype=jnp.int32)
    attended_rows, grad_query_rows = ([], [])
    for slot in range(2):
        block_id = device if slot == 0 else 2 * count - 1 - device
        query_block = query[slot * rows : (slot + 1) * rows].reshape(rows, heads, HD)
        dout_block = d_out[slot * rows : (slot + 1) * rows].reshape(rows, heads, HD)
        query_pos = block_id * rows + line
        query_doc = doc_index(query_pos, doc_lengths)
        key_tiles, value_tiles, allowed_tiles, live, places = ([], [], [], [], [])
        for back in range(REACH, -1, -1):
            source = block_id - back
            clamped = jnp.maximum(source, 0)
            owner = jnp.where(clamped < count, clamped, 2 * count - 1 - clamped)
            place = owner - device + REACH
            start = jnp.where(clamped < count, 0, rows).astype(jnp.int32)
            tile = lax.dynamic_slice(nearby, (place, start, jnp.int32(0)), (1, rows, 2 * HD))[0]
            key_pos = source * rows + line
            key_doc = doc_index(key_pos, doc_lengths)
            allowed_tiles.append(
                (key_pos[None, :] <= query_pos[:, None]) & (key_doc[None, :] == query_doc[:, None])
            )
            live.append(jnp.logical_or(back == 0, key_doc[rows - 1] == query_doc[0]))
            key_tiles.append(tile[:, :HD])
            value_tiles.append(tile[:, HD:])
            places.append((place, start))
        keys = jnp.concatenate(key_tiles, axis=0)
        values = jnp.concatenate(value_tiles, axis=0)
        allowed = jnp.concatenate(allowed_tiles, axis=1)
        attended_parts, grad_query_parts = ([], [])
        key_sums = [jnp.zeros((rows, HD), jnp.float32) for place in places]
        value_sums = [jnp.zeros((rows, HD), jnp.float32) for place in places]
        for first in range(0, heads, group_size):
            query_heads = query_block[:, first : first + group_size]
            dout_heads = dout_block[:, first : first + group_size]
            attended, grad_query, key_parts, value_parts = window_group(
                query_heads, dout_heads, keys, values, allowed
            )
            attended_parts.append(attended)
            grad_query_parts.append(grad_query)
            key_sums = [total + part for total, part in zip(key_sums, key_parts)]
            value_sums = [total + part for total, part in zip(value_sums, value_parts)]
        attended_rows.append(jnp.concatenate(attended_parts, axis=1).reshape(rows, heads * HD))
        grad_query_rows.append(
            jnp.concatenate(grad_query_parts, axis=1).reshape(rows, heads * HD).astype(jnp.bfloat16)
        )
        for index in range(len(places)):
            place, start = places[index]
            update = jnp.concatenate([key_sums[index], value_sums[index]], axis=1)[None]
            current = lax.dynamic_slice(grads, (place, start, jnp.int32(0)), (1, rows, 2 * HD))
            grads = lax.dynamic_update_slice(grads, current + update, (place, start, jnp.int32(0)))
    total = grads[REACH]
    lower = total[:rows]
    upper = total[rows:]
    for offset in offsets:
        if offset == 1:
            moved_both = from_behind(grads[REACH + 1], "ctx", 1)
            lower = lower + moved_both[:rows]
            upper = upper + moved_both[rows:]
        else:
            half = 0 if offset < 0 else 1
            moved = from_behind(
                grads[REACH + offset][half * rows : (half + 1) * rows], "ctx", offset
            )
            if offset < 0:
                lower = lower + moved
            else:
                upper = upper + moved
    total = jnp.concatenate([lower, upper], axis=0)
    attended_all = jnp.concatenate(attended_rows, axis=0)
    grad_query_all = jnp.concatenate(grad_query_rows, axis=0)
    return (
        attended_all,
        grad_query_all,
        total[:, :HD].astype(jnp.bfloat16),
        total[:, HD:].astype(jnp.bfloat16),
    )


def solution(mesh):
    placed = (
        P(("dp", "ctx"), None),
        P(("dp", "ctx"), None),
        P(("dp", "ctx"), None),
        P(("dp", "ctx"), None),
        P("dp"),
    )
    return jax.shard_map(
        body,
        mesh=mesh,
        in_specs=placed,
        out_specs=(
            P(("dp", "ctx"), None),
            P(("dp", "ctx"), None),
            P(("dp", "ctx"), None),
            P(("dp", "ctx"), None),
        ),
        check_vma=False,
    )
```

profile of v0, /device:TPU:25, one launch (start us, length us, event | category | flops | bytes accessed | tf_op | source)
XLA Modules:
  0.0 86.7 jit_solution(18113939921970824222)
XLA Ops:
  0.6 1.0 %constant_dynamic-update-slice_fusion.1 = bf16[768,256]{1,0:T(8,128)(2,1)S(1)} fusion(bf16[768,128]{1,0:T(8,128)(2,1)} %param.6), kind=kLoop, calls=%fused_computation.165 | loop fusion | bytes 393216
  1.7 1.0 %constant_dynamic-update-slice_fusion = bf16[768,256]{1,0:T(8,128)(2,1)S(1)} fusion(bf16[768,256]{1,0:T(8,128)(2,1)S(1)} %constant_dynamic-update-slice_fusion.1, bf16[768,128]{1,0:T(8,128)(2,1)} %param.7), kind=kLoop, calls=%fused_computation.164 | loop fusion | bytes 393216 | tf_op jit(solution)/shard_map/concatenate | solution.py:75
  2.7 0.7 fusion.69
  3.4 3.7 %collective-permute-start.1 = (bf16[384,256]{1,0:T(8,128)(2,1)}, bf16[384,256]{1,0:T(8,128)(2,1)}, u32[]{:S(2)}, u32[]{:S(2)}) collective-permute-start(bf16[384,256]{1,0:T(8,128)(2,1)} %get-tuple-element.60), channel_id=1, source_target_pairs={{0,1},{1,2},{2,3},{3,4},{4,5},{5,6},{6,7},{7,8},{8,9},{9,10},{10,1... | collective-permute-start | bytes 589832 | tf_op jit(solution)/shard_map/ppermute | solution.py:18
  7.1 1.9 %collective-permute-start = (bf16[384,256]{1,0:T(8,128)(2,1)}, bf16[384,256]{1,0:T(8,128)(2,1)}, u32[]{:S(2)}, u32[]{:S(2)}) collective-permute-start(bf16[384,256]{1,0:T(8,128)(2,1)} %get-tuple-element.60), channel_id=1, source_target_pairs={{0,2},{1,3},{2,4},{3,5},{4,6},{5,7},{6,8},{7,9},{8,10},{9,11},{10,... | collective-permute-start | bytes 589832 | tf_op jit(solution)/shard_map/ppermute | solution.py:18
  9.0 2.3 %collective-permute-start.2 = (bf16[768,256]{1,0:T(8,128)(2,1)S(1)}, bf16[768,256]{1,0:T(8,128)(2,1)}, u32[]{:S(2)}, u32[]{:S(2)}) collective-permute-start(bf16[768,256]{1,0:T(8,128)(2,1)S(1)} %constant_dynamic-update-slice_fusion), channel_id=1, source_target_pairs={{1,0},{2,1},{3,2},{4,3},{5,4},{6,5},{7,6},{8,7},{9,8},{10,9},{11,1... | collective-permute-start | bytes 1179656 | tf_op jit(solution)/shard_map/ppermute | solution.py:18
  11.3 3.9 %collective-permute-start.3 = (bf16[384,256]{1,0:T(8,128)(2,1)S(1)}, bf16[384,256]{1,0:T(8,128)(2,1)}, u32[]{:S(2)}, u32[]{:S(2)}) collective-permute-start(bf16[384,256]{1,0:T(8,128)(2,1)S(1)} %get-tuple-element.59), channel_id=1, source_target_pairs={{2,0},{3,1},{4,2},{5,3},{6,4},{7,5},{8,6},{9,7},{10,8},{11,9},{12,... | collective-permute-start | bytes 589832 | tf_op jit(solution)/shard_map/ppermute | solution.py:18
  15.3 0.7 copy.97
  16.2 0.7 sub.185
  16.9 1.2 %fusion.67 = (bf16[384,512]{1,0:T(8,128)(2,1)S(1)}, bf16[384,512]{1,0:T(8,128)(2,1)S(1)}) fusion(bf16[768,512]{1,0:T(8,128)(2,1)} %param.5), kind=kLoop, calls=%fused_computation.183 | loop fusion | bytes 1572864 | tf_op jit(solution)/shard_map/slice | solution.py:101
  18.3 0.6 compare_and_fusion.2
  19.0 0.6 compare_and_fusion.5
  20.7 1.0 %bitcast_dynamic-update-slice_fusion.4 = bf16[5,768,256]{2,1,0:T(8,128)(2,1)S(1)} fusion(bf16[384,256]{1,0:T(8,128)(2,1)} %collective-permute-done), kind=kLoop, calls=%fused_computation.115 | loop fusion | bytes 589824
  21.7 1.0 %bitcast_dynamic-update-slice_fusion.3 = bf16[5,768,256]{2,1,0:T(8,128)(2,1)S(1)} fusion(bf16[5,768,256]{2,1,0:T(8,128)(2,1)S(1)} %bitcast_dynamic-update-slice_fusion.4, bf16[384,256]{1,0:T(8,128)(2,1)} %collective-permute-done.1), kind=kLoop, calls=%fused_computation.114 | loop fusion | bytes 589824
  22.7 1.0 %bitcast_dynamic-update-slice_fusion.1 = bf16[5,768,256]{2,1,0:T(8,128)(2,1)S(1)} fusion(bf16[5,768,256]{2,1,0:T(8,128)(2,1)S(1)} %bitcast_dynamic-update-slice_fusion.2, bf16[768,256]{1,0:T(8,128)(2,1)} %collective-permute-done.2), kind=kLoop, calls=%fused_computation.112 | loop fusion | bytes 786432
  23.7 1.0 %bitcast_dynamic-update-slice_fusion = bf16[5,768,256]{2,1,0:T(8,128)(2,1)S(1)} fusion(bf16[5,768,256]{2,1,0:T(8,128)(2,1)S(1)} %bitcast_dynamic-update-slice_fusion.1, bf16[384,256]{1,0:T(8,128)(2,1)} %collective-permute-done.3), kind=kLoop, calls=%fused_computation.111 | loop fusion | bytes 589824 | tf_op jit(solution)/shard_map/stack | solution.py:95
  24.9 0.8 fusion.79
  25.7 0.8 fusion.78
  27.5 1.4 %select_convert_fusion.3 = (bf16[2,384,1152]{1,2,0:T(8,128)(2,1)S(1)}, bf16[2,384,1152]{1,2,0:T(8,128)(2,1)S(1)}) fusion(f32[2,384,1152]{1,2,0:T(8,128)S(1)} %get-tuple-element.84, f32[2,384]{1,0:T(2,128)S(1)} %log_add_fusion.3, pred[384,1152]{0,1:T(8,128)(4,1)S(1)} %pad_add_fusion, f32[2,384,1152]{1,2,0:T(8,128)S(1)} %get-tuple-element.86, ...), kind=kLoop, calls=%fused_computation.30 | loop fusion | flops 5308416 | bytes 11065344 | tf_op jit(solution)/shard_map/convert_element_type | solution.py:55
  28.9 0.7 convolution_bitcast_fusion.9
  30.1 0.5 multiply_reduce_fusion.3
  30.6 0.6 fusion.16
  31.7 0.7 fusion.23
  32.4 0.7 convolution_bitcast_fusion.8
  33.1 0.6 fusion.17
  34.2 0.7 fusion.22
  34.9 0.8 fusion.77
  35.7 0.8 fusion.76
  37.5 1.6 %select_convert_fusion.1 = (bf16[2,384,1152]{1,2,0:T(8,128)(2,1)S(1)}, bf16[2,384,1152]{1,2,0:T(8,128)(2,1)S(1)}) fusion(f32[2,384,1152]{1,2,0:T(8,128)S(1)} %get-tuple-element.80, f32[2,384]{1,0:T(2,128)S(1)} %log_add_fusion.1, pred[384,1152]{0,1:T(8,128)(4,1)S(1)} %pad_add_fusion.1, f32[2,384,1152]{1,2,0:T(8,128)S(1)} %get-tuple-element.82, ...), kind=kLoop, calls=%fused_computation.26 | loop fusion | flops 5308416 | bytes 11065344 | tf_op jit(solution)/shard_map/convert_element_type | solution.py:55
  39.1 0.7 convolution_bitcast_fusion.5
  40.3 0.5 multiply_reduce_fusion.1
  40.8 0.6 fusion.18
  41.9 0.7 fusion.21
  42.6 0.7 convolution_bitcast_fusion.4
  43.2 0.6 fusion.19
  43.9 0.7 fusion.20
  45.7 1.1 %slice_bitcast_fusion.4 = (f32[384,256]{0,1:T(8,128)}, f32[384,256]{0,1:T(8,128)}, f32[384,256]{0,1:T(8,128)S(1)}) fusion(f32[5,768,256]{1,2,0:T(8,128)S(1)} %fusion.49), kind=kLoop, calls=%fused_computation.86 | loop fusion | bytes 2359296 | tf_op jit(solution)/shard_map/slice | solution.py:158
  46.9 4.5 %collective-permute-start.6 = (f32[768,256]{0,1:T(8,128)S(1)}, f32[768,256]{0,1:T(8,128)}, u32[]{:S(2)}, u32[]{:S(2)}) collective-permute-start(f32[768,256]{0,1:T(8,128)S(1)} %slice_bitcast_fusion), channel_id=1, source_target_pairs={{0,1},{1,2},{2,3},{3,4},{4,5},{5,6},{6,7},{7,8},{8,9},{9,10},{10,1... | collective-permute-start | bytes 2359304 | tf_op jit(solution)/shard_map/ppermute | solution.py:18
  51.5 3.1 %collective-permute-start.4 = (f32[384,256]{0,1:T(8,128)}, f32[384,256]{0,1:T(8,128)}, u32[]{:S(2)}, u32[]{:S(2)}) collective-permute-start(f32[384,256]{0,1:T(8,128)} %get-tuple-element.28), channel_id=1, source_target_pairs={{2,0},{3,1},{4,2},{5,3},{6,4},{7,5},{8,6},{9,7},{10,8},{11,9},{12,... | collective-permute-start | bytes 1179656 | tf_op jit(solution)/shard_map/ppermute | solution.py:18
  54.6 2.9 %collective-permute-start.7 = (f32[384,256]{0,1:T(8,128)}, f32[384,256]{0,1:T(8,128)}, u32[]{:S(2)}, u32[]{:S(2)}) collective-permute-start(f32[384,256]{0,1:T(8,128)} %get-tuple-element.29), channel_id=1, source_target_pairs={{0,2},{1,3},{2,4},{3,5},{4,6},{5,7},{6,8},{7,9},{8,10},{9,11},{10,... | collective-permute-start | bytes 1179656 | tf_op jit(solution)/shard_map/ppermute | solution.py:18
  57.5 1.9 %collective-permute-start.5 = (f32[384,256]{0,1:T(8,128)S(1)}, f32[384,256]{0,1:T(8,128)}, u32[]{:S(2)}, u32[]{:S(2)}) collective-permute-start(f32[384,256]{0,1:T(8,128)S(1)} %get-tuple-element.30), channel_id=1, source_target_pairs={{1,0},{2,1},{3,2},{4,3},{5,4},{6,5},{7,6},{8,7},{9,8},{10,9},{11,1... | collective-permute-start | bytes 1179656 | tf_op jit(solution)/shard_map/ppermute | solution.py:18
  60.8 0.9 %pad_maximum_fusion = bf16[768,512]{1,0:T(8,128)(2,1)} fusion(bf16[384,512]{1,0:T(8,128)(2,1)S(1)} %copy.113, bf16[384,512]{1,0:T(8,128)(2,1)S(1)} %copy.112), kind=kLoop, calls=%fused_computation.71 | loop fusion | flops 1572864 | bytes 1572864 | tf_op jit(solution)/shard_map/concatenate | solution.py:165
  61.8 0.9 %pad_maximum_fusion.1 = bf16[768,512]{1,0:T(8,128)(2,1)} fusion(bf16[384,512]{1,0:T(8,128)(2,1)S(1)} %copy.129, bf16[384,512]{1,0:T(8,128)(2,1)S(1)} %copy.128), kind=kLoop, calls=%fused_computation.72 | loop fusion | flops 1572864 | bytes 1572864 | tf_op jit(solution)/shard_map/concatenate | solution.py:166
  62.7 16.5 %collective-permute-done.4 = f32[384,256]{0,1:T(8,128)} collective-permute-done((f32[384,256]{0,1:T(8,128)}, f32[384,256]{0,1:T(8,128)}, u32[]{:S(2)}, u32[]{:S(2)}) %collective-permute-start.4) | collective-permute-done | bytes 393248 | tf_op jit(solution)/shard_map/ppermute | solution.py:18
  79.2 4.0 %collective-permute-done.5 = f32[384,256]{0,1:T(8,128)} collective-permute-done((f32[384,256]{0,1:T(8,128)S(1)}, f32[384,256]{0,1:T(8,128)}, u32[]{:S(2)}, u32[]{:S(2)}) %collective-permute-start.5) | collective-permute-done | bytes 393248 | tf_op jit(solution)/shard_map/ppermute | solution.py:18
  83.1 1.8 %slice_add_fusion.1 = (bf16[384,256]{0,1:T(8,128)(2,1)S(1)}, bf16[384,256]{0,1:T(8,128)(2,1)S(1)}) fusion(f32[768,256]{0,1:T(8,128)} %collective-permute-done.6, f32[384,256]{0,1:T(8,128)} %collective-permute-done.5, f32[384,256]{0,1:T(8,128)} %collective-permute-done.4, f32[5,768,256]{1,2,0:T(8,128)} %copy-done, f32[384,256]{0,1:T(8,128)} %collective-permute-done.7), kind=kLoop, calls=%fused_computation.84 | loop fusion | flops 688128 | bytes 3145728 | tf_op jit(solution)/shard_map/add | solution.py:153
  85.0 0.8 copy.143
  85.9 0.8 copy.142
  (70 shorter events, 8.8 us)
Async XLA Ops:
  0.6 17.4 %copy-start.1 = (bf16[768,512]{1,0:T(8,128)(2,1)S(1)}, bf16[768,512]{1,0:T(8,128)(2,1)}, u32[]{:S(2)}) copy-start(bf16[768,512]{1,0:T(8,128)(2,1)} %param.8) | copy-start | bytes 2359300
  3.4 18.3 %collective-permute-start.1 = (bf16[384,256]{1,0:T(8,128)(2,1)}, bf16[384,256]{1,0:T(8,128)(2,1)}, u32[]{:S(2)}, u32[]{:S(2)}) collective-permute-start(bf16[384,256]{1,0:T(8,128)(2,1)} %get-tuple-element.60), channel_id=1, source_target_pairs={{0,1},{1,2},{2,3},{3,4},{4,5},{5,6},{6,7},{7,8},{8,9},{9,10},{10,1... | collective-permute-start | bytes 589832 | tf_op jit(solution)/shard_map/ppermute | solution.py:18
  7.1 13.6 %collective-permute-start = (bf16[384,256]{1,0:T(8,128)(2,1)}, bf16[384,256]{1,0:T(8,128)(2,1)}, u32[]{:S(2)}, u32[]{:S(2)}) collective-permute-start(bf16[384,256]{1,0:T(8,128)(2,1)} %get-tuple-element.60), channel_id=1, source_target_pairs={{0,2},{1,3},{2,4},{3,5},{4,6},{5,7},{6,8},{7,9},{8,10},{9,11},{10,... | collective-permute-start | bytes 589832 | tf_op jit(solution)/shard_map/ppermute | solution.py:18
  9.0 13.7 %collective-permute-start.2 = (bf16[768,256]{1,0:T(8,128)(2,1)S(1)}, bf16[768,256]{1,0:T(8,128)(2,1)}, u32[]{:S(2)}, u32[]{:S(2)}) collective-permute-start(bf16[768,256]{1,0:T(8,128)(2,1)S(1)} %constant_dynamic-update-slice_fusion), channel_id=1, source_target_pairs={{1,0},{2,1},{3,2},{4,3},{5,4},{6,5},{7,6},{8,7},{9,8},{10,9},{11,1... | collective-permute-start | bytes 1179656 | tf_op jit(solution)/shard_map/ppermute | solution.py:18
  11.3 12.4 %collective-permute-start.3 = (bf16[384,256]{1,0:T(8,128)(2,1)S(1)}, bf16[384,256]{1,0:T(8,128)(2,1)}, u32[]{:S(2)}, u32[]{:S(2)}) collective-permute-start(bf16[384,256]{1,0:T(8,128)(2,1)S(1)} %get-tuple-element.59), channel_id=1, source_target_pairs={{2,0},{3,1},{4,2},{5,3},{6,4},{7,5},{8,6},{9,7},{10,8},{11,9},{12,... | collective-permute-start | bytes 589832 | tf_op jit(solution)/shard_map/ppermute | solution.py:18
  45.7 14.3 %copy-start = (f32[5,768,256]{1,2,0:T(8,128)}, f32[5,768,256]{1,2,0:T(8,128)S(1)}, u32[]{:S(2)}) copy-start(f32[5,768,256]{1,2,0:T(8,128)S(1)} %fusion.49) | copy-start | bytes 11796484
  46.9 36.3 %collective-permute-start.6 = (f32[768,256]{0,1:T(8,128)S(1)}, f32[768,256]{0,1:T(8,128)}, u32[]{:S(2)}, u32[]{:S(2)}) collective-permute-start(f32[768,256]{0,1:T(8,128)S(1)} %slice_bitcast_fusion), channel_id=1, source_target_pairs={{0,1},{1,2},{2,3},{3,4},{4,5},{5,6},{6,7},{7,8},{8,9},{9,10},{10,1... | collective-permute-start | bytes 2359304 | tf_op jit(solution)/shard_map/ppermute | solution.py:18
  51.5 27.7 %collective-permute-start.4 = (f32[384,256]{0,1:T(8,128)}, f32[384,256]{0,1:T(8,128)}, u32[]{:S(2)}, u32[]{:S(2)}) collective-permute-start(f32[384,256]{0,1:T(8,128)} %get-tuple-element.28), channel_id=1, source_target_pairs={{2,0},{3,1},{4,2},{5,3},{6,4},{7,5},{8,6},{9,7},{10,8},{11,9},{12,... | collective-permute-start | bytes 1179656 | tf_op jit(solution)/shard_map/ppermute | solution.py:18
  54.6 24.6 %collective-permute-start.7 = (f32[384,256]{0,1:T(8,128)}, f32[384,256]{0,1:T(8,128)}, u32[]{:S(2)}, u32[]{:S(2)}) collective-permute-start(f32[384,256]{0,1:T(8,128)} %get-tuple-element.29), channel_id=1, source_target_pairs={{0,2},{1,3},{2,4},{3,5},{4,6},{5,7},{6,8},{7,9},{8,10},{9,11},{10,... | collective-permute-start | bytes 1179656 | tf_op jit(solution)/shard_map/ppermute | solution.py:18
  57.5 25.6 %collective-permute-start.5 = (f32[384,256]{0,1:T(8,128)S(1)}, f32[384,256]{0,1:T(8,128)}, u32[]{:S(2)}, u32[]{:S(2)}) collective-permute-start(f32[384,256]{0,1:T(8,128)S(1)} %get-tuple-element.30), channel_id=1, source_target_pairs={{1,0},{2,1},{3,2},{4,3},{5,4},{6,5},{7,6},{8,7},{9,8},{10,9},{11,1... | collective-permute-start | bytes 1179656 | tf_op jit(solution)/shard_map/ppermute | solution.py:18
where the time goes:
time: 87.2 us; the launch traced here: 86.7 us
  starting transfers between devices  24.3 us (28%)
  waiting for transfers between devices  20.4 us (23%)
  matrix products  14.9 us (17%)
  local copies, waits for them, and re-layouts  13.6 us (16%)
  other arithmetic  11.9 us (14%)
  between operations  1.42 us (2%)
    ppermute x8, starting transfers between devices, from_behind(): lax.ppermute(value, axis, [(source, source + steps) for source in range(f...  24.3 us
    ppermute x8, waiting for transfers between devices, from_behind(): lax.ppermute(value, axis, [(source, source + steps) for source in range(f...  20.4 us
    unnamed x13, local copies, waits for them, and re-layouts  6.05 us
    dot_general x4, matrix products, score_block(): jnp.einsum('rhe,ke->hrk', query_heads, keys, preferred_element_type=jnp.f...  3.18 us
    convert_element_type x2, other arithmetic, window_group(): jnp.where(allowed[None], jnp.exp(scores - log_total), 0.0)  2.93 us
    dot_general x4, matrix products, backward_terms(): jnp.einsum('hrk,rhe->ke', dscore, query_heads, preferred_element_type=jnp...  2.77 us
    dot_general x4, matrix products, backward_terms(): jnp.einsum('hrk,rhe->ke', weights, dout_heads, preferred_element_type=jnp...  2.75 us
    dot_general x4, matrix products, backward_terms(): jnp.einsum('rhe,ke->hrk', dout_heads, values, preferred_element_type=jnp....  2.43 us
  transfers between devices with their start and end apart: 8, of which 2 were waited for; matrix products, arithmetic and copies ran while one was open for 13% of the time, Pallas kernels for 0%

commit v1 on v0

v1 whole, which is shorter than its diff:
```python
import functools
import math

import jax
import jax.numpy as jnp
from jax import lax
from jax.experimental import pallas as pl
from jax.experimental.pallas import tpu as pltpu
from jax.sharding import PartitionSpec as P

HD = 128
TQ = 128

masked_score = -1e30
VMEM_LIMIT = 48 * 1024 * 1024


def dot_nt(a, b):
    return lax.dot_general(a, b, (((1,), (1,)), ((), ())), preferred_element_type=jnp.float32)


def dot_nn(a, b):
    return lax.dot_general(a, b, (((1,), (0,)), ((), ())), preferred_element_type=jnp.float32)


def pack_kernel(rows, meta, key, value, near_out, far_out, sems):
    copies = []
    for slot, (out, half) in enumerate(((near_out, meta[1]), (far_out, meta[0]))):
        start = pl.multiple_of(half * rows, rows)
        for part, src in enumerate((key, value)):
            copies.append(
                pltpu.make_async_copy(
                    src.at[pl.ds(start, rows)],
                    out.at[pl.ds(part * rows, rows)],
                    sems.at[2 * slot + part],
                )
            )
    for copy in copies:
        copy.start()
    for copy in copies:
        copy.wait()


def pack_blocks(meta, key, value):
    rows = key.shape[0] // 2
    shape = jax.ShapeDtypeStruct((2 * rows, HD), key.dtype)
    return pl.pallas_call(
        functools.partial(pack_kernel, rows),
        out_shape=(shape, shape),
        grid_spec=pltpu.PrefetchScalarGridSpec(
            num_scalar_prefetch=1,
            grid=(1,),
            in_specs=[pl.BlockSpec(memory_space=pl.ANY)] * 2,
            out_specs=[pl.BlockSpec(memory_space=pl.ANY)] * 2,
            scratch_shapes=[pltpu.SemaphoreType.DMA((4,))],
        ),
        name="pack_blocks",
    )(meta, key, value)


def window_kernel(
    rows,
    heads,
    docs,
    slot,
    meta,
    doc_lengths,
    query,
    dout,
    key_own,
    value_own,
    prev1,
    prev2,
    *refs,
):
    if slot == 1:
        refs = refs[2:]
    (attended, grad_query, own_out, prev1_out, prev2_out) = refs[:5]
    (keys, values, keys_t, values_t, doc_start, scores, dprobs, weights, dscores, dk, dv) = refs[5:]
    step = pl.program_id(0)
    steps = pl.num_programs(0)
    back = 2 * rows
    width = back + TQ
    scale = 1.0 / math.sqrt(HD)
    base2 = scale * math.log2(math.e)
    block_pos = meta[2 + slot] * rows

    @pl.when(step == 0)
    def _():
        keys[0:rows] = prev2[0:rows]
        keys[rows:back] = prev1[0:rows]
        keys[back : back + rows] = key_own[...]
        values[0:rows] = prev2[rows : 2 * rows]
        values[rows:back] = prev1[rows : 2 * rows]
        values[back : back + rows] = value_own[...]
        for tile in range((back + rows) // TQ):
            part = pl.ds(tile * TQ, TQ)
            keys_t[:, part] = jnp.transpose(keys[part, :])
            values_t[:, part] = jnp.transpose(values[part, :])
        dk[...] = jnp.zeros_like(dk)
        dv[...] = jnp.zeros_like(dv)
        at = (
            block_pos
            + lax.broadcasted_iota(jnp.int32, (8, TQ), 0) * TQ
            + lax.broadcasted_iota(jnp.int32, (8, TQ), 1)
        )

        def one(index, carry):
            start, found = carry
            found = jnp.where(at >= start, start, found)
            return (start + doc_lengths[index], found)

        _, found = lax.fori_loop(
            0, docs, one, (jnp.int32(0), jnp.zeros((8, TQ), jnp.int32)), unroll=8
        )
        doc_start[...] = found

    first = pl.multiple_of(step * TQ, TQ)
    window = pl.ds(first, width)
    query_rows = jnp.concatenate([query[:, h * HD : (h + 1) * HD] for h in range(heads)], axis=0)
    dout_rows = jnp.concatenate([dout[:, h * HD : (h + 1) * HD] for h in range(heads)], axis=0)
    scores[...] = dot_nt(keys[window, :], query_rows)
    dprobs[...] = dot_nt(values[window, :], dout_rows)

    window_pos = block_pos - back + first
    low = doc_start[pl.ds(step, 1), :] - window_pos
    high = lax.broadcasted_iota(jnp.int32, (1, TQ), 1) + back
    chunk = TQ
    row_max = jnp.full((1, heads * TQ), masked_score, jnp.float32)
    for start in range(0, width, chunk):
        at = lax.broadcasted_iota(jnp.int32, (chunk, TQ), 0) + start
        allowed = at >= low
        if start >= back:
            allowed = jnp.logical_and(allowed, at <= high)
        allowed = jnp.concatenate([allowed] * heads, axis=1)
        part = jnp.where(allowed, scores[start : start + chunk, :], masked_score)
        scores[start : start + chunk, :] = part
        row_max = jnp.maximum(row_max, jnp.max(part, axis=0, keepdims=True))
    row_max = row_max * base2
    total = jnp.zeros((1, heads * TQ), jnp.float32)
    delta = jnp.zeros((1, heads * TQ), jnp.float32)
    for start in range(0, width, chunk):
        part = jnp.exp2(scores[start : start + chunk, :] * base2 - row_max)
        scores[start : start + chunk, :] = part
        total = total + jnp.sum(part, axis=0, keepdims=True)
        delta = delta + jnp.sum(part * dprobs[start : start + chunk, :], axis=0, keepdims=True)
    inverse = 1.0 / total
    delta = delta * inverse
    for start in range(0, width, chunk):
        part = scores[start : start + chunk, :] * inverse
        weights[start : start + chunk, :] = part.astype(jnp.bfloat16)
        dscores[start : start + chunk, :] = (
            part * (dprobs[start : start + chunk, :] - delta)
        ).astype(jnp.bfloat16)
    dv[window, :] += dot_nn(weights[...], dout_rows)
    dk[window, :] += dot_nn(dscores[...], query_rows)
    attended_t = dot_nn(values_t[:, window], weights[...])
    grad_query_t = dot_nn(keys_t[:, window], dscores[...]) * scale
    for h in range(heads):
        part = slice(h * TQ, (h + 1) * TQ)
        columns = slice(h * HD, (h + 1) * HD)
        attended[:, columns] = jnp.transpose(attended_t[:, part]).astype(attended.dtype)
        grad_query[:, columns] = jnp.transpose(grad_query_t[:, part]).astype(grad_query.dtype)

    @pl.when(step == steps - 1)
    def _():
        prev2_out[0:rows] = (dk[0:rows] * scale).astype(prev2_out.dtype)
        prev2_out[rows : 2 * rows] = dv[0:rows].astype(prev2_out.dtype)
        prev1_out[0:rows] = (dk[rows:back] * scale).astype(prev1_out.dtype)
        prev1_out[rows : 2 * rows] = dv[rows:back].astype(prev1_out.dtype)
        own_out[0:rows] = dk[back : back + rows] * scale
        own_out[rows : 2 * rows] = dv[back : back + rows]


def window_block(slot, meta, doc_lengths, query, dout, key, value, prev1, prev2, filled):
    rows = key.shape[0] // 2
    heads = query.shape[1] // HD
    steps = rows // TQ
    wide = heads * HD
    tall = 3 * rows
    width = 2 * rows + TQ
    q_spec = pl.BlockSpec((TQ, wide), lambda i, meta, docs: (meta[slot] * steps + i, 0))
    own_spec = pl.BlockSpec((rows, HD), lambda i, meta, docs: (meta[slot], 0))
    whole = pl.BlockSpec((2 * rows, HD), lambda i, meta, docs: (0, 0))
    pair = jax.ShapeDtypeStruct((2 * rows, HD), jnp.bfloat16)
    inputs = [query, dout, key, value, prev1, prev2]
    in_specs = [q_spec, q_spec, own_spec, own_spec, whole, whole]
    aliases = {}
    if filled:
        aliases = {2 + len(inputs): 0, 3 + len(inputs): 1}
        inputs += list(filled)
        in_specs += [pl.BlockSpec(memory_space=pl.ANY)] * 2
    flops = 6 * 2 * steps * width * heads * TQ * HD
    return pl.pallas_call(
        functools.partial(window_kernel, rows, heads, doc_lengths.shape[0], slot),
        out_shape=(
            jax.ShapeDtypeStruct(query.shape, query.dtype),
            jax.ShapeDtypeStruct(query.shape, query.dtype),
            jax.ShapeDtypeStruct((2 * rows, HD), jnp.float32),
            pair,
            pair,
        ),
        grid_spec=pltpu.PrefetchScalarGridSpec(
            num_scalar_prefetch=2,
            grid=(steps,),
            in_specs=in_specs,
            out_specs=[q_spec, q_spec, whole, whole, whole],
            scratch_shapes=[
                pltpu.VMEM((tall, HD), jnp.bfloat16),
                pltpu.VMEM((tall, HD), jnp.bfloat16),
                pltpu.VMEM((HD, tall), jnp.bfloat16),
                pltpu.VMEM((HD, tall), jnp.bfloat16),
                pltpu.VMEM((8, TQ), jnp.int32),
                pltpu.VMEM((width, heads * TQ), jnp.float32),
                pltpu.VMEM((width, heads * TQ), jnp.float32),
                pltpu.VMEM((width, heads * TQ), jnp.bfloat16),
                pltpu.VMEM((width, heads * TQ), jnp.bfloat16),
                pltpu.VMEM((tall, HD), jnp.float32),
                pltpu.VMEM((tall, HD), jnp.float32),
            ],
        ),
        input_output_aliases=aliases,
        compiler_params=pltpu.CompilerParams(vmem_limit_bytes=VMEM_LIMIT),
        cost_estimate=pl.CostEstimate(
            flops=2 * flops, bytes_accessed=4 * rows * wide * 2, transcendentals=0
        ),
        name="window_far" if slot == 0 else "window_near",
    )(meta, doc_lengths, *inputs)


def total_kernel(rows, meta, far_own, far_1, far_2, near_own, near_1, grad_key, grad_value):
    far = far_own[...] + far_1[...].astype(jnp.float32) + far_2[...].astype(jnp.float32)
    near = near_own[...] + near_1[...].astype(jnp.float32)
    for total, half in ((far, meta[0]), (near, meta[1])):
        place = pl.ds(pl.multiple_of(half * rows, rows), rows)
        grad_key[place, :] = total[0:rows].astype(grad_key.dtype)
        grad_value[place, :] = total[rows : 2 * rows].astype(grad_value.dtype)


def total_grads(meta, far_own, far_1, far_2, near_own, near_1):
    rows = far_own.shape[0] // 2
    whole = pl.BlockSpec((2 * rows, HD), lambda i, meta: (0, 0))
    shape = jax.ShapeDtypeStruct((2 * rows, HD), jnp.bfloat16)
    return pl.pallas_call(
        functools.partial(total_kernel, rows),
        out_shape=(shape, shape),
        grid_spec=pltpu.PrefetchScalarGridSpec(
            num_scalar_prefetch=1,
            grid=(1,),
            in_specs=[whole] * 5,
            out_specs=[whole] * 2,
        ),
        compiler_params=pltpu.CompilerParams(vmem_limit_bytes=VMEM_LIMIT),
        name="total_grads",
    )(meta, far_own, far_1, far_2, near_own, near_1)


def body(query, key, value, d_out, doc_lengths):
    count = lax.axis_size("ctx")
    device = lax.axis_index("ctx").astype(jnp.int32)
    odd = device % 2
    mirror = 2 * count - 1 - device
    meta = jnp.stack(
        [odd, 1 - odd, jnp.where(odd == 0, device, mirror), jnp.where(odd == 0, mirror, device)]
    ).astype(jnp.int32)

    def holder(block):
        return block if block < count else 2 * count - 1 - block

    def move(array, pairs):
        return lax.ppermute(array, "ctx", pairs)

    near_on = [(holder(b), holder(b + 2)) for b in range(1, 2 * count - 2, 2)]
    far_on = [(holder(b), holder(b + 2)) for b in range(0, 2 * count - 2, 2)]
    swap = [(d, d ^ 1) for d in range(count)]
    near_back = [(t, s) for s, t in near_on]
    far_back = [(t, s) for s, t in far_on]

    near_kv, far_kv = pack_blocks(meta, key, value)
    near_2 = move(near_kv, near_on)
    far_2 = move(far_kv, far_on)
    near_1 = move(far_kv, swap)
    far_1 = move(near_2, swap)

    attended, grad_query, far_own, far_g1, far_g2 = window_block(
        0, meta, doc_lengths, query, d_out, key, value, far_1, far_2, None
    )
    from_far_2 = move(far_g2, far_back)
    relayed = move(far_g1, swap)
    attended, grad_query, near_own, near_g1, near_g2 = window_block(
        1, meta, doc_lengths, query, d_out, key, value, near_1, near_2, (attended, grad_query)
    )
    near_sum = (near_g2.astype(jnp.float32) + relayed.astype(jnp.float32)).astype(jnp.bfloat16)
    from_near_2 = move(near_sum, near_back)
    from_near_1 = move(near_g1, swap)
    grad_key, grad_value = total_grads(
        meta, far_own, from_near_1, from_far_2, near_own, from_near_2
    )
    return (attended, grad_query, grad_key, grad_value)


def solution(mesh):
    rows = P(("dp", "ctx"), None)
    return jax.shard_map(
        body,
        mesh=mesh,
        in_specs=(rows, rows, rows, rows, P("dp")),
        out_specs=(rows, rows, rows, rows),
        check_vma=False,
    )
```

time: 87.2 us -> 64.2 us (0.74)
  the two profiles are of different devices: /device:TPU:25 before, /device:TPU:0 now
where the time goes in v1:
time: 64.2 us; the launch traced here: 63.9 us
  Pallas kernels  31.4 us (49%)
  starting transfers between devices  17.4 us (27%)
  waiting for transfers between devices  11.5 us (18%)
  local copies, waits for them, and re-layouts  2.28 us (4%)
  between operations  0.75 us (1%)
    ppermute x8, starting transfers between devices, move(): return lax.ppermute(array, 'ctx', pairs)  17.4 us
    pallas_call x2, Pallas kernels, window_block(): pl.pallas_call(functools.partial(window_kernel, rows, heads, doc_lengths....  16.2 us
    pallas_call x1, Pallas kernels, pack_blocks(): pl.pallas_call(functools.partial(pack_kernel, rows), out_shape=(shape, sh...  13.8 us
    ppermute x8, waiting for transfers between devices, move(): return lax.ppermute(array, 'ctx', pairs)  11.5 us
    unnamed x12, local copies, waits for them, and re-layouts  2.28 us
    pallas_call x1, Pallas kernels, total_grads(): pl.pallas_call(functools.partial(total_kernel, rows), out_shape=(shape, s...  1.38 us
  transfers between devices with their start and end apart: 8, of which 3 were waited for; matrix products, arithmetic and copies ran while one was open for 0% of the time, Pallas kernels for 25%

profile of v1, /device:TPU:0, one launch (start us, length us, event | category | flops | bytes accessed | tf_op | source)
XLA Modules:
  0.0 63.9 jit_solution(4910029819349300660)
XLA Ops:
  0.6 0.6 pad_add_fusion.meta
  1.2 0.0 copy-start
  1.2 0.0 copy-start.1
  1.2 13.8 %pack_blocks.1 = (bf16[768,128]{1,0:T(8,128)(2,1)}, bf16[768,128]{1,0:T(8,128)(2,1)}) custom-call(s32[4]{0:T(128)} %pad_add_fusion.meta, bf16[768,128]{1,0:T(8,128)(2,1)} %key_own.3, bf16[768,128]{1,0:T(8,128)(2,1)} %value_own.3), custom_call_target="tpu_custom_call" | custom-call | tf_op jit(solution)/shard_map/pack_blocks/pallas_call | solution.py:47
  15.1 0.0 copy-start.2
  15.1 0.0 copy-start.5
  15.1 1.3 %collective-permute-start.1 = (bf16[768,128]{1,0:T(8,128)(2,1)}, bf16[768,128]{1,0:T(8,128)(2,1)S(1)}, u32[]{:S(2)}, u32[]{:S(2)}) collective-permute-start(bf16[768,128]{1,0:T(8,128)(2,1)} %get-tuple-element.19), channel_id=1, source_target_pairs={{1,3},{3,5},{5,7},{7,9},{9,11},{11,13},{13,15},{15,14},{14,12},{12... | collective-permute-start | bytes 589832 | tf_op jit(solution)/shard_map/ppermute | solution.py:271
  16.4 5.5 %collective-permute-start.3 = (bf16[768,128]{1,0:T(8,128)(2,1)}, bf16[768,128]{1,0:T(8,128)(2,1)S(1)}, u32[]{:S(2)}, u32[]{:S(2)}) collective-permute-start(bf16[768,128]{1,0:T(8,128)(2,1)} %get-tuple-element.18), channel_id=1, source_target_pairs={{0,2},{2,4},{4,6},{6,8},{8,10},{10,12},{12,14},{14,15},{15,13},{13... | collective-permute-start | bytes 589832 | tf_op jit(solution)/shard_map/ppermute | solution.py:271
  21.9 1.9 %collective-permute-done.1.prev2 = bf16[768,128]{1,0:T(8,128)(2,1)S(1)} collective-permute-done((bf16[768,128]{1,0:T(8,128)(2,1)}, bf16[768,128]{1,0:T(8,128)(2,1)S(1)}, u32[]{:S(2)}, u32[]{:S(2)}) %collective-permute-start.1) | collective-permute-done | bytes 196640 | tf_op jit(solution)/shard_map/ppermute | solution.py:271
  23.8 0.0 collective-permute-start.2
  23.8 0.5 collective-permute-start
  24.3 4.3 %collective-permute-done.3.prev2 = bf16[768,128]{1,0:T(8,128)(2,1)S(1)} collective-permute-done((bf16[768,128]{1,0:T(8,128)(2,1)}, bf16[768,128]{1,0:T(8,128)(2,1)S(1)}, u32[]{:S(2)}, u32[]{:S(2)}) %collective-permute-start.3) | collective-permute-done | bytes 196640 | tf_op jit(solution)/shard_map/ppermute | solution.py:271
  28.6 0.0 collective-permute-done.2.prev1
  28.6 0.0 copy-done
  28.6 0.0 copy-done.1
  28.6 0.0 copy-done.2
  28.6 0.0 copy-done.5
  28.7 0.0 copy-start.3
  28.7 1.1 %copy-done.3 = bf16[768,512]{1,0:T(8,128)(2,1)S(1)} copy-done((bf16[768,512]{1,0:T(8,128)(2,1)S(1)}, bf16[768,512]{1,0:T(8,128)(2,1)}, u32[]{:S(2)}) %copy-start.3) | copy-done | bytes 786456
  29.8 0.0 copy-start.4
  29.8 1.1 %copy-done.4 = bf16[768,512]{1,0:T(8,128)(2,1)S(1)} copy-done((bf16[768,512]{1,0:T(8,128)(2,1)S(1)}, bf16[768,512]{1,0:T(8,128)(2,1)}, u32[]{:S(2)}) %copy-start.4) | copy-done | bytes 786456
  30.9 8.1 %window_far.1 = (bf16[768,512]{1,0:T(8,128)(2,1)}, bf16[768,512]{1,0:T(8,128)(2,1)}, f32[768,128]{1,0:T(8,128)S(1)}, bf16[768,128]{1,0:T(8,128)(2,1)S(1)}, bf16[768,128]{1,0:T(8,128)(2,1)S(1)}) custom-call(s32[4]{0:T(128)S(1)} %copy-done.2, s32[32]{0:T(128)S(1)} %copy-done.5, bf16[768,512]{1,0:T(8,128)(2,1)S(1)} %copy-done.3, ...), custom_call_target="tpu_custom_call" | custom-call | flops 4227858432 | bytes 1572864 | tf_op jit(solution)/shard_map/window_far/pallas_call | solution.py:194
  39.0 1.3 %collective-permute-start.5 = (bf16[768,128]{1,0:T(8,128)(2,1)S(1)}, bf16[768,128]{1,0:T(8,128)(2,1)S(1)}, u32[]{:S(2)}, u32[]{:S(2)}) collective-permute-start(bf16[768,128]{1,0:T(8,128)(2,1)S(1)} %get-tuple-element.26), channel_id=1, source_target_pairs={{2,0},{4,2},{6,4},{8,6},{10,8},{12,10},{14,12},{15,14},{13,15},{11... | collective-permute-start | bytes 589832 | tf_op jit(solution)/shard_map/ppermute | solution.py:271
  40.3 0.6 collective-permute-start.6
  40.9 0.0 collective-permute-done.prev1
  40.9 8.1 %window_near.1 = (bf16[768,512]{1,0:T(8,128)(2,1)}, bf16[768,512]{1,0:T(8,128)(2,1)}, f32[768,128]{1,0:T(8,128)S(1)}, bf16[768,128]{1,0:T(8,128)(2,1)S(1)}, bf16[768,128]{1,0:T(8,128)(2,1)S(1)}) custom-call(s32[4]{0:T(128)S(1)} %copy-done.2, s32[32]{0:T(128)S(1)} %copy-done.5, ...), custom_call_target="tpu_custom_call", output_to_operand_aliasing={{0}: (8, {}), {1}: (9, {})} | custom-call | flops 4227858432 | bytes 1572864 | tf_op jit(solution)/shard_map/window_near/pallas_call | solution.py:194
  49.0 0.0 collective-permute-start.4
  49.0 0.0 collective-permute-done.6
  49.0 0.1 add_convert_fusion
  49.1 8.2 %collective-permute-start.7 = (bf16[768,128]{1,0:T(8,128)(2,1)S(1)}, bf16[768,128]{1,0:T(8,128)(2,1)S(1)}, u32[]{:S(2)}, u32[]{:S(2)}) collective-permute-start(bf16[768,128]{1,0:T(8,128)(2,1)S(1)} %add_convert_fusion), channel_id=1, source_target_pairs={{3,1},{5,3},{7,5},{9,7},{11,9},{13,11},{15,13},{14,15},{12,14},{10... | collective-permute-start | bytes 589832 | tf_op jit(solution)/shard_map/ppermute | solution.py:271
  57.3 0.0 collective-permute-done.5.far_2
  57.3 0.0 collective-permute-done.4.far_1
  57.3 5.2 %collective-permute-done.7.near_1 = bf16[768,128]{1,0:T(8,128)(2,1)S(1)} collective-permute-done((bf16[768,128]{1,0:T(8,128)(2,1)S(1)}, bf16[768,128]{1,0:T(8,128)(2,1)S(1)}, u32[]{:S(2)}, u32[]{:S(2)}) %collective-permute-start.7) | collective-permute-done | bytes 196640 | tf_op jit(solution)/shard_map/ppermute | solution.py:271
  62.6 1.4 %total_grads.1 = (bf16[768,128]{1,0:T(8,128)(2,1)}, bf16[768,128]{1,0:T(8,128)(2,1)}) custom-call(s32[4]{0:T(128)S(1)} %copy-done.2, f32[768,128]{1,0:T(8,128)S(1)} %get-tuple-element.24.far_own, bf16[768,128]{1,0:T(8,128)(2,1)S(1)} %collective-permute-done.4.far_1, bf16[768,128]{1,0:T(8,128)(2,1)S(1)} %collective-permute-done.5.far_2, ...), custom_call_target="tpu_custom_call" | custom-call | tf_op jit(solution)/shard_map/total_grads/pallas_call | solution.py:244
Async XLA Ops:
  1.2 27.4 %copy-start = (bf16[768,128]{1,0:T(8,128)(2,1)S(1)}, bf16[768,128]{1,0:T(8,128)(2,1)}, u32[]{:S(2)}) copy-start(bf16[768,128]{1,0:T(8,128)(2,1)} %key_own.3) | copy-start | bytes 589828
  1.2 27.4 %copy-start.1 = (bf16[768,128]{1,0:T(8,128)(2,1)S(1)}, bf16[768,128]{1,0:T(8,128)(2,1)}, u32[]{:S(2)}) copy-start(bf16[768,128]{1,0:T(8,128)(2,1)} %value_own.3) | copy-start | bytes 589828
  15.1 13.6 %copy-start.2 = (s32[4]{0:T(128)S(1)}, s32[4]{0:T(128)}, u32[]{:S(2)}) copy-start(s32[4]{0:T(128)} %pad_add_fusion.meta) | copy-start | bytes 52
  15.1 13.6 %copy-start.5 = (s32[32]{0:T(128)S(1)}, s32[32]{0:T(128)}, u32[]{:S(2)}) copy-start(s32[32]{0:T(128)} %doc_lengths.3) | copy-start | bytes 388
  15.1 8.7 %collective-permute-start.1 = (bf16[768,128]{1,0:T(8,128)(2,1)}, bf16[768,128]{1,0:T(8,128)(2,1)S(1)}, u32[]{:S(2)}, u32[]{:S(2)}) collective-permute-start(bf16[768,128]{1,0:T(8,128)(2,1)} %get-tuple-element.19), channel_id=1, source_target_pairs={{1,3},{3,5},{5,7},{7,9},{9,11},{11,13},{13,15},{15,14},{14,12},{12... | collective-permute-start | bytes 589832 | tf_op jit(solution)/shard_map/ppermute | solution.py:271
  16.4 12.2 %collective-permute-start.3 = (bf16[768,128]{1,0:T(8,128)(2,1)}, bf16[768,128]{1,0:T(8,128)(2,1)S(1)}, u32[]{:S(2)}, u32[]{:S(2)}) collective-permute-start(bf16[768,128]{1,0:T(8,128)(2,1)} %get-tuple-element.18), channel_id=1, source_target_pairs={{0,2},{2,4},{4,6},{6,8},{8,10},{10,12},{12,14},{14,15},{15,13},{13... | collective-permute-start | bytes 589832 | tf_op jit(solution)/shard_map/ppermute | solution.py:271
  23.8 4.8 %collective-permute-start.2 = (bf16[768,128]{1,0:T(8,128)(2,1)S(1)}, bf16[768,128]{1,0:T(8,128)(2,1)S(1)}, u32[]{:S(2)}, u32[]{:S(2)}) collective-permute-start(bf16[768,128]{1,0:T(8,128)(2,1)S(1)} %collective-permute-done.1.prev2), channel_id=1, source_target_pairs={{0,1},{1,0},{2,3},{3,2},{4,5},{5,4},{6,7},{7,6},{8,9},{9,8},{10,11... | collective-permute-start | bytes 589832 | tf_op jit(solution)/shard_map/ppermute | solution.py:271
  23.8 17.1 %collective-permute-start = (bf16[768,128]{1,0:T(8,128)(2,1)}, bf16[768,128]{1,0:T(8,128)(2,1)S(1)}, u32[]{:S(2)}, u32[]{:S(2)}) collective-permute-start(bf16[768,128]{1,0:T(8,128)(2,1)} %get-tuple-element.18), channel_id=1, source_target_pairs={{0,1},{1,0},{2,3},{3,2},{4,5},{5,4},{6,7},{7,6},{8,9},{9,8},{10,11... | collective-permute-start | bytes 589832 | tf_op jit(solution)/shard_map/ppermute | solution.py:271
  28.7 1.1 %copy-start.3 = (bf16[768,512]{1,0:T(8,128)(2,1)S(1)}, bf16[768,512]{1,0:T(8,128)(2,1)}, u32[]{:S(2)}) copy-start(bf16[768,512]{1,0:T(8,128)(2,1)} %query.3) | copy-start | bytes 2359300
  29.8 1.1 %copy-start.4 = (bf16[768,512]{1,0:T(8,128)(2,1)S(1)}, bf16[768,512]{1,0:T(8,128)(2,1)}, u32[]{:S(2)}) copy-start(bf16[768,512]{1,0:T(8,128)(2,1)} %dout.3) | copy-start | bytes 2359300
  39.0 18.3 %collective-permute-start.5 = (bf16[768,128]{1,0:T(8,128)(2,1)S(1)}, bf16[768,128]{1,0:T(8,128)(2,1)S(1)}, u32[]{:S(2)}, u32[]{:S(2)}) collective-permute-start(bf16[768,128]{1,0:T(8,128)(2,1)S(1)} %get-tuple-element.26), channel_id=1, source_target_pairs={{2,0},{4,2},{6,4},{8,6},{10,8},{12,10},{14,12},{15,14},{13,15},{11... | collective-permute-start | bytes 589832 | tf_op jit(solution)/shard_map/ppermute | solution.py:271
  40.3 8.7 %collective-permute-start.6 = (bf16[768,128]{1,0:T(8,128)(2,1)S(1)}, bf16[768,128]{1,0:T(8,128)(2,1)S(1)}, u32[]{:S(2)}, u32[]{:S(2)}) collective-permute-start(bf16[768,128]{1,0:T(8,128)(2,1)S(1)} %get-tuple-element.29), channel_id=1, source_target_pairs={{0,1},{1,0},{2,3},{3,2},{4,5},{5,4},{6,7},{7,6},{8,9},{9,8},{10,11... | collective-permute-start | bytes 589832 | tf_op jit(solution)/shard_map/ppermute | solution.py:271
  49.0 8.3 %collective-permute-start.4 = (bf16[768,128]{1,0:T(8,128)(2,1)S(1)}, bf16[768,128]{1,0:T(8,128)(2,1)S(1)}, u32[]{:S(2)}, u32[]{:S(2)}) collective-permute-start(bf16[768,128]{1,0:T(8,128)(2,1)S(1)} %get-tuple-element.25), channel_id=1, source_target_pairs={{0,1},{1,0},{2,3},{3,2},{4,5},{5,4},{6,7},{7,6},{8,9},{9,8},{10,11... | collective-permute-start | bytes 589832 | tf_op jit(solution)/shard_map/ppermute | solution.py:271
  49.1 13.5 %collective-permute-start.7 = (bf16[768,128]{1,0:T(8,128)(2,1)S(1)}, bf16[768,128]{1,0:T(8,128)(2,1)S(1)}, u32[]{:S(2)}, u32[]{:S(2)}) collective-permute-start(bf16[768,128]{1,0:T(8,128)(2,1)S(1)} %add_convert_fusion), channel_id=1, source_target_pairs={{3,1},{5,3},{7,5},{9,7},{11,9},{13,11},{15,13},{14,15},{12,14},{10... | collective-permute-start | bytes 589832 | tf_op jit(solution)/shard_map/ppermute | solution.py:271

commit v2 on v1

v2 whole, which is shorter than its diff:
```python
import functools
import math

import jax
import jax.numpy as jnp
from jax import lax
from jax.experimental import pallas as pl
from jax.experimental.pallas import tpu as pltpu
from jax.sharding import PartitionSpec as P

HD = 128
TQ = 128

masked_score = -1e30
VMEM_LIMIT = 24 * 1024 * 1024
SCALE = 1.0 / math.sqrt(HD)
VMEM = pl.BlockSpec(memory_space=pltpu.VMEM)
SMEM = pl.BlockSpec(memory_space=pltpu.SMEM)


def dot_nt(a, b):
    return lax.dot_general(a, b, (((1,), (1,)), ((), ())), preferred_element_type=jnp.float32)


def dot_nn(a, b):
    return lax.dot_general(a, b, (((1,), (0,)), ((), ())), preferred_element_type=jnp.float32)


def half_start(rows, slot):
    odd = lax.axis_index("ctx") % 2
    return pl.multiple_of((odd if slot == 0 else 1 - odd) * rows, rows)


def block_number(count, slot):
    device = lax.axis_index("ctx")
    in_lower = device % 2 == slot
    return jnp.where(in_lower, device, 2 * count - 1 - device)


def pack_kernel(rows, key, value, near_out, far_out):
    for slot, out in ((1, near_out), (0, far_out)):
        place = pl.ds(half_start(rows, slot), rows)
        out[0:rows] = key[place, :]
        out[rows : 2 * rows] = value[place, :]


def pack_blocks(key, value):
    rows = key.shape[0] // 2
    shape = jax.ShapeDtypeStruct((2 * rows, HD), key.dtype)
    return pl.pallas_call(
        functools.partial(pack_kernel, rows),
        out_shape=(shape, shape),
        in_specs=[VMEM] * 2,
        out_specs=[VMEM] * 2,
        name="pack_blocks",
    )(key, value)


def head_rows(array, first, heads):
    return jnp.concatenate(
        [array[pl.ds(first, TQ), h * HD : (h + 1) * HD] for h in range(heads)], axis=0
    )


def scores_kernel(
    rows,
    heads,
    docs,
    count,
    slot,
    doc_lengths,
    query,
    dout,
    own_kv,
    prev1,
    prev2,
    weights,
    dscores,
    prev1_out,
    prev2_out,
    keys,
    values,
    scores,
    dprobs,
    dk,
    dv,
):
    back = 2 * rows
    width = back + TQ
    base2 = SCALE * math.log2(math.e)
    block_pos = block_number(count, slot) * rows
    own_rows = half_start(rows, slot)

    for place, source in enumerate((prev2, prev1, own_kv)):
        keys[place * rows : (place + 1) * rows] = source[0:rows]
        values[place * rows : (place + 1) * rows] = source[rows : 2 * rows]
    at = (
        block_pos
        + lax.broadcasted_iota(jnp.int32, (8, TQ), 0) * TQ
        + lax.broadcasted_iota(jnp.int32, (8, TQ), 1)
    )

    def one(index, carry):
        start, found = carry
        found = jnp.where(at >= start, start, found)
        return (start + doc_lengths[index], found)

    _, doc_start = lax.fori_loop(
        0, docs, one, (jnp.int32(0), jnp.zeros((8, TQ), jnp.int32)), unroll=8
    )

    for step in range(rows // TQ):
        first = step * TQ
        query_rows = head_rows(query, own_rows + first, heads)
        dout_rows = head_rows(dout, own_rows + first, heads)
        scores[...] = dot_nt(keys[first : first + width, :], query_rows)
        dprobs[...] = dot_nt(values[first : first + width, :], dout_rows)

        low = doc_start[step : step + 1, :] - (block_pos - back + first)
        high = lax.broadcasted_iota(jnp.int32, (1, TQ), 1) + back
        chunk = TQ
        row_max = jnp.full((1, heads * TQ), masked_score, jnp.float32)
        for start in range(0, width, chunk):
            at = lax.broadcasted_iota(jnp.int32, (chunk, TQ), 0) + start
            allowed = at >= low
            if start >= back:
                allowed = jnp.logical_and(allowed, at <= high)
            allowed = jnp.concatenate([allowed] * heads, axis=1)
            part = jnp.where(allowed, scores[start : start + chunk, :], masked_score)
            scores[start : start + chunk, :] = part
            row_max = jnp.maximum(row_max, jnp.max(part, axis=0, keepdims=True))
        row_max = row_max * base2
        total = jnp.zeros((1, heads * TQ), jnp.float32)
        delta = jnp.zeros((1, heads * TQ), jnp.float32)
        for start in range(0, width, chunk):
            part = jnp.exp2(scores[start : start + chunk, :] * base2 - row_max)
            scores[start : start + chunk, :] = part
            total = total + jnp.sum(part, axis=0, keepdims=True)
            delta = delta + jnp.sum(part * dprobs[start : start + chunk, :], axis=0, keepdims=True)
        inverse = 1.0 / total
        delta = delta * inverse
        out = step * width
        for start in range(0, width, chunk):
            part = scores[start : start + chunk, :] * inverse
            weights[out + start : out + start + chunk, :] = part.astype(jnp.bfloat16)
            dscores[out + start : out + start + chunk, :] = (
                part * (dprobs[start : start + chunk, :] - delta)
            ).astype(jnp.bfloat16)
        for total_ref, terms, side in ((dv, weights, dout_rows), (dk, dscores, query_rows)):
            term = dot_nn(terms[out : out + back - first, :], side)
            if step == 0:
                total_ref[...] = term
            else:
                total_ref[first:back] += term

    prev2_out[0:rows] = (dk[0:rows] * SCALE).astype(prev2_out.dtype)
    prev2_out[rows:back] = dv[0:rows].astype(prev2_out.dtype)
    prev1_out[0:rows] = (dk[rows:back] * SCALE).astype(prev1_out.dtype)
    prev1_out[rows:back] = dv[rows:back].astype(prev1_out.dtype)


def block_scores(slot, count, doc_lengths, query, dout, own_kv, prev1, prev2):
    rows = query.shape[0] // 2
    heads = query.shape[1] // HD
    steps = rows // TQ
    width = 2 * rows + TQ
    pair = jax.ShapeDtypeStruct((2 * rows, HD), jnp.bfloat16)
    kept = jax.ShapeDtypeStruct((steps * width, heads * TQ), jnp.bfloat16)
    return pl.pallas_call(
        functools.partial(scores_kernel, rows, heads, doc_lengths.shape[0], count, slot),
        out_shape=(kept, kept, pair, pair),
        in_specs=[SMEM] + [VMEM] * 5,
        out_specs=[VMEM] * 4,
        scratch_shapes=[
            pltpu.VMEM((3 * rows, HD), jnp.bfloat16),
            pltpu.VMEM((3 * rows, HD), jnp.bfloat16),
            pltpu.VMEM((width, heads * TQ), jnp.float32),
            pltpu.VMEM((width, heads * TQ), jnp.float32),
            pltpu.VMEM((2 * rows, HD), jnp.float32),
            pltpu.VMEM((2 * rows, HD), jnp.float32),
        ],
        compiler_params=pltpu.CompilerParams(vmem_limit_bytes=VMEM_LIMIT),
        cost_estimate=pl.CostEstimate(
            flops=8 * 2 * steps * width * heads * TQ * HD, bytes_accessed=0, transcendentals=0
        ),
        name="scores_far" if slot == 0 else "scores_near",
    )(doc_lengths, query, dout, own_kv, prev1, prev2)


def outputs_kernel(rows, heads, query, dout, *refs):
    blocks = (refs[0:5], refs[5:10])
    (attended, grad_query, far_own, near_own, keys_t, values_t) = refs[10:]
    back = 2 * rows
    width = back + TQ
    for slot, (own_kv, prev1, prev2, weights, dscores) in enumerate(blocks):
        own_out = (far_own, near_own)[slot]
        own_rows = half_start(rows, slot)
        for place, source in enumerate((prev2, prev1, own_kv)):
            for tile in range(rows // TQ):
                part = slice(place * rows + tile * TQ, place * rows + (tile + 1) * TQ)
                row = tile * TQ
                keys_t[:, part] = jnp.transpose(source[row : row + TQ, :])
                values_t[:, part] = jnp.transpose(source[rows + row : rows + row + TQ, :])
        for step in reversed(range(rows // TQ)):
            first = step * TQ
            out = step * width
            tail = slice(out + back - first, out + width)
            query_rows = head_rows(query, own_rows + first, heads)
            dout_rows = head_rows(dout, own_rows + first, heads)
            for offset, terms, side, factor in (
                (0, dscores, query_rows, SCALE),
                (rows, weights, dout_rows, 1.0),
            ):
                term = dot_nn(terms[tail, :], side) * factor
                place = slice(offset, offset + first + TQ)
                if step == rows // TQ - 1:
                    own_out[place] = term
                else:
                    own_out[place] += term
            window = slice(first, first + width)
            attended_t = dot_nn(values_t[:, window], weights[out : out + width, :])
            grad_query_t = dot_nn(keys_t[:, window], dscores[out : out + width, :]) * SCALE
            place = pl.ds(own_rows + first, TQ)
            for h in range(heads):
                part = slice(h * TQ, (h + 1) * TQ)
                columns = slice(h * HD, (h + 1) * HD)
                attended[place, columns] = jnp.transpose(attended_t[:, part]).astype(
                    attended.dtype
                )
                grad_query[place, columns] = jnp.transpose(grad_query_t[:, part]).astype(
                    grad_query.dtype
                )


def block_outputs(query, dout, far, near):
    rows = query.shape[0] // 2
    heads = query.shape[1] // HD
    steps = rows // TQ
    width = 2 * rows + TQ
    wide = jax.ShapeDtypeStruct(query.shape, query.dtype)
    own = jax.ShapeDtypeStruct((2 * rows, HD), jnp.float32)
    return pl.pallas_call(
        functools.partial(outputs_kernel, rows, heads),
        out_shape=(wide, wide, own, own),
        in_specs=[VMEM] * 12,
        out_specs=[VMEM] * 4,
        scratch_shapes=[
            pltpu.VMEM((HD, 3 * rows), jnp.bfloat16),
            pltpu.VMEM((HD, 3 * rows), jnp.bfloat16),
        ],
        compiler_params=pltpu.CompilerParams(vmem_limit_bytes=VMEM_LIMIT),
        cost_estimate=pl.CostEstimate(
            flops=12 * 2 * steps * width * heads * TQ * HD, bytes_accessed=0, transcendentals=0
        ),
        name="block_outputs",
    )(query, dout, *far, *near)


def total_kernel(rows, far_own, far_1, far_2, near_own, near_1, grad_key, grad_value):
    far = far_own[...] + far_1[...].astype(jnp.float32) + far_2[...].astype(jnp.float32)
    near = near_own[...] + near_1[...].astype(jnp.float32)
    for slot, total in ((0, far), (1, near)):
        place = pl.ds(half_start(rows, slot), rows)
        grad_key[place, :] = total[0:rows].astype(grad_key.dtype)
        grad_value[place, :] = total[rows : 2 * rows].astype(grad_value.dtype)


def total_grads(far_own, far_1, far_2, near_own, near_1):
    rows = far_own.shape[0] // 2
    shape = jax.ShapeDtypeStruct((2 * rows, HD), jnp.bfloat16)
    return pl.pallas_call(
        functools.partial(total_kernel, rows),
        out_shape=(shape, shape),
        in_specs=[VMEM] * 5,
        out_specs=[VMEM] * 2,
        compiler_params=pltpu.CompilerParams(vmem_limit_bytes=VMEM_LIMIT),
        name="total_grads",
    )(far_own, far_1, far_2, near_own, near_1)


def body(query, key, value, d_out, doc_lengths):
    count = lax.axis_size("ctx")

    def holder(block):
        return block if block < count else 2 * count - 1 - block

    def move(array, pairs):
        return lax.ppermute(array, "ctx", pairs)

    near_on = [(holder(b), holder(b + 2)) for b in range(1, 2 * count - 2, 2)]
    far_on = [(holder(b), holder(b + 2)) for b in range(0, 2 * count - 2, 2)]
    swap = [(d, d ^ 1) for d in range(count)]
    near_back = [(t, s) for s, t in near_on]
    far_back = [(t, s) for s, t in far_on]

    near_kv, far_kv = pack_blocks(key, value)
    near_2 = move(near_kv, near_on)
    far_2 = move(far_kv, far_on)
    near_1 = move(far_kv, swap)
    far_1 = move(near_2, swap)

    far_w, far_d, far_g1, far_g2 = block_scores(
        0, count, doc_lengths, query, d_out, far_kv, far_1, far_2
    )
    from_far_2 = move(far_g2, far_back)
    relayed = move(far_g1, swap)
    near_w, near_d, near_g1, near_g2 = block_scores(
        1, count, doc_lengths, query, d_out, near_kv, near_1, near_2
    )
    near_sum = (near_g2.astype(jnp.float32) + relayed.astype(jnp.float32)).astype(jnp.bfloat16)
    from_near_2 = move(near_sum, near_back)
    from_near_1 = move(near_g1, swap)
    attended, grad_query, far_own, near_own = block_outputs(
        query,
        d_out,
        (far_kv, far_1, far_2, far_w, far_d),
        (near_kv, near_1, near_2, near_w, near_d),
    )
    grad_key, grad_value = total_grads(far_own, from_near_1, from_far_2, near_own, from_near_2)
    return (attended, grad_query, grad_key, grad_value)


def solution(mesh):
    rows = P(("dp", "ctx"), None)
    return jax.shard_map(
        body,
        mesh=mesh,
        in_specs=(rows, rows, rows, rows, P("dp")),
        out_specs=(rows, rows, rows, rows),
        check_vma=False,
    )
```

time: 64.2 us -> 48.2 us (0.75)
  the two profiles are of different devices: /device:TPU:0 before, /device:TPU:11 now
where the time goes in v2:
time: 48.2 us; the launch traced here: 47.9 us
  starting transfers between devices  19.9 us (41%)
  Pallas kernels  17.4 us (36%)
  waiting for transfers between devices  6 us (12%)
  local copies, waits for them, and re-layouts  3.86 us (8%)
  between operations  0.72 us (1%)
    ppermute x8, starting transfers between devices, move(): return lax.ppermute(array, 'ctx', pairs)  19.9 us
    pallas_call x2, Pallas kernels, block_scores(): pl.pallas_call(functools.partial(scores_kernel, rows, heads, doc_lengths....  10.8 us
    ppermute x8, waiting for transfers between devices, move(): return lax.ppermute(array, 'ctx', pairs)  6 us
    pallas_call x1, Pallas kernels, block_outputs(): pl.pallas_call(functools.partial(outputs_kernel, rows, heads), out_shape=...  4 us
    unnamed x12, local copies, waits for them, and re-layouts  3.86 us
    pallas_call x1, Pallas kernels, pack_blocks(): pl.pallas_call(functools.partial(pack_kernel, rows), out_shape=(shape, sh...  1.79 us
  transfers between devices with their start and end apart: 8, of which 3 were waited for; matrix products, arithmetic and copies ran while one was open for 0% of the time, Pallas kernels for 31%

profile of v2, /device:TPU:11, one launch (start us, length us, event | category | flops | bytes accessed | tf_op | source)
XLA Modules:
  0.0 47.9 jit_solution(6008207204673856451)
XLA Ops:
  0.6 1.8 %pack_blocks.1 = (bf16[768,128]{1,0:T(8,128)(2,1)}, bf16[768,128]{1,0:T(8,128)(2,1)}) custom-call(bf16[768,128]{1,0:T(8,128)(2,1)} %key.1, bf16[768,128]{1,0:T(8,128)(2,1)} %value.1), custom_call_target="tpu_custom_call" | custom-call | tf_op jit(solution)/shard_map/pack_blocks/pallas_call | solution.py:50
  2.4 3.1 %collective-permute-start = (bf16[768,128]{1,0:T(8,128)(2,1)}, bf16[768,128]{1,0:T(8,128)(2,1)S(1)}, u32[]{:S(2)}, u32[]{:S(2)}) collective-permute-start(bf16[768,128]{1,0:T(8,128)(2,1)} %get-tuple-element.21.own_kv.refs_5_), channel_id=1, source_target_pairs={{1,3},{3,5},{5,7},{7,9},{9,11},{11,13},{13,15},{15,14},{14,12},{12... | collective-permute-start | bytes 589832 | tf_op jit(solution)/shard_map/ppermute | solution.py:288
  5.6 3.0 %collective-permute-start.2 = (bf16[768,128]{1,0:T(8,128)(2,1)}, bf16[768,128]{1,0:T(8,128)(2,1)S(1)}, u32[]{:S(2)}, u32[]{:S(2)}) collective-permute-start(bf16[768,128]{1,0:T(8,128)(2,1)} %get-tuple-element.20.own_kv.refs_0_), channel_id=1, source_target_pairs={{0,2},{2,4},{4,6},{6,8},{8,10},{10,12},{12,14},{14,15},{15,13},{13... | collective-permute-start | bytes 589832 | tf_op jit(solution)/shard_map/ppermute | solution.py:288
  8.6 1.4 %collective-permute-done.prev2.refs_7_ = bf16[768,128]{1,0:T(8,128)(2,1)S(1)} collective-permute-done((bf16[768,128]{1,0:T(8,128)(2,1)}, bf16[768,128]{1,0:T(8,128)(2,1)S(1)}, u32[]{:S(2)}, u32[]{:S(2)}) %collective-permute-start) | collective-permute-done | bytes 196640 | tf_op jit(solution)/shard_map/ppermute | solution.py:288
  10.0 6.8 %collective-permute-start.1 = (bf16[768,128]{1,0:T(8,128)(2,1)S(1)}, bf16[768,128]{1,0:T(8,128)(2,1)S(1)}, u32[]{:S(2)}, u32[]{:S(2)}) collective-permute-start(bf16[768,128]{1,0:T(8,128)(2,1)S(1)} %collective-permute-done.prev2.refs_7_), channel_id=1, source_target_pairs={{0,1},{1,0},{2,3},{3,2},{4,5},{5,4},{6,7},{7,6},{8,9},{9,8},{10,11... | collective-permute-start | bytes 589832 | tf_op jit(solution)/shard_map/ppermute | solution.py:288
  16.8 0.0 collective-permute-start.3
  16.8 0.0 collective-permute-done.2.prev2.refs_2_
  16.8 1.3 %collective-permute-done.1.prev1.refs_1_ = bf16[768,128]{1,0:T(8,128)(2,1)S(1)} collective-permute-done((bf16[768,128]{1,0:T(8,128)(2,1)S(1)}, bf16[768,128]{1,0:T(8,128)(2,1)S(1)}, u32[]{:S(2)}, u32[]{:S(2)}) %collective-permute-start.1) | collective-permute-done | bytes 196640 | tf_op jit(solution)/shard_map/ppermute | solution.py:288
  18.1 0.0 copy-start
  18.1 1.1 %copy-done = bf16[768,512]{1,0:T(8,128)(2,1)S(1)} copy-done((bf16[768,512]{1,0:T(8,128)(2,1)S(1)}, bf16[768,512]{1,0:T(8,128)(2,1)}, u32[]{:S(2)}) %copy-start) | copy-done | bytes 786456
  19.2 0.0 copy-start.2
  19.2 1.1 %copy-done.2 = bf16[768,512]{1,0:T(8,128)(2,1)S(1)} copy-done((bf16[768,512]{1,0:T(8,128)(2,1)S(1)}, bf16[768,512]{1,0:T(8,128)(2,1)}, u32[]{:S(2)}) %copy-start.2) | copy-done | bytes 786456
  20.4 0.0 copy-start.4
  20.4 0.9 %copy-done.4 = bf16[768,128]{1,0:T(8,128)(2,1)S(1)} copy-done((bf16[768,128]{1,0:T(8,128)(2,1)S(1)}, bf16[768,128]{1,0:T(8,128)(2,1)}, u32[]{:S(2)}) %copy-start.4) | copy-done | bytes 196632
  21.3 0.0 copy-start.5
  21.3 0.7 %copy-done.5 = s32[32]{0:T(128)S(1)} copy-done((s32[32]{0:T(128)S(1)}, s32[32]{0:T(128)}, u32[]{:S(2)}) %copy-start.5) | copy-done | bytes 152
  22.0 0.0 copy-start.3
  22.0 5.3 %scores_far.1 = (bf16[2688,512]{1,0:T(8,128)(2,1)S(1)}, bf16[2688,512]{1,0:T(8,128)(2,1)S(1)}, bf16[768,128]{1,0:T(8,128)(2,1)S(1)}, bf16[768,128]{1,0:T(8,128)(2,1)S(1)}) custom-call(s32[32]{0:T(128)S(1)} %copy-done.5, bf16[768,512]{1,0:T(8,128)(2,1)S(1)} %copy-done, bf16[768,512]{1,0:T(8,128)(2,1)S(1)} %copy-done.2, bf16[768,128]{1,0:T(8,128)(2,1)S(1)} %copy-done.4, ...), custom_call_target="tpu_custom_call" | custom-call | flops 2818572288 | tf_op jit(solution)/shard_map/scores_far/pallas_call | solution.py:169
  27.3 0.0 copy-start.1
  27.3 0.4 collective-permute-start.6
  27.7 0.0 collective-permute-done.3.prev1.refs_6_
  27.7 0.0 copy-done.3
  27.7 5.5 %scores_near.1 = (bf16[2688,512]{1,0:T(8,128)(2,1)S(1)}, bf16[2688,512]{1,0:T(8,128)(2,1)S(1)}, bf16[768,128]{1,0:T(8,128)(2,1)S(1)}, bf16[768,128]{1,0:T(8,128)(2,1)S(1)}) custom-call(s32[32]{0:T(128)S(1)} %copy-done.5, bf16[768,512]{1,0:T(8,128)(2,1)S(1)} %copy-done, bf16[768,512]{1,0:T(8,128)(2,1)S(1)} %copy-done.2, bf16[768,128]{1,0:T(8,128)(2,1)S(1)} %copy-done.3, ...), custom_call_target="tpu_custom_call" | custom-call | flops 2818572288 | tf_op jit(solution)/shard_map/scores_near/pallas_call | solution.py:169
  33.2 0.2 collective-permute-start.4
  33.4 1.9 %collective-permute-start.5 = (bf16[768,128]{1,0:T(8,128)(2,1)S(1)}, bf16[768,128]{1,0:T(8,128)(2,1)S(1)}, u32[]{:S(2)}, u32[]{:S(2)}) collective-permute-start(bf16[768,128]{1,0:T(8,128)(2,1)S(1)} %get-tuple-element.30), channel_id=1, source_target_pairs={{2,0},{4,2},{6,4},{8,6},{10,8},{12,10},{14,12},{15,14},{13,15},{11... | collective-permute-start | bytes 589832 | tf_op jit(solution)/shard_map/ppermute | solution.py:288
  35.3 0.0 collective-permute-done.6
  35.3 0.1 add_convert_fusion
  35.4 4.4 %collective-permute-start.7 = (bf16[768,128]{1,0:T(8,128)(2,1)S(1)}, bf16[768,128]{1,0:T(8,128)(2,1)S(1)}, u32[]{:S(2)}, u32[]{:S(2)}) collective-permute-start(bf16[768,128]{1,0:T(8,128)(2,1)S(1)} %add_convert_fusion), channel_id=1, source_target_pairs={{3,1},{5,3},{7,5},{9,7},{11,9},{13,11},{15,13},{14,15},{12,14},{10... | collective-permute-start | bytes 589832 | tf_op jit(solution)/shard_map/ppermute | solution.py:288
  39.8 0.0 copy-done.1
  39.8 4.0 %block_outputs.1 = (bf16[768,512]{1,0:T(8,128)(2,1)}, bf16[768,512]{1,0:T(8,128)(2,1)}, f32[768,128]{1,0:T(8,128)S(1)}, f32[768,128]{1,0:T(8,128)S(1)}) custom-call(bf16[768,512]{1,0:T(8,128)(2,1)S(1)} %copy-done.1, bf16[768,512]{1,0:T(8,128)(2,1)S(1)} %copy-done.2, bf16[768,128]{1,0:T(8,128)(2,1)S(1)} %copy-done.4, ...), custom_call_target="tpu_custom_call" | custom-call | flops 4227858432 | tf_op jit(solution)/shard_map/block_outputs/pallas_call | solution.py:242
  43.8 0.0 collective-permute-done.4.far_1
  43.8 0.0 collective-permute-done.5.far_2
  43.8 3.2 %collective-permute-done.7.near_1 = bf16[768,128]{1,0:T(8,128)(2,1)S(1)} collective-permute-done((bf16[768,128]{1,0:T(8,128)(2,1)S(1)}, bf16[768,128]{1,0:T(8,128)(2,1)S(1)}, u32[]{:S(2)}, u32[]{:S(2)}) %collective-permute-start.7) | collective-permute-done | bytes 196640 | tf_op jit(solution)/shard_map/ppermute | solution.py:288
  47.1 0.8 %total_grads.1 = (bf16[768,128]{1,0:T(8,128)(2,1)}, bf16[768,128]{1,0:T(8,128)(2,1)}) custom-call(f32[768,128]{1,0:T(8,128)S(1)} %get-tuple-element.28.far_own, bf16[768,128]{1,0:T(8,128)(2,1)S(1)} %collective-permute-done.4.far_1, bf16[768,128]{1,0:T(8,128)(2,1)S(1)} %collective-permute-done.5.far_2, f32[768,128]{1,0:T(8,128)S(1)} %get-tuple-element.31.near_own, ...), custom_call_target="tpu_custom_call" | custom-call | tf_op jit(solution)/shard_map/total_grads/pallas_call | solution.py:271
Async XLA Ops:
  2.4 7.6 %collective-permute-start = (bf16[768,128]{1,0:T(8,128)(2,1)}, bf16[768,128]{1,0:T(8,128)(2,1)S(1)}, u32[]{:S(2)}, u32[]{:S(2)}) collective-permute-start(bf16[768,128]{1,0:T(8,128)(2,1)} %get-tuple-element.21.own_kv.refs_5_), channel_id=1, source_target_pairs={{1,3},{3,5},{5,7},{7,9},{9,11},{11,13},{13,15},{15,14},{14,12},{12... | collective-permute-start | bytes 589832 | tf_op jit(solution)/shard_map/ppermute | solution.py:288
  5.6 11.2 %collective-permute-start.2 = (bf16[768,128]{1,0:T(8,128)(2,1)}, bf16[768,128]{1,0:T(8,128)(2,1)S(1)}, u32[]{:S(2)}, u32[]{:S(2)}) collective-permute-start(bf16[768,128]{1,0:T(8,128)(2,1)} %get-tuple-element.20.own_kv.refs_0_), channel_id=1, source_target_pairs={{0,2},{2,4},{4,6},{6,8},{8,10},{10,12},{12,14},{14,15},{15,13},{13... | collective-permute-start | bytes 589832 | tf_op jit(solution)/shard_map/ppermute | solution.py:288
  10.0 8.1 %collective-permute-start.1 = (bf16[768,128]{1,0:T(8,128)(2,1)S(1)}, bf16[768,128]{1,0:T(8,128)(2,1)S(1)}, u32[]{:S(2)}, u32[]{:S(2)}) collective-permute-start(bf16[768,128]{1,0:T(8,128)(2,1)S(1)} %collective-permute-done.prev2.refs_7_), channel_id=1, source_target_pairs={{0,1},{1,0},{2,3},{3,2},{4,5},{5,4},{6,7},{7,6},{8,9},{9,8},{10,11... | collective-permute-start | bytes 589832 | tf_op jit(solution)/shard_map/ppermute | solution.py:288
  16.8 10.9 %collective-permute-start.3 = (bf16[768,128]{1,0:T(8,128)(2,1)}, bf16[768,128]{1,0:T(8,128)(2,1)S(1)}, u32[]{:S(2)}, u32[]{:S(2)}) collective-permute-start(bf16[768,128]{1,0:T(8,128)(2,1)} %get-tuple-element.20.own_kv.refs_0_), channel_id=1, source_target_pairs={{0,1},{1,0},{2,3},{3,2},{4,5},{5,4},{6,7},{7,6},{8,9},{9,8},{10,11... | collective-permute-start | bytes 589832 | tf_op jit(solution)/shard_map/ppermute | solution.py:288
  18.1 1.1 %copy-start = (bf16[768,512]{1,0:T(8,128)(2,1)S(1)}, bf16[768,512]{1,0:T(8,128)(2,1)}, u32[]{:S(2)}) copy-start(bf16[768,512]{1,0:T(8,128)(2,1)} %query.5) | copy-start | bytes 2359300
  19.2 1.1 %copy-start.2 = (bf16[768,512]{1,0:T(8,128)(2,1)S(1)}, bf16[768,512]{1,0:T(8,128)(2,1)}, u32[]{:S(2)}) copy-start(bf16[768,512]{1,0:T(8,128)(2,1)} %dout.5) | copy-start | bytes 2359300
  20.4 0.9 %copy-start.4 = (bf16[768,128]{1,0:T(8,128)(2,1)S(1)}, bf16[768,128]{1,0:T(8,128)(2,1)}, u32[]{:S(2)}) copy-start(bf16[768,128]{1,0:T(8,128)(2,1)} %get-tuple-element.20.own_kv.refs_0_) | copy-start | bytes 589828
  21.3 0.7 %copy-start.5 = (s32[32]{0:T(128)S(1)}, s32[32]{0:T(128)}, u32[]{:S(2)}) copy-start(s32[32]{0:T(128)} %doc_lengths.3) | copy-start | bytes 388
  22.0 5.8 %copy-start.3 = (bf16[768,128]{1,0:T(8,128)(2,1)S(1)}, bf16[768,128]{1,0:T(8,128)(2,1)}, u32[]{:S(2)}) copy-start(bf16[768,128]{1,0:T(8,128)(2,1)} %get-tuple-element.21.own_kv.refs_5_) | copy-start | bytes 589828
  27.3 12.6 %copy-start.1 = (bf16[768,512]{1,0:T(8,128)(2,1)S(1)}, bf16[768,512]{1,0:T(8,128)(2,1)}, u32[]{:S(2)}) copy-start(bf16[768,512]{1,0:T(8,128)(2,1)} %query.5) | copy-start | bytes 2359300
  27.3 8.0 %collective-permute-start.6 = (bf16[768,128]{1,0:T(8,128)(2,1)S(1)}, bf16[768,128]{1,0:T(8,128)(2,1)S(1)}, u32[]{:S(2)}, u32[]{:S(2)}) collective-permute-start(bf16[768,128]{1,0:T(8,128)(2,1)S(1)} %get-tuple-element.33), channel_id=1, source_target_pairs={{0,1},{1,0},{2,3},{3,2},{4,5},{5,4},{6,7},{7,6},{8,9},{9,8},{10,11... | collective-permute-start | bytes 589832 | tf_op jit(solution)/shard_map/ppermute | solution.py:288
  33.2 10.6 %collective-permute-start.4 = (bf16[768,128]{1,0:T(8,128)(2,1)S(1)}, bf16[768,128]{1,0:T(8,128)(2,1)S(1)}, u32[]{:S(2)}, u32[]{:S(2)}) collective-permute-start(bf16[768,128]{1,0:T(8,128)(2,1)S(1)} %get-tuple-element.29), channel_id=1, source_target_pairs={{0,1},{1,0},{2,3},{3,2},{4,5},{5,4},{6,7},{7,6},{8,9},{9,8},{10,11... | collective-permute-start | bytes 589832 | tf_op jit(solution)/shard_map/ppermute | solution.py:288
  33.4 10.5 %collective-permute-start.5 = (bf16[768,128]{1,0:T(8,128)(2,1)S(1)}, bf16[768,128]{1,0:T(8,128)(2,1)S(1)}, u32[]{:S(2)}, u32[]{:S(2)}) collective-permute-start(bf16[768,128]{1,0:T(8,128)(2,1)S(1)} %get-tuple-element.30), channel_id=1, source_target_pairs={{2,0},{4,2},{6,4},{8,6},{10,8},{12,10},{14,12},{15,14},{13,15},{11... | collective-permute-start | bytes 589832 | tf_op jit(solution)/shard_map/ppermute | solution.py:288
  35.4 11.7 %collective-permute-start.7 = (bf16[768,128]{1,0:T(8,128)(2,1)S(1)}, bf16[768,128]{1,0:T(8,128)(2,1)S(1)}, u32[]{:S(2)}, u32[]{:S(2)}) collective-permute-start(bf16[768,128]{1,0:T(8,128)(2,1)S(1)} %add_convert_fusion), channel_id=1, source_target_pairs={{3,1},{5,3},{7,5},{9,7},{11,9},{13,11},{15,13},{14,15},{12,14},{10... | collective-permute-start | bytes 589832 | tf_op jit(solution)/shard_map/ppermute | solution.py:288

commit v3 on v2

v3 whole, which is shorter than its diff:
```python
import functools
import math

import jax
import jax.numpy as jnp
from jax import lax
from jax.experimental import pallas as pl
from jax.experimental.pallas import tpu as pltpu
from jax.sharding import PartitionSpec as P

HD = 128
TQ = 128
GROUP = 32

masked_score = -1e30
VMEM_LIMIT = 24 * 1024 * 1024
SCALE = 1.0 / math.sqrt(HD)
VMEM = pl.BlockSpec(memory_space=pltpu.VMEM)
SMEM = pl.BlockSpec(memory_space=pltpu.SMEM)


def dot_nt(a, b):
    return lax.dot_general(a, b, (((1,), (1,)), ((), ())), preferred_element_type=jnp.float32)


def dot_nn(a, b):
    return lax.dot_general(a, b, (((1,), (0,)), ((), ())), preferred_element_type=jnp.float32)


def half_start(rows, slot):
    odd = lax.axis_index("ctx") % 2
    return pl.multiple_of((odd if slot == 0 else 1 - odd) * rows, rows)


def block_number(count, slot):
    device = lax.axis_index("ctx")
    in_lower = device % 2 == slot
    return jnp.where(in_lower, device, 2 * count - 1 - device)


def pack_kernel(rows, key, value, near_out, far_out):
    for slot, out in ((1, near_out), (0, far_out)):
        place = pl.ds(half_start(rows, slot), rows)
        out[0:rows] = key[place, :]
        out[rows : 2 * rows] = value[place, :]


def pack_blocks(key, value):
    rows = key.shape[0] // 2
    shape = jax.ShapeDtypeStruct((2 * rows, HD), key.dtype)
    return pl.pallas_call(
        functools.partial(pack_kernel, rows),
        out_shape=(shape, shape),
        in_specs=[VMEM] * 2,
        out_specs=[VMEM] * 2,
        name="pack_blocks",
    )(key, value)


def prepare_kernel(rows, heads, docs, count, doc_lengths, query, dout, _, *refs):
    for slot in (0, 1):
        query_rows, dout_rows, doc_start = refs[3 * slot : 3 * slot + 3]
        own_rows = half_start(rows, slot)
        for step in range(rows // TQ):
            source = pl.ds(own_rows + step * TQ, TQ)
            for h in range(heads):
                place = slice((step * heads + h) * TQ, (step * heads + h + 1) * TQ)
                columns = slice(h * HD, (h + 1) * HD)
                query_rows[place, :] = query[source, columns]
                dout_rows[place, :] = dout[source, columns]
        at = (
            block_number(count, slot) * rows
            + lax.broadcasted_iota(jnp.int32, (8, TQ), 0) * TQ
            + lax.broadcasted_iota(jnp.int32, (8, TQ), 1)
        )

        def one(index, carry):
            start, found = carry
            found = jnp.where(at >= start, start, found)
            return (start + doc_lengths[index], found)

        _, found = lax.fori_loop(
            0, docs, one, (jnp.int32(0), jnp.zeros((8, TQ), jnp.int32)), unroll=8
        )
        doc_start[...] = found


def prepare(count, doc_lengths, query, dout, after):
    rows = query.shape[0] // 2
    heads = query.shape[1] // HD
    stacked = jax.ShapeDtypeStruct((rows * heads, HD), query.dtype)
    starts = jax.ShapeDtypeStruct((8, TQ), jnp.int32)
    return pl.pallas_call(
        functools.partial(prepare_kernel, rows, heads, doc_lengths.shape[0], count),
        out_shape=(stacked, stacked, starts) * 2,
        in_specs=[SMEM, VMEM, VMEM, pl.BlockSpec(memory_space=pl.ANY)],
        out_specs=[VMEM] * 6,
        compiler_params=pltpu.CompilerParams(vmem_limit_bytes=VMEM_LIMIT),
        cost_estimate=pl.CostEstimate(flops=0, bytes_accessed=4 * 2**20, transcendentals=0),
        name="prepare",
    )(doc_lengths, query, dout, after)


def scores_kernel(
    rows,
    heads,
    count,
    slot,
    query_rows,
    dout_rows,
    doc_start,
    own_kv,
    prev1,
    prev2,
    weights,
    dscores,
    inverses,
    query_scaled,
    dout_scaled,
    prev1_out,
    prev2_out,
    scores,
    dprobs,
    dk,
    dv,
):
    back = 2 * rows
    width = back + TQ
    wide = heads * TQ
    base2 = SCALE * math.log2(math.e)
    block_pos = block_number(count, slot) * rows

    for step in range(rows // TQ):
        first = step * TQ
        tile = slice(step * wide, (step + 1) * wide)
        query_tile = query_rows[tile, :]
        dout_tile = dout_rows[tile, :]
        sources = (
            (prev2, first, rows - first, 0),
            (prev1, 0, rows, rows - first),
            (own_kv, 0, first + TQ, back - first),
        )
        low = doc_start[step : step + 1, :] - (block_pos - back + first)
        high = lax.broadcasted_iota(jnp.int32, (1, TQ), 1) + back
        row_max = jnp.full((8, wide), masked_score, jnp.float32)
        for source, row, length, place in sources:
            product = dot_nt(source[row : row + length, :], query_tile)
            for start in range(0, length, GROUP):
                at = lax.broadcasted_iota(jnp.int32, (GROUP, TQ), 0) + (place + start)
                allowed = at >= low
                if place + start >= back:
                    allowed = jnp.logical_and(allowed, at <= high)
                allowed = jnp.concatenate([allowed] * heads, axis=1)
                part = jnp.where(allowed, product[start : start + GROUP, :], masked_score)
                scores[place + start : place + start + GROUP, :] = part
                for row8 in range(0, GROUP, 8):
                    row_max = jnp.maximum(row_max, part[row8 : row8 + 8, :])
        row_max = jnp.max(row_max, axis=0, keepdims=True) * base2
        total = jnp.zeros((8, wide), jnp.float32)
        delta = jnp.zeros((8, wide), jnp.float32)
        out = step * width
        for source, row, length, place in sources:
            product = dot_nt(source[rows + row : rows + row + length, :], dout_tile)
            for start in range(0, length, GROUP):
                here = slice(place + start, place + start + GROUP)
                there = slice(out + place + start, out + place + start + GROUP)
                dprob = product[start : start + GROUP, :]
                dprobs[here, :] = dprob
                part = jnp.exp2(scores[here, :] * base2 - row_max)
                weights[there, :] = part.astype(jnp.bfloat16)
                term = part * dprob
                for row8 in range(0, GROUP, 8):
                    total = total + part[row8 : row8 + 8, :]
                    delta = delta + term[row8 : row8 + 8, :]
        inverse = 1.0 / jnp.sum(total, axis=0, keepdims=True)
        delta = jnp.sum(delta, axis=0, keepdims=True) * inverse
        inverses[step : step + 1, :] = inverse
        for start in range(0, width, GROUP):
            there = slice(out + start, out + start + GROUP)
            dscores[there, :] = weights[there, :] * (
                dprobs[start : start + GROUP, :] - delta
            ).astype(jnp.bfloat16)
        for h in range(heads):
            part = slice(h * TQ, (h + 1) * TQ)
            place = slice(step * wide + h * TQ, step * wide + (h + 1) * TQ)
            column = jnp.transpose(jnp.broadcast_to(inverse[:, part], (TQ, TQ)))
            query_scaled[place, :] = (query_tile[part].astype(jnp.float32) * column).astype(
                jnp.bfloat16
            )
            dout_scaled[place, :] = (dout_tile[part].astype(jnp.float32) * column).astype(
                jnp.bfloat16
            )
        for total_ref, terms, side in ((dv, weights, dout_scaled), (dk, dscores, query_scaled)):
            term = dot_nn(terms[out : out + back - first, :], side[tile, :])
            if step == 0:
                total_ref[...] = term
            else:
                total_ref[first:back] += term

    prev2_out[0:rows] = (dk[0:rows] * SCALE).astype(prev2_out.dtype)
    prev2_out[rows:back] = dv[0:rows].astype(prev2_out.dtype)
    prev1_out[0:rows] = (dk[rows:back] * SCALE).astype(prev1_out.dtype)
    prev1_out[rows:back] = dv[rows:back].astype(prev1_out.dtype)


def block_scores(slot, count, prepared, own_kv, prev1, prev2):
    rows = own_kv.shape[0] // 2
    heads = prepared[0].shape[0] // rows
    steps = rows // TQ
    width = 2 * rows + TQ
    wide = heads * TQ
    pair = jax.ShapeDtypeStruct((2 * rows, HD), jnp.bfloat16)
    kept = jax.ShapeDtypeStruct((steps * width, wide), jnp.bfloat16)
    inverses = jax.ShapeDtypeStruct((8, wide), jnp.float32)
    stacked = jax.ShapeDtypeStruct((rows * heads, HD), jnp.bfloat16)
    return pl.pallas_call(
        functools.partial(scores_kernel, rows, heads, count, slot),
        out_shape=(kept, kept, inverses, stacked, stacked, pair, pair),
        in_specs=[VMEM] * 6,
        out_specs=[VMEM] * 7,
        scratch_shapes=[
            pltpu.VMEM((width, wide), jnp.float32),
            pltpu.VMEM((width, wide), jnp.float32),
            pltpu.VMEM((2 * rows, HD), jnp.float32),
            pltpu.VMEM((2 * rows, HD), jnp.float32),
        ],
        compiler_params=pltpu.CompilerParams(vmem_limit_bytes=VMEM_LIMIT),
        cost_estimate=pl.CostEstimate(
            flops=4 * 2 * steps * width * heads * TQ * HD, bytes_accessed=0, transcendentals=0
        ),
        name="scores_far" if slot == 0 else "scores_near",
    )(*prepared, own_kv, prev1, prev2)


def outputs_kernel(rows, heads, from_far_2, *refs):
    blocks = (refs[0:8], refs[8:16])
    (attended, grad_query, far_own, near_own, keys_t, values_t) = refs[16:]
    back = 2 * rows
    width = back + TQ
    wide = heads * TQ
    for slot, block in enumerate(blocks):
        (own_kv, prev1, prev2, weights, dscores, inverses, query_scaled, dout_scaled) = block
        own_out = (far_own, near_own)[slot]
        own_rows = half_start(rows, slot)
        for place, source in enumerate((prev2, prev1, own_kv)):
            for tile in range(rows // TQ):
                part = slice(place * rows + tile * TQ, place * rows + (tile + 1) * TQ)
                row = tile * TQ
                keys_t[:, part] = jnp.transpose(source[row : row + TQ, :])
                values_t[:, part] = jnp.transpose(source[rows + row : rows + row + TQ, :])
        for step in reversed(range(rows // TQ)):
            first = step * TQ
            out = step * width
            tile = slice(step * wide, (step + 1) * wide)
            tail = slice(out + back - first, out + width)
            for offset, terms, side, factor in (
                (0, dscores, query_scaled, SCALE),
                (rows, weights, dout_scaled, 1.0),
            ):
                term = dot_nn(terms[tail, :], side[tile, :]) * factor
                place = slice(offset, offset + first + TQ)
                if step < rows // TQ - 1:
                    own_out[place] += term
                elif slot == 0:
                    own_out[place] = term + from_far_2[place].astype(jnp.float32)
                else:
                    own_out[place] = term
            window = slice(first, first + width)
            inverse = inverses[step : step + 1, :]
            attended_t = dot_nn(values_t[:, window], weights[out : out + width, :]) * inverse
            grad_query_t = dot_nn(keys_t[:, window], dscores[out : out + width, :]) * (
                inverse * SCALE
            )
            place = pl.ds(own_rows + first, TQ)
            for h in range(heads):
                part = slice(h * TQ, (h + 1) * TQ)
                columns = slice(h * HD, (h + 1) * HD)
                attended[place, columns] = jnp.transpose(attended_t[:, part]).astype(
                    attended.dtype
                )
                grad_query[place, columns] = jnp.transpose(grad_query_t[:, part]).astype(
                    grad_query.dtype
                )


def block_outputs(query, from_far_2, far, near):
    rows = query.shape[0] // 2
    heads = query.shape[1] // HD
    wide = jax.ShapeDtypeStruct(query.shape, query.dtype)
    own = jax.ShapeDtypeStruct((2 * rows, HD), jnp.float32)
    return pl.pallas_call(
        functools.partial(outputs_kernel, rows, heads),
        out_shape=(wide, wide, own, own),
        in_specs=[VMEM] * 17,
        out_specs=[VMEM] * 4,
        scratch_shapes=[
            pltpu.VMEM((HD, 3 * rows), jnp.bfloat16),
            pltpu.VMEM((HD, 3 * rows), jnp.bfloat16),
        ],
        compiler_params=pltpu.CompilerParams(vmem_limit_bytes=VMEM_LIMIT),
        cost_estimate=pl.CostEstimate(flops=0, bytes_accessed=0, transcendentals=0),
        name="block_outputs",
    )(from_far_2, *far, *near)


def total_kernel(rows, far_own, far_1, near_own, near_1, grad_key, grad_value):
    far = far_own[...] + far_1[...].astype(jnp.float32)
    near = near_own[...] + near_1[...].astype(jnp.float32)
    for slot, total in ((0, far), (1, near)):
        place = pl.ds(half_start(rows, slot), rows)
        grad_key[place, :] = total[0:rows].astype(grad_key.dtype)
        grad_value[place, :] = total[rows : 2 * rows].astype(grad_value.dtype)


def total_grads(far_own, far_1, near_own, near_1):
    rows = far_own.shape[0] // 2
    shape = jax.ShapeDtypeStruct((2 * rows, HD), jnp.bfloat16)
    return pl.pallas_call(
        functools.partial(total_kernel, rows),
        out_shape=(shape, shape),
        in_specs=[VMEM] * 4,
        out_specs=[VMEM] * 2,
        compiler_params=pltpu.CompilerParams(vmem_limit_bytes=VMEM_LIMIT),
        name="total_grads",
    )(far_own, far_1, near_own, near_1)


def body(query, key, value, d_out, doc_lengths):
    count = lax.axis_size("ctx")

    def holder(block):
        return block if block < count else 2 * count - 1 - block

    def move(array, pairs):
        return lax.ppermute(array, "ctx", pairs)

    near_on = [(holder(b), holder(b + 2)) for b in range(1, 2 * count - 2, 2)]
    far_on = [(holder(b), holder(b + 2)) for b in range(0, 2 * count - 2, 2)]
    swap = [(d, d ^ 1) for d in range(count)]
    near_back = [(t, s) for s, t in near_on]
    far_back = [(t, s) for s, t in far_on]

    near_kv, far_kv = pack_blocks(key, value)
    near_2 = move(near_kv, near_on)
    far_2 = move(far_kv, far_on)
    near_1 = move(far_kv, swap)
    prepared = prepare(count, doc_lengths, query, d_out, near_kv)
    near_2, prepared = lax.optimization_barrier((near_2, prepared))
    far_1 = move(near_2, swap)

    *far_kept, far_g1, far_g2 = block_scores(0, count, prepared[0:3], far_kv, far_1, far_2)
    from_far_2 = move(far_g2, far_back)
    relayed = move(far_g1, swap)
    *near_kept, near_g1, near_g2 = block_scores(1, count, prepared[3:6], near_kv, near_1, near_2)
    near_sum = (near_g2.astype(jnp.float32) + relayed.astype(jnp.float32)).astype(jnp.bfloat16)
    from_near_2 = move(near_sum, near_back)
    near_g1, from_far_2 = lax.optimization_barrier((near_g1, from_far_2))
    from_near_1 = move(near_g1, swap)
    attended, grad_query, far_own, near_own = block_outputs(
        query,
        from_far_2,
        (far_kv, far_1, far_2, *far_kept),
        (near_kv, near_1, near_2, *near_kept),
    )
    grad_key, grad_value = total_grads(far_own, from_near_1, near_own, from_near_2)
    return (attended, grad_query, grad_key, grad_value)


def solution(mesh):
    rows = P(("dp", "ctx"), None)
    return jax.shard_map(
        body,
        mesh=mesh,
        in_specs=(rows, rows, rows, rows, P("dp")),
        out_specs=(rows, rows, rows, rows),
        check_vma=False,
    )
```

time: 48.2 us -> 43.7 us (0.907)
  the two profiles are of different devices: /device:TPU:11 before, /device:TPU:0 now
where the time goes in v3:
time: 43.7 us; the launch traced here: 43.1 us
  starting transfers between devices  17.7 us (41%)
  Pallas kernels  17.5 us (40%)
  local copies, waits for them, and re-layouts  4.78 us (11%)
  waiting for transfers between devices  2.37 us (5%)
  between operations  0.76 us (2%)
    ppermute x8, starting transfers between devices, move(): return lax.ppermute(array, 'ctx', pairs)  17.7 us
    pallas_call x2, Pallas kernels, block_scores(): pl.pallas_call(functools.partial(scores_kernel, rows, heads, count, slot)...  9.89 us
    unnamed x14, local copies, waits for them, and re-layouts  4.78 us
    pallas_call x1, Pallas kernels, block_outputs(): pl.pallas_call(functools.partial(outputs_kernel, rows, heads), out_shape=...  4.08 us
    ppermute x8, waiting for transfers between devices, move(): return lax.ppermute(array, 'ctx', pairs)  2.37 us
    pallas_call x1, Pallas kernels, pack_blocks(): pl.pallas_call(functools.partial(pack_kernel, rows), out_shape=(shape, sh...  1.79 us
    pallas_call x1, Pallas kernels, prepare(): pl.pallas_call(functools.partial(prepare_kernel, rows, heads, doc_lengths...  0.91 us
  transfers between devices with their start and end apart: 8, of which 2 were waited for; matrix products, arithmetic and copies ran while one was open for 0% of the time, Pallas kernels for 35%

profile of v3, /device:TPU:0, one launch (start us, length us, event | category | flops | bytes accessed | tf_op | source)
XLA Modules:
  0.0 43.1 jit_solution(2931233456690810058)
XLA Ops:
  0.6 1.8 %pack_blocks.1 = (bf16[768,128]{1,0:T(8,128)(2,1)}, bf16[768,128]{1,0:T(8,128)(2,1)}) custom-call(bf16[768,128]{1,0:T(8,128)(2,1)} %key.1, bf16[768,128]{1,0:T(8,128)(2,1)} %value.1), custom_call_target="tpu_custom_call" | custom-call | tf_op jit(solution)/shard_map/pack_blocks/pallas_call | solution.py:51
  2.4 1.3 %collective-permute-start = (bf16[768,128]{1,0:T(8,128)(2,1)}, bf16[768,128]{1,0:T(8,128)(2,1)S(1)}, u32[]{:S(2)}, u32[]{:S(2)}) collective-permute-start(bf16[768,128]{1,0:T(8,128)(2,1)} %get-tuple-element.41._.own_kv.refs_8_), channel_id=1, source_target_pairs={{1,3},{3,5},{5,7},{7,9},{9,11},{11,13},{13,15},{15,14},{14,12},{12... | collective-permute-start | bytes 589832 | tf_op jit(solution)/shard_map/ppermute | solution.py:335
  3.7 5.5 %collective-permute-start.3 = (bf16[768,128]{1,0:T(8,128)(2,1)}, bf16[768,128]{1,0:T(8,128)(2,1)S(1)}, u32[]{:S(2)}, u32[]{:S(2)}) collective-permute-start(bf16[768,128]{1,0:T(8,128)(2,1)} %get-tuple-element.51.own_kv.refs_0_), channel_id=1, source_target_pairs={{0,2},{2,4},{4,6},{6,8},{8,10},{10,12},{12,14},{14,15},{15,13},{13... | collective-permute-start | bytes 589832 | tf_op jit(solution)/shard_map/ppermute | solution.py:335
  9.2 0.0 copy-start
  9.2 1.1 %copy-done = bf16[768,512]{1,0:T(8,128)(2,1)S(1)} copy-done((bf16[768,512]{1,0:T(8,128)(2,1)S(1)}, bf16[768,512]{1,0:T(8,128)(2,1)}, u32[]{:S(2)}) %copy-start) | copy-done | bytes 786456
  10.4 0.0 copy-start.1
  10.4 1.1 %copy-done.1 = bf16[768,512]{1,0:T(8,128)(2,1)S(1)} copy-done((bf16[768,512]{1,0:T(8,128)(2,1)S(1)}, bf16[768,512]{1,0:T(8,128)(2,1)}, u32[]{:S(2)}) %copy-start.1) | copy-done | bytes 786456
  11.5 0.0 copy-start.2
  11.5 0.9 %copy-done.2 = bf16[768,128]{1,0:T(8,128)(2,1)S(1)} copy-done((bf16[768,128]{1,0:T(8,128)(2,1)S(1)}, bf16[768,128]{1,0:T(8,128)(2,1)}, u32[]{:S(2)}) %copy-start.2) | copy-done | bytes 196632
  12.4 0.0 copy-start.6
  12.4 0.7 %copy-done.6 = s32[32]{0:T(128)S(1)} copy-done((s32[32]{0:T(128)S(1)}, s32[32]{0:T(128)}, u32[]{:S(2)}) %copy-start.6) | copy-done | bytes 152
  13.1 0.9 %prepare.1 = (bf16[1536,128]{1,0:T(8,128)(2,1)S(1)}, bf16[1536,128]{1,0:T(8,128)(2,1)S(1)}, s32[8,128]{1,0:T(8,128)S(1)}, bf16[1536,128]{1,0:T(8,128)(2,1)S(1)},...) custom-call(s32[32]{0:T(128)S(1)} %copy-done.6, bf16[768,512]{1,0:T(8,128)(2,1)S(1)} %copy-done, ...), custom_call_target="tpu_custom_call" | custom-call | bytes 4194304 | tf_op jit(solution)/shard_map/prepare/pallas_call | solution.py:93
  14.0 0.0 copy-start.3
  14.0 0.0 collective-permute-done.prev2.refs_10_
  14.0 0.1 collective-permute-start.2
  14.1 0.5 %collective-permute-start.1 = (bf16[768,128]{1,0:T(8,128)(2,1)}, bf16[768,128]{1,0:T(8,128)(2,1)S(1)}, u32[]{:S(2)}, u32[]{:S(2)}) collective-permute-start(bf16[768,128]{1,0:T(8,128)(2,1)} %get-tuple-element.51.own_kv.refs_0_), channel_id=1, source_target_pairs={{0,1},{1,0},{2,3},{3,2},{4,5},{5,4},{6,7},{7,6},{8,9},{9,8},{10,11... | collective-permute-start | bytes 589832 | tf_op jit(solution)/shard_map/ppermute | solution.py:335
  14.6 1.4 %collective-permute-done.3.prev2.refs_2_ = bf16[768,128]{1,0:T(8,128)(2,1)S(1)} collective-permute-done((bf16[768,128]{1,0:T(8,128)(2,1)}, bf16[768,128]{1,0:T(8,128)(2,1)S(1)}, u32[]{:S(2)}, u32[]{:S(2)}) %collective-permute-start.3) | collective-permute-done | bytes 196640 | tf_op jit(solution)/shard_map/ppermute | solution.py:335
  16.0 0.0 collective-permute-done.2.prev1.refs_1_
  16.0 0.0 copy-start.4
  16.0 0.9 %copy-done.4 = bf16[768,128]{1,0:T(8,128)(2,1)S(1)} copy-done((bf16[768,128]{1,0:T(8,128)(2,1)S(1)}, bf16[768,128]{1,0:T(8,128)(2,1)}, u32[]{:S(2)}) %copy-start.4) | copy-done | bytes 196632
  16.9 4.9 %scores_far.1 = (bf16[2688,512]{1,0:T(8,128)(2,1)S(1)}, bf16[2688,512]{1,0:T(8,128)(2,1)S(1)}, f32[8,512]{1,0:T(8,128)S(1)}, bf16[1536,128]{1,0:T(8,128)(2,1)S(1...) custom-call(bf16[1536,128]{1,0:T(8,128)(2,1)S(1)} %get-tuple-element.54.query_rows, ...), custom_call_target="tpu_custom_call" | custom-call | flops 1409286144 | tf_op jit(solution)/shard_map/scores_far/pallas_call | solution.py:216
  21.8 1.3 %collective-permute-start.4 = (bf16[768,128]{1,0:T(8,128)(2,1)S(1)}, bf16[768,128]{1,0:T(8,128)(2,1)S(1)}, u32[]{:S(2)}, u32[]{:S(2)}) collective-permute-start(bf16[768,128]{1,0:T(8,128)(2,1)S(1)} %get-tuple-element.57), channel_id=1, source_target_pairs={{2,0},{4,2},{6,4},{8,6},{10,8},{12,10},{14,12},{15,14},{13,15},{11... | collective-permute-start | bytes 589832 | tf_op jit(solution)/shard_map/ppermute | solution.py:335
  23.1 0.0 copy-start.5
  23.1 3.0 %collective-permute-start.6 = (bf16[768,128]{1,0:T(8,128)(2,1)S(1)}, bf16[768,128]{1,0:T(8,128)(2,1)S(1)}, u32[]{:S(2)}, u32[]{:S(2)}) collective-permute-start(bf16[768,128]{1,0:T(8,128)(2,1)S(1)} %get-tuple-element.75), channel_id=1, source_target_pairs={{0,1},{1,0},{2,3},{3,2},{4,5},{5,4},{6,7},{7,6},{8,9},{9,8},{10,11... | collective-permute-start | bytes 589832 | tf_op jit(solution)/shard_map/ppermute | solution.py:335
  26.1 0.0 collective-permute-done.1.prev1.refs_9_
  26.1 0.0 copy-done.3
  26.1 5.0 %scores_near.1 = (bf16[2688,512]{1,0:T(8,128)(2,1)S(1)}, bf16[2688,512]{1,0:T(8,128)(2,1)S(1)}, f32[8,512]{1,0:T(8,128)S(1)}, bf16[1536,128]{1,0:T(8,128)(2,1)S(...) custom-call(bf16[1536,128]{1,0:T(8,128)(2,1)S(1)} %get-tuple-element.48.query_rows, ...), custom_call_target="tpu_custom_call" | custom-call | flops 1409286144 | tf_op jit(solution)/shard_map/scores_near/pallas_call | solution.py:216
  31.1 0.0 collective-permute-done.4.from_far_2
  31.1 0.1 collective-permute-start.5
  31.2 0.0 collective-permute-done.6
  31.2 0.1 add_convert_fusion
  31.3 5.9 %collective-permute-start.7 = (bf16[768,128]{1,0:T(8,128)(2,1)S(1)}, bf16[768,128]{1,0:T(8,128)(2,1)S(1)}, u32[]{:S(2)}, u32[]{:S(2)}) collective-permute-start(bf16[768,128]{1,0:T(8,128)(2,1)S(1)} %add_convert_fusion), channel_id=1, source_target_pairs={{3,1},{5,3},{7,5},{9,7},{11,9},{13,11},{15,13},{14,15},{12,14},{10... | collective-permute-start | bytes 589832 | tf_op jit(solution)/shard_map/ppermute | solution.py:335
  37.2 0.0 copy-done.5
  37.3 4.1 %block_outputs.1 = (bf16[768,512]{1,0:T(8,128)(2,1)}, bf16[768,512]{1,0:T(8,128)(2,1)}, f32[768,128]{1,0:T(8,128)S(1)}, f32[768,128]{1,0:T(8,128)S(1)}) custom-call(bf16[768,128]{1,0:T(8,128)(2,1)S(1)} %collective-permute-done.4.from_far_2, bf16[768,128]{1,0:T(8,128)(2,1)S(1)} %copy-done.5, bf16[768,128]{1,0:T(8,128)(2,1)S(1)} %collective-permute-done.2.prev1.refs_1_, ...), custom_call_target="tpu_custom_call" | custom-call | tf_op jit(solution)/shard_map/block_outputs/pallas_call | solution.py:291
  41.3 0.0 collective-permute-done.5.far_1
  41.3 1.0 %collective-permute-done.7.near_1 = bf16[768,128]{1,0:T(8,128)(2,1)S(1)} collective-permute-done((bf16[768,128]{1,0:T(8,128)(2,1)S(1)}, bf16[768,128]{1,0:T(8,128)(2,1)S(1)}, u32[]{:S(2)}, u32[]{:S(2)}) %collective-permute-start.7) | collective-permute-done | bytes 196640 | tf_op jit(solution)/shard_map/ppermute | solution.py:335
  42.3 0.8 %total_grads.1 = (bf16[768,128]{1,0:T(8,128)(2,1)}, bf16[768,128]{1,0:T(8,128)(2,1)}) custom-call(f32[768,128]{1,0:T(8,128)S(1)} %get-tuple-element.71.far_own, bf16[768,128]{1,0:T(8,128)(2,1)S(1)} %collective-permute-done.5.far_1, f32[768,128]{1,0:T(8,128)S(1)} %get-tuple-element.73.near_own, bf16[768,128]{1,0:T(8,128)(2,1)S(1)} %collective-permute-done.7.near_1), custom_call_target="tpu_custom_call" | custom-call | tf_op jit(solution)/shard_map/total_grads/pallas_call | solution.py:318
Async XLA Ops:
  2.4 11.6 %collective-permute-start = (bf16[768,128]{1,0:T(8,128)(2,1)}, bf16[768,128]{1,0:T(8,128)(2,1)S(1)}, u32[]{:S(2)}, u32[]{:S(2)}) collective-permute-start(bf16[768,128]{1,0:T(8,128)(2,1)} %get-tuple-element.41._.own_kv.refs_8_), channel_id=1, source_target_pairs={{1,3},{3,5},{5,7},{7,9},{9,11},{11,13},{13,15},{15,14},{14,12},{12... | collective-permute-start | bytes 589832 | tf_op jit(solution)/shard_map/ppermute | solution.py:335
  3.7 12.2 %collective-permute-start.3 = (bf16[768,128]{1,0:T(8,128)(2,1)}, bf16[768,128]{1,0:T(8,128)(2,1)S(1)}, u32[]{:S(2)}, u32[]{:S(2)}) collective-permute-start(bf16[768,128]{1,0:T(8,128)(2,1)} %get-tuple-element.51.own_kv.refs_0_), channel_id=1, source_target_pairs={{0,2},{2,4},{4,6},{6,8},{8,10},{10,12},{12,14},{14,15},{15,13},{13... | collective-permute-start | bytes 589832 | tf_op jit(solution)/shard_map/ppermute | solution.py:335
  9.2 1.1 %copy-start = (bf16[768,512]{1,0:T(8,128)(2,1)S(1)}, bf16[768,512]{1,0:T(8,128)(2,1)}, u32[]{:S(2)}) copy-start(bf16[768,512]{1,0:T(8,128)(2,1)} %query.1) | copy-start | bytes 2359300
  10.4 1.1 %copy-start.1 = (bf16[768,512]{1,0:T(8,128)(2,1)S(1)}, bf16[768,512]{1,0:T(8,128)(2,1)}, u32[]{:S(2)}) copy-start(bf16[768,512]{1,0:T(8,128)(2,1)} %dout.1) | copy-start | bytes 2359300
  11.5 0.9 %copy-start.2 = (bf16[768,128]{1,0:T(8,128)(2,1)S(1)}, bf16[768,128]{1,0:T(8,128)(2,1)}, u32[]{:S(2)}) copy-start(bf16[768,128]{1,0:T(8,128)(2,1)} %get-tuple-element.41._.own_kv.refs_8_) | copy-start | bytes 589828
  12.4 0.7 %copy-start.6 = (s32[32]{0:T(128)S(1)}, s32[32]{0:T(128)}, u32[]{:S(2)}) copy-start(s32[32]{0:T(128)} %doc_lengths.1) | copy-start | bytes 388
  14.0 12.1 %copy-start.3 = (bf16[768,128]{1,0:T(8,128)(2,1)S(1)}, bf16[768,128]{1,0:T(8,128)(2,1)}, u32[]{:S(2)}) copy-start(bf16[768,128]{1,0:T(8,128)(2,1)} %get-tuple-element.41._.own_kv.refs_8_) | copy-start | bytes 589828
  14.0 1.9 %collective-permute-start.2 = (bf16[768,128]{1,0:T(8,128)(2,1)S(1)}, bf16[768,128]{1,0:T(8,128)(2,1)S(1)}, u32[]{:S(2)}, u32[]{:S(2)}) collective-permute-start(bf16[768,128]{1,0:T(8,128)(2,1)S(1)} %collective-permute-done.prev2.refs_10_), channel_id=1, source_target_pairs={{0,1},{1,0},{2,3},{3,2},{4,5},{5,4},{6,7},{7,6},{8,9},{9,8},{10,11... | collective-permute-start | bytes 589832 | tf_op jit(solution)/shard_map/ppermute | solution.py:335
  14.1 12.0 %collective-permute-start.1 = (bf16[768,128]{1,0:T(8,128)(2,1)}, bf16[768,128]{1,0:T(8,128)(2,1)S(1)}, u32[]{:S(2)}, u32[]{:S(2)}) collective-permute-start(bf16[768,128]{1,0:T(8,128)(2,1)} %get-tuple-element.51.own_kv.refs_0_), channel_id=1, source_target_pairs={{0,1},{1,0},{2,3},{3,2},{4,5},{5,4},{6,7},{7,6},{8,9},{9,8},{10,11... | collective-permute-start | bytes 589832 | tf_op jit(solution)/shard_map/ppermute | solution.py:335
  16.0 0.9 %copy-start.4 = (bf16[768,128]{1,0:T(8,128)(2,1)S(1)}, bf16[768,128]{1,0:T(8,128)(2,1)}, u32[]{:S(2)}) copy-start(bf16[768,128]{1,0:T(8,128)(2,1)} %get-tuple-element.51.own_kv.refs_0_) | copy-start | bytes 589828
  21.8 9.4 %collective-permute-start.4 = (bf16[768,128]{1,0:T(8,128)(2,1)S(1)}, bf16[768,128]{1,0:T(8,128)(2,1)S(1)}, u32[]{:S(2)}, u32[]{:S(2)}) collective-permute-start(bf16[768,128]{1,0:T(8,128)(2,1)S(1)} %get-tuple-element.57), channel_id=1, source_target_pairs={{2,0},{4,2},{6,4},{8,6},{10,8},{12,10},{14,12},{15,14},{13,15},{11... | collective-permute-start | bytes 589832 | tf_op jit(solution)/shard_map/ppermute | solution.py:335
  23.1 14.2 %copy-start.5 = (bf16[768,128]{1,0:T(8,128)(2,1)S(1)}, bf16[768,128]{1,0:T(8,128)(2,1)}, u32[]{:S(2)}) copy-start(bf16[768,128]{1,0:T(8,128)(2,1)} %get-tuple-element.51.own_kv.refs_0_) | copy-start | bytes 589828
  23.1 8.2 %collective-permute-start.6 = (bf16[768,128]{1,0:T(8,128)(2,1)S(1)}, bf16[768,128]{1,0:T(8,128)(2,1)S(1)}, u32[]{:S(2)}, u32[]{:S(2)}) collective-permute-start(bf16[768,128]{1,0:T(8,128)(2,1)S(1)} %get-tuple-element.75), channel_id=1, source_target_pairs={{0,1},{1,0},{2,3},{3,2},{4,5},{5,4},{6,7},{7,6},{8,9},{9,8},{10,11... | collective-permute-start | bytes 589832 | tf_op jit(solution)/shard_map/ppermute | solution.py:335
  31.1 10.2 %collective-permute-start.5 = (bf16[768,128]{1,0:T(8,128)(2,1)S(1)}, bf16[768,128]{1,0:T(8,128)(2,1)S(1)}, u32[]{:S(2)}, u32[]{:S(2)}) collective-permute-start(bf16[768,128]{1,0:T(8,128)(2,1)S(1)} %get-tuple-element.72), channel_id=1, source_target_pairs={{0,1},{1,0},{2,3},{3,2},{4,5},{5,4},{6,7},{7,6},{8,9},{9,8},{10,11... | collective-permute-start | bytes 589832 | tf_op jit(solution)/shard_map/ppermute | solution.py:335
  31.3 11.0 %collective-permute-start.7 = (bf16[768,128]{1,0:T(8,128)(2,1)S(1)}, bf16[768,128]{1,0:T(8,128)(2,1)S(1)}, u32[]{:S(2)}, u32[]{:S(2)}) collective-permute-start(bf16[768,128]{1,0:T(8,128)(2,1)S(1)} %add_convert_fusion), channel_id=1, source_target_pairs={{3,1},{5,3},{7,5},{9,7},{11,9},{13,11},{15,13},{14,15},{12,14},{10... | collective-permute-start | bytes 589832 | tf_op jit(solution)/shard_map/ppermute | solution.py:335

commit v4 on v3

--- a/solution.py
+++ b/solution.py
@@ -19,10 +19,6 @@
 SMEM = pl.BlockSpec(memory_space=pltpu.SMEM)
 
 
-def dot_nt(a, b):
-    return lax.dot_general(a, b, (((1,), (1,)), ((), ())), preferred_element_type=jnp.float32)
-
-
 def dot_nn(a, b):
     return lax.dot_general(a, b, (((1,), (0,)), ((), ())), preferred_element_type=jnp.float32)
 
@@ -57,17 +53,25 @@
     )(key, value)
 
 
-def prepare_kernel(rows, heads, docs, count, doc_lengths, query, dout, _, *refs):
+def prepare_kernel(rows, heads, docs, count, doc_lengths, query, dout, key, value, *refs):
+    wide = heads * TQ
     for slot in (0, 1):
-        query_rows, dout_rows, doc_start = refs[3 * slot : 3 * slot + 3]
+        own_kv, query_rows, dout_rows, query_t, dout_t, doc_start = refs[6 * slot : 6 * slot + 6]
         own_rows = half_start(rows, slot)
+        own_kv[0:rows] = key[pl.ds(own_rows, rows), :]
+        own_kv[rows : 2 * rows] = value[pl.ds(own_rows, rows), :]
         for step in range(rows // TQ):
             source = pl.ds(own_rows + step * TQ, TQ)
             for h in range(heads):
-                place = slice((step * heads + h) * TQ, (step * heads + h + 1) * TQ)
+                place = slice(step * wide + h * TQ, step * wide + (h + 1) * TQ)
                 columns = slice(h * HD, (h + 1) * HD)
-                query_rows[place, :] = query[source, columns]
-                dout_rows[place, :] = dout[source, columns]
+                for wide_ref, rows_ref, t_ref in (
+                    (query, query_rows, query_t),
+                    (dout, dout_rows, dout_t),
+                ):
+                    part = wide_ref[source, columns]
+                    rows_ref[place, :] = part
+                    t_ref[:, place] = jnp.transpose(part)
         at = (
             block_number(count, slot) * rows
             + lax.broadcasted_iota(jnp.int32, (8, TQ), 0) * TQ
@@ -85,20 +89,22 @@
         doc_start[...] = found
 
 
-def prepare(count, doc_lengths, query, dout, after):
+def prepare(count, doc_lengths, query, dout, key, value):
     rows = query.shape[0] // 2
     heads = query.shape[1] // HD
+    pair = jax.ShapeDtypeStruct((2 * rows, HD), key.dtype)
     stacked = jax.ShapeDtypeStruct((rows * heads, HD), query.dtype)
+    stacked_t = jax.ShapeDtypeStruct((HD, rows * heads), query.dtype)
     starts = jax.ShapeDtypeStruct((8, TQ), jnp.int32)
     return pl.pallas_call(
         functools.partial(prepare_kernel, rows, heads, doc_lengths.shape[0], count),
-        out_shape=(stacked, stacked, starts) * 2,
-        in_specs=[SMEM, VMEM, VMEM, pl.BlockSpec(memory_space=pl.ANY)],
-        out_specs=[VMEM] * 6,
+        out_shape=(pair, stacked, stacked, stacked_t, stacked_t, starts) * 2,
+        in_specs=[SMEM] + [VMEM] * 4,
+        out_specs=[VMEM] * 12,
         compiler_params=pltpu.CompilerParams(vmem_limit_bytes=VMEM_LIMIT),
         cost_estimate=pl.CostEstimate(flops=0, bytes_accessed=4 * 2**20, transcendentals=0),
         name="prepare",
-    )(doc_lengths, query, dout, after)
+    )(doc_lengths, query, dout, key, value)
 
 
 def scores_kernel(
@@ -106,10 +112,12 @@
     heads,
     count,
     slot,
+    own_kv,
     query_rows,
     dout_rows,
+    query_t,
+    dout_t,
     doc_start,
-    own_kv,
     prev1,
     prev2,
     weights,
@@ -119,8 +127,8 @@
     dout_scaled,
     prev1_out,
     prev2_out,
-    scores,
-    dprobs,
+    all_scores,
+    all_dprobs,
     dk,
     dv,
 ):
@@ -133,8 +141,7 @@
     for step in range(rows // TQ):
         first = step * TQ
         tile = slice(step * wide, (step + 1) * wide)
-        query_tile = query_rows[tile, :]
-        dout_tile = dout_rows[tile, :]
+        scores, dprobs = all_scores.at[step], all_dprobs.at[step]
         sources = (
             (prev2, first, rows - first, 0),
             (prev1, 0, rows, rows - first),
@@ -142,25 +149,29 @@
         )
         low = doc_start[step : step + 1, :] - (block_pos - back + first)
         high = lax.broadcasted_iota(jnp.int32, (1, TQ), 1) + back
-        row_max = jnp.full((8, wide), masked_score, jnp.float32)
+        row_max = [jnp.full((8, TQ), masked_score, jnp.float32)] * heads
         for source, row, length, place in sources:
-            product = dot_nt(source[row : row + length, :], query_tile)
+            product = dot_nn(source[row : row + length, :], query_t[:, tile])
             for start in range(0, length, GROUP):
                 at = lax.broadcasted_iota(jnp.int32, (GROUP, TQ), 0) + (place + start)
                 allowed = at >= low
                 if place + start >= back:
                     allowed = jnp.logical_and(allowed, at <= high)
-                allowed = jnp.concatenate([allowed] * heads, axis=1)
-                part = jnp.where(allowed, product[start : start + GROUP, :], masked_score)
-                scores[place + start : place + start + GROUP, :] = part
-                for row8 in range(0, GROUP, 8):
-                    row_max = jnp.maximum(row_max, part[row8 : row8 + 8, :])
-        row_max = jnp.max(row_max, axis=0, keepdims=True) * base2
+                here = slice(place + start, place + start + GROUP)
+                for h in range(heads):
+                    lanes = slice(h * TQ, (h + 1) * TQ)
+                    part = jnp.where(allowed, product[start : start + GROUP, lanes], masked_score)
+                    scores[here, lanes] = part
+                    for row8 in range(0, GROUP, 8):
+                        row_max[h] = jnp.maximum(row_max[h], part[row8 : row8 + 8, :])
+        row_max = jnp.concatenate(
+            [jnp.max(part, axis=0, keepdims=True) * base2 for part in row_max], axis=1
+        )
         total = jnp.zeros((8, wide), jnp.float32)
         delta = jnp.zeros((8, wide), jnp.float32)
         out = step * width
         for source, row, length, place in sources:
-            product = dot_nt(source[rows + row : rows + row + length, :], dout_tile)
+            product = dot_nn(source[rows + row : rows + row + length, :], dout_t[:, tile])
             for start in range(0, length, GROUP):
                 here = slice(place + start, place + start + GROUP)
                 there = slice(out + place + start, out + place + start + GROUP)
@@ -184,12 +195,10 @@
             part = slice(h * TQ, (h + 1) * TQ)
             place = slice(step * wide + h * TQ, step * wide + (h + 1) * TQ)
             column = jnp.transpose(jnp.broadcast_to(inverse[:, part], (TQ, TQ)))
-            query_scaled[place, :] = (query_tile[part].astype(jnp.float32) * column).astype(
-                jnp.bfloat16
-            )
-            dout_scaled[place, :] = (dout_tile[part].astype(jnp.float32) * column).astype(
-                jnp.bfloat16
-            )
+            for rows_ref, scaled in ((query_rows, query_scaled), (dout_rows, dout_scaled)):
+                scaled[place, :] = (rows_ref[place, :].astype(jnp.float32) * column).astype(
+                    jnp.bfloat16
+                )
         for total_ref, terms, side in ((dv, weights, dout_scaled), (dk, dscores, query_scaled)):
             term = dot_nn(terms[out : out + back - first, :], side[tile, :])
             if step == 0:
@@ -203,9 +212,9 @@
     prev1_out[rows:back] = dv[rows:back].astype(prev1_out.dtype)
 
 
-def block_scores(slot, count, prepared, own_kv, prev1, prev2):
-    rows = own_kv.shape[0] // 2
-    heads = prepared[0].shape[0] // rows
+def block_scores(slot, count, prepared, prev1, prev2):
+    rows = prev1.shape[0] // 2
+    heads = prepared[1].shape[0] // rows
     steps = rows // TQ
     width = 2 * rows + TQ
     wide = heads * TQ
@@ -216,11 +225,11 @@
     return pl.pallas_call(
         functools.partial(scores_kernel, rows, heads, count, slot),
         out_shape=(kept, kept, inverses, stacked, stacked, pair, pair),
-        in_specs=[VMEM] * 6,
+        in_specs=[VMEM] * 8,
         out_specs=[VMEM] * 7,
         scratch_shapes=[
-            pltpu.VMEM((width, wide), jnp.float32),
-            pltpu.VMEM((width, wide), jnp.float32),
+            pltpu.VMEM((steps, width, wide), jnp.float32),
+            pltpu.VMEM((steps, width, wide), jnp.float32),
             pltpu.VMEM((2 * rows, HD), jnp.float32),
             pltpu.VMEM((2 * rows, HD), jnp.float32),
         ],
@@ -229,7 +238,7 @@
             flops=4 * 2 * steps * width * heads * TQ * HD, bytes_accessed=0, transcendentals=0
         ),
         name="scores_far" if slot == 0 else "scores_near",
-    )(*prepared, own_kv, prev1, prev2)
+    )(*prepared, prev1, prev2)
 
 
 def outputs_kernel(rows, heads, from_far_2, *refs):
@@ -341,17 +350,18 @@
     far_back = [(t, s) for s, t in far_on]
 
     near_kv, far_kv = pack_blocks(key, value)
-    near_2 = move(near_kv, near_on)
+    partner_near = move(near_kv, swap)
     far_2 = move(far_kv, far_on)
+    far_1 = move(partner_near, far_on)
     near_1 = move(far_kv, swap)
-    prepared = prepare(count, doc_lengths, query, d_out, near_kv)
-    near_2, prepared = lax.optimization_barrier((near_2, prepared))
-    far_1 = move(near_2, swap)
-
-    *far_kept, far_g1, far_g2 = block_scores(0, count, prepared[0:3], far_kv, far_1, far_2)
+    prepared = prepare(count, doc_lengths, query, d_out, key, value)
+    far_1, prepared = lax.optimization_barrier((far_1, prepared))
+    near_2 = move(far_1, swap)
+
+    *far_kept, far_g1, far_g2 = block_scores(0, count, prepared[0:6], far_1, far_2)
     from_far_2 = move(far_g2, far_back)
     relayed = move(far_g1, swap)
-    *near_kept, near_g1, near_g2 = block_scores(1, count, prepared[3:6], near_kv, near_1, near_2)
+    *near_kept, near_g1, near_g2 = block_scores(1, count, prepared[6:12], near_1, near_2)
     near_sum = (near_g2.astype(jnp.float32) + relayed.astype(jnp.float32)).astype(jnp.bfloat16)
     from_near_2 = move(near_sum, near_back)
     near_g1, from_far_2 = lax.optimization_barrier((near_g1, from_far_2))
@@ -359,8 +369,8 @@
     attended, grad_query, far_own, near_own = block_outputs(
         query,
         from_far_2,
-        (far_kv, far_1, far_2, *far_kept),
-        (near_kv, near_1, near_2, *near_kept),
+        (prepared[0], far_1, far_2, *far_kept),
+        (prepared[6], near_1, near_2, *near_kept),
     )
     grad_key, grad_value = total_grads(far_own, from_near_1, near_own, from_near_2)
     return (attended, grad_query, grad_key, grad_value)

time: 43.7 us -> 41.3 us (0.945)
  starting transfers between devices: 17.7 us -> 15.5 us
    ppermute x8 -> x9, starting transfers between devices: 17.7 us -> 15.5 us  [move(): return lax.ppermute(array, 'ctx', pairs)]
    ppermute x8 -> x9, waiting for transfers between devices: 2.37 us -> 2.24 us  [move(): return lax.ppermute(array, 'ctx', pairs)]
    unnamed x14 -> x10, local copies, waits for them, and re-layouts: 4.78 us -> 4.77 us
  transfers between devices with their start and end apart: 8 -> 9, of which waited for: 2 -> 2; matrix products, arithmetic and copies ran while one was open for 0% -> 0% of each run, Pallas kernels for 35% -> 37%
where the time goes in v4:
time: 41.3 us; the launch traced here: 41 us
  Pallas kernels  17.7 us (43%)
  starting transfers between devices  15.5 us (38%)
  local copies, waits for them, and re-layouts  4.77 us (12%)
  waiting for transfers between devices  2.24 us (5%)
  between operations  0.77 us (2%)
    ppermute x9, starting transfers between devices, move(): return lax.ppermute(array, 'ctx', pairs)  15.5 us
    pallas_call x2, Pallas kernels, block_scores(): pl.pallas_call(functools.partial(scores_kernel, rows, heads, count, slot)...  9.72 us
    unnamed x10, local copies, waits for them, and re-layouts  4.77 us
    pallas_call x1, Pallas kernels, block_outputs(): pl.pallas_call(functools.partial(outputs_kernel, rows, heads), out_shape=...  4.05 us
    ppermute x9, waiting for transfers between devices, move(): return lax.ppermute(array, 'ctx', pairs)  2.24 us
    pallas_call x1, Pallas kernels, pack_blocks(): pl.pallas_call(functools.partial(pack_kernel, rows), out_shape=(shape, sh...  1.79 us
    pallas_call x1, Pallas kernels, prepare(): pl.pallas_call(functools.partial(prepare_kernel, rows, heads, doc_lengths...  1.31 us
  transfers between devices with their start and end apart: 9, of which 2 were waited for; matrix products, arithmetic and copies ran while one was open for 0% of the time, Pallas kernels for 37%

profile of v4, /device:TPU:0, one launch (start us, length us, event | category | flops | bytes accessed | tf_op | source)
XLA Modules:
  0.0 41.0 jit_solution(13779521863243845275)
XLA Ops:
  0.6 1.8 %pack_blocks.1 = (bf16[768,128]{1,0:T(8,128)(2,1)}, bf16[768,128]{1,0:T(8,128)(2,1)}) custom-call(bf16[768,128]{1,0:T(8,128)(2,1)} %key.3, bf16[768,128]{1,0:T(8,128)(2,1)} %value.3), custom_call_target="tpu_custom_call" | custom-call | tf_op jit(solution)/shard_map/pack_blocks/pallas_call | solution.py:47
  2.4 0.5 %collective-permute-start = (bf16[768,128]{1,0:T(8,128)(2,1)}, bf16[768,128]{1,0:T(8,128)(2,1)S(1)}, u32[]{:S(2)}, u32[]{:S(2)}) collective-permute-start(bf16[768,128]{1,0:T(8,128)(2,1)} %get-tuple-element.53), channel_id=1, source_target_pairs={{0,1},{1,0},{2,3},{3,2},{4,5},{5,4},{6,7},{7,6},{8,9},{9,8},{10,11... | collective-permute-start | bytes 589832 | tf_op jit(solution)/shard_map/ppermute | solution.py:344
  2.9 1.3 %collective-permute-done = bf16[768,128]{1,0:T(8,128)(2,1)S(1)} collective-permute-done((bf16[768,128]{1,0:T(8,128)(2,1)}, bf16[768,128]{1,0:T(8,128)(2,1)S(1)}, u32[]{:S(2)}, u32[]{:S(2)}) %collective-permute-start) | collective-permute-done | bytes 196640 | tf_op jit(solution)/shard_map/ppermute | solution.py:344
  4.2 4.8 %collective-permute-start.1 = (bf16[768,128]{1,0:T(8,128)(2,1)S(1)}, bf16[768,128]{1,0:T(8,128)(2,1)S(1)}, u32[]{:S(2)}, u32[]{:S(2)}) collective-permute-start(bf16[768,128]{1,0:T(8,128)(2,1)S(1)} %collective-permute-done), channel_id=1, source_target_pairs={{0,2},{2,4},{4,6},{6,8},{8,10},{10,12},{12,14},{14,15},{15,13},{13... | collective-permute-start | bytes 589832 | tf_op jit(solution)/shard_map/ppermute | solution.py:344
  9.0 3.4 %collective-permute-start.4 = (bf16[768,128]{1,0:T(8,128)(2,1)}, bf16[768,128]{1,0:T(8,128)(2,1)S(1)}, u32[]{:S(2)}, u32[]{:S(2)}) collective-permute-start(bf16[768,128]{1,0:T(8,128)(2,1)} %get-tuple-element.72), channel_id=1, source_target_pairs={{0,2},{2,4},{4,6},{6,8},{8,10},{10,12},{12,14},{14,15},{15,13},{13... | collective-permute-start | bytes 589832 | tf_op jit(solution)/shard_map/ppermute | solution.py:344
  12.4 0.1 collective-permute-start.2
  12.5 0.0 copy-start
  12.5 0.9 %copy-done = bf16[768,128]{1,0:T(8,128)(2,1)S(1)} copy-done((bf16[768,128]{1,0:T(8,128)(2,1)S(1)}, bf16[768,128]{1,0:T(8,128)(2,1)}, u32[]{:S(2)}) %copy-start) | copy-done | bytes 196632
  13.4 0.0 copy-start.1
  13.4 0.9 %copy-done.1 = bf16[768,128]{1,0:T(8,128)(2,1)S(1)} copy-done((bf16[768,128]{1,0:T(8,128)(2,1)S(1)}, bf16[768,128]{1,0:T(8,128)(2,1)}, u32[]{:S(2)}) %copy-start.1) | copy-done | bytes 196632
  14.3 0.0 copy-start.2
  14.3 1.1 %copy-done.2 = bf16[768,512]{1,0:T(8,128)(2,1)S(1)} copy-done((bf16[768,512]{1,0:T(8,128)(2,1)S(1)}, bf16[768,512]{1,0:T(8,128)(2,1)}, u32[]{:S(2)}) %copy-start.2) | copy-done | bytes 786456
  15.5 0.0 copy-start.3
  15.5 1.1 %copy-done.3 = bf16[768,512]{1,0:T(8,128)(2,1)S(1)} copy-done((bf16[768,512]{1,0:T(8,128)(2,1)S(1)}, bf16[768,512]{1,0:T(8,128)(2,1)}, u32[]{:S(2)}) %copy-start.3) | copy-done | bytes 786456
  16.6 0.0 copy-start.4
  16.6 0.7 %copy-done.4 = s32[32]{0:T(128)S(1)} copy-done((s32[32]{0:T(128)S(1)}, s32[32]{0:T(128)}, u32[]{:S(2)}) %copy-start.4) | copy-done | bytes 152
  17.2 1.3 %prepare.1 = (bf16[768,128]{1,0:T(8,128)(2,1)S(1)}, bf16[1536,128]{1,0:T(8,128)(2,1)S(1)}, bf16[1536,128]{1,0:T(8,128)(2,1)S(1)}, bf16[128,1536]{1,0:T(8,128)(2,...) custom-call(s32[32]{0:T(128)S(1)} %copy-done.4, ...), custom_call_target="tpu_custom_call" | custom-call | bytes 4194304 | tf_op jit(solution)/shard_map/prepare/pallas_call | solution.py:99
  18.6 0.0 collective-permute-done.1.prev1.refs_1_
  18.6 0.6 %collective-permute-start.3 = (bf16[768,128]{1,0:T(8,128)(2,1)S(1)}, bf16[768,128]{1,0:T(8,128)(2,1)S(1)}, u32[]{:S(2)}, u32[]{:S(2)}) collective-permute-start(bf16[768,128]{1,0:T(8,128)(2,1)S(1)} %collective-permute-done.1.prev1.refs_1_), channel_id=1, source_target_pairs={{0,1},{1,0},{2,3},{3,2},{4,5},{5,4},{6,7},{7,6},{8,9},{9,8},{10,11... | collective-permute-start | bytes 589832 | tf_op jit(solution)/shard_map/ppermute | solution.py:344
  19.1 0.0 collective-permute-done.4.prev2.refs_2_
  19.1 4.8 %scores_far.1 = (bf16[2688,512]{1,0:T(8,128)(2,1)S(1)}, bf16[2688,512]{1,0:T(8,128)(2,1)S(1)}, f32[8,512]{1,0:T(8,128)S(1)}, bf16[1536,128]{1,0:T(8,128)(2,1)S(1...) custom-call(bf16[768,128]{1,0:T(8,128)(2,1)S(1)} %get-tuple-element.75.own_kv.refs_0_, ...), custom_call_target="tpu_custom_call" | custom-call | flops 1409286144 | tf_op jit(solution)/shard_map/scores_far/pallas_call | solution.py:225
  24.0 0.1 collective-permute-start.7
  24.0 1.3 %collective-permute-start.5 = (bf16[768,128]{1,0:T(8,128)(2,1)S(1)}, bf16[768,128]{1,0:T(8,128)(2,1)S(1)}, u32[]{:S(2)}, u32[]{:S(2)}) collective-permute-start(bf16[768,128]{1,0:T(8,128)(2,1)S(1)} %get-tuple-element.81), channel_id=1, source_target_pairs={{2,0},{4,2},{6,4},{8,6},{10,8},{12,10},{14,12},{15,14},{13,15},{11... | collective-permute-start | bytes 589832 | tf_op jit(solution)/shard_map/ppermute | solution.py:344
  25.3 0.0 collective-permute-done.2.prev1.refs_9_
  25.3 0.0 collective-permute-done.3.prev2.refs_10_
  25.4 4.9 %scores_near.1 = (bf16[2688,512]{1,0:T(8,128)(2,1)S(1)}, bf16[2688,512]{1,0:T(8,128)(2,1)S(1)}, f32[8,512]{1,0:T(8,128)S(1)}, bf16[1536,128]{1,0:T(8,128)(2,1)S(...) custom-call(bf16[768,128]{1,0:T(8,128)(2,1)S(1)} %get-tuple-element.66.own_kv.refs_8_,, ...), custom_call_target="tpu_custom_call" | custom-call | flops 1409286144 | tf_op jit(solution)/shard_map/scores_near/pallas_call | solution.py:225
  30.3 0.0 collective-permute-done.7
  30.3 0.1 add_convert_fusion
  30.3 4.7 %collective-permute-start.8 = (bf16[768,128]{1,0:T(8,128)(2,1)S(1)}, bf16[768,128]{1,0:T(8,128)(2,1)S(1)}, u32[]{:S(2)}, u32[]{:S(2)}) collective-permute-start(bf16[768,128]{1,0:T(8,128)(2,1)S(1)} %add_convert_fusion), channel_id=1, source_target_pairs={{3,1},{5,3},{7,5},{9,7},{11,9},{13,11},{15,13},{14,15},{12,14},{10... | collective-permute-start | bytes 589832 | tf_op jit(solution)/shard_map/ppermute | solution.py:344
  35.1 0.0 collective-permute-done.5.from_far_2
  35.1 0.1 collective-permute-start.6
  35.2 4.1 %block_outputs.1 = (bf16[768,512]{1,0:T(8,128)(2,1)}, bf16[768,512]{1,0:T(8,128)(2,1)}, f32[768,128]{1,0:T(8,128)S(1)}, f32[768,128]{1,0:T(8,128)S(1)}) custom-call(bf16[768,128]{1,0:T(8,128)(2,1)S(1)} %collective-permute-done.5.from_far_2, bf16[768,128]{1,0:T(8,128)(2,1)S(1)} %get-tuple-element.75.own_kv.refs_0_, ...), custom_call_target="tpu_custom_call" | custom-call | tf_op jit(solution)/shard_map/block_outputs/pallas_call | solution.py:300
  39.2 0.9 %collective-permute-done.8.near_1 = bf16[768,128]{1,0:T(8,128)(2,1)S(1)} collective-permute-done((bf16[768,128]{1,0:T(8,128)(2,1)S(1)}, bf16[768,128]{1,0:T(8,128)(2,1)S(1)}, u32[]{:S(2)}, u32[]{:S(2)}) %collective-permute-start.8) | collective-permute-done | bytes 196640 | tf_op jit(solution)/shard_map/ppermute | solution.py:344
  40.2 0.0 collective-permute-done.6.far_1
  40.2 0.8 %total_grads.1 = (bf16[768,128]{1,0:T(8,128)(2,1)}, bf16[768,128]{1,0:T(8,128)(2,1)}) custom-call(f32[768,128]{1,0:T(8,128)S(1)} %get-tuple-element.95.far_own, bf16[768,128]{1,0:T(8,128)(2,1)S(1)} %collective-permute-done.6.far_1, f32[768,128]{1,0:T(8,128)S(1)} %get-tuple-element.97.near_own, bf16[768,128]{1,0:T(8,128)(2,1)S(1)} %collective-permute-done.8.near_1), custom_call_target="tpu_custom_call" | custom-call | tf_op jit(solution)/shard_map/total_grads/pallas_call | solution.py:327
Async XLA Ops:
  2.4 1.7 %collective-permute-start = (bf16[768,128]{1,0:T(8,128)(2,1)}, bf16[768,128]{1,0:T(8,128)(2,1)S(1)}, u32[]{:S(2)}, u32[]{:S(2)}) collective-permute-start(bf16[768,128]{1,0:T(8,128)(2,1)} %get-tuple-element.53), channel_id=1, source_target_pairs={{0,1},{1,0},{2,3},{3,2},{4,5},{5,4},{6,7},{7,6},{8,9},{9,8},{10,11... | collective-permute-start | bytes 589832 | tf_op jit(solution)/shard_map/ppermute | solution.py:344
  4.2 14.4 %collective-permute-start.1 = (bf16[768,128]{1,0:T(8,128)(2,1)S(1)}, bf16[768,128]{1,0:T(8,128)(2,1)S(1)}, u32[]{:S(2)}, u32[]{:S(2)}) collective-permute-start(bf16[768,128]{1,0:T(8,128)(2,1)S(1)} %collective-permute-done), channel_id=1, source_target_pairs={{0,2},{2,4},{4,6},{6,8},{8,10},{10,12},{12,14},{14,15},{15,13},{13... | collective-permute-start | bytes 589832 | tf_op jit(solution)/shard_map/ppermute | solution.py:344
  9.0 10.2 %collective-permute-start.4 = (bf16[768,128]{1,0:T(8,128)(2,1)}, bf16[768,128]{1,0:T(8,128)(2,1)S(1)}, u32[]{:S(2)}, u32[]{:S(2)}) collective-permute-start(bf16[768,128]{1,0:T(8,128)(2,1)} %get-tuple-element.72), channel_id=1, source_target_pairs={{0,2},{2,4},{4,6},{6,8},{8,10},{10,12},{12,14},{14,15},{15,13},{13... | collective-permute-start | bytes 589832 | tf_op jit(solution)/shard_map/ppermute | solution.py:344
  12.4 12.9 %collective-permute-start.2 = (bf16[768,128]{1,0:T(8,128)(2,1)}, bf16[768,128]{1,0:T(8,128)(2,1)S(1)}, u32[]{:S(2)}, u32[]{:S(2)}) collective-permute-start(bf16[768,128]{1,0:T(8,128)(2,1)} %get-tuple-element.72), channel_id=1, source_target_pairs={{0,1},{1,0},{2,3},{3,2},{4,5},{5,4},{6,7},{7,6},{8,9},{9,8},{10,11... | collective-permute-start | bytes 589832 | tf_op jit(solution)/shard_map/ppermute | solution.py:344
  12.5 0.9 %copy-start = (bf16[768,128]{1,0:T(8,128)(2,1)S(1)}, bf16[768,128]{1,0:T(8,128)(2,1)}, u32[]{:S(2)}) copy-start(bf16[768,128]{1,0:T(8,128)(2,1)} %key.3) | copy-start | bytes 589828
  13.4 0.9 %copy-start.1 = (bf16[768,128]{1,0:T(8,128)(2,1)S(1)}, bf16[768,128]{1,0:T(8,128)(2,1)}, u32[]{:S(2)}) copy-start(bf16[768,128]{1,0:T(8,128)(2,1)} %value.3) | copy-start | bytes 589828
  14.3 1.1 %copy-start.2 = (bf16[768,512]{1,0:T(8,128)(2,1)S(1)}, bf16[768,512]{1,0:T(8,128)(2,1)}, u32[]{:S(2)}) copy-start(bf16[768,512]{1,0:T(8,128)(2,1)} %query.1) | copy-start | bytes 2359300
  15.5 1.1 %copy-start.3 = (bf16[768,512]{1,0:T(8,128)(2,1)S(1)}, bf16[768,512]{1,0:T(8,128)(2,1)}, u32[]{:S(2)}) copy-start(bf16[768,512]{1,0:T(8,128)(2,1)} %dout.1) | copy-start | bytes 2359300
  16.6 0.7 %copy-start.4 = (s32[32]{0:T(128)S(1)}, s32[32]{0:T(128)}, u32[]{:S(2)}) copy-start(s32[32]{0:T(128)} %doc_lengths.1) | copy-start | bytes 388
  18.6 6.8 %collective-permute-start.3 = (bf16[768,128]{1,0:T(8,128)(2,1)S(1)}, bf16[768,128]{1,0:T(8,128)(2,1)S(1)}, u32[]{:S(2)}, u32[]{:S(2)}) collective-permute-start(bf16[768,128]{1,0:T(8,128)(2,1)S(1)} %collective-permute-done.1.prev1.refs_1_), channel_id=1, source_target_pairs={{0,1},{1,0},{2,3},{3,2},{4,5},{5,4},{6,7},{7,6},{8,9},{9,8},{10,11... | collective-permute-start | bytes 589832 | tf_op jit(solution)/shard_map/ppermute | solution.py:344
  24.0 6.3 %collective-permute-start.7 = (bf16[768,128]{1,0:T(8,128)(2,1)S(1)}, bf16[768,128]{1,0:T(8,128)(2,1)S(1)}, u32[]{:S(2)}, u32[]{:S(2)}) collective-permute-start(bf16[768,128]{1,0:T(8,128)(2,1)S(1)} %get-tuple-element.99), channel_id=1, source_target_pairs={{0,1},{1,0},{2,3},{3,2},{4,5},{5,4},{6,7},{7,6},{8,9},{9,8},{10,11... | collective-permute-start | bytes 589832 | tf_op jit(solution)/shard_map/ppermute | solution.py:344
  24.0 11.1 %collective-permute-start.5 = (bf16[768,128]{1,0:T(8,128)(2,1)S(1)}, bf16[768,128]{1,0:T(8,128)(2,1)S(1)}, u32[]{:S(2)}, u32[]{:S(2)}) collective-permute-start(bf16[768,128]{1,0:T(8,128)(2,1)S(1)} %get-tuple-element.81), channel_id=1, source_target_pairs={{2,0},{4,2},{6,4},{8,6},{10,8},{12,10},{14,12},{15,14},{13,15},{11... | collective-permute-start | bytes 589832 | tf_op jit(solution)/shard_map/ppermute | solution.py:344
  30.3 9.8 %collective-permute-start.8 = (bf16[768,128]{1,0:T(8,128)(2,1)S(1)}, bf16[768,128]{1,0:T(8,128)(2,1)S(1)}, u32[]{:S(2)}, u32[]{:S(2)}) collective-permute-start(bf16[768,128]{1,0:T(8,128)(2,1)S(1)} %add_convert_fusion), channel_id=1, source_target_pairs={{3,1},{5,3},{7,5},{9,7},{11,9},{13,11},{15,13},{14,15},{12,14},{10... | collective-permute-start | bytes 589832 | tf_op jit(solution)/shard_map/ppermute | solution.py:344
  35.1 5.1 %collective-permute-start.6 = (bf16[768,128]{1,0:T(8,128)(2,1)S(1)}, bf16[768,128]{1,0:T(8,128)(2,1)S(1)}, u32[]{:S(2)}, u32[]{:S(2)}) collective-permute-start(bf16[768,128]{1,0:T(8,128)(2,1)S(1)} %get-tuple-element.96), channel_id=1, source_target_pairs={{0,1},{1,0},{2,3},{3,2},{4,5},{5,4},{6,7},{7,6},{8,9},{9,8},{10,11... | collective-permute-start | bytes 589832 | tf_op jit(solution)/shard_map/ppermute | solution.py:344

commit v5 on v4

--- a/solution.py
+++ b/solution.py
@@ -16,7 +16,8 @@
 VMEM_LIMIT = 24 * 1024 * 1024
 SCALE = 1.0 / math.sqrt(HD)
 VMEM = pl.BlockSpec(memory_space=pltpu.VMEM)
-SMEM = pl.BlockSpec(memory_space=pltpu.SMEM)
+HBM = pl.BlockSpec(memory_space=pltpu.HBM)
+CHUNK = 128
 
 
 def dot_nn(a, b):
@@ -34,11 +35,30 @@
     return jnp.where(in_lower, device, 2 * count - 1 - device)
 
 
-def pack_kernel(rows, key, value, near_out, far_out):
-    for slot, out in ((1, near_out), (0, far_out)):
-        place = pl.ds(half_start(rows, slot), rows)
-        out[0:rows] = key[place, :]
-        out[rows : 2 * rows] = value[place, :]
+def in_hbm(array):
+    return pltpu.with_memory_space_constraint(array, pltpu.HBM)
+
+
+def load_block(rows, slot, key, value, out, sems):
+    place = pl.ds(half_start(rows, slot), rows)
+    return [
+        pltpu.make_async_copy(key.at[place], out.at[0:rows], sems.at[2 * slot]),
+        pltpu.make_async_copy(value.at[place], out.at[rows : 2 * rows], sems.at[2 * slot + 1]),
+    ]
+
+
+def run_copies(copies):
+    for copy in copies:
+        copy.start()
+    for copy in copies:
+        copy.wait()
+
+
+def pack_kernel(rows, key, value, near_out, far_out, sems):
+    run_copies(
+        load_block(rows, 1, key, value, near_out, sems)
+        + load_block(rows, 0, key, value, far_out, sems)
+    )
 
 
 def pack_blocks(key, value):
@@ -47,19 +67,30 @@
     return pl.pallas_call(
         functools.partial(pack_kernel, rows),
         out_shape=(shape, shape),
-        in_specs=[VMEM] * 2,
+        in_specs=[HBM] * 2,
         out_specs=[VMEM] * 2,
+        scratch_shapes=[pltpu.SemaphoreType.DMA((4,))],
         name="pack_blocks",
-    )(key, value)
-
-
-def prepare_kernel(rows, heads, docs, count, doc_lengths, query, dout, key, value, *refs):
+    )(in_hbm(key), in_hbm(value))
+
+
+def prepare_kernel(rows, heads, docs, count, *refs):
+    (doc_hbm, query_hbm, dout_hbm, key, value) = refs[0:5]
+    (doc_lengths, query, dout, sems) = refs[17:]
+    refs = refs[5:17]
     wide = heads * TQ
+    run_copies(
+        [
+            pltpu.make_async_copy(query_hbm, query, sems.at[4]),
+            pltpu.make_async_copy(dout_hbm, dout, sems.at[5]),
+            pltpu.make_async_copy(doc_hbm, doc_lengths, sems.at[6]),
+        ]
+        + load_block(rows, 0, key, value, refs[0], sems)
+        + load_block(rows, 1, key, value, refs[6], sems)
+    )
     for slot in (0, 1):
-        own_kv, query_rows, dout_rows, query_t, dout_t, doc_start = refs[6 * slot : 6 * slot + 6]
+        _, query_rows, dout_rows, query_t, dout_t, doc_start = refs[6 * slot : 6 * slot + 6]
         own_rows = half_start(rows, slot)
-        own_kv[0:rows] = key[pl.ds(own_rows, rows), :]
-        own_kv[rows : 2 * rows] = value[pl.ds(own_rows, rows), :]
         for step in range(rows // TQ):
             source = pl.ds(own_rows + step * TQ, TQ)
             for h in range(heads):
@@ -99,12 +130,18 @@
     return pl.pallas_call(
         functools.partial(prepare_kernel, rows, heads, doc_lengths.shape[0], count),
         out_shape=(pair, stacked, stacked, stacked_t, stacked_t, starts) * 2,
-        in_specs=[SMEM] + [VMEM] * 4,
+        in_specs=[HBM] * 5,
         out_specs=[VMEM] * 12,
+        scratch_shapes=[
+            pltpu.SMEM(doc_lengths.shape, doc_lengths.dtype),
+            pltpu.VMEM(query.shape, query.dtype),
+            pltpu.VMEM(dout.shape, dout.dtype),
+            pltpu.SemaphoreType.DMA((7,)),
+        ],
         compiler_params=pltpu.CompilerParams(vmem_limit_bytes=VMEM_LIMIT),
         cost_estimate=pl.CostEstimate(flops=0, bytes_accessed=4 * 2**20, transcendentals=0),
         name="prepare",
-    )(doc_lengths, query, dout, key, value)
+    )(*(in_hbm(array) for array in (doc_lengths, query, dout, key, value)))
 
 
 def scores_kernel(
@@ -127,70 +164,76 @@
     dout_scaled,
     prev1_out,
     prev2_out,
-    all_scores,
-    all_dprobs,
+    scores,
+    dprobs,
     dk,
     dv,
 ):
     back = 2 * rows
     width = back + TQ
     wide = heads * TQ
+    steps = rows // TQ
     base2 = SCALE * math.log2(math.e)
     block_pos = block_number(count, slot) * rows
-
-    for step in range(rows // TQ):
-        first = step * TQ
+    chunks = width // CHUNK
+
+    def source(step, chunk):
+        row = step * TQ + chunk * CHUNK
+        return (prev2, prev1, own_kv)[row // rows], row % rows
+
+    def score_chunk(step, chunk, row_max):
+        low = doc_start[step : step + 1, :] - (block_pos - back + step * TQ)
+        high = lax.broadcasted_iota(jnp.int32, (1, TQ), 1) + back
+        array, row = source(step, chunk)
         tile = slice(step * wide, (step + 1) * wide)
-        scores, dprobs = all_scores.at[step], all_dprobs.at[step]
-        sources = (
-            (prev2, first, rows - first, 0),
-            (prev1, 0, rows, rows - first),
-            (own_kv, 0, first + TQ, back - first),
+        product = dot_nn(array[row : row + CHUNK, :], query_t[:, tile])
+        for start in range(0, CHUNK, GROUP):
+            place = chunk * CHUNK + start
+            at = lax.broadcasted_iota(jnp.int32, (GROUP, TQ), 0) + place
+            allowed = at >= low
+            if place >= back:
+                allowed = jnp.logical_and(allowed, at <= high)
+            for h in range(heads):
+                lanes = slice(h * TQ, (h + 1) * TQ)
+                part = jnp.where(allowed, product[start : start + GROUP, lanes], masked_score)
+                scores[step, place : place + GROUP, lanes] = part
+                for row8 in range(0, GROUP, 8):
+                    row_max[h] = jnp.maximum(row_max[h], part[row8 : row8 + 8, :])
+
+    def start_max():
+        return [jnp.full((8, TQ), masked_score, jnp.float32)] * heads
+
+    following = start_max()
+    for chunk in range(chunks):
+        score_chunk(0, chunk, following)
+    for step in range(steps):
+        tile = slice(step * wide, (step + 1) * wide)
+        out = step * width
+        row_max = jnp.concatenate(
+            [jnp.max(part, axis=0, keepdims=True) * base2 for part in following], axis=1
         )
-        low = doc_start[step : step + 1, :] - (block_pos - back + first)
-        high = lax.broadcasted_iota(jnp.int32, (1, TQ), 1) + back
-        row_max = [jnp.full((8, TQ), masked_score, jnp.float32)] * heads
-        for source, row, length, place in sources:
-            product = dot_nn(source[row : row + length, :], query_t[:, tile])
-            for start in range(0, length, GROUP):
-                at = lax.broadcasted_iota(jnp.int32, (GROUP, TQ), 0) + (place + start)
-                allowed = at >= low
-                if place + start >= back:
-                    allowed = jnp.logical_and(allowed, at <= high)
-                here = slice(place + start, place + start + GROUP)
-                for h in range(heads):
-                    lanes = slice(h * TQ, (h + 1) * TQ)
-                    part = jnp.where(allowed, product[start : start + GROUP, lanes], masked_score)
-                    scores[here, lanes] = part
-                    for row8 in range(0, GROUP, 8):
-                        row_max[h] = jnp.maximum(row_max[h], part[row8 : row8 + 8, :])
-        row_max = jnp.concatenate(
-            [jnp.max(part, axis=0, keepdims=True) * base2 for part in row_max], axis=1
-        )
+        following = start_max()
         total = jnp.zeros((8, wide), jnp.float32)
         delta = jnp.zeros((8, wide), jnp.float32)
-        out = step * width
-        for source, row, length, place in sources:
-            product = dot_nn(source[rows + row : rows + row + length, :], dout_t[:, tile])
-            for start in range(0, length, GROUP):
-                here = slice(place + start, place + start + GROUP)
-                there = slice(out + place + start, out + place + start + GROUP)
+        for chunk in range(chunks):
+            array, row = source(step, chunk)
+            product = dot_nn(array[rows + row : rows + row + CHUNK, :], dout_t[:, tile])
+            for start in range(0, CHUNK, GROUP):
+                place = chunk * CHUNK + start
+                there = slice(out + place, out + place + GROUP)
                 dprob = product[start : start + GROUP, :]
-                dprobs[here, :] = dprob
-                part = jnp.exp2(scores[here, :] * base2 - row_max)
+                dprobs[step, place : place + GROUP, :] = dprob.astype(jnp.bfloat16)
+                part = jnp.exp2(scores[step, place : place + GROUP, :] * base2 - row_max)
                 weights[there, :] = part.astype(jnp.bfloat16)
                 term = part * dprob
                 for row8 in range(0, GROUP, 8):
                     total = total + part[row8 : row8 + 8, :]
                     delta = delta + term[row8 : row8 + 8, :]
+            if step + 1 < steps:
+                score_chunk(step + 1, chunk, following)
         inverse = 1.0 / jnp.sum(total, axis=0, keepdims=True)
-        delta = jnp.sum(delta, axis=0, keepdims=True) * inverse
+        delta = (jnp.sum(delta, axis=0, keepdims=True) * inverse).astype(jnp.bfloat16)
         inverses[step : step + 1, :] = inverse
-        for start in range(0, width, GROUP):
-            there = slice(out + start, out + start + GROUP)
-            dscores[there, :] = weights[there, :] * (
-                dprobs[start : start + GROUP, :] - delta
-            ).astype(jnp.bfloat16)
         for h in range(heads):
             part = slice(h * TQ, (h + 1) * TQ)
             place = slice(step * wide + h * TQ, step * wide + (h + 1) * TQ)
@@ -199,12 +242,22 @@
                 scaled[place, :] = (rows_ref[place, :].astype(jnp.float32) * column).astype(
                     jnp.bfloat16
                 )
-        for total_ref, terms, side in ((dv, weights, dout_scaled), (dk, dscores, query_scaled)):
-            term = dot_nn(terms[out : out + back - first, :], side[tile, :])
-            if step == 0:
-                total_ref[...] = term
-            else:
-                total_ref[first:back] += term
+        for chunk in range(chunks):
+            place = slice(chunk * CHUNK, (chunk + 1) * CHUNK)
+            there = slice(out + chunk * CHUNK, out + (chunk + 1) * CHUNK)
+            dscores[there, :] = weights[there, :] * (dprobs[step, place, :] - delta)
+            row = step * TQ + chunk * CHUNK
+            if row >= back:
+                continue
+            for total_ref, terms, side in (
+                (dv, weights, dout_scaled),
+                (dk, dscores, query_scaled),
+            ):
+                term = dot_nn(terms[there, :], side[tile, :])
+                if step == 0 or chunk == chunks - 1:
+                    total_ref[row : row + CHUNK] = term
+                else:
+                    total_ref[row : row + CHUNK] += term
 
     prev2_out[0:rows] = (dk[0:rows] * SCALE).astype(prev2_out.dtype)
     prev2_out[rows:back] = dv[0:rows].astype(prev2_out.dtype)
@@ -229,7 +282,7 @@
         out_specs=[VMEM] * 7,
         scratch_shapes=[
             pltpu.VMEM((steps, width, wide), jnp.float32),
-            pltpu.VMEM((steps, width, wide), jnp.float32),
+            pltpu.VMEM((steps, width, wide), jnp.bfloat16),
             pltpu.VMEM((2 * rows, HD), jnp.float32),
             pltpu.VMEM((2 * rows, HD), jnp.float32),
         ],

time: 41.3 us -> 40.9 us (level)
  local copies, waits for them, and re-layouts: 4.77 us -> 0 us
  waiting for transfers between devices: 2.24 us -> 6.06 us
  Pallas kernels: 17.7 us -> 18.2 us
    unnamed x10 -> x0, local copies, waits for them, and re-layouts: 4.77 us -> none
    ppermute x9, waiting for transfers between devices: 2.24 us -> 6.06 us  [move(): return lax.ppermute(array, 'ctx', pairs)]
    pallas_call x1, Pallas kernels: 1.31 us -> 2.24 us  [prepare(): pl.pallas_call(functools.partial(prepare_kernel, rows, heads, doc_lengths...]
    pallas_call x2, Pallas kernels: 9.72 us -> 9.3 us  [block_scores(): pl.pallas_call(functools.partial(scores_kernel, rows, heads, count, slot)...]
  transfers between devices with their start and end apart: 9 -> 9, of which waited for: 2 -> 4; matrix products, arithmetic and copies ran while one was open for 0% -> 0% of each run, Pallas kernels for 37% -> 39%
where the time goes in v5:
time: 40.9 us; the launch traced here: 40.4 us
  Pallas kernels  18.2 us (44%)
  starting transfers between devices  15.3 us (37%)
  waiting for transfers between devices  6.06 us (15%)
  between operations  0.76 us (2%)
    ppermute x9, starting transfers between devices, move(): return lax.ppermute(array, 'ctx', pairs)  15.3 us
    pallas_call x2, Pallas kernels, block_scores(): pl.pallas_call(functools.partial(scores_kernel, rows, heads, count, slot)...  9.3 us
    ppermute x9, waiting for transfers between devices, move(): return lax.ppermute(array, 'ctx', pairs)  6.06 us
    pallas_call x1, Pallas kernels, block_outputs(): pl.pallas_call(functools.partial(outputs_kernel, rows, heads), out_shape=...  4.04 us
    pallas_call x1, Pallas kernels, prepare(): pl.pallas_call(functools.partial(prepare_kernel, rows, heads, doc_lengths...  2.24 us
    pallas_call x1, Pallas kernels, pack_blocks(): pl.pallas_call(functools.partial(pack_kernel, rows), out_shape=(shape, sh...  1.82 us
  transfers between devices with their start and end apart: 9, of which 4 were waited for; matrix products, arithmetic and copies ran while one was open for 0% of the time, Pallas kernels for 39%

profile of v5, /device:TPU:0, one launch (start us, length us, event | category | flops | bytes accessed | tf_op | source)
XLA Modules:
  0.0 40.4 jit_solution(12317647492446799634)
XLA Ops:
  0.6 1.8 %pack_blocks.1 = (bf16[768,128]{1,0:T(8,128)(2,1)}, bf16[768,128]{1,0:T(8,128)(2,1)}) custom-call(bf16[768,128]{1,0:T(8,128)(2,1)} %refs_3_.1, bf16[768,128]{1,0:T(8,128)(2,1)} %refs_4_.1), custom_call_target="tpu_custom_call" | custom-call | tf_op jit(solution)/shard_map/pack_blocks/pallas_call | solution.py:67
  2.5 0.5 %collective-permute-start = (bf16[768,128]{1,0:T(8,128)(2,1)}, bf16[768,128]{1,0:T(8,128)(2,1)S(1)}, u32[]{:S(2)}, u32[]{:S(2)}) collective-permute-start(bf16[768,128]{1,0:T(8,128)(2,1)} %get-tuple-element.53), channel_id=1, source_target_pairs={{0,1},{1,0},{2,3},{3,2},{4,5},{5,4},{6,7},{7,6},{8,9},{9,8},{10,11... | collective-permute-start | bytes 589832 | tf_op jit(solution)/shard_map/ppermute | solution.py:397
  3.0 1.3 %collective-permute-done = bf16[768,128]{1,0:T(8,128)(2,1)S(1)} collective-permute-done((bf16[768,128]{1,0:T(8,128)(2,1)}, bf16[768,128]{1,0:T(8,128)(2,1)S(1)}, u32[]{:S(2)}, u32[]{:S(2)}) %collective-permute-start) | collective-permute-done | bytes 196640 | tf_op jit(solution)/shard_map/ppermute | solution.py:397
  4.3 4.8 %collective-permute-start.1 = (bf16[768,128]{1,0:T(8,128)(2,1)S(1)}, bf16[768,128]{1,0:T(8,128)(2,1)S(1)}, u32[]{:S(2)}, u32[]{:S(2)}) collective-permute-start(bf16[768,128]{1,0:T(8,128)(2,1)S(1)} %collective-permute-done), channel_id=1, source_target_pairs={{0,2},{2,4},{4,6},{6,8},{8,10},{10,12},{12,14},{14,15},{15,13},{13... | collective-permute-start | bytes 589832 | tf_op jit(solution)/shard_map/ppermute | solution.py:397
  9.1 3.4 %collective-permute-start.4 = (bf16[768,128]{1,0:T(8,128)(2,1)}, bf16[768,128]{1,0:T(8,128)(2,1)S(1)}, u32[]{:S(2)}, u32[]{:S(2)}) collective-permute-start(bf16[768,128]{1,0:T(8,128)(2,1)} %get-tuple-element.72), channel_id=1, source_target_pairs={{0,2},{2,4},{4,6},{6,8},{8,10},{10,12},{12,14},{14,15},{15,13},{13... | collective-permute-start | bytes 589832 | tf_op jit(solution)/shard_map/ppermute | solution.py:397
  12.5 0.1 collective-permute-start.2
  12.6 2.2 %prepare.1 = (bf16[768,128]{1,0:T(8,128)(2,1)S(1)}, bf16[1536,128]{1,0:T(8,128)(2,1)S(1)}, bf16[1536,128]{1,0:T(8,128)(2,1)S(1)}, bf16[128,1536]{1,0:T(8,128)(2,...) custom-call(s32[32]{0:T(128)} %refs_0_.1, ...), custom_call_target="tpu_custom_call" | custom-call | bytes 4194304 | tf_op jit(solution)/shard_map/prepare/pallas_call | solution.py:130
  14.8 1.6 %collective-permute-done.1.prev1.refs_1_ = bf16[768,128]{1,0:T(8,128)(2,1)S(1)} collective-permute-done((bf16[768,128]{1,0:T(8,128)(2,1)S(1)}, bf16[768,128]{1,0:T(8,128)(2,1)S(1)}, u32[]{:S(2)}, u32[]{:S(2)}) %collective-permute-start.1) | collective-permute-done | bytes 196640 | tf_op jit(solution)/shard_map/ppermute | solution.py:397
  16.4 0.0 collective-permute-start.3
  16.4 2.2 %collective-permute-done.4.prev2.refs_2_ = bf16[768,128]{1,0:T(8,128)(2,1)S(1)} collective-permute-done((bf16[768,128]{1,0:T(8,128)(2,1)}, bf16[768,128]{1,0:T(8,128)(2,1)S(1)}, u32[]{:S(2)}, u32[]{:S(2)}) %collective-permute-start.4) | collective-permute-done | bytes 196640 | tf_op jit(solution)/shard_map/ppermute | solution.py:397
  18.6 4.5 %scores_far.1 = (bf16[2688,512]{1,0:T(8,128)(2,1)S(1)}, bf16[2688,512]{1,0:T(8,128)(2,1)S(1)}, f32[8,512]{1,0:T(8,128)S(1)}, bf16[1536,128]{1,0:T(8,128)(2,1)S(1...) custom-call(bf16[768,128]{1,0:T(8,128)(2,1)S(1)} %get-tuple-element.75.own_kv.refs_0_, ...), custom_call_target="tpu_custom_call" | custom-call | flops 1409286144 | tf_op jit(solution)/shard_map/scores_far/pallas_call | solution.py:278
  23.1 0.1 collective-permute-start.7
  23.2 1.3 %collective-permute-start.5 = (bf16[768,128]{1,0:T(8,128)(2,1)S(1)}, bf16[768,128]{1,0:T(8,128)(2,1)S(1)}, u32[]{:S(2)}, u32[]{:S(2)}) collective-permute-start(bf16[768,128]{1,0:T(8,128)(2,1)S(1)} %get-tuple-element.81), channel_id=1, source_target_pairs={{2,0},{4,2},{6,4},{8,6},{10,8},{12,10},{14,12},{15,14},{13,15},{11... | collective-permute-start | bytes 589832 | tf_op jit(solution)/shard_map/ppermute | solution.py:397
  24.5 0.0 collective-permute-done.2.prev1.refs_9_
  24.5 0.0 collective-permute-done.3.prev2.refs_10_
  24.5 4.8 %scores_near.1 = (bf16[2688,512]{1,0:T(8,128)(2,1)S(1)}, bf16[2688,512]{1,0:T(8,128)(2,1)S(1)}, f32[8,512]{1,0:T(8,128)S(1)}, bf16[1536,128]{1,0:T(8,128)(2,1)S(...) custom-call(bf16[768,128]{1,0:T(8,128)(2,1)S(1)} %get-tuple-element.66.own_kv.refs_8_,, ...), custom_call_target="tpu_custom_call" | custom-call | flops 1409286144 | tf_op jit(solution)/shard_map/scores_near/pallas_call | solution.py:278
  29.4 0.0 collective-permute-done.7
  29.4 0.1 add_convert_fusion
  29.4 5.1 %collective-permute-start.8 = (bf16[768,128]{1,0:T(8,128)(2,1)S(1)}, bf16[768,128]{1,0:T(8,128)(2,1)S(1)}, u32[]{:S(2)}, u32[]{:S(2)}) collective-permute-start(bf16[768,128]{1,0:T(8,128)(2,1)S(1)} %add_convert_fusion), channel_id=1, source_target_pairs={{3,1},{5,3},{7,5},{9,7},{11,9},{13,11},{15,13},{14,15},{12,14},{10... | collective-permute-start | bytes 589832 | tf_op jit(solution)/shard_map/ppermute | solution.py:397
  34.5 0.0 collective-permute-done.5.from_far_2
  34.5 0.1 collective-permute-start.6
  34.6 4.0 %block_outputs.1 = (bf16[768,512]{1,0:T(8,128)(2,1)}, bf16[768,512]{1,0:T(8,128)(2,1)}, f32[768,128]{1,0:T(8,128)S(1)}, f32[768,128]{1,0:T(8,128)S(1)}) custom-call(bf16[768,128]{1,0:T(8,128)(2,1)S(1)} %collective-permute-done.5.from_far_2, bf16[768,128]{1,0:T(8,128)(2,1)S(1)} %get-tuple-element.75.own_kv.refs_0_, ...), custom_call_target="tpu_custom_call" | custom-call | tf_op jit(solution)/shard_map/block_outputs/pallas_call | solution.py:353
  38.7 1.0 %collective-permute-done.8.near_1 = bf16[768,128]{1,0:T(8,128)(2,1)S(1)} collective-permute-done((bf16[768,128]{1,0:T(8,128)(2,1)S(1)}, bf16[768,128]{1,0:T(8,128)(2,1)S(1)}, u32[]{:S(2)}, u32[]{:S(2)}) %collective-permute-start.8) | collective-permute-done | bytes 196640 | tf_op jit(solution)/shard_map/ppermute | solution.py:397
  39.6 0.0 collective-permute-done.6.far_1
  39.6 0.8 %total_grads.1 = (bf16[768,128]{1,0:T(8,128)(2,1)}, bf16[768,128]{1,0:T(8,128)(2,1)}) custom-call(f32[768,128]{1,0:T(8,128)S(1)} %get-tuple-element.95.far_own, bf16[768,128]{1,0:T(8,128)(2,1)S(1)} %collective-permute-done.6.far_1, f32[768,128]{1,0:T(8,128)S(1)} %get-tuple-element.97.near_own, bf16[768,128]{1,0:T(8,128)(2,1)S(1)} %collective-permute-done.8.near_1), custom_call_target="tpu_custom_call" | custom-call | tf_op jit(solution)/shard_map/total_grads/pallas_call | solution.py:380
Async XLA Ops:
  2.5 1.8 %collective-permute-start = (bf16[768,128]{1,0:T(8,128)(2,1)}, bf16[768,128]{1,0:T(8,128)(2,1)S(1)}, u32[]{:S(2)}, u32[]{:S(2)}) collective-permute-start(bf16[768,128]{1,0:T(8,128)(2,1)} %get-tuple-element.53), channel_id=1, source_target_pairs={{0,1},{1,0},{2,3},{3,2},{4,5},{5,4},{6,7},{7,6},{8,9},{9,8},{10,11... | collective-permute-start | bytes 589832 | tf_op jit(solution)/shard_map/ppermute | solution.py:397
  4.3 12.2 %collective-permute-start.1 = (bf16[768,128]{1,0:T(8,128)(2,1)S(1)}, bf16[768,128]{1,0:T(8,128)(2,1)S(1)}, u32[]{:S(2)}, u32[]{:S(2)}) collective-permute-start(bf16[768,128]{1,0:T(8,128)(2,1)S(1)} %collective-permute-done), channel_id=1, source_target_pairs={{0,2},{2,4},{4,6},{6,8},{8,10},{10,12},{12,14},{14,15},{15,13},{13... | collective-permute-start | bytes 589832 | tf_op jit(solution)/shard_map/ppermute | solution.py:397
  9.1 9.6 %collective-permute-start.4 = (bf16[768,128]{1,0:T(8,128)(2,1)}, bf16[768,128]{1,0:T(8,128)(2,1)S(1)}, u32[]{:S(2)}, u32[]{:S(2)}) collective-permute-start(bf16[768,128]{1,0:T(8,128)(2,1)} %get-tuple-element.72), channel_id=1, source_target_pairs={{0,2},{2,4},{4,6},{6,8},{8,10},{10,12},{12,14},{14,15},{15,13},{13... | collective-permute-start | bytes 589832 | tf_op jit(solution)/shard_map/ppermute | solution.py:397
  12.5 12.0 %collective-permute-start.2 = (bf16[768,128]{1,0:T(8,128)(2,1)}, bf16[768,128]{1,0:T(8,128)(2,1)S(1)}, u32[]{:S(2)}, u32[]{:S(2)}) collective-permute-start(bf16[768,128]{1,0:T(8,128)(2,1)} %get-tuple-element.72), channel_id=1, source_target_pairs={{0,1},{1,0},{2,3},{3,2},{4,5},{5,4},{6,7},{7,6},{8,9},{9,8},{10,11... | collective-permute-start | bytes 589832 | tf_op jit(solution)/shard_map/ppermute | solution.py:397
  16.4 8.1 %collective-permute-start.3 = (bf16[768,128]{1,0:T(8,128)(2,1)S(1)}, bf16[768,128]{1,0:T(8,128)(2,1)S(1)}, u32[]{:S(2)}, u32[]{:S(2)}) collective-permute-start(bf16[768,128]{1,0:T(8,128)(2,1)S(1)} %collective-permute-done.1.prev1.refs_1_), channel_id=1, source_target_pairs={{0,1},{1,0},{2,3},{3,2},{4,5},{5,4},{6,7},{7,6},{8,9},{9,8},{10,11... | collective-permute-start | bytes 589832 | tf_op jit(solution)/shard_map/ppermute | solution.py:397
  23.1 6.2 %collective-permute-start.7 = (bf16[768,128]{1,0:T(8,128)(2,1)S(1)}, bf16[768,128]{1,0:T(8,128)(2,1)S(1)}, u32[]{:S(2)}, u32[]{:S(2)}) collective-permute-start(bf16[768,128]{1,0:T(8,128)(2,1)S(1)} %get-tuple-element.99), channel_id=1, source_target_pairs={{0,1},{1,0},{2,3},{3,2},{4,5},{5,4},{6,7},{7,6},{8,9},{9,8},{10,11... | collective-permute-start | bytes 589832 | tf_op jit(solution)/shard_map/ppermute | solution.py:397
  23.2 11.3 %collective-permute-start.5 = (bf16[768,128]{1,0:T(8,128)(2,1)S(1)}, bf16[768,128]{1,0:T(8,128)(2,1)S(1)}, u32[]{:S(2)}, u32[]{:S(2)}) collective-permute-start(bf16[768,128]{1,0:T(8,128)(2,1)S(1)} %get-tuple-element.81), channel_id=1, source_target_pairs={{2,0},{4,2},{6,4},{8,6},{10,8},{12,10},{14,12},{15,14},{13,15},{11... | collective-permute-start | bytes 589832 | tf_op jit(solution)/shard_map/ppermute | solution.py:397
  29.4 10.2 %collective-permute-start.8 = (bf16[768,128]{1,0:T(8,128)(2,1)S(1)}, bf16[768,128]{1,0:T(8,128)(2,1)S(1)}, u32[]{:S(2)}, u32[]{:S(2)}) collective-permute-start(bf16[768,128]{1,0:T(8,128)(2,1)S(1)} %add_convert_fusion), channel_id=1, source_target_pairs={{3,1},{5,3},{7,5},{9,7},{11,9},{13,11},{15,13},{14,15},{12,14},{10... | collective-permute-start | bytes 589832 | tf_op jit(solution)/shard_map/ppermute | solution.py:397
  34.5 5.1 %collective-permute-start.6 = (bf16[768,128]{1,0:T(8,128)(2,1)S(1)}, bf16[768,128]{1,0:T(8,128)(2,1)S(1)}, u32[]{:S(2)}, u32[]{:S(2)}) collective-permute-start(bf16[768,128]{1,0:T(8,128)(2,1)S(1)} %get-tuple-element.96), channel_id=1, source_target_pairs={{0,1},{1,0},{2,3},{3,2},{4,5},{5,4},{6,7},{7,6},{8,9},{9,8},{10,11... | collective-permute-start | bytes 589832 | tf_op jit(solution)/shard_map/ppermute | solution.py:397

commit v6 on v5

--- a/solution.py
+++ b/solution.py
@@ -18,6 +18,10 @@
 VMEM = pl.BlockSpec(memory_space=pltpu.VMEM)
 HBM = pl.BlockSpec(memory_space=pltpu.HBM)
 CHUNK = 128
+
+
+def dot_nt(a, b):
+    return lax.dot_general(a, b, (((1,), (1,)), ((), ())), preferred_element_type=jnp.float32)
 
 
 def dot_nn(a, b):
@@ -76,8 +80,8 @@
 
 def prepare_kernel(rows, heads, docs, count, *refs):
     (doc_hbm, query_hbm, dout_hbm, key, value) = refs[0:5]
-    (doc_lengths, query, dout, sems) = refs[17:]
-    refs = refs[5:17]
+    (doc_lengths, query, dout, sems) = refs[13:]
+    refs = refs[5:13]
     wide = heads * TQ
     run_copies(
         [
@@ -86,23 +90,18 @@
             pltpu.make_async_copy(doc_hbm, doc_lengths, sems.at[6]),
         ]
         + load_block(rows, 0, key, value, refs[0], sems)
-        + load_block(rows, 1, key, value, refs[6], sems)
+        + load_block(rows, 1, key, value, refs[4], sems)
     )
     for slot in (0, 1):
-        _, query_rows, dout_rows, query_t, dout_t, doc_start = refs[6 * slot : 6 * slot + 6]
+        _, query_t, dout_t, doc_start = refs[4 * slot : 4 * slot + 4]
         own_rows = half_start(rows, slot)
         for step in range(rows // TQ):
             source = pl.ds(own_rows + step * TQ, TQ)
             for h in range(heads):
                 place = slice(step * wide + h * TQ, step * wide + (h + 1) * TQ)
                 columns = slice(h * HD, (h + 1) * HD)
-                for wide_ref, rows_ref, t_ref in (
-                    (query, query_rows, query_t),
-                    (dout, dout_rows, dout_t),
-                ):
-                    part = wide_ref[source, columns]
-                    rows_ref[place, :] = part
-                    t_ref[:, place] = jnp.transpose(part)
+                query_t[:, place] = jnp.transpose(query[source, columns])
+                dout_t[:, place] = jnp.transpose(dout[source, columns])
         at = (
             block_number(count, slot) * rows
             + lax.broadcasted_iota(jnp.int32, (8, TQ), 0) * TQ
@@ -124,14 +123,13 @@
     rows = query.shape[0] // 2
     heads = query.shape[1] // HD
     pair = jax.ShapeDtypeStruct((2 * rows, HD), key.dtype)
-    stacked = jax.ShapeDtypeStruct((rows * heads, HD), query.dtype)
     stacked_t = jax.ShapeDtypeStruct((HD, rows * heads), query.dtype)
     starts = jax.ShapeDtypeStruct((8, TQ), jnp.int32)
     return pl.pallas_call(
         functools.partial(prepare_kernel, rows, heads, doc_lengths.shape[0], count),
-        out_shape=(pair, stacked, stacked, stacked_t, stacked_t, starts) * 2,
+        out_shape=(pair, stacked_t, stacked_t, starts) * 2,
         in_specs=[HBM] * 5,
-        out_specs=[VMEM] * 12,
+        out_specs=[VMEM] * 8,
         scratch_shapes=[
             pltpu.SMEM(doc_lengths.shape, doc_lengths.dtype),
             pltpu.VMEM(query.shape, query.dtype),
@@ -150,8 +148,6 @@
     count,
     slot,
     own_kv,
-    query_rows,
-    dout_rows,
     query_t,
     dout_t,
     doc_start,
@@ -234,57 +230,46 @@
         inverse = 1.0 / jnp.sum(total, axis=0, keepdims=True)
         delta = (jnp.sum(delta, axis=0, keepdims=True) * inverse).astype(jnp.bfloat16)
         inverses[step : step + 1, :] = inverse
-        for h in range(heads):
-            part = slice(h * TQ, (h + 1) * TQ)
-            place = slice(step * wide + h * TQ, step * wide + (h + 1) * TQ)
-            column = jnp.transpose(jnp.broadcast_to(inverse[:, part], (TQ, TQ)))
-            for rows_ref, scaled in ((query_rows, query_scaled), (dout_rows, dout_scaled)):
-                scaled[place, :] = (rows_ref[place, :].astype(jnp.float32) * column).astype(
-                    jnp.bfloat16
-                )
-        for chunk in range(chunks):
-            place = slice(chunk * CHUNK, (chunk + 1) * CHUNK)
-            there = slice(out + chunk * CHUNK, out + (chunk + 1) * CHUNK)
-            dscores[there, :] = weights[there, :] * (dprobs[step, place, :] - delta)
-            row = step * TQ + chunk * CHUNK
-            if row >= back:
-                continue
-            for total_ref, terms, side in (
-                (dv, weights, dout_scaled),
-                (dk, dscores, query_scaled),
-            ):
-                term = dot_nn(terms[there, :], side[tile, :])
-                if step == 0 or chunk == chunks - 1:
-                    total_ref[row : row + CHUNK] = term
-                else:
-                    total_ref[row : row + CHUNK] += term
-
-    prev2_out[0:rows] = (dk[0:rows] * SCALE).astype(prev2_out.dtype)
-    prev2_out[rows:back] = dv[0:rows].astype(prev2_out.dtype)
-    prev1_out[0:rows] = (dk[rows:back] * SCALE).astype(prev1_out.dtype)
-    prev1_out[rows:back] = dv[rows:back].astype(prev1_out.dtype)
+        for array, scaled in ((query_t, query_scaled), (dout_t, dout_scaled)):
+            scaled[:, tile] = (array[:, tile].astype(jnp.float32) * inverse).astype(jnp.bfloat16)
+        delta = jnp.broadcast_to(delta, (16, wide))
+        for start in range(0, width, 16):
+            there = slice(out + start, out + start + 16)
+            dscores[there, :] = weights[there, :] * (dprobs[step, start : start + 16, :] - delta)
+        first = step * TQ
+        there = slice(out, out + back - first)
+        for total_ref, terms, side in ((dv, weights, dout_scaled), (dk, dscores, query_scaled)):
+            term = dot_nt(side[:, tile], terms[there, :])
+            if step == 0:
+                total_ref[...] = term
+            else:
+                total_ref[:, first:back] += term
+
+    for out, place in ((prev2_out, slice(0, rows)), (prev1_out, slice(rows, back))):
+        out[0:HD] = (dk[:, place] * SCALE).astype(out.dtype)
+        out[HD : 2 * HD] = dv[:, place].astype(out.dtype)
 
 
 def block_scores(slot, count, prepared, prev1, prev2):
     rows = prev1.shape[0] // 2
-    heads = prepared[1].shape[0] // rows
+    heads = prepared[1].shape[1] // rows
     steps = rows // TQ
     width = 2 * rows + TQ
     wide = heads * TQ
-    pair = jax.ShapeDtypeStruct((2 * rows, HD), jnp.bfloat16)
+    pair = jax.ShapeDtypeStruct((2 * HD, rows), jnp.bfloat16)
     kept = jax.ShapeDtypeStruct((steps * width, wide), jnp.bfloat16)
     inverses = jax.ShapeDtypeStruct((8, wide), jnp.float32)
-    stacked = jax.ShapeDtypeStruct((rows * heads, HD), jnp.bfloat16)
+    stacked = jax.ShapeDtypeStruct((HD, rows * heads), jnp.bfloat16)
     return pl.pallas_call(
         functools.partial(scores_kernel, rows, heads, count, slot),
         out_shape=(kept, kept, inverses, stacked, stacked, pair, pair),
-        in_specs=[VMEM] * 8,
+        in_specs=[VMEM] * 6,
         out_specs=[VMEM] * 7,
         scratch_shapes=[
             pltpu.VMEM((steps, width, wide), jnp.float32),
             pltpu.VMEM((steps, width, wide), jnp.bfloat16),
-            pltpu.VMEM((2 * rows, HD), jnp.float32),
-            pltpu.VMEM((2 * rows, HD), jnp.float32),
+            pltpu.VMEM((HD, 2 * rows), jnp.float32),
+            pltpu.VMEM((HD, 2 * rows), jnp.float32),
         ],
         compiler_params=pltpu.CompilerParams(vmem_limit_bytes=VMEM_LIMIT),
         cost_estimate=pl.CostEstimate(
@@ -317,16 +302,19 @@
             tail = slice(out + back - first, out + width)
             for offset, terms, side, factor in (
                 (0, dscores, query_scaled, SCALE),
-                (rows, weights, dout_scaled, 1.0),
+                (HD, weights, dout_scaled, 1.0),
             ):
-                term = dot_nn(terms[tail, :], side[tile, :]) * factor
-                place = slice(offset, offset + first + TQ)
+                term = dot_nt(side[:, tile], terms[tail, :]) * factor
+                side_rows = slice(offset, offset + HD)
+                place = slice(0, first + TQ)
                 if step < rows // TQ - 1:
-                    own_out[place] += term
+                    own_out[side_rows, place] += term
                 elif slot == 0:
-                    own_out[place] = term + from_far_2[place].astype(jnp.float32)
+                    own_out[side_rows, place] = term + from_far_2[side_rows, place].astype(
+                        jnp.float32
+                    )
                 else:
-                    own_out[place] = term
+                    own_out[side_rows, place] = term
             window = slice(first, first + width)
             inverse = inverses[step : step + 1, :]
             attended_t = dot_nn(values_t[:, window], weights[out : out + width, :]) * inverse
@@ -349,7 +337,7 @@
     rows = query.shape[0] // 2
     heads = query.shape[1] // HD
     wide = jax.ShapeDtypeStruct(query.shape, query.dtype)
-    own = jax.ShapeDtypeStruct((2 * rows, HD), jnp.float32)
+    own = jax.ShapeDtypeStruct((2 * HD, rows), jnp.float32)
     return pl.pallas_call(
         functools.partial(outputs_kernel, rows, heads),
         out_shape=(wide, wide, own, own),
@@ -370,12 +358,12 @@
     near = near_own[...] + near_1[...].astype(jnp.float32)
     for slot, total in ((0, far), (1, near)):
         place = pl.ds(half_start(rows, slot), rows)
-        grad_key[place, :] = total[0:rows].astype(grad_key.dtype)
-        grad_value[place, :] = total[rows : 2 * rows].astype(grad_value.dtype)
+        grad_key[place, :] = jnp.transpose(total[0:HD]).astype(grad_key.dtype)
+        grad_value[place, :] = jnp.transpose(total[HD : 2 * HD]).astype(grad_value.dtype)
 
 
 def total_grads(far_own, far_1, near_own, near_1):
-    rows = far_own.shape[0] // 2
+    rows = far_own.shape[1]
     shape = jax.ShapeDtypeStruct((2 * rows, HD), jnp.bfloat16)
     return pl.pallas_call(
         functools.partial(total_kernel, rows),
@@ -398,23 +386,23 @@
 
     near_on = [(holder(b), holder(b + 2)) for b in range(1, 2 * count - 2, 2)]
     far_on = [(holder(b), holder(b + 2)) for b in range(0, 2 * count - 2, 2)]
+    near_to_far = [(holder(b), holder(b + 1)) for b in range(1, 2 * count - 2, 2)]
     swap = [(d, d ^ 1) for d in range(count)]
     near_back = [(t, s) for s, t in near_on]
     far_back = [(t, s) for s, t in far_on]
 
     near_kv, far_kv = pack_blocks(key, value)
-    partner_near = move(near_kv, swap)
+    far_1 = move(near_kv, near_to_far)
     far_2 = move(far_kv, far_on)
-    far_1 = move(partner_near, far_on)
     near_1 = move(far_kv, swap)
     prepared = prepare(count, doc_lengths, query, d_out, key, value)
     far_1, prepared = lax.optimization_barrier((far_1, prepared))
     near_2 = move(far_1, swap)
 
-    *far_kept, far_g1, far_g2 = block_scores(0, count, prepared[0:6], far_1, far_2)
+    *far_kept, far_g1, far_g2 = block_scores(0, count, prepared[0:4], far_1, far_2)
     from_far_2 = move(far_g2, far_back)
     relayed = move(far_g1, swap)
-    *near_kept, near_g1, near_g2 = block_scores(1, count, prepared[6:12], near_1, near_2)
+    *near_kept, near_g1, near_g2 = block_scores(1, count, prepared[4:8], near_1, near_2)
     near_sum = (near_g2.astype(jnp.float32) + relayed.astype(jnp.float32)).astype(jnp.bfloat16)
     from_near_2 = move(near_sum, near_back)
     near_g1, from_far_2 = lax.optimization_barrier((near_g1, from_far_2))
@@ -423,7 +411,7 @@
         query,
         from_far_2,
         (prepared[0], far_1, far_2, *far_kept),
-        (prepared[6], near_1, near_2, *near_kept),
+        (prepared[4], near_1, near_2, *near_kept),
     )
     grad_key, grad_value = total_grads(far_own, from_near_1, near_own, from_near_2)
     return (attended, grad_query, grad_key, grad_value)

time: 40.9 us -> 38.2 us (0.934)
  waiting for transfers between devices: 6.06 us -> 1.82 us
  starting transfers between devices: 15.3 us -> 17.5 us
  Pallas kernels: 18.2 us -> 17.5 us
    ppermute x9 -> x8, waiting for transfers between devices: 6.06 us -> 1.82 us  [move(): return lax.ppermute(array, 'ctx', pairs)]
    ppermute x9 -> x8, starting transfers between devices: 15.3 us -> 17.5 us  [move(): return lax.ppermute(array, 'ctx', pairs)]
    pallas_call x2, Pallas kernels: 9.3 us -> 8.48 us  [block_scores(): pl.pallas_call(functools.partial(scores_kernel, rows, heads, count, slot)...]
  transfers between devices with their start and end apart: 9 -> 8, of which waited for: 4 -> 2; matrix products, arithmetic and copies ran while one was open for 0% -> 0% of each run, Pallas kernels for 39% -> 39%
where the time goes in v6:
time: 38.2 us; the launch traced here: 37.7 us
  Pallas kernels  17.5 us (46%)
  starting transfers between devices  17.5 us (46%)
  waiting for transfers between devices  1.82 us (5%)
  between operations  0.76 us (2%)
    ppermute x8, starting transfers between devices, move(): return lax.ppermute(array, 'ctx', pairs)  17.5 us
    pallas_call x2, Pallas kernels, block_scores(): pl.pallas_call(functools.partial(scores_kernel, rows, heads, count, slot)...  8.48 us
    pallas_call x1, Pallas kernels, block_outputs(): pl.pallas_call(functools.partial(outputs_kernel, rows, heads), out_shape=...  4.16 us
    pallas_call x1, Pallas kernels, prepare(): pl.pallas_call(functools.partial(prepare_kernel, rows, heads, doc_lengths...  2.11 us
    pallas_call x1, Pallas kernels, pack_blocks(): pl.pallas_call(functools.partial(pack_kernel, rows), out_shape=(shape, sh...  1.82 us
    ppermute x8, waiting for transfers between devices, move(): return lax.ppermute(array, 'ctx', pairs)  1.82 us
    pallas_call x1, Pallas kernels, total_grads(): pl.pallas_call(functools.partial(total_kernel, rows), out_shape=(shape, s...  0.92 us
  transfers between devices with their start and end apart: 8, of which 2 were waited for; matrix products, arithmetic and copies ran while one was open for 0% of the time, Pallas kernels for 39%

profile of v6, /device:TPU:0, one launch (start us, length us, event | category | flops | bytes accessed | tf_op | source)
XLA Modules:
  0.0 37.7 jit_solution(8496135180553308681)
XLA Ops:
  0.6 1.8 %pack_blocks.1 = (bf16[768,128]{1,0:T(8,128)(2,1)}, bf16[768,128]{1,0:T(8,128)(2,1)}) custom-call(bf16[768,128]{1,0:T(8,128)(2,1)} %refs_3_.1, bf16[768,128]{1,0:T(8,128)(2,1)} %refs_4_.1), custom_call_target="tpu_custom_call" | custom-call | tf_op jit(solution)/shard_map/pack_blocks/pallas_call | solution.py:71
  2.5 0.7 %collective-permute-start = (bf16[768,128]{1,0:T(8,128)(2,1)}, bf16[768,128]{1,0:T(8,128)(2,1)S(1)}, u32[]{:S(2)}, u32[]{:S(2)}) collective-permute-start(bf16[768,128]{1,0:T(8,128)(2,1)} %get-tuple-element.45), channel_id=1, source_target_pairs={{1,2},{3,4},{5,6},{7,8},{9,10},{11,12},{13,14},{15,15},{14,13},{12... | collective-permute-start | bytes 589832 | tf_op jit(solution)/shard_map/ppermute | solution.py:385
  3.1 6.1 %collective-permute-start.3 = (bf16[768,128]{1,0:T(8,128)(2,1)}, bf16[768,128]{1,0:T(8,128)(2,1)S(1)}, u32[]{:S(2)}, u32[]{:S(2)}) collective-permute-start(bf16[768,128]{1,0:T(8,128)(2,1)} %get-tuple-element.58), channel_id=1, source_target_pairs={{0,2},{2,4},{4,6},{6,8},{8,10},{10,12},{12,14},{14,15},{15,13},{13... | collective-permute-start | bytes 589832 | tf_op jit(solution)/shard_map/ppermute | solution.py:385
  9.3 0.1 collective-permute-start.1
  9.4 2.1 %prepare.1 = (bf16[768,128]{1,0:T(8,128)(2,1)S(1)}, bf16[128,1536]{1,0:T(8,128)(2,1)S(1)}, bf16[128,1536]{1,0:T(8,128)(2,1)S(1)}, s32[8,128]{1,0:T(8,128)S(1)}, ...) custom-call(s32[32]{0:T(128)} %refs_0_.1, ...), custom_call_target="tpu_custom_call" | custom-call | bytes 4194304 | tf_op jit(solution)/shard_map/prepare/pallas_call | solution.py:128
  11.5 0.0 collective-permute-done.prev1.refs_1_
  11.5 4.1 %collective-permute-start.2 = (bf16[768,128]{1,0:T(8,128)(2,1)S(1)}, bf16[768,128]{1,0:T(8,128)(2,1)S(1)}, u32[]{:S(2)}, u32[]{:S(2)}) collective-permute-start(bf16[768,128]{1,0:T(8,128)(2,1)S(1)} %collective-permute-done.prev1.refs_1_), channel_id=1, source_target_pairs={{0,1},{1,0},{2,3},{3,2},{4,5},{5,4},{6,7},{7,6},{8,9},{9,8},{10,11... | collective-permute-start | bytes 589832 | tf_op jit(solution)/shard_map/ppermute | solution.py:385
  15.6 1.0 %collective-permute-done.3.prev2.refs_2_ = bf16[768,128]{1,0:T(8,128)(2,1)S(1)} collective-permute-done((bf16[768,128]{1,0:T(8,128)(2,1)}, bf16[768,128]{1,0:T(8,128)(2,1)S(1)}, u32[]{:S(2)}, u32[]{:S(2)}) %collective-permute-start.3) | collective-permute-done | bytes 196640 | tf_op jit(solution)/shard_map/ppermute | solution.py:385
  16.6 4.1 %scores_far.1 = (bf16[2688,512]{1,0:T(8,128)(2,1)S(1)}, bf16[2688,512]{1,0:T(8,128)(2,1)S(1)}, f32[8,512]{1,0:T(8,128)S(1)}, bf16[128,1536]{1,0:T(8,128)(2,1)S(1...) custom-call(bf16[768,128]{1,0:T(8,128)(2,1)S(1)} %get-tuple-element.61.own_kv.refs_0_, ...), custom_call_target="tpu_custom_call" | custom-call | flops 1409286144 | tf_op jit(solution)/shard_map/scores_far/pallas_call | solution.py:263
  20.6 0.1 collective-permute-start.6
  20.7 1.3 %collective-permute-start.4 = (bf16[256,384]{1,0:T(8,128)(2,1)S(1)}, bf16[256,384]{1,0:T(8,128)(2,1)S(1)}, u32[]{:S(2)}, u32[]{:S(2)}) collective-permute-start(bf16[256,384]{1,0:T(8,128)(2,1)S(1)} %get-tuple-element.65), channel_id=1, source_target_pairs={{2,0},{4,2},{6,4},{8,6},{10,8},{12,10},{14,12},{15,14},{13,15},{11... | collective-permute-start | bytes 589832 | tf_op jit(solution)/shard_map/ppermute | solution.py:385
  22.0 0.0 collective-permute-done.1.prev1.refs_9_
  22.0 0.0 collective-permute-done.2.prev2.refs_10_
  22.0 4.4 %scores_near.1 = (bf16[2688,512]{1,0:T(8,128)(2,1)S(1)}, bf16[2688,512]{1,0:T(8,128)(2,1)S(1)}, f32[8,512]{1,0:T(8,128)S(1)}, bf16[128,1536]{1,0:T(8,128)(2,1)S(...) custom-call(bf16[768,128]{1,0:T(8,128)(2,1)S(1)} %get-tuple-element.54.own_kv.refs_8_,, ...), custom_call_target="tpu_custom_call" | custom-call | flops 1409286144 | tf_op jit(solution)/shard_map/scores_near/pallas_call | solution.py:263
  26.5 0.0 collective-permute-done.6
  26.5 0.1 add_convert_fusion
  26.5 5.1 %collective-permute-start.7 = (bf16[256,384]{1,0:T(8,128)(2,1)S(1)}, bf16[256,384]{1,0:T(8,128)(2,1)S(1)}, u32[]{:S(2)}, u32[]{:S(2)}) collective-permute-start(bf16[256,384]{1,0:T(8,128)(2,1)S(1)} %add_convert_fusion), channel_id=1, source_target_pairs={{3,1},{5,3},{7,5},{9,7},{11,9},{13,11},{15,13},{14,15},{12,14},{10... | collective-permute-start | bytes 589832 | tf_op jit(solution)/shard_map/ppermute | solution.py:385
  31.7 0.0 collective-permute-done.4.from_far_2
  31.7 0.1 collective-permute-start.5
  31.7 4.2 %block_outputs.1 = (bf16[768,512]{1,0:T(8,128)(2,1)}, bf16[768,512]{1,0:T(8,128)(2,1)}, f32[256,384]{1,0:T(8,128)S(1)}, f32[256,384]{1,0:T(8,128)S(1)}) custom-call(bf16[256,384]{1,0:T(8,128)(2,1)S(1)} %collective-permute-done.4.from_far_2, bf16[768,128]{1,0:T(8,128)(2,1)S(1)} %get-tuple-element.61.own_kv.refs_0_, ...), custom_call_target="tpu_custom_call" | custom-call | tf_op jit(solution)/shard_map/block_outputs/pallas_call | solution.py:341
  35.9 0.8 %collective-permute-done.7.near_1 = bf16[256,384]{1,0:T(8,128)(2,1)S(1)} collective-permute-done((bf16[256,384]{1,0:T(8,128)(2,1)S(1)}, bf16[256,384]{1,0:T(8,128)(2,1)S(1)}, u32[]{:S(2)}, u32[]{:S(2)}) %collective-permute-start.7) | collective-permute-done | bytes 196640 | tf_op jit(solution)/shard_map/ppermute | solution.py:385
  36.7 0.0 collective-permute-done.5.far_1
  36.7 0.9 %total_grads.1 = (bf16[768,128]{1,0:T(8,128)(2,1)}, bf16[768,128]{1,0:T(8,128)(2,1)}) custom-call(f32[256,384]{1,0:T(8,128)S(1)} %get-tuple-element.79.far_own, bf16[256,384]{1,0:T(8,128)(2,1)S(1)} %collective-permute-done.5.far_1, f32[256,384]{1,0:T(8,128)S(1)} %get-tuple-element.81.near_own, bf16[256,384]{1,0:T(8,128)(2,1)S(1)} %collective-permute-done.7.near_1), custom_call_target="tpu_custom_call" | custom-call | tf_op jit(solution)/shard_map/total_grads/pallas_call | solution.py:368
Async XLA Ops:
  2.5 9.0 %collective-permute-start = (bf16[768,128]{1,0:T(8,128)(2,1)}, bf16[768,128]{1,0:T(8,128)(2,1)S(1)}, u32[]{:S(2)}, u32[]{:S(2)}) collective-permute-start(bf16[768,128]{1,0:T(8,128)(2,1)} %get-tuple-element.45), channel_id=1, source_target_pairs={{1,2},{3,4},{5,6},{7,8},{9,10},{11,12},{13,14},{15,15},{14,13},{12... | collective-permute-start | bytes 589832 | tf_op jit(solution)/shard_map/ppermute | solution.py:385
  3.1 13.4 %collective-permute-start.3 = (bf16[768,128]{1,0:T(8,128)(2,1)}, bf16[768,128]{1,0:T(8,128)(2,1)S(1)}, u32[]{:S(2)}, u32[]{:S(2)}) collective-permute-start(bf16[768,128]{1,0:T(8,128)(2,1)} %get-tuple-element.58), channel_id=1, source_target_pairs={{0,2},{2,4},{4,6},{6,8},{8,10},{10,12},{12,14},{14,15},{15,13},{13... | collective-permute-start | bytes 589832 | tf_op jit(solution)/shard_map/ppermute | solution.py:385
  9.3 12.7 %collective-permute-start.1 = (bf16[768,128]{1,0:T(8,128)(2,1)}, bf16[768,128]{1,0:T(8,128)(2,1)S(1)}, u32[]{:S(2)}, u32[]{:S(2)}) collective-permute-start(bf16[768,128]{1,0:T(8,128)(2,1)} %get-tuple-element.58), channel_id=1, source_target_pairs={{0,1},{1,0},{2,3},{3,2},{4,5},{5,4},{6,7},{7,6},{8,9},{9,8},{10,11... | collective-permute-start | bytes 589832 | tf_op jit(solution)/shard_map/ppermute | solution.py:385
  11.5 10.6 %collective-permute-start.2 = (bf16[768,128]{1,0:T(8,128)(2,1)S(1)}, bf16[768,128]{1,0:T(8,128)(2,1)S(1)}, u32[]{:S(2)}, u32[]{:S(2)}) collective-permute-start(bf16[768,128]{1,0:T(8,128)(2,1)S(1)} %collective-permute-done.prev1.refs_1_), channel_id=1, source_target_pairs={{0,1},{1,0},{2,3},{3,2},{4,5},{5,4},{6,7},{7,6},{8,9},{9,8},{10,11... | collective-permute-start | bytes 589832 | tf_op jit(solution)/shard_map/ppermute | solution.py:385
  20.6 5.8 %collective-permute-start.6 = (bf16[256,384]{1,0:T(8,128)(2,1)S(1)}, bf16[256,384]{1,0:T(8,128)(2,1)S(1)}, u32[]{:S(2)}, u32[]{:S(2)}) collective-permute-start(bf16[256,384]{1,0:T(8,128)(2,1)S(1)} %get-tuple-element.83), channel_id=1, source_target_pairs={{0,1},{1,0},{2,3},{3,2},{4,5},{5,4},{6,7},{7,6},{8,9},{9,8},{10,11... | collective-permute-start | bytes 589832 | tf_op jit(solution)/shard_map/ppermute | solution.py:385
  20.7 10.9 %collective-permute-start.4 = (bf16[256,384]{1,0:T(8,128)(2,1)S(1)}, bf16[256,384]{1,0:T(8,128)(2,1)S(1)}, u32[]{:S(2)}, u32[]{:S(2)}) collective-permute-start(bf16[256,384]{1,0:T(8,128)(2,1)S(1)} %get-tuple-element.65), channel_id=1, source_target_pairs={{2,0},{4,2},{6,4},{8,6},{10,8},{12,10},{14,12},{15,14},{13,15},{11... | collective-permute-start | bytes 589832 | tf_op jit(solution)/shard_map/ppermute | solution.py:385
  26.5 10.2 %collective-permute-start.7 = (bf16[256,384]{1,0:T(8,128)(2,1)S(1)}, bf16[256,384]{1,0:T(8,128)(2,1)S(1)}, u32[]{:S(2)}, u32[]{:S(2)}) collective-permute-start(bf16[256,384]{1,0:T(8,128)(2,1)S(1)} %add_convert_fusion), channel_id=1, source_target_pairs={{3,1},{5,3},{7,5},{9,7},{11,9},{13,11},{15,13},{14,15},{12,14},{10... | collective-permute-start | bytes 589832 | tf_op jit(solution)/shard_map/ppermute | solution.py:385
  31.7 5.1 %collective-permute-start.5 = (bf16[256,384]{1,0:T(8,128)(2,1)S(1)}, bf16[256,384]{1,0:T(8,128)(2,1)S(1)}, u32[]{:S(2)}, u32[]{:S(2)}) collective-permute-start(bf16[256,384]{1,0:T(8,128)(2,1)S(1)} %get-tuple-element.80), channel_id=1, source_target_pairs={{0,1},{1,0},{2,3},{3,2},{4,5},{5,4},{6,7},{7,6},{8,9},{9,8},{10,11... | collective-permute-start | bytes 589832 | tf_op jit(solution)/shard_map/ppermute | solution.py:385

commit v7 on v6

--- a/solution.py
+++ b/solution.py
@@ -142,6 +142,148 @@
     )(*(in_hbm(array) for array in (doc_lengths, query, dout, key, value)))
 
 
+class Window:
+    def __init__(self, rows, slot):
+        self.tiles = rows // TQ
+        self.chunks = 2 * self.tiles + 1
+        self.steps = range(self.tiles)
+        self.late = [(2 - slot) * self.tiles - step for step in self.steps]
+        self.early = [self.chunks - late for late in self.late]
+        self.prev = [2 * self.tiles - step for step in self.steps]
+        self.own = [self.chunks - prev for prev in self.prev]
+
+
+def chunk_rows(counts, step, first=0, count=None):
+    start = sum(counts[:step]) + first
+    count = counts[step] - first if count is None else count
+    return slice(start * CHUNK, (start + count) * CHUNK)
+
+
+def exponentials(jobs, rows, heads, block_pos, scores):
+    back = 2 * rows
+    wide = heads * TQ
+    base2 = SCALE * math.log2(math.e)
+
+    def score(job, index, row_max):
+        step, chunks, (query_t, _, doc_start), _, _ = jobs[job]
+        chunk, keys, row = chunks[index][0:3]
+        low = doc_start[step : step + 1, :] - (block_pos(job) - back + step * TQ)
+        high = lax.broadcasted_iota(jnp.int32, (1, TQ), 1) + back
+        tile = slice(step * wide, (step + 1) * wide)
+        product = dot_nn(keys[row : row + CHUNK, :], query_t[:, tile])
+        for start in range(0, CHUNK, GROUP):
+            place = chunk * CHUNK + start
+            at = lax.broadcasted_iota(jnp.int32, (GROUP, TQ), 0) + place
+            allowed = at >= low
+            if place >= back:
+                allowed = jnp.logical_and(allowed, at <= high)
+            for h in range(heads):
+                lanes = slice(h * TQ, (h + 1) * TQ)
+                part = jnp.where(allowed, product[start : start + GROUP, lanes], masked_score)
+                scores[job % 2, place : place + GROUP, lanes] = part
+                for row8 in range(0, GROUP, 8):
+                    row_max[h] = jnp.maximum(row_max[h], part[row8 : row8 + 8, :])
+
+    def start_max():
+        return [jnp.full((8, TQ), masked_score, jnp.float32)] * heads
+
+    following = start_max()
+    for index in range(len(jobs[0][1])):
+        score(0, index, following)
+    for job, (step, chunks, (_, dout_t, _), first_max, end) in enumerate(jobs):
+        tile = slice(step * wide, (step + 1) * wide)
+        row_max = jnp.concatenate(
+            [jnp.max(part, axis=0, keepdims=True) * base2 for part in following], axis=1
+        )
+        if first_max is not None:
+            row_max = jnp.maximum(row_max, first_max)
+        following = start_max()
+        ahead = len(jobs[job + 1][1]) if job + 1 < len(jobs) else 0
+        done = 0
+        total = jnp.zeros((8, wide), jnp.float32)
+        delta = jnp.zeros((8, wide), jnp.float32)
+        for index, (chunk, keys, row, weights, dprobs, kept) in enumerate(chunks):
+            product = dot_nn(keys[rows + row : rows + row + CHUNK, :], dout_t[:, tile])
+            for start in range(0, CHUNK, GROUP):
+                place = chunk * CHUNK + start
+                there = slice(kept.start + start, kept.start + start + GROUP)
+                dprob = product[start : start + GROUP, :]
+                dprobs[there, :] = dprob.astype(jnp.bfloat16)
+                part = jnp.exp2(scores[job % 2, place : place + GROUP, :] * base2 - row_max)
+                weights[there, :] = part.astype(jnp.bfloat16)
+                term = part * dprob
+                for row8 in range(0, GROUP, 8):
+                    total = total + part[row8 : row8 + 8, :]
+                    delta = delta + term[row8 : row8 + 8, :]
+            while done * len(chunks) < ahead * (index + 1):
+                score(job + 1, done, following)
+                done += 1
+        end(
+            row_max,
+            jnp.sum(total, axis=0, keepdims=True),
+            jnp.sum(delta, axis=0, keepdims=True),
+        )
+
+
+def early_kernel(rows, heads, count, near_1, *refs):
+    inputs, outs, scores = (refs[0:4], refs[4:8]), (refs[8:11], refs[11:14]), refs[14]
+    jobs = []
+    for slot in (0, 1):
+        window = Window(rows, slot)
+        own_kv, query_t, dout_t, doc_start = inputs[slot]
+        weights, dprobs, stats = outs[slot]
+        for step in window.steps:
+            chunks = []
+            for index in range(window.early[step]):
+                chunk = window.late[step] + index
+                row = step * TQ + chunk * CHUNK
+                keys = own_kv if row >= 2 * rows else near_1
+                kept = chunk_rows(window.early, step, index, 1)
+                chunks.append((chunk, keys, row % rows, weights, dprobs, kept))
+
+            def end(*found, stats=stats, step=step):
+                for kind, value in enumerate(found):
+                    stats[8 * kind + step : 8 * kind + step + 1, :] = value
+
+            jobs.append((step, chunks, (query_t, dout_t, doc_start), None, end))
+    tiles = rows // TQ
+    positions = [block_number(count, slot) * rows for slot in (0, 1)]
+    exponentials(jobs, rows, heads, lambda job: positions[job // tiles], scores)
+
+
+def early_scores(count, prepared, near_1):
+    rows = near_1.shape[0] // 2
+    heads = prepared[1].shape[1] // rows
+    wide = heads * TQ
+    out_shape = []
+    for slot in (0, 1):
+        kept = (sum(Window(rows, slot).early) * CHUNK, wide)
+        out_shape += [jax.ShapeDtypeStruct(kept, jnp.bfloat16)] * 2
+        out_shape.append(jax.ShapeDtypeStruct((24, wide), jnp.float32))
+    return pl.pallas_call(
+        functools.partial(early_kernel, rows, heads, count),
+        out_shape=out_shape,
+        in_specs=[VMEM] * 9,
+        out_specs=[VMEM] * 6,
+        scratch_shapes=[pltpu.VMEM((2, 2 * rows + TQ, wide), jnp.float32)],
+        compiler_params=pltpu.CompilerParams(vmem_limit_bytes=VMEM_LIMIT),
+        cost_estimate=pl.CostEstimate(flops=2**31, bytes_accessed=0, transcendentals=0),
+        name="early_scores",
+    )(near_1, *prepared)
+
+
+def scaled_by(array, tile, factor):
+    return (array[:, tile].astype(jnp.float32) * factor).astype(jnp.bfloat16)
+
+
+def dscore_rows(dscores, there, weights, dprobs, kept, delta):
+    delta = jnp.broadcast_to(delta, (16, delta.shape[1]))
+    for start in range(0, there.stop - there.start, 16):
+        out = slice(there.start + start, there.start + start + 16)
+        place = slice(kept.start + start, kept.start + start + 16)
+        dscores[out, :] = weights[place, :] * (dprobs[place, :] - delta)
+
+
 def scores_kernel(
     rows,
     heads,
@@ -151,142 +293,111 @@
     query_t,
     dout_t,
     doc_start,
+    early_w,
+    early_dprobs,
+    early_stats,
     prev1,
     prev2,
-    weights,
+    late_w,
     dscores,
-    inverses,
-    query_scaled,
-    dout_scaled,
+    stats,
     prev1_out,
     prev2_out,
     scores,
-    dprobs,
+    late_dprobs,
     dk,
     dv,
 ):
     back = 2 * rows
-    width = back + TQ
     wide = heads * TQ
-    steps = rows // TQ
-    base2 = SCALE * math.log2(math.e)
-    block_pos = block_number(count, slot) * rows
-    chunks = width // CHUNK
-
-    def source(step, chunk):
-        row = step * TQ + chunk * CHUNK
-        return (prev2, prev1, own_kv)[row // rows], row % rows
-
-    def score_chunk(step, chunk, row_max):
-        low = doc_start[step : step + 1, :] - (block_pos - back + step * TQ)
-        high = lax.broadcasted_iota(jnp.int32, (1, TQ), 1) + back
-        array, row = source(step, chunk)
-        tile = slice(step * wide, (step + 1) * wide)
-        product = dot_nn(array[row : row + CHUNK, :], query_t[:, tile])
-        for start in range(0, CHUNK, GROUP):
-            place = chunk * CHUNK + start
-            at = lax.broadcasted_iota(jnp.int32, (GROUP, TQ), 0) + place
-            allowed = at >= low
-            if place >= back:
-                allowed = jnp.logical_and(allowed, at <= high)
-            for h in range(heads):
-                lanes = slice(h * TQ, (h + 1) * TQ)
-                part = jnp.where(allowed, product[start : start + GROUP, lanes], masked_score)
-                scores[step, place : place + GROUP, lanes] = part
-                for row8 in range(0, GROUP, 8):
-                    row_max[h] = jnp.maximum(row_max[h], part[row8 : row8 + 8, :])
-
-    def start_max():
-        return [jnp.full((8, TQ), masked_score, jnp.float32)] * heads
-
-    following = start_max()
-    for chunk in range(chunks):
-        score_chunk(0, chunk, following)
-    for step in range(steps):
-        tile = slice(step * wide, (step + 1) * wide)
-        out = step * width
-        row_max = jnp.concatenate(
-            [jnp.max(part, axis=0, keepdims=True) * base2 for part in following], axis=1
-        )
-        following = start_max()
-        total = jnp.zeros((8, wide), jnp.float32)
-        delta = jnp.zeros((8, wide), jnp.float32)
-        for chunk in range(chunks):
-            array, row = source(step, chunk)
-            product = dot_nn(array[rows + row : rows + row + CHUNK, :], dout_t[:, tile])
-            for start in range(0, CHUNK, GROUP):
-                place = chunk * CHUNK + start
-                there = slice(out + place, out + place + GROUP)
-                dprob = product[start : start + GROUP, :]
-                dprobs[step, place : place + GROUP, :] = dprob.astype(jnp.bfloat16)
-                part = jnp.exp2(scores[step, place : place + GROUP, :] * base2 - row_max)
-                weights[there, :] = part.astype(jnp.bfloat16)
-                term = part * dprob
-                for row8 in range(0, GROUP, 8):
-                    total = total + part[row8 : row8 + 8, :]
-                    delta = delta + term[row8 : row8 + 8, :]
-            if step + 1 < steps:
-                score_chunk(step + 1, chunk, following)
-        inverse = 1.0 / jnp.sum(total, axis=0, keepdims=True)
-        delta = (jnp.sum(delta, axis=0, keepdims=True) * inverse).astype(jnp.bfloat16)
-        inverses[step : step + 1, :] = inverse
-        for array, scaled in ((query_t, query_scaled), (dout_t, dout_scaled)):
-            scaled[:, tile] = (array[:, tile].astype(jnp.float32) * inverse).astype(jnp.bfloat16)
-        delta = jnp.broadcast_to(delta, (16, wide))
-        for start in range(0, width, 16):
-            there = slice(out + start, out + start + 16)
-            dscores[there, :] = weights[there, :] * (dprobs[step, start : start + 16, :] - delta)
-        first = step * TQ
-        there = slice(out, out + back - first)
-        for total_ref, terms, side in ((dv, weights, dout_scaled), (dk, dscores, query_scaled)):
-            term = dot_nt(side[:, tile], terms[there, :])
-            if step == 0:
-                total_ref[...] = term
-            else:
-                total_ref[:, first:back] += term
-
+    window = Window(rows, slot)
+    position = block_number(count, slot) * rows
+    jobs = []
+    for step in window.steps:
+        chunks = []
+        for chunk in range(window.late[step]):
+            row = step * TQ + chunk * CHUNK
+            keys = (prev2, prev1)[row // rows]
+            kept = chunk_rows(window.late, step, chunk, 1)
+            chunks.append((chunk, keys, row % rows, late_w, late_dprobs, kept))
+
+        def end(row_max, total, delta, step=step):
+            tile = slice(step * wide, (step + 1) * wide)
+            early = [early_stats[8 * kind + step : 8 * kind + step + 1, :] for kind in range(3)]
+            shrink = jnp.exp2(early[0] - row_max)
+            late_factor = 1.0 / (total + early[1] * shrink)
+            early_factor = late_factor * shrink
+            delta = delta * late_factor + early[2] * early_factor
+            for kind, value in enumerate((late_factor, early_factor, delta)):
+                stats[8 * kind + step : 8 * kind + step + 1, :] = value
+            delta = delta.astype(jnp.bfloat16)
+            first = step * TQ
+            late = window.late[step]
+            parts = [(0, late, late_w, late_dprobs, chunk_rows(window.late, step), late_factor)]
+            if window.prev[step] > late:
+                beyond = window.prev[step] - late
+                kept = chunk_rows(window.early, step, 0, beyond)
+                parts.append((late, beyond, early_w, early_dprobs, kept, early_factor))
+            for start, length, weights, dprobs, kept, factor in parts:
+                there = chunk_rows(window.prev, step, start, length)
+                dscore_rows(dscores, there, weights, dprobs, kept, delta)
+                columns = slice(first + start * CHUNK, first + (start + length) * CHUNK)
+                for total_ref, terms, at, side in (
+                    (dv, weights, kept, dout_t),
+                    (dk, dscores, there, query_t),
+                ):
+                    term = dot_nt(scaled_by(side, tile, factor), terms[at, :])
+                    if step == 0:
+                        total_ref[:, columns] = term
+                    else:
+                        total_ref[:, columns] += term
+
+        first_max = early_stats[step : step + 1, :]
+        jobs.append((step, chunks, (query_t, dout_t, doc_start), first_max, end))
+    exponentials(jobs, rows, heads, lambda job: position, scores)
     for out, place in ((prev2_out, slice(0, rows)), (prev1_out, slice(rows, back))):
         out[0:HD] = (dk[:, place] * SCALE).astype(out.dtype)
         out[HD : 2 * HD] = dv[:, place].astype(out.dtype)
 
 
-def block_scores(slot, count, prepared, prev1, prev2):
+def block_scores(slot, count, prepared, early, prev1, prev2):
     rows = prev1.shape[0] // 2
     heads = prepared[1].shape[1] // rows
-    steps = rows // TQ
-    width = 2 * rows + TQ
     wide = heads * TQ
+    window = Window(rows, slot)
+    late = (sum(window.late) * CHUNK, wide)
     pair = jax.ShapeDtypeStruct((2 * HD, rows), jnp.bfloat16)
-    kept = jax.ShapeDtypeStruct((steps * width, wide), jnp.bfloat16)
-    inverses = jax.ShapeDtypeStruct((8, wide), jnp.float32)
-    stacked = jax.ShapeDtypeStruct((HD, rows * heads), jnp.bfloat16)
     return pl.pallas_call(
         functools.partial(scores_kernel, rows, heads, count, slot),
-        out_shape=(kept, kept, inverses, stacked, stacked, pair, pair),
-        in_specs=[VMEM] * 6,
-        out_specs=[VMEM] * 7,
+        out_shape=(
+            jax.ShapeDtypeStruct(late, jnp.bfloat16),
+            jax.ShapeDtypeStruct((sum(window.prev) * CHUNK, wide), jnp.bfloat16),
+            jax.ShapeDtypeStruct((24, wide), jnp.float32),
+            pair,
+            pair,
+        ),
+        in_specs=[VMEM] * 9,
+        out_specs=[VMEM] * 5,
         scratch_shapes=[
-            pltpu.VMEM((steps, width, wide), jnp.float32),
-            pltpu.VMEM((steps, width, wide), jnp.bfloat16),
+            pltpu.VMEM((2, 2 * rows + TQ, wide), jnp.float32),
+            pltpu.VMEM(late, jnp.bfloat16),
             pltpu.VMEM((HD, 2 * rows), jnp.float32),
             pltpu.VMEM((HD, 2 * rows), jnp.float32),
         ],
         compiler_params=pltpu.CompilerParams(vmem_limit_bytes=VMEM_LIMIT),
-        cost_estimate=pl.CostEstimate(
-            flops=4 * 2 * steps * width * heads * TQ * HD, bytes_accessed=0, transcendentals=0
-        ),
+        cost_estimate=pl.CostEstimate(flops=2**32, bytes_accessed=0, transcendentals=0),
         name="scores_far" if slot == 0 else "scores_near",
-    )(*prepared, prev1, prev2)
+    )(*prepared, *early, prev1, prev2)
 
 
 def outputs_kernel(rows, heads, from_far_2, *refs):
-    blocks = (refs[0:8], refs[8:16])
-    (attended, grad_query, far_own, near_own, keys_t, values_t) = refs[16:]
-    back = 2 * rows
-    width = back + TQ
+    blocks = (refs[0:10], refs[10:20])
+    (attended, grad_query, far_own, near_own, keys_t, values_t, own_dscores) = refs[20:]
     wide = heads * TQ
     for slot, block in enumerate(blocks):
-        (own_kv, prev1, prev2, weights, dscores, inverses, query_scaled, dout_scaled) = block
+        (own_kv, query_t, dout_t, early_w, early_dprobs, prev1, prev2) = block[0:7]
+        (late_w, dscores, stats) = block[7:10]
+        window = Window(rows, slot)
         own_out = (far_own, near_own)[slot]
         own_rows = half_start(rows, slot)
         for place, source in enumerate((prev2, prev1, own_kv)):
@@ -295,16 +406,23 @@
                 row = tile * TQ
                 keys_t[:, part] = jnp.transpose(source[row : row + TQ, :])
                 values_t[:, part] = jnp.transpose(source[rows + row : rows + row + TQ, :])
-        for step in reversed(range(rows // TQ)):
+        for step in reversed(window.steps):
             first = step * TQ
-            out = step * width
             tile = slice(step * wide, (step + 1) * wide)
-            tail = slice(out + back - first, out + width)
-            for offset, terms, side, factor in (
-                (0, dscores, query_scaled, SCALE),
-                (HD, weights, dout_scaled, 1.0),
+            late_factor, early_factor, delta = (
+                stats[8 * kind + step : 8 * kind + step + 1, :] for kind in range(3)
+            )
+            late, prev, own = window.late[step], window.prev[step], window.own[step]
+            own_w = chunk_rows(window.early, step, prev - late, own)
+            own_d = chunk_rows(window.own, step)
+            dscore_rows(
+                own_dscores, own_d, early_w, early_dprobs, own_w, delta.astype(jnp.bfloat16)
+            )
+            for offset, terms, at, side, factor in (
+                (0, own_dscores, own_d, query_t, SCALE),
+                (HD, early_w, own_w, dout_t, 1.0),
             ):
-                term = dot_nt(side[:, tile], terms[tail, :]) * factor
+                term = dot_nt(scaled_by(side, tile, early_factor), terms[at, :]) * factor
                 side_rows = slice(offset, offset + HD)
                 place = slice(0, first + TQ)
                 if step < rows // TQ - 1:
@@ -315,20 +433,35 @@
                     )
                 else:
                     own_out[side_rows, place] = term
-            window = slice(first, first + width)
-            inverse = inverses[step : step + 1, :]
-            attended_t = dot_nn(values_t[:, window], weights[out : out + width, :]) * inverse
-            grad_query_t = dot_nn(keys_t[:, window], dscores[out : out + width, :]) * (
-                inverse * SCALE
+
+            def columns(start, length):
+                return slice(first + start * CHUNK, first + (start + length) * CHUNK)
+
+            attended_t = (
+                dot_nn(values_t[:, columns(0, late)], late_w[chunk_rows(window.late, step), :])
+                * late_factor
+                + dot_nn(
+                    values_t[:, columns(late, window.early[step])],
+                    early_w[chunk_rows(window.early, step), :],
+                )
+                * early_factor
             )
+            late_rows = chunk_rows(window.prev, step, 0, late)
+            early_t = dot_nn(keys_t[:, columns(prev, own)], own_dscores[own_d, :])
+            if prev > late:
+                early_t += dot_nn(
+                    keys_t[:, columns(late, prev - late)],
+                    dscores[chunk_rows(window.prev, step, late, prev - late), :],
+                )
+            grad_query_t = dot_nn(keys_t[:, columns(0, late)], dscores[late_rows, :]) * (
+                late_factor * SCALE
+            ) + early_t * (early_factor * SCALE)
             place = pl.ds(own_rows + first, TQ)
             for h in range(heads):
                 part = slice(h * TQ, (h + 1) * TQ)
-                columns = slice(h * HD, (h + 1) * HD)
-                attended[place, columns] = jnp.transpose(attended_t[:, part]).astype(
-                    attended.dtype
-                )
-                grad_query[place, columns] = jnp.transpose(grad_query_t[:, part]).astype(
+                head = slice(h * HD, (h + 1) * HD)
+                attended[place, head] = jnp.transpose(attended_t[:, part]).astype(attended.dtype)
+                grad_query[place, head] = jnp.transpose(grad_query_t[:, part]).astype(
                     grad_query.dtype
                 )
 
@@ -336,16 +469,17 @@
 def block_outputs(query, from_far_2, far, near):
     rows = query.shape[0] // 2
     heads = query.shape[1] // HD
-    wide = jax.ShapeDtypeStruct(query.shape, query.dtype)
+    shape = jax.ShapeDtypeStruct(query.shape, query.dtype)
     own = jax.ShapeDtypeStruct((2 * HD, rows), jnp.float32)
     return pl.pallas_call(
         functools.partial(outputs_kernel, rows, heads),
-        out_shape=(wide, wide, own, own),
-        in_specs=[VMEM] * 17,
+        out_shape=(shape, shape, own, own),
+        in_specs=[VMEM] * 21,
         out_specs=[VMEM] * 4,
         scratch_shapes=[
             pltpu.VMEM((HD, 3 * rows), jnp.bfloat16),
             pltpu.VMEM((HD, 3 * rows), jnp.bfloat16),
+            pltpu.VMEM((sum(Window(rows, 0).own) * CHUNK, heads * TQ), jnp.bfloat16),
         ],
         compiler_params=pltpu.CompilerParams(vmem_limit_bytes=VMEM_LIMIT),
         cost_estimate=pl.CostEstimate(flops=0, bytes_accessed=0, transcendentals=0),
@@ -396,13 +530,20 @@
     far_2 = move(far_kv, far_on)
     near_1 = move(far_kv, swap)
     prepared = prepare(count, doc_lengths, query, d_out, key, value)
-    far_1, prepared = lax.optimization_barrier((far_1, prepared))
+    far_ready, near_ready = prepared[0:4], prepared[4:8]
+    early = early_scores(count, prepared, near_1)
+    far_early, near_early = early[0:3], early[3:6]
+    far_1, far_early, near_early = lax.optimization_barrier((far_1, far_early, near_early))
     near_2 = move(far_1, swap)
 
-    *far_kept, far_g1, far_g2 = block_scores(0, count, prepared[0:4], far_1, far_2)
+    far_w, far_d, far_stats, far_g1, far_g2 = block_scores(
+        0, count, far_ready, far_early, far_1, far_2
+    )
     from_far_2 = move(far_g2, far_back)
     relayed = move(far_g1, swap)
-    *near_kept, near_g1, near_g2 = block_scores(1, count, prepared[4:8], near_1, near_2)
+    near_w, near_d, near_stats, near_g1, near_g2 = block_scores(
+        1, count, near_ready, near_early, near_1, near_2
+    )
     near_sum = (near_g2.astype(jnp.float32) + relayed.astype(jnp.float32)).astype(jnp.bfloat16)
     from_near_2 = move(near_sum, near_back)
     near_g1, from_far_2 = lax.optimization_barrier((near_g1, from_far_2))
@@ -410,8 +551,8 @@
     attended, grad_query, far_own, near_own = block_outputs(
         query,
         from_far_2,
-        (prepared[0], far_1, far_2, *far_kept),
-        (prepared[4], near_1, near_2, *near_kept),
+        (*far_ready[0:3], *far_early[0:2], far_1, far_2, far_w, far_d, far_stats),
+        (*near_ready[0:3], *near_early[0:2], near_1, near_2, near_w, near_d, near_stats),
     )
     grad_key, grad_value = total_grads(far_own, from_near_1, near_own, from_near_2)
     return (attended, grad_query, grad_key, grad_value)

time: 38.2 us -> 36.5 us (0.955)
  waiting for transfers between devices: 1.82 us -> 0.61 us
  starting transfers between devices: 17.5 us -> 17.1 us
    pallas_call x2, Pallas kernels: 8.48 us -> 5.93 us  [block_scores(): pl.pallas_call(functools.partial(scores_kernel, rows, heads, count, slot)...]
    pallas_call x0 -> x1, Pallas kernels: none -> 2.48 us  [early_scores(): pl.pallas_call(functools.partial(early_kernel, rows, heads, count), out_s...]
    ppermute x8, waiting for transfers between devices: 1.82 us -> 0.61 us  [move(): return lax.ppermute(array, 'ctx', pairs)]
    ppermute x8, starting transfers between devices: 17.5 us -> 17.1 us  [move(): return lax.ppermute(array, 'ctx', pairs)]
  transfers between devices with their start and end apart: 8 -> 8, of which waited for: 2 -> 1; matrix products, arithmetic and copies ran while one was open for 0% -> 0% of each run, Pallas kernels for 39% -> 41%
where the time goes in v7:
time: 36.5 us; the launch traced here: 36.2 us
  Pallas kernels  17.7 us (48%)
  starting transfers between devices  17.1 us (47%)
  between operations  0.76 us (2%)
  waiting for transfers between devices  0.61 us (2%)
    ppermute x8, starting transfers between devices, move(): return lax.ppermute(array, 'ctx', pairs)  17.1 us
    pallas_call x2, Pallas kernels, block_scores(): pl.pallas_call(functools.partial(scores_kernel, rows, heads, count, slot)...  5.93 us
    pallas_call x1, Pallas kernels, block_outputs(): pl.pallas_call(functools.partial(outputs_kernel, rows, heads), out_shape=...  4.41 us
    pallas_call x1, Pallas kernels, early_scores(): pl.pallas_call(functools.partial(early_kernel, rows, heads, count), out_s...  2.48 us
    pallas_call x1, Pallas kernels, prepare(): pl.pallas_call(functools.partial(prepare_kernel, rows, heads, doc_lengths...  2.11 us
    pallas_call x1, Pallas kernels, pack_blocks(): pl.pallas_call(functools.partial(pack_kernel, rows), out_shape=(shape, sh...  1.82 us
    pallas_call x1, Pallas kernels, total_grads(): pl.pallas_call(functools.partial(total_kernel, rows), out_shape=(shape, s...  0.93 us
  transfers between devices with their start and end apart: 8, of which 1 were waited for; matrix products, arithmetic and copies ran while one was open for 0% of the time, Pallas kernels for 41%

profile of v7, /device:TPU:0, one launch (start us, length us, event | category | flops | bytes accessed | tf_op | source)
XLA Modules:
  0.0 36.2 jit_solution(11589813567982141557)
XLA Ops:
  0.6 1.8 %pack_blocks.1 = (bf16[768,128]{1,0:T(8,128)(2,1)}, bf16[768,128]{1,0:T(8,128)(2,1)}) custom-call(bf16[768,128]{1,0:T(8,128)(2,1)} %key.1, bf16[768,128]{1,0:T(8,128)(2,1)} %value.1), custom_call_target="tpu_custom_call" | custom-call | tf_op jit(solution)/shard_map/pack_blocks/pallas_call | solution.py:71
  2.5 0.5 %collective-permute-start.1 = (bf16[768,128]{1,0:T(8,128)(2,1)}, bf16[768,128]{1,0:T(8,128)(2,1)S(1)}, u32[]{:S(2)}, u32[]{:S(2)}) collective-permute-start(bf16[768,128]{1,0:T(8,128)(2,1)} %get-tuple-element.50), channel_id=1, source_target_pairs={{0,1},{1,0},{2,3},{3,2},{4,5},{5,4},{6,7},{7,6},{8,9},{9,8},{10,11... | collective-permute-start | bytes 589832 | tf_op jit(solution)/shard_map/ppermute | solution.py:519
  3.0 4.4 %collective-permute-start.3 = (bf16[768,128]{1,0:T(8,128)(2,1)}, bf16[768,128]{1,0:T(8,128)(2,1)S(1)}, u32[]{:S(2)}, u32[]{:S(2)}) collective-permute-start(bf16[768,128]{1,0:T(8,128)(2,1)} %get-tuple-element.50), channel_id=1, source_target_pairs={{0,2},{2,4},{4,6},{6,8},{8,10},{10,12},{12,14},{14,15},{15,13},{13... | collective-permute-start | bytes 589832 | tf_op jit(solution)/shard_map/ppermute | solution.py:519
  7.4 0.7 %collective-permute-start = (bf16[768,128]{1,0:T(8,128)(2,1)}, bf16[768,128]{1,0:T(8,128)(2,1)S(1)}, u32[]{:S(2)}, u32[]{:S(2)}) collective-permute-start(bf16[768,128]{1,0:T(8,128)(2,1)} %get-tuple-element.49), channel_id=1, source_target_pairs={{1,2},{3,4},{5,6},{7,8},{9,10},{11,12},{13,14},{15,15},{14,13},{12... | collective-permute-start | bytes 589832 | tf_op jit(solution)/shard_map/ppermute | solution.py:519
  8.1 2.1 %prepare.1 = (bf16[768,128]{1,0:T(8,128)(2,1)S(1)}, bf16[128,1536]{1,0:T(8,128)(2,1)S(1)}, bf16[128,1536]{1,0:T(8,128)(2,1)S(1)}, s32[8,128]{1,0:T(8,128)S(1)}, ...) custom-call(s32[32]{0:T(128)} %refs_0_.1, ...), custom_call_target="tpu_custom_call" | custom-call | bytes 4194304 | tf_op jit(solution)/shard_map/prepare/pallas_call | solution.py:128
  10.2 0.0 collective-permute-done.1.near_1.prev1.refs_15_
  10.2 2.5 %early_scores.1 = (bf16[768,512]{1,0:T(8,128)(2,1)S(1)}, bf16[768,512]{1,0:T(8,128)(2,1)S(1)}, f32[24,512]{1,0:T(8,128)S(1)}, bf16[1920,512]{1,0:T(8,128)(2,1)S(...) custom-call(bf16[768,128]{1,0:T(8,128)(2,1)S(1)} %collective-permute-done.1.near_1.prev1.refs_15_, ...), custom_call_target="tpu_custom_call" | custom-call | flops 2147483648 | tf_op jit(solution)/shard_map/early_scores/pallas_call | solution.py:263
  12.7 0.0 collective-permute-done.prev1.refs_5_
  12.7 4.6 %collective-permute-start.2 = (bf16[768,128]{1,0:T(8,128)(2,1)S(1)}, bf16[768,128]{1,0:T(8,128)(2,1)S(1)}, u32[]{:S(2)}, u32[]{:S(2)}) collective-permute-start(bf16[768,128]{1,0:T(8,128)(2,1)S(1)} %collective-permute-done.prev1.refs_5_), channel_id=1, source_target_pairs={{0,1},{1,0},{2,3},{3,2},{4,5},{5,4},{6,7},{7,6},{8,9},{9,8},{10,11... | collective-permute-start | bytes 589832 | tf_op jit(solution)/shard_map/ppermute | solution.py:519
  17.3 0.0 collective-permute-done.3.prev2.refs_6_
  17.3 3.5 %scores_far.1 = (bf16[1920,512]{1,0:T(8,128)(2,1)S(1)}, bf16[1920,512]{1,0:T(8,128)(2,1)S(1)}, f32[24,512]{1,0:T(8,128)S(1)}, bf16[256,384]{1,0:T(8,128)(2,1)S(1)}, bf16[256,384]{1,0:T(8,128)(2,1)S(1)}) custom-call(bf16[768,128]{1,0:T(8,128)(2,1)S(1)} %get-tuple-element.51.refs_0_.own_kv, bf16[128,1536]{1,0:T(8,128)(2,1)S(1)} %get-tuple-element.52.refs_1_.query_t, ...), custom_call_target="tpu_custom_call" | custom-call | flops 4294967296 | tf_op jit(solution)/shard_map/scores_far/pallas_call | solution.py:370
  20.8 0.1 collective-permute-start.6
  20.9 1.3 %collective-permute-start.4 = (bf16[256,384]{1,0:T(8,128)(2,1)S(1)}, bf16[256,384]{1,0:T(8,128)(2,1)S(1)}, u32[]{:S(2)}, u32[]{:S(2)}) collective-permute-start(bf16[256,384]{1,0:T(8,128)(2,1)S(1)} %get-tuple-element.69), channel_id=1, source_target_pairs={{2,0},{4,2},{6,4},{8,6},{10,8},{12,10},{14,12},{15,14},{13,15},{11... | collective-permute-start | bytes 589832 | tf_op jit(solution)/shard_map/ppermute | solution.py:519
  22.2 0.0 collective-permute-done.2.prev2.refs_16_
  22.2 2.4 %scores_near.1 = (bf16[768,512]{1,0:T(8,128)(2,1)S(1)}, bf16[1920,512]{1,0:T(8,128)(2,1)S(1)}, f32[24,512]{1,0:T(8,128)S(1)}, bf16[256,384]{1,0:T(8,128)(2,1)S(1)}, bf16[256,384]{1,0:T(8,128)(2,1)S(1)}) custom-call(bf16[768,128]{1,0:T(8,128)(2,1)S(1)} %get-tuple-element.45.refs_4_.own_kv.refs_10_, ...), custom_call_target="tpu_custom_call" | custom-call | flops 4294967296 | tf_op jit(solution)/shard_map/scores_near/pallas_call | solution.py:370
  24.7 0.0 collective-permute-done.6
  24.7 0.1 add_convert_fusion
  24.7 5.5 %collective-permute-start.7 = (bf16[256,384]{1,0:T(8,128)(2,1)S(1)}, bf16[256,384]{1,0:T(8,128)(2,1)S(1)}, u32[]{:S(2)}, u32[]{:S(2)}) collective-permute-start(bf16[256,384]{1,0:T(8,128)(2,1)S(1)} %add_convert_fusion), channel_id=1, source_target_pairs={{3,1},{5,3},{7,5},{9,7},{11,9},{13,11},{15,13},{14,15},{12,14},{10... | collective-permute-start | bytes 589832 | tf_op jit(solution)/shard_map/ppermute | solution.py:519
  30.2 0.0 collective-permute-done.4.from_far_2
  30.2 0.1 collective-permute-start.5
  30.3 4.4 %block_outputs.1 = (bf16[768,512]{1,0:T(8,128)(2,1)}, bf16[768,512]{1,0:T(8,128)(2,1)}, f32[256,384]{1,0:T(8,128)S(1)}, f32[256,384]{1,0:T(8,128)S(1)}) custom-call(bf16[256,384]{1,0:T(8,128)(2,1)S(1)} %collective-permute-done.4.from_far_2, bf16[768,128]{1,0:T(8,128)(2,1)S(1)} %get-tuple-element.51.refs_0_.own_kv, ...), custom_call_target="tpu_custom_call" | custom-call | tf_op jit(solution)/shard_map/block_outputs/pallas_call | solution.py:474
  34.7 0.6 %collective-permute-done.7.near_1 = bf16[256,384]{1,0:T(8,128)(2,1)S(1)} collective-permute-done((bf16[256,384]{1,0:T(8,128)(2,1)S(1)}, bf16[256,384]{1,0:T(8,128)(2,1)S(1)}, u32[]{:S(2)}, u32[]{:S(2)}) %collective-permute-start.7) | collective-permute-done | bytes 196640 | tf_op jit(solution)/shard_map/ppermute | solution.py:519
  35.3 0.0 collective-permute-done.5.far_1
  35.3 0.9 %total_grads.1 = (bf16[768,128]{1,0:T(8,128)(2,1)}, bf16[768,128]{1,0:T(8,128)(2,1)}) custom-call(f32[256,384]{1,0:T(8,128)S(1)} %get-tuple-element.79.far_own, bf16[256,384]{1,0:T(8,128)(2,1)S(1)} %collective-permute-done.5.far_1, f32[256,384]{1,0:T(8,128)S(1)} %get-tuple-element.81.near_own, bf16[256,384]{1,0:T(8,128)(2,1)S(1)} %collective-permute-done.7.near_1), custom_call_target="tpu_custom_call" | custom-call | tf_op jit(solution)/shard_map/total_grads/pallas_call | solution.py:502
Async XLA Ops:
  2.5 7.8 %collective-permute-start.1 = (bf16[768,128]{1,0:T(8,128)(2,1)}, bf16[768,128]{1,0:T(8,128)(2,1)S(1)}, u32[]{:S(2)}, u32[]{:S(2)}) collective-permute-start(bf16[768,128]{1,0:T(8,128)(2,1)} %get-tuple-element.50), channel_id=1, source_target_pairs={{0,1},{1,0},{2,3},{3,2},{4,5},{5,4},{6,7},{7,6},{8,9},{9,8},{10,11... | collective-permute-start | bytes 589832 | tf_op jit(solution)/shard_map/ppermute | solution.py:519
  3.0 14.4 %collective-permute-start.3 = (bf16[768,128]{1,0:T(8,128)(2,1)}, bf16[768,128]{1,0:T(8,128)(2,1)S(1)}, u32[]{:S(2)}, u32[]{:S(2)}) collective-permute-start(bf16[768,128]{1,0:T(8,128)(2,1)} %get-tuple-element.50), channel_id=1, source_target_pairs={{0,2},{2,4},{4,6},{6,8},{8,10},{10,12},{12,14},{14,15},{15,13},{13... | collective-permute-start | bytes 589832 | tf_op jit(solution)/shard_map/ppermute | solution.py:519
  7.4 5.3 %collective-permute-start = (bf16[768,128]{1,0:T(8,128)(2,1)}, bf16[768,128]{1,0:T(8,128)(2,1)S(1)}, u32[]{:S(2)}, u32[]{:S(2)}) collective-permute-start(bf16[768,128]{1,0:T(8,128)(2,1)} %get-tuple-element.49), channel_id=1, source_target_pairs={{1,2},{3,4},{5,6},{7,8},{9,10},{11,12},{13,14},{15,15},{14,13},{12... | collective-permute-start | bytes 589832 | tf_op jit(solution)/shard_map/ppermute | solution.py:519
  12.7 9.5 %collective-permute-start.2 = (bf16[768,128]{1,0:T(8,128)(2,1)S(1)}, bf16[768,128]{1,0:T(8,128)(2,1)S(1)}, u32[]{:S(2)}, u32[]{:S(2)}) collective-permute-start(bf16[768,128]{1,0:T(8,128)(2,1)S(1)} %collective-permute-done.prev1.refs_5_), channel_id=1, source_target_pairs={{0,1},{1,0},{2,3},{3,2},{4,5},{5,4},{6,7},{7,6},{8,9},{9,8},{10,11... | collective-permute-start | bytes 589832 | tf_op jit(solution)/shard_map/ppermute | solution.py:519
  20.8 3.8 %collective-permute-start.6 = (bf16[256,384]{1,0:T(8,128)(2,1)S(1)}, bf16[256,384]{1,0:T(8,128)(2,1)S(1)}, u32[]{:S(2)}, u32[]{:S(2)}) collective-permute-start(bf16[256,384]{1,0:T(8,128)(2,1)S(1)} %get-tuple-element.83), channel_id=1, source_target_pairs={{0,1},{1,0},{2,3},{3,2},{4,5},{5,4},{6,7},{7,6},{8,9},{9,8},{10,11... | collective-permute-start | bytes 589832 | tf_op jit(solution)/shard_map/ppermute | solution.py:519
  20.9 9.3 %collective-permute-start.4 = (bf16[256,384]{1,0:T(8,128)(2,1)S(1)}, bf16[256,384]{1,0:T(8,128)(2,1)S(1)}, u32[]{:S(2)}, u32[]{:S(2)}) collective-permute-start(bf16[256,384]{1,0:T(8,128)(2,1)S(1)} %get-tuple-element.69), channel_id=1, source_target_pairs={{2,0},{4,2},{6,4},{8,6},{10,8},{12,10},{14,12},{15,14},{13,15},{11... | collective-permute-start | bytes 589832 | tf_op jit(solution)/shard_map/ppermute | solution.py:519
  24.7 10.6 %collective-permute-start.7 = (bf16[256,384]{1,0:T(8,128)(2,1)S(1)}, bf16[256,384]{1,0:T(8,128)(2,1)S(1)}, u32[]{:S(2)}, u32[]{:S(2)}) collective-permute-start(bf16[256,384]{1,0:T(8,128)(2,1)S(1)} %add_convert_fusion), channel_id=1, source_target_pairs={{3,1},{5,3},{7,5},{9,7},{11,9},{13,11},{15,13},{14,15},{12,14},{10... | collective-permute-start | bytes 589832 | tf_op jit(solution)/shard_map/ppermute | solution.py:519
  30.2 5.1 %collective-permute-start.5 = (bf16[256,384]{1,0:T(8,128)(2,1)S(1)}, bf16[256,384]{1,0:T(8,128)(2,1)S(1)}, u32[]{:S(2)}, u32[]{:S(2)}) collective-permute-start(bf16[256,384]{1,0:T(8,128)(2,1)S(1)} %get-tuple-element.80), channel_id=1, source_target_pairs={{0,1},{1,0},{2,3},{3,2},{4,5},{5,4},{6,7},{7,6},{8,9},{9,8},{10,11... | collective-permute-start | bytes 589832 | tf_op jit(solution)/shard_map/ppermute | solution.py:519

commit v8 on v7

v8 whole, which is shorter than its diff:
```python
import functools
import math

import jax
import jax.numpy as jnp
from jax import lax
from jax.experimental import pallas as pl
from jax.experimental.pallas import tpu as pltpu
from jax.sharding import PartitionSpec as P

HD = 128
TQ = 128
GROUP = 32

masked_score = -1e30
VMEM_LIMIT = 24 * 1024 * 1024
SCALE = 1.0 / math.sqrt(HD)
VMEM = pl.BlockSpec(memory_space=pltpu.VMEM)
HBM = pl.BlockSpec(memory_space=pltpu.HBM)
CHUNK = 128


def dot_nt(a, b):
    return lax.dot_general(a, b, (((1,), (1,)), ((), ())), preferred_element_type=jnp.float32)


def dot_nn(a, b):
    return lax.dot_general(a, b, (((1,), (0,)), ((), ())), preferred_element_type=jnp.float32)


def half_start(rows, slot):
    odd = lax.axis_index("ctx") % 2
    return pl.multiple_of((odd if slot == 0 else 1 - odd) * rows, rows)


def block_number(count, slot):
    device = lax.axis_index("ctx")
    in_lower = device % 2 == slot
    return jnp.where(in_lower, device, 2 * count - 1 - device)


def in_hbm(array):
    return pltpu.with_memory_space_constraint(array, pltpu.HBM)


def load_block(rows, slot, key, value, out, sems):
    place = pl.ds(half_start(rows, slot), rows)
    return [
        pltpu.make_async_copy(key.at[place], out.at[0:rows], sems.at[2 * slot]),
        pltpu.make_async_copy(value.at[place], out.at[rows : 2 * rows], sems.at[2 * slot + 1]),
    ]


def run_copies(copies):
    for copy in copies:
        copy.start()
    for copy in copies:
        copy.wait()


def pack_kernel(rows, key, value, near_out, far_out, sems):
    run_copies(
        load_block(rows, 1, key, value, near_out, sems)
        + load_block(rows, 0, key, value, far_out, sems)
    )


def pack_blocks(key, value):
    rows = key.shape[0] // 2
    shape = jax.ShapeDtypeStruct((2 * rows, HD), key.dtype)
    return pl.pallas_call(
        functools.partial(pack_kernel, rows),
        out_shape=(shape, shape),
        in_specs=[HBM] * 2,
        out_specs=[VMEM] * 2,
        scratch_shapes=[pltpu.SemaphoreType.DMA((4,))],
        name="pack_blocks",
    )(in_hbm(key), in_hbm(value))


def prepare_kernel(rows, heads, docs, count, *refs):
    (doc_hbm, query_hbm, dout_hbm, key, value) = refs[0:5]
    (doc_lengths, query, dout, sems) = refs[13:]
    refs = refs[5:13]
    wide = heads * TQ
    run_copies(
        [
            pltpu.make_async_copy(query_hbm, query, sems.at[4]),
            pltpu.make_async_copy(dout_hbm, dout, sems.at[5]),
            pltpu.make_async_copy(doc_hbm, doc_lengths, sems.at[6]),
        ]
        + load_block(rows, 0, key, value, refs[0], sems)
        + load_block(rows, 1, key, value, refs[4], sems)
    )
    for slot in (0, 1):
        _, query_t, dout_t, doc_start = refs[4 * slot : 4 * slot + 4]
        own_rows = half_start(rows, slot)
        for step in range(rows // TQ):
            source = pl.ds(own_rows + step * TQ, TQ)
            for h in range(heads):
                place = slice(step * wide + h * TQ, step * wide + (h + 1) * TQ)
                columns = slice(h * HD, (h + 1) * HD)
                query_t[:, place] = jnp.transpose(query[source, columns])
                dout_t[:, place] = jnp.transpose(dout[source, columns])
        at = (
            block_number(count, slot) * rows
            + lax.broadcasted_iota(jnp.int32, (8, TQ), 0) * TQ
            + lax.broadcasted_iota(jnp.int32, (8, TQ), 1)
        )

        def one(index, carry):
            start, found = carry
            found = jnp.where(at >= start, start, found)
            return (start + doc_lengths[index], found)

        _, found = lax.fori_loop(
            0, docs, one, (jnp.int32(0), jnp.zeros((8, TQ), jnp.int32)), unroll=8
        )
        doc_start[...] = found


def prepare(count, doc_lengths, query, dout, key, value):
    rows = query.shape[0] // 2
    heads = query.shape[1] // HD
    pair = jax.ShapeDtypeStruct((2 * rows, HD), key.dtype)
    stacked_t = jax.ShapeDtypeStruct((HD, rows * heads), query.dtype)
    starts = jax.ShapeDtypeStruct((8, TQ), jnp.int32)
    return pl.pallas_call(
        functools.partial(prepare_kernel, rows, heads, doc_lengths.shape[0], count),
        out_shape=(pair, stacked_t, stacked_t, starts) * 2,
        in_specs=[HBM] * 5,
        out_specs=[VMEM] * 8,
        scratch_shapes=[
            pltpu.SMEM(doc_lengths.shape, doc_lengths.dtype),
            pltpu.VMEM(query.shape, query.dtype),
            pltpu.VMEM(dout.shape, dout.dtype),
            pltpu.SemaphoreType.DMA((7,)),
        ],
        compiler_params=pltpu.CompilerParams(vmem_limit_bytes=VMEM_LIMIT),
        cost_estimate=pl.CostEstimate(flops=0, bytes_accessed=4 * 2**20, transcendentals=0),
        name="prepare",
    )(*(in_hbm(array) for array in (doc_lengths, query, dout, key, value)))


class Window:
    def __init__(self, rows):
        self.tiles = rows // TQ
        self.chunks = 2 * self.tiles + 1
        self.steps = range(self.tiles)
        self.late = [self.tiles - step for step in self.steps]
        self.early = [self.chunks - late for late in self.late]


def chunk_rows(counts, step, first=0, count=None):
    start = sum(counts[:step]) + first
    count = counts[step] - first if count is None else count
    return slice(start * CHUNK, (start + count) * CHUNK)


def exponentials(jobs, rows, heads, block_pos, scores):
    back = 2 * rows
    wide = heads * TQ
    base2 = SCALE * math.log2(math.e)

    def score(job, index, row_max):
        step, chunks, (query_t, _, doc_start), _, _ = jobs[job]
        chunk, keys, row = chunks[index][0:3]
        low = doc_start[step : step + 1, :] - (block_pos - back + step * TQ)
        high = lax.broadcasted_iota(jnp.int32, (1, TQ), 1) + back
        tile = slice(step * wide, (step + 1) * wide)
        product = dot_nn(keys[row : row + CHUNK, :], query_t[:, tile])
        for start in range(0, CHUNK, GROUP):
            place = chunk * CHUNK + start
            at = lax.broadcasted_iota(jnp.int32, (GROUP, TQ), 0) + place
            allowed = at >= low
            if place >= back:
                allowed = jnp.logical_and(allowed, at <= high)
            for h in range(heads):
                lanes = slice(h * TQ, (h + 1) * TQ)
                part = jnp.where(allowed, product[start : start + GROUP, lanes], masked_score)
                scores[job % 2, place : place + GROUP, lanes] = part
                for row8 in range(0, GROUP, 8):
                    row_max[h] = jnp.maximum(row_max[h], part[row8 : row8 + 8, :])

    def start_max():
        return [jnp.full((8, TQ), masked_score, jnp.float32)] * heads

    following = start_max()
    for index in range(len(jobs[0][1])):
        score(0, index, following)
    for job, (step, chunks, (_, dout_t, _), first_max, end) in enumerate(jobs):
        tile = slice(step * wide, (step + 1) * wide)
        row_max = jnp.concatenate(
            [jnp.max(part, axis=0, keepdims=True) * base2 for part in following], axis=1
        )
        if first_max is not None:
            row_max = jnp.maximum(row_max, first_max)
        following = start_max()
        ahead = len(jobs[job + 1][1]) if job + 1 < len(jobs) else 0
        done = 0
        total = jnp.zeros((8, wide), jnp.float32)
        delta = jnp.zeros((8, wide), jnp.float32)
        for index, (chunk, keys, row, weights, dprobs, kept) in enumerate(chunks):
            product = dot_nn(keys[rows + row : rows + row + CHUNK, :], dout_t[:, tile])
            for start in range(0, CHUNK, GROUP):
                place = chunk * CHUNK + start
                there = slice(kept.start + start, kept.start + start + GROUP)
                dprob = product[start : start + GROUP, :]
                dprobs[there, :] = dprob.astype(jnp.bfloat16)
                part = jnp.exp2(scores[job % 2, place : place + GROUP, :] * base2 - row_max)
                weights[there, :] = part.astype(jnp.bfloat16)
                term = part * dprob
                for row8 in range(0, GROUP, 8):
                    total = total + part[row8 : row8 + 8, :]
                    delta = delta + term[row8 : row8 + 8, :]
            while done * len(chunks) < ahead * (index + 1):
                score(job + 1, done, following)
                done += 1
        end(
            row_max,
            jnp.sum(total, axis=0, keepdims=True),
            jnp.sum(delta, axis=0, keepdims=True),
        )


def early_kernel(
    rows,
    heads,
    count,
    slot,
    own_kv,
    query_t,
    dout_t,
    doc_start,
    prev1,
    weights,
    dprobs,
    stats,
    scores,
):
    window = Window(rows)
    position = block_number(count, slot) * rows
    jobs = []
    for step in window.steps:
        chunks = []
        for index in range(window.early[step]):
            chunk = window.late[step] + index
            row = step * TQ + chunk * CHUNK
            keys = own_kv if row >= 2 * rows else prev1
            kept = chunk_rows(window.early, step, index, 1)
            chunks.append((chunk, keys, row % rows, weights, dprobs, kept))

        def end(*found, step=step):
            for kind, value in enumerate(found):
                stats[8 * kind + step : 8 * kind + step + 1, :] = value

        jobs.append((step, chunks, (query_t, dout_t, doc_start), None, end))
    exponentials(jobs, rows, heads, position, scores)


def early_scores(slot, count, ready, prev1):
    rows = prev1.shape[0] // 2
    heads = ready[1].shape[1] // rows
    wide = heads * TQ
    kept = jax.ShapeDtypeStruct((sum(Window(rows).early) * CHUNK, wide), jnp.bfloat16)
    return pl.pallas_call(
        functools.partial(early_kernel, rows, heads, count, slot),
        out_shape=(kept, kept, jax.ShapeDtypeStruct((24, wide), jnp.float32)),
        in_specs=[VMEM] * 5,
        out_specs=[VMEM] * 3,
        scratch_shapes=[pltpu.VMEM((2, 2 * rows + TQ, wide), jnp.float32)],
        compiler_params=pltpu.CompilerParams(vmem_limit_bytes=VMEM_LIMIT),
        cost_estimate=pl.CostEstimate(flops=0, bytes_accessed=0, transcendentals=0),
        name="early_far" if slot == 0 else "early_near",
    )(*ready, prev1)


def scaled_by(array, tile, factor):
    return (array[:, tile].astype(jnp.float32) * factor).astype(jnp.bfloat16)


def dscore_rows(dscores, there, weights, dprobs, kept, delta):
    delta = jnp.broadcast_to(delta, (16, delta.shape[1]))
    for start in range(0, there.stop - there.start, 16):
        out = slice(there.start + start, there.start + start + 16)
        place = slice(kept.start + start, kept.start + start + 16)
        dscores[out, :] = weights[place, :] * (dprobs[place, :] - delta)


def add_products(step, columns, products):
    for total_ref, side, terms in products:
        term = dot_nt(side, terms)
        if step == 0:
            total_ref[:, columns] = term
        else:
            total_ref[:, columns] += term


def late_kernel(
    rows,
    heads,
    count,
    slot,
    query_t,
    dout_t,
    doc_start,
    early_stats,
    prev2,
    weights,
    dscores,
    stats,
    prev2_out,
    scores,
    dprobs,
    dk,
    dv,
):
    wide = heads * TQ
    window = Window(rows)
    jobs = []
    for step in window.steps:
        chunks = []
        for chunk in range(window.late[step]):
            kept = chunk_rows(window.late, step, chunk, 1)
            chunks.append((chunk, prev2, step * TQ + chunk * CHUNK, weights, dprobs, kept))

        def end(row_max, total, delta, step=step):
            tile = slice(step * wide, (step + 1) * wide)
            early = [early_stats[8 * kind + step : 8 * kind + step + 1, :] for kind in range(3)]
            shrink = jnp.exp2(early[0] - row_max)
            late_factor = 1.0 / (total + early[1] * shrink)
            early_factor = late_factor * shrink
            delta = delta * late_factor + early[2] * early_factor
            for kind, value in enumerate((late_factor, early_factor, delta)):
                stats[8 * kind + step : 8 * kind + step + 1, :] = value
            there = chunk_rows(window.late, step)
            dscore_rows(dscores, there, weights, dprobs, there, delta.astype(jnp.bfloat16))
            add_products(
                step,
                slice(step * TQ, rows),
                (
                    (dv, scaled_by(dout_t, tile, late_factor), weights[there, :]),
                    (dk, scaled_by(query_t, tile, late_factor), dscores[there, :]),
                ),
            )

        first_max = early_stats[step : step + 1, :]
        jobs.append((step, chunks, (query_t, dout_t, doc_start), first_max, end))
    exponentials(jobs, rows, heads, block_number(count, slot) * rows, scores)
    prev2_out[0:HD] = (dk[...] * SCALE).astype(prev2_out.dtype)
    prev2_out[HD : 2 * HD] = dv[...].astype(prev2_out.dtype)


def late_scores(slot, count, ready, early, prev2):
    rows = prev2.shape[0] // 2
    heads = ready[1].shape[1] // rows
    wide = heads * TQ
    late = (sum(Window(rows).late) * CHUNK, wide)
    return pl.pallas_call(
        functools.partial(late_kernel, rows, heads, count, slot),
        out_shape=(
            jax.ShapeDtypeStruct(late, jnp.bfloat16),
            jax.ShapeDtypeStruct(late, jnp.bfloat16),
            jax.ShapeDtypeStruct((24, wide), jnp.float32),
            jax.ShapeDtypeStruct((2 * HD, rows), jnp.bfloat16),
        ),
        in_specs=[VMEM] * 5,
        out_specs=[VMEM] * 4,
        scratch_shapes=[
            pltpu.VMEM((2, rows, wide), jnp.float32),
            pltpu.VMEM(late, jnp.bfloat16),
            pltpu.VMEM((HD, rows), jnp.float32),
            pltpu.VMEM((HD, rows), jnp.float32),
        ],
        compiler_params=pltpu.CompilerParams(vmem_limit_bytes=VMEM_LIMIT),
        cost_estimate=pl.CostEstimate(flops=2**31, bytes_accessed=0, transcendentals=0),
        name="late_far" if slot == 0 else "late_near",
    )(*ready[1:4], early[2], prev2)


def grads_kernel(
    rows, heads, query_t, dout_t, weights, dprobs, stats, dscores, prev1_out, own_out, dk, dv
):
    wide = heads * TQ
    window = Window(rows)
    for step in reversed(window.steps):
        tile = slice(step * wide, (step + 1) * wide)
        factor = stats[8 + step : 8 + step + 1, :]
        delta = stats[16 + step : 16 + step + 1, :].astype(jnp.bfloat16)
        there = chunk_rows(window.early, step)
        dscore_rows(dscores, there, weights, dprobs, there, delta)
        add_products(
            window.tiles - 1 - step,
            slice(0, window.early[step] * CHUNK),
            (
                (dv, scaled_by(dout_t, tile, factor), weights[there, :]),
                (dk, scaled_by(query_t, tile, factor), dscores[there, :]),
            ),
        )
    prev1_out[0:HD] = (dk[:, 0:rows] * SCALE).astype(prev1_out.dtype)
    prev1_out[HD : 2 * HD] = dv[:, 0:rows].astype(prev1_out.dtype)
    own_out[0:HD] = dk[:, rows : 2 * rows] * SCALE
    own_out[HD : 2 * HD] = dv[:, rows : 2 * rows]


def early_grads(slot, ready, early, stats):
    rows = ready[0].shape[0] // 2
    heads = ready[1].shape[1] // rows
    return pl.pallas_call(
        functools.partial(grads_kernel, rows, heads),
        out_shape=(
            jax.ShapeDtypeStruct(early[0].shape, jnp.bfloat16),
            jax.ShapeDtypeStruct((2 * HD, rows), jnp.bfloat16),
            jax.ShapeDtypeStruct((2 * HD, rows), jnp.float32),
        ),
        in_specs=[VMEM] * 5,
        out_specs=[VMEM] * 3,
        scratch_shapes=[pltpu.VMEM((HD, 2 * rows), jnp.float32)] * 2,
        compiler_params=pltpu.CompilerParams(vmem_limit_bytes=VMEM_LIMIT),
        cost_estimate=pl.CostEstimate(flops=2**31, bytes_accessed=0, transcendentals=0),
        name="grads_far" if slot == 0 else "grads_near",
    )(*ready[1:3], *early[0:2], stats)


def outputs_kernel(rows, heads, *refs):
    blocks = (refs[0:8], refs[8:16])
    (attended, grad_query, keys_t, values_t) = refs[16:]
    window = Window(rows)
    for slot, block in enumerate(blocks):
        (own_kv, prev1, prev2, early_w, early_d, late_w, late_d, stats) = block
        own_rows = half_start(rows, slot)
        for place, source in enumerate((prev2, prev1, own_kv)):
            for tile in range(rows // TQ):
                part = slice(place * rows + tile * TQ, place * rows + (tile + 1) * TQ)
                row = tile * TQ
                keys_t[:, part] = jnp.transpose(source[row : row + TQ, :])
                values_t[:, part] = jnp.transpose(source[rows + row : rows + row + TQ, :])
        for step in window.steps:
            late_columns = slice(step * TQ, rows)
            early_columns = slice(rows, 2 * rows + (step + 1) * TQ)
            late_rows = chunk_rows(window.late, step)
            early_rows = chunk_rows(window.early, step)
            place = pl.ds(own_rows + step * TQ, TQ)
            for out, side, late, early, scale in (
                (attended, values_t, late_w, early_w, 1.0),
                (grad_query, keys_t, late_d, early_d, SCALE),
            ):
                found = dot_nn(side[:, late_columns], late[late_rows, :]) * (
                    stats[step : step + 1, :] * scale
                ) + dot_nn(side[:, early_columns], early[early_rows, :]) * (
                    stats[8 + step : 8 + step + 1, :] * scale
                )
                for h in range(heads):
                    part = found[:, h * TQ : (h + 1) * TQ]
                    out[place, h * HD : (h + 1) * HD] = jnp.transpose(part).astype(out.dtype)


def block_outputs(query, far, near):
    rows = query.shape[0] // 2
    heads = query.shape[1] // HD
    shape = jax.ShapeDtypeStruct(query.shape, query.dtype)
    return pl.pallas_call(
        functools.partial(outputs_kernel, rows, heads),
        out_shape=(shape, shape),
        in_specs=[VMEM] * 16,
        out_specs=[VMEM] * 2,
        scratch_shapes=[pltpu.VMEM((HD, 3 * rows), jnp.bfloat16)] * 2,
        compiler_params=pltpu.CompilerParams(vmem_limit_bytes=VMEM_LIMIT),
        cost_estimate=pl.CostEstimate(flops=2**30, bytes_accessed=0, transcendentals=0),
        name="block_outputs",
    )(*far, *near)


def total_kernel(rows, far_own, far_1, far_2, near_own, near_1, grad_key, grad_value):
    far = far_own[...] + far_1[...].astype(jnp.float32) + far_2[...].astype(jnp.float32)
    near = near_own[...] + near_1[...].astype(jnp.float32)
    for slot, total in ((0, far), (1, near)):
        place = pl.ds(half_start(rows, slot), rows)
        grad_key[place, :] = jnp.transpose(total[0:HD]).astype(grad_key.dtype)
        grad_value[place, :] = jnp.transpose(total[HD : 2 * HD]).astype(grad_value.dtype)


def total_grads(*parts):
    rows = parts[0].shape[1]
    shape = jax.ShapeDtypeStruct((2 * rows, HD), jnp.bfloat16)
    return pl.pallas_call(
        functools.partial(total_kernel, rows),
        out_shape=(shape, shape),
        in_specs=[VMEM] * 5,
        out_specs=[VMEM] * 2,
        compiler_params=pltpu.CompilerParams(vmem_limit_bytes=VMEM_LIMIT),
        name="total_grads",
    )(*parts)


def body(query, key, value, d_out, doc_lengths):
    count = lax.axis_size("ctx")

    def holder(block):
        return block if block < count else 2 * count - 1 - block

    def move(array, pairs):
        return lax.ppermute(array, "ctx", pairs)

    near_on = [(holder(b), holder(b + 2)) for b in range(1, 2 * count - 2, 2)]
    far_on = [(holder(b), holder(b + 2)) for b in range(0, 2 * count - 2, 2)]
    near_to_far = [(holder(b), holder(b + 1)) for b in range(1, 2 * count - 2, 2)]
    swap = [(d, d ^ 1) for d in range(count)]
    near_back = [(t, s) for s, t in near_on]
    far_back = [(t, s) for s, t in far_on]

    near_kv, far_kv = pack_blocks(key, value)
    far_1 = move(near_kv, near_to_far)
    near_1 = move(far_kv, swap)
    far_2 = move(far_kv, far_on)
    prepared = prepare(count, doc_lengths, query, d_out, key, value)
    far_ready, near_ready = prepared[0:4], prepared[4:8]
    near_early = early_scores(1, count, near_ready, near_1)
    far_1, near_early = lax.optimization_barrier((far_1, near_early))
    near_2 = move(far_1, swap)
    far_early = early_scores(0, count, far_ready, far_1)

    far_w, far_d, far_stats, far_g2 = late_scores(0, count, far_ready, far_early, far_2)
    from_far_2 = move(far_g2, far_back)
    far_early_d, far_g1, far_own = early_grads(0, far_ready, far_early, far_stats)
    relayed = move(far_g1, swap)
    near_w, near_d, near_stats, near_g2 = late_scores(1, count, near_ready, near_early, near_2)
    near_sum = (near_g2.astype(jnp.float32) + relayed.astype(jnp.float32)).astype(jnp.bfloat16)
    from_near_2 = move(near_sum, near_back)
    near_early_d, near_g1, near_own = early_grads(1, near_ready, near_early, near_stats)
    from_near_1 = move(near_g1, swap)
    attended, grad_query = block_outputs(
        query,
        (far_ready[0], far_1, far_2, far_early[0], far_early_d, far_w, far_d, far_stats),
        (near_ready[0], near_1, near_2, near_early[0], near_early_d, near_w, near_d, near_stats),
    )
    grad_key, grad_value = total_grads(far_own, from_near_1, from_far_2, near_own, from_near_2)
    return (attended, grad_query, grad_key, grad_value)


def solution(mesh):
    rows = P(("dp", "ctx"), None)
    return jax.shard_map(
        body,
        mesh=mesh,
        in_specs=(rows, rows, rows, rows, P("dp")),
        out_specs=(rows, rows, rows, rows),
        check_vma=False,
    )
```

time: 36.5 us -> 38.9 us (1.066)
  waiting for transfers between devices: 0.61 us -> 2.27 us
  starting transfers between devices: 17.1 us -> 17.9 us
    ppermute x8, waiting for transfers between devices: 0.61 us -> 2.27 us  [move(): return lax.ppermute(array, 'ctx', pairs)]
    pallas_call x3 -> x6, Pallas kernels: 8.41 us -> 9.79 us  [the longest x2 3.51 us: early_scores(): pl.pallas_call(functools.partial(early_kernel, rows, heads, count, slot),...]
    pallas_call x1, Pallas kernels: 4.41 us -> 3.03 us  [block_outputs(): pl.pallas_call(functools.partial(outputs_kernel, rows, heads), out_shape=...]
    ppermute x8, starting transfers between devices: 17.1 us -> 17.9 us  [move(): return lax.ppermute(array, 'ctx', pairs)]
  transfers between devices with their start and end apart: 8 -> 8, of which waited for: 1 -> 1; matrix products, arithmetic and copies ran while one was open for 0% -> 0% of each run, Pallas kernels for 41% -> 39%
where the time goes in v8:
time: 38.9 us; the launch traced here: 38.6 us
  starting transfers between devices  17.9 us (46%)
  Pallas kernels  17.7 us (46%)
  waiting for transfers between devices  2.27 us (6%)
  between operations  0.74 us (2%)
    ppermute x8, starting transfers between devices, move(): return lax.ppermute(array, 'ctx', pairs)  17.9 us
    pallas_call x2, Pallas kernels, early_scores(): pl.pallas_call(functools.partial(early_kernel, rows, heads, count, slot),...  3.51 us
    pallas_call x2, Pallas kernels, late_scores(): pl.pallas_call(functools.partial(late_kernel, rows, heads, count, slot),...  3.49 us
    pallas_call x1, Pallas kernels, block_outputs(): pl.pallas_call(functools.partial(outputs_kernel, rows, heads), out_shape=...  3.03 us
    pallas_call x2, Pallas kernels, early_grads(): pl.pallas_call(functools.partial(grads_kernel, rows, heads), out_shape=(j...  2.79 us
    ppermute x8, waiting for transfers between devices, move(): return lax.ppermute(array, 'ctx', pairs)  2.27 us
    pallas_call x1, Pallas kernels, prepare(): pl.pallas_call(functools.partial(prepare_kernel, rows, heads, doc_lengths...  2.11 us
    pallas_call x1, Pallas kernels, pack_blocks(): pl.pallas_call(functools.partial(pack_kernel, rows), out_shape=(shape, sh...  1.82 us
  transfers between devices with their start and end apart: 8, of which 1 were waited for; matrix products, arithmetic and copies ran while one was open for 0% of the time, Pallas kernels for 39%

profile of v8, /device:TPU:0, one launch (start us, length us, event | category | flops | bytes accessed | tf_op | source)
XLA Modules:
  0.0 38.6 jit_solution(4931001206824899706)
XLA Ops:
  0.6 1.8 %pack_blocks.1 = (bf16[768,128]{1,0:T(8,128)(2,1)}, bf16[768,128]{1,0:T(8,128)(2,1)}) custom-call(bf16[768,128]{1,0:T(8,128)(2,1)} %key.1, bf16[768,128]{1,0:T(8,128)(2,1)} %value.1), custom_call_target="tpu_custom_call" | custom-call | tf_op jit(solution)/shard_map/pack_blocks/pallas_call | solution.py:71
  2.5 0.5 %collective-permute-start.1 = (bf16[768,128]{1,0:T(8,128)(2,1)}, bf16[768,128]{1,0:T(8,128)(2,1)S(1)}, u32[]{:S(2)}, u32[]{:S(2)}) collective-permute-start(bf16[768,128]{1,0:T(8,128)(2,1)} %get-tuple-element.48), channel_id=1, source_target_pairs={{0,1},{1,0},{2,3},{3,2},{4,5},{5,4},{6,7},{7,6},{8,9},{9,8},{10,11... | collective-permute-start | bytes 589832 | tf_op jit(solution)/shard_map/ppermute | solution.py:503
  3.0 0.7 %collective-permute-start = (bf16[768,128]{1,0:T(8,128)(2,1)}, bf16[768,128]{1,0:T(8,128)(2,1)S(1)}, u32[]{:S(2)}, u32[]{:S(2)}) collective-permute-start(bf16[768,128]{1,0:T(8,128)(2,1)} %get-tuple-element.43), channel_id=1, source_target_pairs={{1,2},{3,4},{5,6},{7,8},{9,10},{11,12},{13,14},{15,15},{14,13},{12... | collective-permute-start | bytes 589832 | tf_op jit(solution)/shard_map/ppermute | solution.py:503
  3.6 5.7 %collective-permute-start.2 = (bf16[768,128]{1,0:T(8,128)(2,1)}, bf16[768,128]{1,0:T(8,128)(2,1)S(1)}, u32[]{:S(2)}, u32[]{:S(2)}) collective-permute-start(bf16[768,128]{1,0:T(8,128)(2,1)} %get-tuple-element.48), channel_id=1, source_target_pairs={{0,2},{2,4},{4,6},{6,8},{8,10},{10,12},{12,14},{14,15},{15,13},{13... | collective-permute-start | bytes 589832 | tf_op jit(solution)/shard_map/ppermute | solution.py:503
  9.4 2.1 %prepare.1 = (bf16[768,128]{1,0:T(8,128)(2,1)S(1)}, bf16[128,1536]{1,0:T(8,128)(2,1)S(1)}, bf16[128,1536]{1,0:T(8,128)(2,1)S(1)}, s32[8,128]{1,0:T(8,128)S(1)}, ...) custom-call(s32[32]{0:T(128)} %refs_0_.1, ...), custom_call_target="tpu_custom_call" | custom-call | bytes 4194304 | tf_op jit(solution)/shard_map/prepare/pallas_call | solution.py:128
  11.5 0.0 collective-permute-done.1.prev1.refs_9_
  11.5 1.8 %early_near.1 = (bf16[1920,512]{1,0:T(8,128)(2,1)S(1)}, bf16[1920,512]{1,0:T(8,128)(2,1)S(1)}, f32[24,512]{1,0:T(8,128)S(1)}) custom-call(bf16[768,128]{1,0:T(8,128)(2,1)S(1)} %get-tuple-element.44.own_kv.refs_8_, bf16[128,1536]{1,0:T(8,128)(2,1)S(1)} %get-tuple-element.45.query_t, bf16[128,1536]{1,0:T(8,128)(2,1)S(1)} %get-tuple-element.46.dout_t, ...), custom_call_target="tpu_custom_call" | custom-call | tf_op jit(solution)/shard_map/early_near/pallas_call | solution.py:266
  13.3 0.0 collective-permute-done.prev1.refs_1_
  13.3 1.6 %collective-permute-start.3 = (bf16[768,128]{1,0:T(8,128)(2,1)S(1)}, bf16[768,128]{1,0:T(8,128)(2,1)S(1)}, u32[]{:S(2)}, u32[]{:S(2)}) collective-permute-start(bf16[768,128]{1,0:T(8,128)(2,1)S(1)} %collective-permute-done.prev1.refs_1_), channel_id=1, source_target_pairs={{0,1},{1,0},{2,3},{3,2},{4,5},{5,4},{6,7},{7,6},{8,9},{9,8},{10,11... | collective-permute-start | bytes 589832 | tf_op jit(solution)/shard_map/ppermute | solution.py:503
  14.9 1.7 %early_far.1 = (bf16[1920,512]{1,0:T(8,128)(2,1)S(1)}, bf16[1920,512]{1,0:T(8,128)(2,1)S(1)}, f32[24,512]{1,0:T(8,128)S(1)}) custom-call(bf16[768,128]{1,0:T(8,128)(2,1)S(1)} %get-tuple-element.42.own_kv.refs_0_, bf16[128,1536]{1,0:T(8,128)(2,1)S(1)} %get-tuple-element.53.query_t, bf16[128,1536]{1,0:T(8,128)(2,1)S(1)} %get-tuple-element.54.dout_t, ...), custom_call_target="tpu_custom_call" | custom-call | tf_op jit(solution)/shard_map/early_far/pallas_call | solution.py:266
  16.6 0.0 collective-permute-done.2.prev2.refs_2_
  16.7 1.7 %late_far.1 = (bf16[768,512]{1,0:T(8,128)(2,1)S(1)}, bf16[768,512]{1,0:T(8,128)(2,1)S(1)}, f32[24,512]{1,0:T(8,128)S(1)}, bf16[256,384]{1,0:T(8,128)(2,1)S(1)}) custom-call(bf16[128,1536]{1,0:T(8,128)(2,1)S(1)} %get-tuple-element.53.query_t, bf16[128,1536]{1,0:T(8,128)(2,1)S(1)} %get-tuple-element.54.dout_t, s32[8,128]{1,0:T(8,128)S(1)} %get-tuple-element.55.doc_start, ...), custom_call_target="tpu_custom_call" | custom-call | flops 2147483648 | tf_op jit(solution)/shard_map/late_far/pallas_call | solution.py:359
  18.4 1.3 %collective-permute-start.5 = (bf16[256,384]{1,0:T(8,128)(2,1)S(1)}, bf16[256,384]{1,0:T(8,128)(2,1)S(1)}, u32[]{:S(2)}, u32[]{:S(2)}) collective-permute-start(bf16[256,384]{1,0:T(8,128)(2,1)S(1)} %get-tuple-element.74), channel_id=1, source_target_pairs={{2,0},{4,2},{6,4},{8,6},{10,8},{12,10},{14,12},{15,14},{13,15},{11... | collective-permute-start | bytes 589832 | tf_op jit(solution)/shard_map/ppermute | solution.py:503
  19.7 1.4 %grads_far.1 = (bf16[1920,512]{1,0:T(8,128)(2,1)S(1)}, bf16[256,384]{1,0:T(8,128)(2,1)S(1)}, f32[256,384]{1,0:T(8,128)S(1)}) custom-call(bf16[128,1536]{1,0:T(8,128)(2,1)S(1)} %get-tuple-element.53.query_t, bf16[128,1536]{1,0:T(8,128)(2,1)S(1)} %get-tuple-element.54.dout_t, bf16[1920,512]{1,0:T(8,128)(2,1)S(1)} %get-tuple-element.56.weights.refs_3_, ...), custom_call_target="tpu_custom_call" | custom-call | flops 2147483648 | tf_op jit(solution)/shard_map/grads_far/pallas_call | solution.py:409
  21.1 3.3 %collective-permute-start.6 = (bf16[256,384]{1,0:T(8,128)(2,1)S(1)}, bf16[256,384]{1,0:T(8,128)(2,1)S(1)}, u32[]{:S(2)}, u32[]{:S(2)}) collective-permute-start(bf16[256,384]{1,0:T(8,128)(2,1)S(1)} %get-tuple-element.77), channel_id=1, source_target_pairs={{0,1},{1,0},{2,3},{3,2},{4,5},{5,4},{6,7},{7,6},{8,9},{9,8},{10,11... | collective-permute-start | bytes 589832 | tf_op jit(solution)/shard_map/ppermute | solution.py:503
  24.4 0.0 collective-permute-done.3.prev2.refs_10_
  24.4 1.8 %late_near.1 = (bf16[768,512]{1,0:T(8,128)(2,1)S(1)}, bf16[768,512]{1,0:T(8,128)(2,1)S(1)}, f32[24,512]{1,0:T(8,128)S(1)}, bf16[256,384]{1,0:T(8,128)(2,1)S(1)}) custom-call(bf16[128,1536]{1,0:T(8,128)(2,1)S(1)} %get-tuple-element.45.query_t, bf16[128,1536]{1,0:T(8,128)(2,1)S(1)} %get-tuple-element.46.dout_t, s32[8,128]{1,0:T(8,128)S(1)} %get-tuple-element.47.doc_start, ...), custom_call_target="tpu_custom_call" | custom-call | flops 2147483648 | tf_op jit(solution)/shard_map/late_near/pallas_call | solution.py:359
  26.2 1.4 %grads_near.1 = (bf16[1920,512]{1,0:T(8,128)(2,1)S(1)}, bf16[256,384]{1,0:T(8,128)(2,1)S(1)}, f32[256,384]{1,0:T(8,128)S(1)}) custom-call(bf16[128,1536]{1,0:T(8,128)(2,1)S(1)} %get-tuple-element.45.query_t, bf16[128,1536]{1,0:T(8,128)(2,1)S(1)} %get-tuple-element.46.dout_t, bf16[1920,512]{1,0:T(8,128)(2,1)S(1)} %get-tuple-element.63.weights.refs_11_, ...), custom_call_target="tpu_custom_call" | custom-call | flops 2147483648 | tf_op jit(solution)/shard_map/grads_near/pallas_call | solution.py:409
  27.6 0.1 collective-permute-start.4
  27.7 0.0 collective-permute-done.6
  27.7 0.1 add_convert_fusion
  27.7 4.7 %collective-permute-start.7 = (bf16[256,384]{1,0:T(8,128)(2,1)S(1)}, bf16[256,384]{1,0:T(8,128)(2,1)S(1)}, u32[]{:S(2)}, u32[]{:S(2)}) collective-permute-start(bf16[256,384]{1,0:T(8,128)(2,1)S(1)} %add_convert_fusion), channel_id=1, source_target_pairs={{3,1},{5,3},{7,5},{9,7},{11,9},{13,11},{15,13},{14,15},{12,14},{10... | collective-permute-start | bytes 589832 | tf_op jit(solution)/shard_map/ppermute | solution.py:503
  32.4 3.0 %block_outputs.1 = (bf16[768,512]{1,0:T(8,128)(2,1)}, bf16[768,512]{1,0:T(8,128)(2,1)}) custom-call(bf16[768,128]{1,0:T(8,128)(2,1)S(1)} %get-tuple-element.42.own_kv.refs_0_, bf16[768,128]{1,0:T(8,128)(2,1)S(1)} %collective-permute-done.prev1.refs_1_, bf16[768,128]{1,0:T(8,128)(2,1)S(1)} %collective-permute-done.2.prev2.refs_2_, ...), custom_call_target="tpu_custom_call" | custom-call | flops 1073741824 | tf_op jit(solution)/shard_map/block_outputs/pallas_call | solution.py:462
  35.5 0.0 collective-permute-done.5.far_2
  35.5 0.0 collective-permute-done.4.far_1
  35.5 2.2 %collective-permute-done.7.near_1 = bf16[256,384]{1,0:T(8,128)(2,1)S(1)} collective-permute-done((bf16[256,384]{1,0:T(8,128)(2,1)S(1)}, bf16[256,384]{1,0:T(8,128)(2,1)S(1)}, u32[]{:S(2)}, u32[]{:S(2)}) %collective-permute-start.7) | collective-permute-done | bytes 196640 | tf_op jit(solution)/shard_map/ppermute | solution.py:503
  37.7 0.9 %total_grads.1 = (bf16[768,128]{1,0:T(8,128)(2,1)}, bf16[768,128]{1,0:T(8,128)(2,1)}) custom-call(f32[256,384]{1,0:T(8,128)S(1)} %get-tuple-element.72.far_own, bf16[256,384]{1,0:T(8,128)(2,1)S(1)} %collective-permute-done.4.far_1, bf16[256,384]{1,0:T(8,128)(2,1)S(1)} %collective-permute-done.5.far_2, f32[256,384]{1,0:T(8,128)S(1)} %get-tuple-element.75.near_own, ...), custom_call_target="tpu_custom_call" | custom-call | tf_op jit(solution)/shard_map/total_grads/pallas_call | solution.py:486
Async XLA Ops:
  2.5 9.0 %collective-permute-start.1 = (bf16[768,128]{1,0:T(8,128)(2,1)}, bf16[768,128]{1,0:T(8,128)(2,1)S(1)}, u32[]{:S(2)}, u32[]{:S(2)}) collective-permute-start(bf16[768,128]{1,0:T(8,128)(2,1)} %get-tuple-element.48), channel_id=1, source_target_pairs={{0,1},{1,0},{2,3},{3,2},{4,5},{5,4},{6,7},{7,6},{8,9},{9,8},{10,11... | collective-permute-start | bytes 589832 | tf_op jit(solution)/shard_map/ppermute | solution.py:503
  3.0 10.3 %collective-permute-start = (bf16[768,128]{1,0:T(8,128)(2,1)}, bf16[768,128]{1,0:T(8,128)(2,1)S(1)}, u32[]{:S(2)}, u32[]{:S(2)}) collective-permute-start(bf16[768,128]{1,0:T(8,128)(2,1)} %get-tuple-element.43), channel_id=1, source_target_pairs={{1,2},{3,4},{5,6},{7,8},{9,10},{11,12},{13,14},{15,15},{14,13},{12... | collective-permute-start | bytes 589832 | tf_op jit(solution)/shard_map/ppermute | solution.py:503
  3.6 13.0 %collective-permute-start.2 = (bf16[768,128]{1,0:T(8,128)(2,1)}, bf16[768,128]{1,0:T(8,128)(2,1)S(1)}, u32[]{:S(2)}, u32[]{:S(2)}) collective-permute-start(bf16[768,128]{1,0:T(8,128)(2,1)} %get-tuple-element.48), channel_id=1, source_target_pairs={{0,2},{2,4},{4,6},{6,8},{8,10},{10,12},{12,14},{14,15},{15,13},{13... | collective-permute-start | bytes 589832 | tf_op jit(solution)/shard_map/ppermute | solution.py:503
  13.3 11.1 %collective-permute-start.3 = (bf16[768,128]{1,0:T(8,128)(2,1)S(1)}, bf16[768,128]{1,0:T(8,128)(2,1)S(1)}, u32[]{:S(2)}, u32[]{:S(2)}) collective-permute-start(bf16[768,128]{1,0:T(8,128)(2,1)S(1)} %collective-permute-done.prev1.refs_1_), channel_id=1, source_target_pairs={{0,1},{1,0},{2,3},{3,2},{4,5},{5,4},{6,7},{7,6},{8,9},{9,8},{10,11... | collective-permute-start | bytes 589832 | tf_op jit(solution)/shard_map/ppermute | solution.py:503
  18.4 17.1 %collective-permute-start.5 = (bf16[256,384]{1,0:T(8,128)(2,1)S(1)}, bf16[256,384]{1,0:T(8,128)(2,1)S(1)}, u32[]{:S(2)}, u32[]{:S(2)}) collective-permute-start(bf16[256,384]{1,0:T(8,128)(2,1)S(1)} %get-tuple-element.74), channel_id=1, source_target_pairs={{2,0},{4,2},{6,4},{8,6},{10,8},{12,10},{14,12},{15,14},{13,15},{11... | collective-permute-start | bytes 589832 | tf_op jit(solution)/shard_map/ppermute | solution.py:503
  21.1 6.6 %collective-permute-start.6 = (bf16[256,384]{1,0:T(8,128)(2,1)S(1)}, bf16[256,384]{1,0:T(8,128)(2,1)S(1)}, u32[]{:S(2)}, u32[]{:S(2)}) collective-permute-start(bf16[256,384]{1,0:T(8,128)(2,1)S(1)} %get-tuple-element.77), channel_id=1, source_target_pairs={{0,1},{1,0},{2,3},{3,2},{4,5},{5,4},{6,7},{7,6},{8,9},{9,8},{10,11... | collective-permute-start | bytes 589832 | tf_op jit(solution)/shard_map/ppermute | solution.py:503
  27.6 7.9 %collective-permute-start.4 = (bf16[256,384]{1,0:T(8,128)(2,1)S(1)}, bf16[256,384]{1,0:T(8,128)(2,1)S(1)}, u32[]{:S(2)}, u32[]{:S(2)}) collective-permute-start(bf16[256,384]{1,0:T(8,128)(2,1)S(1)} %get-tuple-element.73), channel_id=1, source_target_pairs={{0,1},{1,0},{2,3},{3,2},{4,5},{5,4},{6,7},{7,6},{8,9},{9,8},{10,11... | collective-permute-start | bytes 589832 | tf_op jit(solution)/shard_map/ppermute | solution.py:503
  27.7 10.0 %collective-permute-start.7 = (bf16[256,384]{1,0:T(8,128)(2,1)S(1)}, bf16[256,384]{1,0:T(8,128)(2,1)S(1)}, u32[]{:S(2)}, u32[]{:S(2)}) collective-permute-start(bf16[256,384]{1,0:T(8,128)(2,1)S(1)} %add_convert_fusion), channel_id=1, source_target_pairs={{3,1},{5,3},{7,5},{9,7},{11,9},{13,11},{15,13},{14,15},{12,14},{10... | collective-permute-start | bytes 589832 | tf_op jit(solution)/shard_map/ppermute | solution.py:503

commit v9 on v8

--- a/solution.py
+++ b/solution.py
@@ -143,11 +143,13 @@
 
 
 class Window:
-    def __init__(self, rows):
+    def __init__(self, rows, slot):
         self.tiles = rows // TQ
         self.chunks = 2 * self.tiles + 1
         self.steps = range(self.tiles)
-        self.late = [self.tiles - step for step in self.steps]
+        self.first = [self.tiles - step for step in self.steps]
+        self.rest = [self.chunks - first for first in self.first]
+        self.late = [first + (1 - slot) * self.tiles for first in self.first]
         self.early = [self.chunks - late for late in self.late]
 
 
@@ -165,7 +167,7 @@
     def score(job, index, row_max):
         step, chunks, (query_t, _, doc_start), _, _ = jobs[job]
         chunk, keys, row = chunks[index][0:3]
-        low = doc_start[step : step + 1, :] - (block_pos - back + step * TQ)
+        low = doc_start[step : step + 1, :] - (block_pos(job) - back + step * TQ)
         high = lax.broadcasted_iota(jnp.int32, (1, TQ), 1) + back
         tile = slice(step * wide, (step + 1) * wide)
         product = dot_nn(keys[row : row + CHUNK, :], query_t[:, tile])
@@ -223,56 +225,51 @@
         )
 
 
-def early_kernel(
-    rows,
-    heads,
-    count,
-    slot,
-    own_kv,
-    query_t,
-    dout_t,
-    doc_start,
-    prev1,
-    weights,
-    dprobs,
-    stats,
-    scores,
-):
-    window = Window(rows)
-    position = block_number(count, slot) * rows
+def early_kernel(rows, heads, count, near_1, *refs):
+    inputs, outs, scores = (refs[0:4], refs[4:8]), (refs[8:11], refs[11:14]), refs[14]
     jobs = []
-    for step in window.steps:
-        chunks = []
-        for index in range(window.early[step]):
-            chunk = window.late[step] + index
-            row = step * TQ + chunk * CHUNK
-            keys = own_kv if row >= 2 * rows else prev1
-            kept = chunk_rows(window.early, step, index, 1)
-            chunks.append((chunk, keys, row % rows, weights, dprobs, kept))
-
-        def end(*found, step=step):
-            for kind, value in enumerate(found):
-                stats[8 * kind + step : 8 * kind + step + 1, :] = value
-
-        jobs.append((step, chunks, (query_t, dout_t, doc_start), None, end))
-    exponentials(jobs, rows, heads, position, scores)
-
-
-def early_scores(slot, count, ready, prev1):
-    rows = prev1.shape[0] // 2
-    heads = ready[1].shape[1] // rows
+    for slot in (0, 1):
+        window = Window(rows, slot)
+        own_kv, query_t, dout_t, doc_start = inputs[slot]
+        weights, dprobs, stats = outs[slot]
+        for step in window.steps:
+            chunks = []
+            for index in range(window.early[step]):
+                chunk = window.late[step] + index
+                row = step * TQ + chunk * CHUNK
+                keys = own_kv if row >= 2 * rows else near_1
+                kept = chunk_rows(window.early, step, index, 1)
+                chunks.append((chunk, keys, row % rows, weights, dprobs, kept))
+
+            def end(*found, stats=stats, step=step):
+                for kind, value in enumerate(found):
+                    stats[8 * kind + step : 8 * kind + step + 1, :] = value
+
+            jobs.append((step, chunks, (query_t, dout_t, doc_start), None, end))
+    tiles = rows // TQ
+    positions = [block_number(count, slot) * rows for slot in (0, 1)]
+    exponentials(jobs, rows, heads, lambda job: positions[job // tiles], scores)
+
+
+def early_scores(count, prepared, near_1):
+    rows = near_1.shape[0] // 2
+    heads = prepared[1].shape[1] // rows
     wide = heads * TQ
-    kept = jax.ShapeDtypeStruct((sum(Window(rows).early) * CHUNK, wide), jnp.bfloat16)
-    return pl.pallas_call(
-        functools.partial(early_kernel, rows, heads, count, slot),
-        out_shape=(kept, kept, jax.ShapeDtypeStruct((24, wide), jnp.float32)),
-        in_specs=[VMEM] * 5,
-        out_specs=[VMEM] * 3,
+    out_shape = []
+    for slot in (0, 1):
+        kept = (sum(Window(rows, slot).early) * CHUNK, wide)
+        out_shape += [jax.ShapeDtypeStruct(kept, jnp.bfloat16)] * 2
+        out_shape.append(jax.ShapeDtypeStruct((24, wide), jnp.float32))
+    return pl.pallas_call(
+        functools.partial(early_kernel, rows, heads, count),
+        out_shape=out_shape,
+        in_specs=[VMEM] * 9,
+        out_specs=[VMEM] * 6,
         scratch_shapes=[pltpu.VMEM((2, 2 * rows + TQ, wide), jnp.float32)],
         compiler_params=pltpu.CompilerParams(vmem_limit_bytes=VMEM_LIMIT),
         cost_estimate=pl.CostEstimate(flops=0, bytes_accessed=0, transcendentals=0),
-        name="early_far" if slot == 0 else "early_near",
-    )(*ready, prev1)
+        name="early_scores",
+    )(near_1, *prepared)
 
 
 def scaled_by(array, tile, factor):
@@ -287,10 +284,10 @@
         dscores[out, :] = weights[place, :] * (dprobs[place, :] - delta)
 
 
-def add_products(step, columns, products):
+def add_products(new, columns, products):
     for total_ref, side, terms in products:
         term = dot_nt(side, terms)
-        if step == 0:
+        if new:
             total_ref[:, columns] = term
         else:
             total_ref[:, columns] += term
@@ -305,24 +302,27 @@
     dout_t,
     doc_start,
     early_stats,
+    prev1,
     prev2,
     weights,
+    dprobs,
     dscores,
     stats,
     prev2_out,
     scores,
-    dprobs,
     dk,
     dv,
 ):
     wide = heads * TQ
-    window = Window(rows)
+    window = Window(rows, slot)
+    position = block_number(count, slot) * rows
     jobs = []
     for step in window.steps:
         chunks = []
         for chunk in range(window.late[step]):
+            row = step * TQ + chunk * CHUNK
             kept = chunk_rows(window.late, step, chunk, 1)
-            chunks.append((chunk, prev2, step * TQ + chunk * CHUNK, weights, dprobs, kept))
+            chunks.append((chunk, (prev2, prev1)[row // rows], row % rows, weights, dprobs, kept))
 
         def end(row_max, total, delta, step=step):
             tile = slice(step * wide, (step + 1) * wide)
@@ -333,101 +333,113 @@
             delta = delta * late_factor + early[2] * early_factor
             for kind, value in enumerate((late_factor, early_factor, delta)):
                 stats[8 * kind + step : 8 * kind + step + 1, :] = value
-            there = chunk_rows(window.late, step)
-            dscore_rows(dscores, there, weights, dprobs, there, delta.astype(jnp.bfloat16))
+            kept = chunk_rows(window.late, step, 0, window.first[step])
+            there = chunk_rows(window.first, step)
+            dscore_rows(dscores, there, weights, dprobs, kept, delta.astype(jnp.bfloat16))
             add_products(
-                step,
+                step == 0,
                 slice(step * TQ, rows),
                 (
-                    (dv, scaled_by(dout_t, tile, late_factor), weights[there, :]),
+                    (dv, scaled_by(dout_t, tile, late_factor), weights[kept, :]),
                     (dk, scaled_by(query_t, tile, late_factor), dscores[there, :]),
                 ),
             )
 
         first_max = early_stats[step : step + 1, :]
         jobs.append((step, chunks, (query_t, dout_t, doc_start), first_max, end))
-    exponentials(jobs, rows, heads, block_number(count, slot) * rows, scores)
+    exponentials(jobs, rows, heads, lambda job: position, scores)
     prev2_out[0:HD] = (dk[...] * SCALE).astype(prev2_out.dtype)
     prev2_out[HD : 2 * HD] = dv[...].astype(prev2_out.dtype)
 
 
-def late_scores(slot, count, ready, early, prev2):
+def late_scores(slot, count, ready, early, prev1, prev2):
     rows = prev2.shape[0] // 2
     heads = ready[1].shape[1] // rows
     wide = heads * TQ
-    late = (sum(Window(rows).late) * CHUNK, wide)
+    window = Window(rows, slot)
+    late = jax.ShapeDtypeStruct((sum(window.late) * CHUNK, wide), jnp.bfloat16)
     return pl.pallas_call(
         functools.partial(late_kernel, rows, heads, count, slot),
         out_shape=(
-            jax.ShapeDtypeStruct(late, jnp.bfloat16),
-            jax.ShapeDtypeStruct(late, jnp.bfloat16),
+            late,
+            late,
+            jax.ShapeDtypeStruct((sum(window.first) * CHUNK, wide), jnp.bfloat16),
             jax.ShapeDtypeStruct((24, wide), jnp.float32),
             jax.ShapeDtypeStruct((2 * HD, rows), jnp.bfloat16),
         ),
-        in_specs=[VMEM] * 5,
-        out_specs=[VMEM] * 4,
+        in_specs=[VMEM] * 6,
+        out_specs=[VMEM] * 5,
         scratch_shapes=[
-            pltpu.VMEM((2, rows, wide), jnp.float32),
-            pltpu.VMEM(late, jnp.bfloat16),
+            pltpu.VMEM((2, 2 * rows, wide), jnp.float32),
             pltpu.VMEM((HD, rows), jnp.float32),
             pltpu.VMEM((HD, rows), jnp.float32),
         ],
         compiler_params=pltpu.CompilerParams(vmem_limit_bytes=VMEM_LIMIT),
         cost_estimate=pl.CostEstimate(flops=2**31, bytes_accessed=0, transcendentals=0),
         name="late_far" if slot == 0 else "late_near",
-    )(*ready[1:4], early[2], prev2)
-
-
-def grads_kernel(
-    rows, heads, query_t, dout_t, weights, dprobs, stats, dscores, prev1_out, own_out, dk, dv
-):
+    )(*ready[1:4], early[2], prev1, prev2)
+
+
+def grads_kernel(rows, heads, slot, query_t, dout_t, stats, *refs):
+    (late_w, late_dprobs, early_w, early_dprobs) = refs[0:4] if slot == 0 else (None, None) + refs[0:2]
+    (dscores, prev1_out, own_out, dk, dv) = refs[4:] if slot == 0 else refs[2:]
     wide = heads * TQ
-    window = Window(rows)
+    window = Window(rows, slot)
     for step in reversed(window.steps):
         tile = slice(step * wide, (step + 1) * wide)
-        factor = stats[8 + step : 8 + step + 1, :]
-        delta = stats[16 + step : 16 + step + 1, :].astype(jnp.bfloat16)
-        there = chunk_rows(window.early, step)
-        dscore_rows(dscores, there, weights, dprobs, there, delta)
-        add_products(
-            window.tiles - 1 - step,
-            slice(0, window.early[step] * CHUNK),
-            (
-                (dv, scaled_by(dout_t, tile, factor), weights[there, :]),
-                (dk, scaled_by(query_t, tile, factor), dscores[there, :]),
-            ),
+        late_factor, early_factor, delta = (
+            stats[8 * kind + step : 8 * kind + step + 1, :] for kind in range(3)
         )
+        beyond = window.late[step] - window.first[step]
+        parts = [(beyond, early_w, early_dprobs, chunk_rows(window.early, step), early_factor)]
+        if beyond:
+            kept = chunk_rows(window.late, step, window.first[step])
+            parts.append((0, late_w, late_dprobs, kept, late_factor))
+        for start, weights, dprobs, kept, factor in parts:
+            length = (kept.stop - kept.start) // CHUNK
+            there = chunk_rows(window.rest, step, start, length)
+            dscore_rows(dscores, there, weights, dprobs, kept, delta.astype(jnp.bfloat16))
+            add_products(
+                step == window.tiles - 1,
+                slice(start * CHUNK, (start + length) * CHUNK),
+                (
+                    (dv, scaled_by(dout_t, tile, factor), weights[kept, :]),
+                    (dk, scaled_by(query_t, tile, factor), dscores[there, :]),
+                ),
+            )
     prev1_out[0:HD] = (dk[:, 0:rows] * SCALE).astype(prev1_out.dtype)
     prev1_out[HD : 2 * HD] = dv[:, 0:rows].astype(prev1_out.dtype)
     own_out[0:HD] = dk[:, rows : 2 * rows] * SCALE
     own_out[HD : 2 * HD] = dv[:, rows : 2 * rows]
 
 
-def early_grads(slot, ready, early, stats):
+def rest_grads(slot, ready, early, late):
     rows = ready[0].shape[0] // 2
     heads = ready[1].shape[1] // rows
-    return pl.pallas_call(
-        functools.partial(grads_kernel, rows, heads),
+    rest = (sum(Window(rows, slot).rest) * CHUNK, heads * TQ)
+    operands = (*ready[1:3], late[3], *(late[0:2] if slot == 0 else ()), *early[0:2])
+    return pl.pallas_call(
+        functools.partial(grads_kernel, rows, heads, slot),
         out_shape=(
-            jax.ShapeDtypeStruct(early[0].shape, jnp.bfloat16),
+            jax.ShapeDtypeStruct(rest, jnp.bfloat16),
             jax.ShapeDtypeStruct((2 * HD, rows), jnp.bfloat16),
             jax.ShapeDtypeStruct((2 * HD, rows), jnp.float32),
         ),
-        in_specs=[VMEM] * 5,
+        in_specs=[VMEM] * len(operands),
         out_specs=[VMEM] * 3,
         scratch_shapes=[pltpu.VMEM((HD, 2 * rows), jnp.float32)] * 2,
         compiler_params=pltpu.CompilerParams(vmem_limit_bytes=VMEM_LIMIT),
-        cost_estimate=pl.CostEstimate(flops=2**31, bytes_accessed=0, transcendentals=0),
+        cost_estimate=pl.CostEstimate(flops=2**31 if slot else 0, bytes_accessed=0, transcendentals=0),
         name="grads_far" if slot == 0 else "grads_near",
-    )(*ready[1:3], *early[0:2], stats)
+    )(*operands)
 
 
 def outputs_kernel(rows, heads, *refs):
     blocks = (refs[0:8], refs[8:16])
     (attended, grad_query, keys_t, values_t) = refs[16:]
-    window = Window(rows)
     for slot, block in enumerate(blocks):
-        (own_kv, prev1, prev2, early_w, early_d, late_w, late_d, stats) = block
+        (own_kv, prev1, prev2, early_w, rest_d, late_w, first_d, stats) = block
+        window = Window(rows, slot)
         own_rows = half_start(rows, slot)
         for place, source in enumerate((prev2, prev1, own_kv)):
             for tile in range(rows // TQ):
@@ -436,20 +448,24 @@
                 keys_t[:, part] = jnp.transpose(source[row : row + TQ, :])
                 values_t[:, part] = jnp.transpose(source[rows + row : rows + row + TQ, :])
         for step in window.steps:
-            late_columns = slice(step * TQ, rows)
-            early_columns = slice(rows, 2 * rows + (step + 1) * TQ)
-            late_rows = chunk_rows(window.late, step)
-            early_rows = chunk_rows(window.early, step)
+            first, late = window.first[step], window.late[step]
+
+            def product(side, terms, counts, start, skip, length):
+                columns = slice(step * TQ + start * CHUNK, step * TQ + (start + length) * CHUNK)
+                return dot_nn(side[:, columns], terms[chunk_rows(counts, step, skip, length), :])
+
+            early = window.chunks - late
+            late_factor = stats[step : step + 1, :]
+            early_factor = stats[8 + step : 8 + step + 1, :]
+            attended_t = product(values_t, late_w, window.late, 0, 0, late) * late_factor
+            attended_t += product(values_t, early_w, window.early, late, 0, early) * early_factor
+            late_t = product(keys_t, first_d, window.first, 0, 0, first)
+            if late > first:
+                late_t += product(keys_t, rest_d, window.rest, first, 0, late - first)
+            early_t = product(keys_t, rest_d, window.rest, late, late - first, early)
+            grad_query_t = late_t * (late_factor * SCALE) + early_t * (early_factor * SCALE)
             place = pl.ds(own_rows + step * TQ, TQ)
-            for out, side, late, early, scale in (
-                (attended, values_t, late_w, early_w, 1.0),
-                (grad_query, keys_t, late_d, early_d, SCALE),
-            ):
-                found = dot_nn(side[:, late_columns], late[late_rows, :]) * (
-                    stats[step : step + 1, :] * scale
-                ) + dot_nn(side[:, early_columns], early[early_rows, :]) * (
-                    stats[8 + step : 8 + step + 1, :] * scale
-                )
+            for out, found in ((attended, attended_t), (grad_query, grad_query_t)):
                 for h in range(heads):
                     part = found[:, h * TQ : (h + 1) * TQ]
                     out[place, h * HD : (h + 1) * HD] = jnp.transpose(part).astype(out.dtype)
@@ -466,15 +482,14 @@
         out_specs=[VMEM] * 2,
         scratch_shapes=[pltpu.VMEM((HD, 3 * rows), jnp.bfloat16)] * 2,
         compiler_params=pltpu.CompilerParams(vmem_limit_bytes=VMEM_LIMIT),
-        cost_estimate=pl.CostEstimate(flops=2**30, bytes_accessed=0, transcendentals=0),
+        cost_estimate=pl.CostEstimate(flops=0, bytes_accessed=0, transcendentals=0),
         name="block_outputs",
     )(*far, *near)
 
 
-def total_kernel(rows, far_own, far_1, far_2, near_own, near_1, grad_key, grad_value):
+def total_kernel(rows, far_own, far_1, far_2, near, grad_key, grad_value):
     far = far_own[...] + far_1[...].astype(jnp.float32) + far_2[...].astype(jnp.float32)
-    near = near_own[...] + near_1[...].astype(jnp.float32)
-    for slot, total in ((0, far), (1, near)):
+    for slot, total in ((0, far), (1, near[...])):
         place = pl.ds(half_start(rows, slot), rows)
         grad_key[place, :] = jnp.transpose(total[0:HD]).astype(grad_key.dtype)
         grad_value[place, :] = jnp.transpose(total[HD : 2 * HD]).astype(grad_value.dtype)
@@ -486,7 +501,7 @@
     return pl.pallas_call(
         functools.partial(total_kernel, rows),
         out_shape=(shape, shape),
-        in_specs=[VMEM] * 5,
+        in_specs=[VMEM] * 4,
         out_specs=[VMEM] * 2,
         compiler_params=pltpu.CompilerParams(vmem_limit_bytes=VMEM_LIMIT),
         name="total_grads",
@@ -515,26 +530,29 @@
     far_2 = move(far_kv, far_on)
     prepared = prepare(count, doc_lengths, query, d_out, key, value)
     far_ready, near_ready = prepared[0:4], prepared[4:8]
-    near_early = early_scores(1, count, near_ready, near_1)
-    far_1, near_early = lax.optimization_barrier((far_1, near_early))
+    far_early, near_early = (lambda found: (found[0:3], found[3:6]))(
+        early_scores(count, prepared, near_1)
+    )
+    far_late = late_scores(0, count, far_ready, far_early, far_1, far_2)
+    from_far_2 = move(far_late[4], far_back)
+    far_1, far_stats = lax.optimization_barrier((far_1, far_late[3]))
     near_2 = move(far_1, swap)
-    far_early = early_scores(0, count, far_ready, far_1)
-
-    far_w, far_d, far_stats, far_g2 = late_scores(0, count, far_ready, far_early, far_2)
-    from_far_2 = move(far_g2, far_back)
-    far_early_d, far_g1, far_own = early_grads(0, far_ready, far_early, far_stats)
+    near_2, far_early = lax.optimization_barrier((near_2, far_early))
+    far_rest_d, far_g1, far_own = rest_grads(0, far_ready, far_early, far_late)
     relayed = move(far_g1, swap)
-    near_w, near_d, near_stats, near_g2 = late_scores(1, count, near_ready, near_early, near_2)
-    near_sum = (near_g2.astype(jnp.float32) + relayed.astype(jnp.float32)).astype(jnp.bfloat16)
+    near_late = late_scores(1, count, near_ready, near_early, near_1, near_2)
+    near_sum = near_late[4].astype(jnp.float32) + relayed.astype(jnp.float32)
+    near_sum, from_far_2 = lax.optimization_barrier((near_sum.astype(jnp.bfloat16), from_far_2))
     from_near_2 = move(near_sum, near_back)
-    near_early_d, near_g1, near_own = early_grads(1, near_ready, near_early, near_stats)
+    near_rest_d, near_g1, near_own = rest_grads(1, near_ready, near_early, near_late)
     from_near_1 = move(near_g1, swap)
     attended, grad_query = block_outputs(
         query,
-        (far_ready[0], far_1, far_2, far_early[0], far_early_d, far_w, far_d, far_stats),
-        (near_ready[0], near_1, near_2, near_early[0], near_early_d, near_w, near_d, near_stats),
+        (far_ready[0], far_1, far_2, far_early[0], far_rest_d, far_late[0], *far_late[2:4]),
+        (near_ready[0], near_1, near_2, near_early[0], near_rest_d, near_late[0], *near_late[2:4]),
     )
-    grad_key, grad_value = total_grads(far_own, from_near_1, from_far_2, near_own, from_near_2)
+    near_total = near_own + from_near_2.astype(jnp.float32)
+    grad_key, grad_value = total_grads(far_own, from_near_1, from_far_2, near_total)
     return (attended, grad_query, grad_key, grad_value)
 
 

time: 38.9 us -> 38.9 us (level)
  starting transfers between devices: 17.9 us -> 15.9 us
  waiting for transfers between devices: 2.27 us -> 3.57 us
  Pallas kernels: 17.7 us -> 18.2 us
    ppermute x8, starting transfers between devices: 17.9 us -> 15.9 us  [move(): return lax.ppermute(array, 'ctx', pairs)]
    pallas_call x2, Pallas kernels: 3.49 us -> 5.17 us  [late_scores(): pl.pallas_call(functools.partial(late_kernel, rows, heads, count, slot),...]
    ppermute x8, waiting for transfers between devices: 2.27 us -> 3.57 us  [move(): return lax.ppermute(array, 'ctx', pairs)]
    pallas_call x4 -> x3, Pallas kernels: 6.3 us -> 5.15 us  [the longest x2 2.7 us: rest_grads(): pl.pallas_call(functools.partial(grads_kernel, rows, heads, slot), out_sh...]
  transfers between devices with their start and end apart: 8 -> 8, of which waited for: 1 -> 3; matrix products, arithmetic and copies ran while one was open for 0% -> 0% of each run, Pallas kernels for 39% -> 33%
where the time goes in v9:
time: 38.9 us; the launch traced here: 38.6 us
  Pallas kernels  18.2 us (47%)
  starting transfers between devices  15.9 us (41%)
  waiting for transfers between devices  3.57 us (9%)
  between operations  0.76 us (2%)
    ppermute x8, starting transfers between devices, move(): return lax.ppermute(array, 'ctx', pairs)  15.9 us
    pallas_call x2, Pallas kernels, late_scores(): pl.pallas_call(functools.partial(late_kernel, rows, heads, count, slot),...  5.17 us
    ppermute x8, waiting for transfers between devices, move(): return lax.ppermute(array, 'ctx', pairs)  3.57 us
    pallas_call x1, Pallas kernels, block_outputs(): pl.pallas_call(functools.partial(outputs_kernel, rows, heads), out_shape=...  3.07 us
    pallas_call x2, Pallas kernels, rest_grads(): pl.pallas_call(functools.partial(grads_kernel, rows, heads, slot), out_sh...  2.7 us
    pallas_call x1, Pallas kernels, early_scores(): pl.pallas_call(functools.partial(early_kernel, rows, heads, count), out_s...  2.44 us
    pallas_call x1, Pallas kernels, prepare(): pl.pallas_call(functools.partial(prepare_kernel, rows, heads, doc_lengths...  2.11 us
    pallas_call x1, Pallas kernels, pack_blocks(): pl.pallas_call(functools.partial(pack_kernel, rows), out_shape=(shape, sh...  1.82 us
  transfers between devices with their start and end apart: 8, of which 3 were waited for; matrix products, arithmetic and copies ran while one was open for 0% of the time, Pallas kernels for 33%

profile of v9, /device:TPU:0, one launch (start us, length us, event | category | flops | bytes accessed | tf_op | source)
XLA Modules:
  0.0 38.6 jit_solution(7920031254810680418)
XLA Ops:
  0.6 1.8 %pack_blocks.1 = (bf16[768,128]{1,0:T(8,128)(2,1)}, bf16[768,128]{1,0:T(8,128)(2,1)}) custom-call(bf16[768,128]{1,0:T(8,128)(2,1)} %key.1, bf16[768,128]{1,0:T(8,128)(2,1)} %value.1), custom_call_target="tpu_custom_call" | custom-call | tf_op jit(solution)/shard_map/pack_blocks/pallas_call | solution.py:71
  2.5 0.5 %collective-permute-start.1 = (bf16[768,128]{1,0:T(8,128)(2,1)}, bf16[768,128]{1,0:T(8,128)(2,1)S(1)}, u32[]{:S(2)}, u32[]{:S(2)}) collective-permute-start(bf16[768,128]{1,0:T(8,128)(2,1)} %get-tuple-element.50), channel_id=1, source_target_pairs={{0,1},{1,0},{2,3},{3,2},{4,5},{5,4},{6,7},{7,6},{8,9},{9,8},{10,11... | collective-permute-start | bytes 589832 | tf_op jit(solution)/shard_map/ppermute | solution.py:518
  3.0 0.7 %collective-permute-start = (bf16[768,128]{1,0:T(8,128)(2,1)}, bf16[768,128]{1,0:T(8,128)(2,1)S(1)}, u32[]{:S(2)}, u32[]{:S(2)}) collective-permute-start(bf16[768,128]{1,0:T(8,128)(2,1)} %get-tuple-element.46), channel_id=1, source_target_pairs={{1,2},{3,4},{5,6},{7,8},{9,10},{11,12},{13,14},{15,15},{14,13},{12... | collective-permute-start | bytes 589832 | tf_op jit(solution)/shard_map/ppermute | solution.py:518
  3.6 5.7 %collective-permute-start.2 = (bf16[768,128]{1,0:T(8,128)(2,1)}, bf16[768,128]{1,0:T(8,128)(2,1)S(1)}, u32[]{:S(2)}, u32[]{:S(2)}) collective-permute-start(bf16[768,128]{1,0:T(8,128)(2,1)} %get-tuple-element.50), channel_id=1, source_target_pairs={{0,2},{2,4},{4,6},{6,8},{8,10},{10,12},{12,14},{14,15},{15,13},{13... | collective-permute-start | bytes 589832 | tf_op jit(solution)/shard_map/ppermute | solution.py:518
  9.4 2.1 %prepare.1 = (bf16[768,128]{1,0:T(8,128)(2,1)S(1)}, bf16[128,1536]{1,0:T(8,128)(2,1)S(1)}, bf16[128,1536]{1,0:T(8,128)(2,1)S(1)}, s32[8,128]{1,0:T(8,128)S(1)}, ...) custom-call(s32[32]{0:T(128)} %refs_0_.1, ...), custom_call_target="tpu_custom_call" | custom-call | bytes 4194304 | tf_op jit(solution)/shard_map/prepare/pallas_call | solution.py:128
  11.5 0.0 collective-permute-done.1.near_1.prev1.refs_9_
  11.5 2.4 %early_scores.1 = (bf16[768,512]{1,0:T(8,128)(2,1)S(1)}, bf16[768,512]{1,0:T(8,128)(2,1)S(1)}, f32[24,512]{1,0:T(8,128)S(1)}, bf16[1920,512]{1,0:T(8,128)(2,1)S(...) custom-call(bf16[768,128]{1,0:T(8,128)(2,1)S(1)} %collective-permute-done.1.near_1.prev1.refs_9_, ...), custom_call_target="tpu_custom_call" | custom-call | tf_op jit(solution)/shard_map/early_scores/pallas_call | solution.py:263
  13.9 0.0 collective-permute-done.prev1.refs_1_
  13.9 2.7 %collective-permute-done.2.prev2.refs_2_ = bf16[768,128]{1,0:T(8,128)(2,1)S(1)} collective-permute-done((bf16[768,128]{1,0:T(8,128)(2,1)}, bf16[768,128]{1,0:T(8,128)(2,1)S(1)}, u32[]{:S(2)}, u32[]{:S(2)}) %collective-permute-start.2) | collective-permute-done | bytes 196640 | tf_op jit(solution)/shard_map/ppermute | solution.py:518
  16.7 2.8 %late_far.1 = (bf16[1920,512]{1,0:T(8,128)(2,1)S(1)}, bf16[1920,512]{1,0:T(8,128)(2,1)S(1)}, bf16[768,512]{1,0:T(8,128)(2,1)S(1)}, f32[24,512]{1,0:T(8,128)S(1)}, bf16[256,384]{1,0:T(8,128)(2,1)S(1)}) custom-call(bf16[128,1536]{1,0:T(8,128)(2,1)S(1)} %get-tuple-element.47.refs_1_.query_t, bf16[128,1536]{1,0:T(8,128)(2,1)S(1)} %get-tuple-element.48.refs_2_.dout_t, ...), custom_call_target="tpu_custom_call" | custom-call | flops 2147483648 | tf_op jit(solution)/shard_map/late_far/pallas_call | solution.py:361
  19.4 0.1 collective-permute-start.3
  19.5 1.3 %collective-permute-start.6 = (bf16[256,384]{1,0:T(8,128)(2,1)S(1)}, bf16[256,384]{1,0:T(8,128)(2,1)S(1)}, u32[]{:S(2)}, u32[]{:S(2)}) collective-permute-start(bf16[256,384]{1,0:T(8,128)(2,1)S(1)} %get-tuple-element.80), channel_id=1, source_target_pairs={{2,0},{4,2},{6,4},{8,6},{10,8},{12,10},{14,12},{15,14},{13,15},{11... | collective-permute-start | bytes 589832 | tf_op jit(solution)/shard_map/ppermute | solution.py:518
  20.8 0.1 collective-permute-done.3.prev2.refs_10_
  20.9 1.3 %grads_far.1 = (bf16[1920,512]{1,0:T(8,128)(2,1)S(1)}, bf16[256,384]{1,0:T(8,128)(2,1)S(1)}, f32[256,384]{1,0:T(8,128)S(1)}) custom-call(bf16[128,1536]{1,0:T(8,128)(2,1)S(1)} %get-tuple-element.47.refs_1_.query_t, bf16[128,1536]{1,0:T(8,128)(2,1)S(1)} %get-tuple-element.48.refs_2_.dout_t, f32[24,512]{1,0:T(8,128)S(1)} %get-tuple-element.56.stats.refs_7_, ...), custom_call_target="tpu_custom_call" | custom-call | tf_op jit(solution)/shard_map/grads_far/pallas_call | solution.py:421
  22.3 3.2 %collective-permute-start.5 = (bf16[256,384]{1,0:T(8,128)(2,1)S(1)}, bf16[256,384]{1,0:T(8,128)(2,1)S(1)}, u32[]{:S(2)}, u32[]{:S(2)}) collective-permute-start(bf16[256,384]{1,0:T(8,128)(2,1)S(1)} %get-tuple-element.79), channel_id=1, source_target_pairs={{0,1},{1,0},{2,3},{3,2},{4,5},{5,4},{6,7},{7,6},{8,9},{9,8},{10,11... | collective-permute-start | bytes 589832 | tf_op jit(solution)/shard_map/ppermute | solution.py:518
  25.4 2.4 %late_near.1 = (bf16[768,512]{1,0:T(8,128)(2,1)S(1)}, bf16[768,512]{1,0:T(8,128)(2,1)}, bf16[768,512]{1,0:T(8,128)(2,1)S(1)}, f32[24,512]{1,0:T(8,128)S(1)}, bf16[256,384]{1,0:T(8,128)(2,1)S(1)}) custom-call(bf16[128,1536]{1,0:T(8,128)(2,1)S(1)} %get-tuple-element.52.refs_5_.query_t, bf16[128,1536]{1,0:T(8,128)(2,1)S(1)} %get-tuple-element.53.refs_6_.dout_t, ...), custom_call_target="tpu_custom_call" | custom-call | flops 2147483648 | tf_op jit(solution)/shard_map/late_near/pallas_call | solution.py:361
  27.8 0.0 collective-permute-done.5
  27.8 0.1 add_convert_fusion
  27.9 0.0 collective-permute-done.6.far_2
  27.9 4.5 %collective-permute-start.7 = (bf16[256,384]{1,0:T(8,128)(2,1)S(1)}, bf16[256,384]{1,0:T(8,128)(2,1)S(1)}, u32[]{:S(2)}, u32[]{:S(2)}) collective-permute-start(bf16[256,384]{1,0:T(8,128)(2,1)S(1)} %add_convert_fusion), channel_id=1, source_target_pairs={{3,1},{5,3},{7,5},{9,7},{11,9},{13,11},{15,13},{14,15},{12,14},{10... | collective-permute-start | bytes 589832 | tf_op jit(solution)/shard_map/ppermute | solution.py:518
  32.4 1.4 %grads_near.1 = (bf16[1920,512]{1,0:T(8,128)(2,1)S(1)}, bf16[256,384]{1,0:T(8,128)(2,1)S(1)}, f32[256,384]{1,0:T(8,128)S(1)}) custom-call(bf16[128,1536]{1,0:T(8,128)(2,1)S(1)} %get-tuple-element.52.refs_5_.query_t, bf16[128,1536]{1,0:T(8,128)(2,1)S(1)} %get-tuple-element.53.refs_6_.dout_t, f32[24,512]{1,0:T(8,128)S(1)} %get-tuple-element.69.stats.refs_15_, ...), custom_call_target="tpu_custom_call" | custom-call | flops 2147483648 | tf_op jit(solution)/shard_map/grads_near/pallas_call | solution.py:421
  33.8 0.1 collective-permute-start.4
  33.8 3.1 %block_outputs.1 = (bf16[768,512]{1,0:T(8,128)(2,1)}, bf16[768,512]{1,0:T(8,128)(2,1)}) custom-call(bf16[768,128]{1,0:T(8,128)(2,1)S(1)} %get-tuple-element.45.refs_0_, bf16[768,128]{1,0:T(8,128)(2,1)S(1)} %collective-permute-done.prev1.refs_1_, bf16[768,128]{1,0:T(8,128)(2,1)S(1)} %collective-permute-done.2.prev2.refs_2_, ...), custom_call_target="tpu_custom_call" | custom-call | tf_op jit(solution)/shard_map/block_outputs/pallas_call | solution.py:478
  36.9 0.7 %collective-permute-done.7 = bf16[256,384]{1,0:T(8,128)(2,1)S(1)} collective-permute-done((bf16[256,384]{1,0:T(8,128)(2,1)S(1)}, bf16[256,384]{1,0:T(8,128)(2,1)S(1)}, u32[]{:S(2)}, u32[]{:S(2)}) %collective-permute-start.7) | collective-permute-done | bytes 196640 | tf_op jit(solution)/shard_map/ppermute | solution.py:518
  37.7 0.0 collective-permute-done.4.far_1
  37.7 0.9 %total_grads.1 = (bf16[768,128]{1,0:T(8,128)(2,1)}, bf16[768,128]{1,0:T(8,128)(2,1)}) custom-call(f32[256,384]{1,0:T(8,128)S(1)} %get-tuple-element.76.far_own, bf16[256,384]{1,0:T(8,128)(2,1)S(1)} %collective-permute-done.4.far_1, bf16[256,384]{1,0:T(8,128)(2,1)S(1)} %collective-permute-done.6.far_2, f32[256,384]{1,0:T(8,128)S(1)} %convert_add_fusion.near), custom_call_target="tpu_custom_call" | custom-call | tf_op jit(solution)/shard_map/total_grads/pallas_call | solution.py:501
  (1 shorter events, 0.0 us)
Async XLA Ops:
  2.5 9.0 %collective-permute-start.1 = (bf16[768,128]{1,0:T(8,128)(2,1)}, bf16[768,128]{1,0:T(8,128)(2,1)S(1)}, u32[]{:S(2)}, u32[]{:S(2)}) collective-permute-start(bf16[768,128]{1,0:T(8,128)(2,1)} %get-tuple-element.50), channel_id=1, source_target_pairs={{0,1},{1,0},{2,3},{3,2},{4,5},{5,4},{6,7},{7,6},{8,9},{9,8},{10,11... | collective-permute-start | bytes 589832 | tf_op jit(solution)/shard_map/ppermute | solution.py:518
  3.0 11.0 %collective-permute-start = (bf16[768,128]{1,0:T(8,128)(2,1)}, bf16[768,128]{1,0:T(8,128)(2,1)S(1)}, u32[]{:S(2)}, u32[]{:S(2)}) collective-permute-start(bf16[768,128]{1,0:T(8,128)(2,1)} %get-tuple-element.46), channel_id=1, source_target_pairs={{1,2},{3,4},{5,6},{7,8},{9,10},{11,12},{13,14},{15,15},{14,13},{12... | collective-permute-start | bytes 589832 | tf_op jit(solution)/shard_map/ppermute | solution.py:518
  3.6 13.0 %collective-permute-start.2 = (bf16[768,128]{1,0:T(8,128)(2,1)}, bf16[768,128]{1,0:T(8,128)(2,1)S(1)}, u32[]{:S(2)}, u32[]{:S(2)}) collective-permute-start(bf16[768,128]{1,0:T(8,128)(2,1)} %get-tuple-element.50), channel_id=1, source_target_pairs={{0,2},{2,4},{4,6},{6,8},{8,10},{10,12},{12,14},{14,15},{15,13},{13... | collective-permute-start | bytes 589832 | tf_op jit(solution)/shard_map/ppermute | solution.py:518
  19.4 1.5 %collective-permute-start.3 = (bf16[768,128]{1,0:T(8,128)(2,1)S(1)}, bf16[768,128]{1,0:T(8,128)(2,1)S(1)}, u32[]{:S(2)}, u32[]{:S(2)}) collective-permute-start(bf16[768,128]{1,0:T(8,128)(2,1)S(1)} %collective-permute-done.prev1.refs_1_), channel_id=1, source_target_pairs={{0,1},{1,0},{2,3},{3,2},{4,5},{5,4},{6,7},{7,6},{8,9},{9,8},{10,11... | collective-permute-start | bytes 589832 | tf_op jit(solution)/shard_map/ppermute | solution.py:518
  19.5 8.4 %collective-permute-start.6 = (bf16[256,384]{1,0:T(8,128)(2,1)S(1)}, bf16[256,384]{1,0:T(8,128)(2,1)S(1)}, u32[]{:S(2)}, u32[]{:S(2)}) collective-permute-start(bf16[256,384]{1,0:T(8,128)(2,1)S(1)} %get-tuple-element.80), channel_id=1, source_target_pairs={{2,0},{4,2},{6,4},{8,6},{10,8},{12,10},{14,12},{15,14},{13,15},{11... | collective-permute-start | bytes 589832 | tf_op jit(solution)/shard_map/ppermute | solution.py:518
  22.3 5.6 %collective-permute-start.5 = (bf16[256,384]{1,0:T(8,128)(2,1)S(1)}, bf16[256,384]{1,0:T(8,128)(2,1)S(1)}, u32[]{:S(2)}, u32[]{:S(2)}) collective-permute-start(bf16[256,384]{1,0:T(8,128)(2,1)S(1)} %get-tuple-element.79), channel_id=1, source_target_pairs={{0,1},{1,0},{2,3},{3,2},{4,5},{5,4},{6,7},{7,6},{8,9},{9,8},{10,11... | collective-permute-start | bytes 589832 | tf_op jit(solution)/shard_map/ppermute | solution.py:518
  27.9 9.7 %collective-permute-start.7 = (bf16[256,384]{1,0:T(8,128)(2,1)S(1)}, bf16[256,384]{1,0:T(8,128)(2,1)S(1)}, u32[]{:S(2)}, u32[]{:S(2)}) collective-permute-start(bf16[256,384]{1,0:T(8,128)(2,1)S(1)} %add_convert_fusion), channel_id=1, source_target_pairs={{3,1},{5,3},{7,5},{9,7},{11,9},{13,11},{15,13},{14,15},{12,14},{10... | collective-permute-start | bytes 589832 | tf_op jit(solution)/shard_map/ppermute | solution.py:518
  33.8 3.9 %collective-permute-start.4 = (bf16[256,384]{1,0:T(8,128)(2,1)S(1)}, bf16[256,384]{1,0:T(8,128)(2,1)S(1)}, u32[]{:S(2)}, u32[]{:S(2)}) collective-permute-start(bf16[256,384]{1,0:T(8,128)(2,1)S(1)} %get-tuple-element.77), channel_id=1, source_target_pairs={{0,1},{1,0},{2,3},{3,2},{4,5},{5,4},{6,7},{7,6},{8,9},{9,8},{10,11... | collective-permute-start | bytes 589832 | tf_op jit(solution)/shard_map/ppermute | solution.py:518

commit v10 on v9

--- a/solution.py
+++ b/solution.py
@@ -305,14 +305,9 @@
     prev1,
     prev2,
     weights,
-    dprobs,
-    dscores,
-    stats,
-    prev2_out,
-    scores,
-    dk,
-    dv,
+    *refs,
 ):
+    (dprobs, dscores, stats, prev2_out, scores, dk, dv) = refs if slot == 0 else refs[-1:] + refs[:-1]
     wide = heads * TQ
     window = Window(rows, slot)
     position = block_number(count, slot) * rows
@@ -361,18 +356,18 @@
     return pl.pallas_call(
         functools.partial(late_kernel, rows, heads, count, slot),
         out_shape=(
-            late,
-            late,
+            *([late] * (2 - slot)),
             jax.ShapeDtypeStruct((sum(window.first) * CHUNK, wide), jnp.bfloat16),
             jax.ShapeDtypeStruct((24, wide), jnp.float32),
             jax.ShapeDtypeStruct((2 * HD, rows), jnp.bfloat16),
         ),
         in_specs=[VMEM] * 6,
-        out_specs=[VMEM] * 5,
+        out_specs=[VMEM] * (5 - slot),
         scratch_shapes=[
-            pltpu.VMEM((2, 2 * rows, wide), jnp.float32),
+            pltpu.VMEM((2, max(window.late) * CHUNK, wide), jnp.float32),
             pltpu.VMEM((HD, rows), jnp.float32),
             pltpu.VMEM((HD, rows), jnp.float32),
+            *([pltpu.VMEM(late.shape, late.dtype)] * slot),
         ],
         compiler_params=pltpu.CompilerParams(vmem_limit_bytes=VMEM_LIMIT),
         cost_estimate=pl.CostEstimate(flops=2**31, bytes_accessed=0, transcendentals=0),
@@ -417,7 +412,7 @@
     rows = ready[0].shape[0] // 2
     heads = ready[1].shape[1] // rows
     rest = (sum(Window(rows, slot).rest) * CHUNK, heads * TQ)
-    operands = (*ready[1:3], late[3], *(late[0:2] if slot == 0 else ()), *early[0:2])
+    operands = (*ready[1:3], late[-2], *(late[0:2] if slot == 0 else ()), *early[0:2])
     return pl.pallas_call(
         functools.partial(grads_kernel, rows, heads, slot),
         out_shape=(
@@ -534,22 +529,22 @@
         early_scores(count, prepared, near_1)
     )
     far_late = late_scores(0, count, far_ready, far_early, far_1, far_2)
-    from_far_2 = move(far_late[4], far_back)
-    far_1, far_stats = lax.optimization_barrier((far_1, far_late[3]))
+    from_far_2 = move(far_late[-1], far_back)
+    far_1, far_stats = lax.optimization_barrier((far_1, far_late[-2]))
     near_2 = move(far_1, swap)
     near_2, far_early = lax.optimization_barrier((near_2, far_early))
     far_rest_d, far_g1, far_own = rest_grads(0, far_ready, far_early, far_late)
     relayed = move(far_g1, swap)
     near_late = late_scores(1, count, near_ready, near_early, near_1, near_2)
-    near_sum = near_late[4].astype(jnp.float32) + relayed.astype(jnp.float32)
-    near_sum, from_far_2 = lax.optimization_barrier((near_sum.astype(jnp.bfloat16), from_far_2))
-    from_near_2 = move(near_sum, near_back)
+    near_sum = near_late[-1].astype(jnp.float32) + relayed.astype(jnp.float32)
+    from_near_2 = move(near_sum.astype(jnp.bfloat16), near_back)
     near_rest_d, near_g1, near_own = rest_grads(1, near_ready, near_early, near_late)
+    near_g1, from_far_2 = lax.optimization_barrier((near_g1, from_far_2))
     from_near_1 = move(near_g1, swap)
     attended, grad_query = block_outputs(
         query,
-        (far_ready[0], far_1, far_2, far_early[0], far_rest_d, far_late[0], *far_late[2:4]),
-        (near_ready[0], near_1, near_2, near_early[0], near_rest_d, near_late[0], *near_late[2:4]),
+        (far_ready[0], far_1, far_2, far_early[0], far_rest_d, far_late[0], *far_late[-3:-1]),
+        (near_ready[0], near_1, near_2, near_early[0], near_rest_d, near_late[0], *near_late[-3:-1]),
     )
     near_total = near_own + from_near_2.astype(jnp.float32)
     grad_key, grad_value = total_grads(far_own, from_near_1, from_far_2, near_total)

time: 38.9 us -> 37.1 us (0.954)
  starting transfers between devices: 15.9 us -> 14.9 us
  Pallas kernels: 18.2 us -> 17.6 us
    ppermute x8, starting transfers between devices: 15.9 us -> 14.9 us  [move(): return lax.ppermute(array, 'ctx', pairs)]
    pallas_call x2, Pallas kernels: 5.17 us -> 4.49 us  [late_scores(): pl.pallas_call(functools.partial(late_kernel, rows, heads, count, slot),...]
where the time goes in v10:
time: 37.1 us; the launch traced here: 36.8 us
  Pallas kernels  17.6 us (47%)
  starting transfers between devices  14.9 us (40%)
  waiting for transfers between devices  3.51 us (9%)
  between operations  0.77 us (2%)
    ppermute x8, starting transfers between devices, move(): return lax.ppermute(array, 'ctx', pairs)  14.9 us
    pallas_call x2, Pallas kernels, late_scores(): pl.pallas_call(functools.partial(late_kernel, rows, heads, count, slot),...  4.49 us
    ppermute x8, waiting for transfers between devices, move(): return lax.ppermute(array, 'ctx', pairs)  3.51 us
    pallas_call x1, Pallas kernels, block_outputs(): pl.pallas_call(functools.partial(outputs_kernel, rows, heads), out_shape=...  3.07 us
    pallas_call x2, Pallas kernels, rest_grads(): pl.pallas_call(functools.partial(grads_kernel, rows, heads, slot), out_sh...  2.71 us
    pallas_call x1, Pallas kernels, early_scores(): pl.pallas_call(functools.partial(early_kernel, rows, heads, count), out_s...  2.44 us
    pallas_call x1, Pallas kernels, prepare(): pl.pallas_call(functools.partial(prepare_kernel, rows, heads, doc_lengths...  2.11 us
    pallas_call x1, Pallas kernels, pack_blocks(): pl.pallas_call(functools.partial(pack_kernel, rows), out_shape=(shape, sh...  1.82 us
  transfers between devices with their start and end apart: 8, of which 3 were waited for; matrix products, arithmetic and copies ran while one was open for 0% of the time, Pallas kernels for 33%

profile of v10, /device:TPU:0, one launch (start us, length us, event | category | flops | bytes accessed | tf_op | source)
XLA Modules:
  0.0 36.8 jit_solution(6346527884218523525)
XLA Ops:
  0.6 1.8 %pack_blocks.1 = (bf16[768,128]{1,0:T(8,128)(2,1)}, bf16[768,128]{1,0:T(8,128)(2,1)}) custom-call(bf16[768,128]{1,0:T(8,128)(2,1)} %key.1, bf16[768,128]{1,0:T(8,128)(2,1)} %value.1), custom_call_target="tpu_custom_call" | custom-call | tf_op jit(solution)/shard_map/pack_blocks/pallas_call | solution.py:71
  2.5 0.5 %collective-permute-start.1 = (bf16[768,128]{1,0:T(8,128)(2,1)}, bf16[768,128]{1,0:T(8,128)(2,1)S(1)}, u32[]{:S(2)}, u32[]{:S(2)}) collective-permute-start(bf16[768,128]{1,0:T(8,128)(2,1)} %get-tuple-element.50), channel_id=1, source_target_pairs={{0,1},{1,0},{2,3},{3,2},{4,5},{5,4},{6,7},{7,6},{8,9},{9,8},{10,11... | collective-permute-start | bytes 589832 | tf_op jit(solution)/shard_map/ppermute | solution.py:513
  3.0 0.7 %collective-permute-start = (bf16[768,128]{1,0:T(8,128)(2,1)}, bf16[768,128]{1,0:T(8,128)(2,1)S(1)}, u32[]{:S(2)}, u32[]{:S(2)}) collective-permute-start(bf16[768,128]{1,0:T(8,128)(2,1)} %get-tuple-element.46), channel_id=1, source_target_pairs={{1,2},{3,4},{5,6},{7,8},{9,10},{11,12},{13,14},{15,15},{14,13},{12... | collective-permute-start | bytes 589832 | tf_op jit(solution)/shard_map/ppermute | solution.py:513
  3.6 5.7 %collective-permute-start.2 = (bf16[768,128]{1,0:T(8,128)(2,1)}, bf16[768,128]{1,0:T(8,128)(2,1)S(1)}, u32[]{:S(2)}, u32[]{:S(2)}) collective-permute-start(bf16[768,128]{1,0:T(8,128)(2,1)} %get-tuple-element.50), channel_id=1, source_target_pairs={{0,2},{2,4},{4,6},{6,8},{8,10},{10,12},{12,14},{14,15},{15,13},{13... | collective-permute-start | bytes 589832 | tf_op jit(solution)/shard_map/ppermute | solution.py:513
  9.4 2.1 %prepare.1 = (bf16[768,128]{1,0:T(8,128)(2,1)S(1)}, bf16[128,1536]{1,0:T(8,128)(2,1)S(1)}, bf16[128,1536]{1,0:T(8,128)(2,1)S(1)}, s32[8,128]{1,0:T(8,128)S(1)}, ...) custom-call(s32[32]{0:T(128)} %refs_0_.1, ...), custom_call_target="tpu_custom_call" | custom-call | bytes 4194304 | tf_op jit(solution)/shard_map/prepare/pallas_call | solution.py:128
  11.5 0.0 collective-permute-done.1.near_1.prev1.refs_9_
  11.5 2.4 %early_scores.1 = (bf16[768,512]{1,0:T(8,128)(2,1)S(1)}, bf16[768,512]{1,0:T(8,128)(2,1)S(1)}, f32[24,512]{1,0:T(8,128)S(1)}, bf16[1920,512]{1,0:T(8,128)(2,1)S(...) custom-call(bf16[768,128]{1,0:T(8,128)(2,1)S(1)} %collective-permute-done.1.near_1.prev1.refs_9_, ...), custom_call_target="tpu_custom_call" | custom-call | tf_op jit(solution)/shard_map/early_scores/pallas_call | solution.py:263
  13.9 0.0 collective-permute-done.prev1.refs_1_
  13.9 2.7 %collective-permute-done.2.prev2.refs_2_ = bf16[768,128]{1,0:T(8,128)(2,1)S(1)} collective-permute-done((bf16[768,128]{1,0:T(8,128)(2,1)}, bf16[768,128]{1,0:T(8,128)(2,1)S(1)}, u32[]{:S(2)}, u32[]{:S(2)}) %collective-permute-start.2) | collective-permute-done | bytes 196640 | tf_op jit(solution)/shard_map/ppermute | solution.py:513
  16.7 2.8 %late_far.1 = (bf16[1920,512]{1,0:T(8,128)(2,1)S(1)}, bf16[1920,512]{1,0:T(8,128)(2,1)S(1)}, bf16[768,512]{1,0:T(8,128)(2,1)S(1)}, f32[24,512]{1,0:T(8,128)S(1)}, bf16[256,384]{1,0:T(8,128)(2,1)S(1)}) custom-call(bf16[128,1536]{1,0:T(8,128)(2,1)S(1)} %get-tuple-element.47.refs_1_.query_t, bf16[128,1536]{1,0:T(8,128)(2,1)S(1)} %get-tuple-element.48.refs_2_.dout_t, ...), custom_call_target="tpu_custom_call" | custom-call | flops 2147483648 | tf_op jit(solution)/shard_map/late_far/pallas_call | solution.py:356
  19.4 0.1 collective-permute-start.3
  19.5 1.3 %collective-permute-start.4 = (bf16[256,384]{1,0:T(8,128)(2,1)S(1)}, bf16[256,384]{1,0:T(8,128)(2,1)S(1)}, u32[]{:S(2)}, u32[]{:S(2)}) collective-permute-start(bf16[256,384]{1,0:T(8,128)(2,1)S(1)} %get-tuple-element.78), channel_id=1, source_target_pairs={{2,0},{4,2},{6,4},{8,6},{10,8},{12,10},{14,12},{15,14},{13,15},{11... | collective-permute-start | bytes 589832 | tf_op jit(solution)/shard_map/ppermute | solution.py:513
  20.8 0.1 collective-permute-done.3.prev2.refs_10_
  20.9 1.3 %grads_far.1 = (bf16[1920,512]{1,0:T(8,128)(2,1)S(1)}, bf16[256,384]{1,0:T(8,128)(2,1)S(1)}, f32[256,384]{1,0:T(8,128)S(1)}) custom-call(bf16[128,1536]{1,0:T(8,128)(2,1)S(1)} %get-tuple-element.47.refs_1_.query_t, bf16[128,1536]{1,0:T(8,128)(2,1)S(1)} %get-tuple-element.48.refs_2_.dout_t, f32[24,512]{1,0:T(8,128)S(1)} %get-tuple-element.56.stats.refs_7_, ...), custom_call_target="tpu_custom_call" | custom-call | tf_op jit(solution)/shard_map/grads_far/pallas_call | solution.py:416
  22.3 3.2 %collective-permute-start.6 = (bf16[256,384]{1,0:T(8,128)(2,1)S(1)}, bf16[256,384]{1,0:T(8,128)(2,1)S(1)}, u32[]{:S(2)}, u32[]{:S(2)}) collective-permute-start(bf16[256,384]{1,0:T(8,128)(2,1)S(1)} %get-tuple-element.83), channel_id=1, source_target_pairs={{0,1},{1,0},{2,3},{3,2},{4,5},{5,4},{6,7},{7,6},{8,9},{9,8},{10,11... | collective-permute-start | bytes 589832 | tf_op jit(solution)/shard_map/ppermute | solution.py:513
  25.4 1.7 %late_near.1 = (bf16[768,512]{1,0:T(8,128)(2,1)S(1)}, bf16[768,512]{1,0:T(8,128)(2,1)S(1)}, f32[24,512]{1,0:T(8,128)S(1)}, bf16[256,384]{1,0:T(8,128)(2,1)S(1)}) custom-call(bf16[128,1536]{1,0:T(8,128)(2,1)S(1)} %get-tuple-element.52.refs_5_.query_t, bf16[128,1536]{1,0:T(8,128)(2,1)S(1)} %get-tuple-element.53.refs_6_.dout_t, ...), custom_call_target="tpu_custom_call" | custom-call | flops 2147483648 | tf_op jit(solution)/shard_map/late_near/pallas_call | solution.py:356
  27.1 0.0 collective-permute-done.6
  27.1 0.1 add_convert_fusion
  27.2 3.4 %collective-permute-start.7 = (bf16[256,384]{1,0:T(8,128)(2,1)S(1)}, bf16[256,384]{1,0:T(8,128)(2,1)S(1)}, u32[]{:S(2)}, u32[]{:S(2)}) collective-permute-start(bf16[256,384]{1,0:T(8,128)(2,1)S(1)} %add_convert_fusion), channel_id=1, source_target_pairs={{3,1},{5,3},{7,5},{9,7},{11,9},{13,11},{15,13},{14,15},{12,14},{10... | collective-permute-start | bytes 589832 | tf_op jit(solution)/shard_map/ppermute | solution.py:513
  30.6 1.4 %grads_near.1 = (bf16[1920,512]{1,0:T(8,128)(2,1)S(1)}, bf16[256,384]{1,0:T(8,128)(2,1)S(1)}, f32[256,384]{1,0:T(8,128)S(1)}) custom-call(bf16[128,1536]{1,0:T(8,128)(2,1)S(1)} %get-tuple-element.52.refs_5_.query_t, bf16[128,1536]{1,0:T(8,128)(2,1)S(1)} %get-tuple-element.53.refs_6_.dout_t, f32[24,512]{1,0:T(8,128)S(1)} %get-tuple-element.69.stats.refs_15_, ...), custom_call_target="tpu_custom_call" | custom-call | flops 2147483648 | tf_op jit(solution)/shard_map/grads_near/pallas_call | solution.py:416
  32.0 0.0 collective-permute-done.4.far_2
  32.1 0.1 collective-permute-start.5
  32.1 3.1 %block_outputs.1 = (bf16[768,512]{1,0:T(8,128)(2,1)}, bf16[768,512]{1,0:T(8,128)(2,1)}) custom-call(bf16[768,128]{1,0:T(8,128)(2,1)S(1)} %get-tuple-element.45.refs_0_, bf16[768,128]{1,0:T(8,128)(2,1)S(1)} %collective-permute-done.prev1.refs_1_, bf16[768,128]{1,0:T(8,128)(2,1)S(1)} %collective-permute-done.2.prev2.refs_2_, ...), custom_call_target="tpu_custom_call" | custom-call | tf_op jit(solution)/shard_map/block_outputs/pallas_call | solution.py:473
  35.2 0.7 %collective-permute-done.7 = bf16[256,384]{1,0:T(8,128)(2,1)S(1)} collective-permute-done((bf16[256,384]{1,0:T(8,128)(2,1)S(1)}, bf16[256,384]{1,0:T(8,128)(2,1)S(1)}, u32[]{:S(2)}, u32[]{:S(2)}) %collective-permute-start.7) | collective-permute-done | bytes 196640 | tf_op jit(solution)/shard_map/ppermute | solution.py:513
  35.9 0.0 collective-permute-done.5.far_1
  35.9 0.9 %total_grads.1 = (bf16[768,128]{1,0:T(8,128)(2,1)}, bf16[768,128]{1,0:T(8,128)(2,1)}) custom-call(f32[256,384]{1,0:T(8,128)S(1)} %get-tuple-element.76.far_own, bf16[256,384]{1,0:T(8,128)(2,1)S(1)} %collective-permute-done.5.far_1, bf16[256,384]{1,0:T(8,128)(2,1)S(1)} %collective-permute-done.4.far_2, f32[256,384]{1,0:T(8,128)S(1)} %convert_add_fusion.near), custom_call_target="tpu_custom_call" | custom-call | tf_op jit(solution)/shard_map/total_grads/pallas_call | solution.py:496
  (1 shorter events, 0.0 us)
Async XLA Ops:
  2.5 9.0 %collective-permute-start.1 = (bf16[768,128]{1,0:T(8,128)(2,1)}, bf16[768,128]{1,0:T(8,128)(2,1)S(1)}, u32[]{:S(2)}, u32[]{:S(2)}) collective-permute-start(bf16[768,128]{1,0:T(8,128)(2,1)} %get-tuple-element.50), channel_id=1, source_target_pairs={{0,1},{1,0},{2,3},{3,2},{4,5},{5,4},{6,7},{7,6},{8,9},{9,8},{10,11... | collective-permute-start | bytes 589832 | tf_op jit(solution)/shard_map/ppermute | solution.py:513
  3.0 11.0 %collective-permute-start = (bf16[768,128]{1,0:T(8,128)(2,1)}, bf16[768,128]{1,0:T(8,128)(2,1)S(1)}, u32[]{:S(2)}, u32[]{:S(2)}) collective-permute-start(bf16[768,128]{1,0:T(8,128)(2,1)} %get-tuple-element.46), channel_id=1, source_target_pairs={{1,2},{3,4},{5,6},{7,8},{9,10},{11,12},{13,14},{15,15},{14,13},{12... | collective-permute-start | bytes 589832 | tf_op jit(solution)/shard_map/ppermute | solution.py:513
  3.6 13.0 %collective-permute-start.2 = (bf16[768,128]{1,0:T(8,128)(2,1)}, bf16[768,128]{1,0:T(8,128)(2,1)S(1)}, u32[]{:S(2)}, u32[]{:S(2)}) collective-permute-start(bf16[768,128]{1,0:T(8,128)(2,1)} %get-tuple-element.50), channel_id=1, source_target_pairs={{0,2},{2,4},{4,6},{6,8},{8,10},{10,12},{12,14},{14,15},{15,13},{13... | collective-permute-start | bytes 589832 | tf_op jit(solution)/shard_map/ppermute | solution.py:513
  19.4 1.5 %collective-permute-start.3 = (bf16[768,128]{1,0:T(8,128)(2,1)S(1)}, bf16[768,128]{1,0:T(8,128)(2,1)S(1)}, u32[]{:S(2)}, u32[]{:S(2)}) collective-permute-start(bf16[768,128]{1,0:T(8,128)(2,1)S(1)} %collective-permute-done.prev1.refs_1_), channel_id=1, source_target_pairs={{0,1},{1,0},{2,3},{3,2},{4,5},{5,4},{6,7},{7,6},{8,9},{9,8},{10,11... | collective-permute-start | bytes 589832 | tf_op jit(solution)/shard_map/ppermute | solution.py:513
  19.5 12.5 %collective-permute-start.4 = (bf16[256,384]{1,0:T(8,128)(2,1)S(1)}, bf16[256,384]{1,0:T(8,128)(2,1)S(1)}, u32[]{:S(2)}, u32[]{:S(2)}) collective-permute-start(bf16[256,384]{1,0:T(8,128)(2,1)S(1)} %get-tuple-element.78), channel_id=1, source_target_pairs={{2,0},{4,2},{6,4},{8,6},{10,8},{12,10},{14,12},{15,14},{13,15},{11... | collective-permute-start | bytes 589832 | tf_op jit(solution)/shard_map/ppermute | solution.py:513
  22.3 4.9 %collective-permute-start.6 = (bf16[256,384]{1,0:T(8,128)(2,1)S(1)}, bf16[256,384]{1,0:T(8,128)(2,1)S(1)}, u32[]{:S(2)}, u32[]{:S(2)}) collective-permute-start(bf16[256,384]{1,0:T(8,128)(2,1)S(1)} %get-tuple-element.83), channel_id=1, source_target_pairs={{0,1},{1,0},{2,3},{3,2},{4,5},{5,4},{6,7},{7,6},{8,9},{9,8},{10,11... | collective-permute-start | bytes 589832 | tf_op jit(solution)/shard_map/ppermute | solution.py:513
  27.2 8.7 %collective-permute-start.7 = (bf16[256,384]{1,0:T(8,128)(2,1)S(1)}, bf16[256,384]{1,0:T(8,128)(2,1)S(1)}, u32[]{:S(2)}, u32[]{:S(2)}) collective-permute-start(bf16[256,384]{1,0:T(8,128)(2,1)S(1)} %add_convert_fusion), channel_id=1, source_target_pairs={{3,1},{5,3},{7,5},{9,7},{11,9},{13,11},{15,13},{14,15},{12,14},{10... | collective-permute-start | bytes 589832 | tf_op jit(solution)/shard_map/ppermute | solution.py:513
  32.1 3.9 %collective-permute-start.5 = (bf16[256,384]{1,0:T(8,128)(2,1)S(1)}, bf16[256,384]{1,0:T(8,128)(2,1)S(1)}, u32[]{:S(2)}, u32[]{:S(2)}) collective-permute-start(bf16[256,384]{1,0:T(8,128)(2,1)S(1)} %get-tuple-element.79), channel_id=1, source_target_pairs={{0,1},{1,0},{2,3},{3,2},{4,5},{5,4},{6,7},{7,6},{8,9},{9,8},{10,11... | collective-permute-start | bytes 589832 | tf_op jit(solution)/shard_map/ppermute | solution.py:513

commit v11 on v10

--- a/solution.py
+++ b/solution.py
@@ -58,42 +58,21 @@
         copy.wait()
 
 
-def pack_kernel(rows, key, value, near_out, far_out, sems):
-    run_copies(
-        load_block(rows, 1, key, value, near_out, sems)
-        + load_block(rows, 0, key, value, far_out, sems)
-    )
-
-
-def pack_blocks(key, value):
-    rows = key.shape[0] // 2
-    shape = jax.ShapeDtypeStruct((2 * rows, HD), key.dtype)
-    return pl.pallas_call(
-        functools.partial(pack_kernel, rows),
-        out_shape=(shape, shape),
-        in_specs=[HBM] * 2,
-        out_specs=[VMEM] * 2,
-        scratch_shapes=[pltpu.SemaphoreType.DMA((4,))],
-        name="pack_blocks",
-    )(in_hbm(key), in_hbm(value))
-
-
 def prepare_kernel(rows, heads, docs, count, *refs):
-    (doc_hbm, query_hbm, dout_hbm, key, value) = refs[0:5]
+    (far_kv, near_kv, doc_hbm, query_hbm, dout_hbm) = refs[0:5]
     (doc_lengths, query, dout, sems) = refs[13:]
     refs = refs[5:13]
     wide = heads * TQ
     run_copies(
         [
-            pltpu.make_async_copy(query_hbm, query, sems.at[4]),
-            pltpu.make_async_copy(dout_hbm, dout, sems.at[5]),
-            pltpu.make_async_copy(doc_hbm, doc_lengths, sems.at[6]),
+            pltpu.make_async_copy(query_hbm, query, sems.at[0]),
+            pltpu.make_async_copy(dout_hbm, dout, sems.at[1]),
+            pltpu.make_async_copy(doc_hbm, doc_lengths, sems.at[2]),
         ]
-        + load_block(rows, 0, key, value, refs[0], sems)
-        + load_block(rows, 1, key, value, refs[4], sems)
     )
     for slot in (0, 1):
-        _, query_t, dout_t, doc_start = refs[4 * slot : 4 * slot + 4]
+        own_kv, query_t, dout_t, doc_start = refs[4 * slot : 4 * slot + 4]
+        own_kv[...] = (far_kv, near_kv)[slot][...]
         own_rows = half_start(rows, slot)
         for step in range(rows // TQ):
             source = pl.ds(own_rows + step * TQ, TQ)
@@ -119,27 +98,27 @@
         doc_start[...] = found
 
 
-def prepare(count, doc_lengths, query, dout, key, value):
+def prepare(count, doc_lengths, query, dout, far_kv, near_kv):
     rows = query.shape[0] // 2
     heads = query.shape[1] // HD
-    pair = jax.ShapeDtypeStruct((2 * rows, HD), key.dtype)
+    pair = jax.ShapeDtypeStruct(far_kv.shape, far_kv.dtype)
     stacked_t = jax.ShapeDtypeStruct((HD, rows * heads), query.dtype)
     starts = jax.ShapeDtypeStruct((8, TQ), jnp.int32)
     return pl.pallas_call(
         functools.partial(prepare_kernel, rows, heads, doc_lengths.shape[0], count),
         out_shape=(pair, stacked_t, stacked_t, starts) * 2,
-        in_specs=[HBM] * 5,
+        in_specs=[VMEM] * 2 + [HBM] * 3,
         out_specs=[VMEM] * 8,
         scratch_shapes=[
             pltpu.SMEM(doc_lengths.shape, doc_lengths.dtype),
             pltpu.VMEM(query.shape, query.dtype),
             pltpu.VMEM(dout.shape, dout.dtype),
-            pltpu.SemaphoreType.DMA((7,)),
+            pltpu.SemaphoreType.DMA((3,)),
         ],
         compiler_params=pltpu.CompilerParams(vmem_limit_bytes=VMEM_LIMIT),
         cost_estimate=pl.CostEstimate(flops=0, bytes_accessed=4 * 2**20, transcendentals=0),
         name="prepare",
-    )(*(in_hbm(array) for array in (doc_lengths, query, dout, key, value)))
+    )(far_kv, near_kv, *(in_hbm(array) for array in (doc_lengths, query, dout)))
 
 
 class Window:
@@ -225,51 +204,44 @@
         )
 
 
-def early_kernel(rows, heads, count, near_1, *refs):
-    inputs, outs, scores = (refs[0:4], refs[4:8]), (refs[8:11], refs[11:14]), refs[14]
+def early_kernel(rows, heads, count, slot, own_kv, query_t, dout_t, doc_start, *refs):
+    (weights, dprobs, stats, scores) = refs[-4:]
+    prev1 = refs[0] if slot == 1 else None
+    window = Window(rows, slot)
+    position = block_number(count, slot) * rows
     jobs = []
-    for slot in (0, 1):
-        window = Window(rows, slot)
-        own_kv, query_t, dout_t, doc_start = inputs[slot]
-        weights, dprobs, stats = outs[slot]
-        for step in window.steps:
-            chunks = []
-            for index in range(window.early[step]):
-                chunk = window.late[step] + index
-                row = step * TQ + chunk * CHUNK
-                keys = own_kv if row >= 2 * rows else near_1
-                kept = chunk_rows(window.early, step, index, 1)
-                chunks.append((chunk, keys, row % rows, weights, dprobs, kept))
-
-            def end(*found, stats=stats, step=step):
-                for kind, value in enumerate(found):
-                    stats[8 * kind + step : 8 * kind + step + 1, :] = value
-
-            jobs.append((step, chunks, (query_t, dout_t, doc_start), None, end))
-    tiles = rows // TQ
-    positions = [block_number(count, slot) * rows for slot in (0, 1)]
-    exponentials(jobs, rows, heads, lambda job: positions[job // tiles], scores)
-
-
-def early_scores(count, prepared, near_1):
-    rows = near_1.shape[0] // 2
-    heads = prepared[1].shape[1] // rows
+    for step in window.steps:
+        chunks = []
+        for index in range(window.early[step]):
+            chunk = window.late[step] + index
+            row = step * TQ + chunk * CHUNK
+            keys = own_kv if row >= 2 * rows else prev1
+            kept = chunk_rows(window.early, step, index, 1)
+            chunks.append((chunk, keys, row % rows, weights, dprobs, kept))
+
+        def end(*found, step=step):
+            for kind, value in enumerate(found):
+                stats[8 * kind + step : 8 * kind + step + 1, :] = value
+
+        jobs.append((step, chunks, (query_t, dout_t, doc_start), None, end))
+    exponentials(jobs, rows, heads, lambda job: position, scores)
+
+
+def early_scores(slot, count, ready, *prev1):
+    rows = ready[0].shape[0] // 2
+    heads = ready[1].shape[1] // rows
     wide = heads * TQ
-    out_shape = []
-    for slot in (0, 1):
-        kept = (sum(Window(rows, slot).early) * CHUNK, wide)
-        out_shape += [jax.ShapeDtypeStruct(kept, jnp.bfloat16)] * 2
-        out_shape.append(jax.ShapeDtypeStruct((24, wide), jnp.float32))
+    kept = jax.ShapeDtypeStruct((sum(Window(rows, slot).early) * CHUNK, wide), jnp.bfloat16)
     return pl.pallas_call(
-        functools.partial(early_kernel, rows, heads, count),
-        out_shape=out_shape,
-        in_specs=[VMEM] * 9,
-        out_specs=[VMEM] * 6,
+        functools.partial(early_kernel, rows, heads, count, slot),
+        out_shape=(kept, kept, jax.ShapeDtypeStruct((24, wide), jnp.float32)),
+        in_specs=[VMEM] * (4 + len(prev1)),
+        out_specs=[VMEM] * 3,
         scratch_shapes=[pltpu.VMEM((2, 2 * rows + TQ, wide), jnp.float32)],
         compiler_params=pltpu.CompilerParams(vmem_limit_bytes=VMEM_LIMIT),
-        cost_estimate=pl.CostEstimate(flops=0, bytes_accessed=0, transcendentals=0),
-        name="early_scores",
-    )(near_1, *prepared)
+        cost_estimate=pl.CostEstimate(flops=0 if slot else 2**33, bytes_accessed=0, transcendentals=0),
+        name="early_far" if slot == 0 else "early_near",
+    )(*ready, *prev1)
 
 
 def scaled_by(array, tile, factor):
@@ -519,15 +491,19 @@
     near_back = [(t, s) for s, t in near_on]
     far_back = [(t, s) for s, t in far_on]
 
-    near_kv, far_kv = pack_blocks(key, value)
+    rows = key.shape[0] // 2
+    odd = lax.axis_index("ctx") % 2 == 1
+    lower = jnp.concatenate([key[:rows], value[:rows]], axis=0)
+    upper = jnp.concatenate([key[rows:], value[rows:]], axis=0)
+    near_kv, far_kv = jnp.where(odd, lower, upper), jnp.where(odd, upper, lower)
     far_1 = move(near_kv, near_to_far)
-    near_1 = move(far_kv, swap)
     far_2 = move(far_kv, far_on)
-    prepared = prepare(count, doc_lengths, query, d_out, key, value)
+    prepared = prepare(count, doc_lengths, query, d_out, far_kv, near_kv)
     far_ready, near_ready = prepared[0:4], prepared[4:8]
-    far_early, near_early = (lambda found: (found[0:3], found[3:6]))(
-        early_scores(count, prepared, near_1)
-    )
+    near_1 = move(far_ready[0], swap)
+    far_early = early_scores(0, count, far_ready)
+    near_early = early_scores(1, count, near_ready, near_1)
+    far_1, near_early = lax.optimization_barrier((far_1, near_early))
     far_late = late_scores(0, count, far_ready, far_early, far_1, far_2)
     from_far_2 = move(far_late[-1], far_back)
     far_1, far_stats = lax.optimization_barrier((far_1, far_late[-2]))

time: 37.1 us -> 35.5 us (0.957)
  Pallas kernels: 17.6 us -> 15.7 us
  local copies, waits for them, and re-layouts: 0 us -> 1.06 us
  waiting for transfers between devices: 3.51 us -> 2.98 us
    pallas_call x2, Pallas kernels: 4.27 us -> 2.48 us  [early_scores(): pl.pallas_call(functools.partial(early_kernel, rows, heads, count, slot),...]
    slice x0 -> x1, local copies, waits for them, and re-layouts: none -> 1.06 us  [body(): upper = jnp.concatenate([key[rows:], value[rows:]], axis=0)]
    ppermute x8, waiting for transfers between devices: 3.51 us -> 2.98 us  [move(): return lax.ppermute(array, 'ctx', pairs)]
  transfers between devices with their start and end apart: 8 -> 8, of which waited for: 3 -> 4; matrix products, arithmetic and copies ran while one was open for 0% -> 0% of each run, Pallas kernels for 33% -> 34%
where the time goes in v11:
time: 35.5 us; the launch traced here: 35.3 us
  Pallas kernels  15.7 us (44%)
  starting transfers between devices  14.6 us (41%)
  waiting for transfers between devices  2.98 us (8%)
  local copies, waits for them, and re-layouts  1.06 us (3%)
  between operations  0.8 us (2%)
    ppermute x8, starting transfers between devices, move(): return lax.ppermute(array, 'ctx', pairs)  14.6 us
    pallas_call x2, Pallas kernels, late_scores(): pl.pallas_call(functools.partial(late_kernel, rows, heads, count, slot),...  4.48 us
    pallas_call x1, Pallas kernels, block_outputs(): pl.pallas_call(functools.partial(outputs_kernel, rows, heads), out_shape=...  3.07 us
    ppermute x8, waiting for transfers between devices, move(): return lax.ppermute(array, 'ctx', pairs)  2.98 us
    pallas_call x2, Pallas kernels, rest_grads(): pl.pallas_call(functools.partial(grads_kernel, rows, heads, slot), out_sh...  2.7 us
    pallas_call x2, Pallas kernels, early_scores(): pl.pallas_call(functools.partial(early_kernel, rows, heads, count, slot),...  2.48 us
    pallas_call x1, Pallas kernels, prepare(): pl.pallas_call(functools.partial(prepare_kernel, rows, heads, doc_lengths...  2.01 us
    slice x1, local copies, waits for them, and re-layouts, body(): upper = jnp.concatenate([key[rows:], value[rows:]], axis=0)  1.06 us
  transfers between devices with their start and end apart: 8, of which 4 were waited for; matrix products, arithmetic and copies ran while one was open for 0% of the time, Pallas kernels for 34%

profile of v11, /device:TPU:0, one launch (start us, length us, event | category | flops | bytes accessed | tf_op | source)
XLA Modules:
  0.0 35.3 jit_solution(11704704824737226636)
XLA Ops:
  0.6 1.1 %fusion = (bf16[384,128]{1,0:T(8,128)(2,1)S(1)}, bf16[384,128]{1,0:T(8,128)(2,1)S(1)}, bf16[384,128]{1,0:T(8,128)(2,1)S(1)}, bf16[384,128]{1,0:T(8,128)(2,1)S(1)}) fusion(bf16[768,128]{1,0:T(8,128)(2,1)} %param.6, bf16[768,128]{1,0:T(8,128)(2,1)} %param.7), kind=kLoop, calls=%fused_computation.6 | loop fusion | bytes 786432 | tf_op jit(solution)/shard_map/slice | solution.py:497
  1.7 0.1 broadcast_select_fusion
  1.8 0.7 %collective-permute-start = (bf16[768,128]{1,0:T(8,128)(2,1)S(1)}, bf16[768,128]{1,0:T(8,128)(2,1)S(1)}, u32[]{:S(2)}, u32[]{:S(2)}) collective-permute-start(bf16[768,128]{1,0:T(8,128)(2,1)S(1)} %get-tuple-element.90.refs_1_), channel_id=1, source_target_pairs={{1,2},{3,4},{5,6},{7,8},{9,10},{11,12},{13,14},{15,15},{14,13},{12... | collective-permute-start | bytes 589832 | tf_op jit(solution)/shard_map/ppermute | solution.py:485
  2.5 6.1 %collective-permute-start.2 = (bf16[768,128]{1,0:T(8,128)(2,1)S(1)}, bf16[768,128]{1,0:T(8,128)(2,1)S(1)}, u32[]{:S(2)}, u32[]{:S(2)}) collective-permute-start(bf16[768,128]{1,0:T(8,128)(2,1)S(1)} %get-tuple-element.91.refs_0_), channel_id=1, source_target_pairs={{0,2},{2,4},{4,6},{6,8},{8,10},{10,12},{12,14},{14,15},{15,13},{13... | collective-permute-start | bytes 589832 | tf_op jit(solution)/shard_map/ppermute | solution.py:485
  8.6 2.0 %prepare.1 = (bf16[768,128]{1,0:T(8,128)(2,1)S(1)}, bf16[128,1536]{1,0:T(8,128)(2,1)S(1)}, bf16[128,1536]{1,0:T(8,128)(2,1)S(1)}, s32[8,128]{1,0:T(8,128)S(1)}, ...) custom-call(bf16[768,128]{1,0:T(8,128)(2,1)S(1)} %get-tuple-element., ...), custom_call_target="tpu_custom_call" | custom-call | bytes 4194304 | tf_op jit(solution)/shard_map/prepare/pallas_call | solution.py:107
  10.6 0.1 collective-permute-start.1
  10.7 0.8 %early_far.1 = (bf16[768,512]{1,0:T(8,128)(2,1)S(1)}, bf16[768,512]{1,0:T(8,128)(2,1)S(1)}, f32[24,512]{1,0:T(8,128)S(1)}) custom-call(bf16[768,128]{1,0:T(8,128)(2,1)S(1)} %get-tuple-element.47.own_kv.refs_0_, bf16[128,1536]{1,0:T(8,128)(2,1)S(1)} %get-tuple-element.56.query_t, bf16[128,1536]{1,0:T(8,128)(2,1)S(1)} %get-tuple-element.57.dout_t, ...), custom_call_target="tpu_custom_call" | custom-call | flops 8589934592 | tf_op jit(solution)/shard_map/early_far/pallas_call | solution.py:235
  11.5 0.6 %collective-permute-done.1.refs_0_.prev1.refs_9_ = bf16[768,128]{1,0:T(8,128)(2,1)S(1)} collective-permute-done((bf16[768,128]{1,0:T(8,128)(2,1)S(1)}, bf16[768,128]{1,0:T(8,128)(2,1)S(1)}, u32[]{:S(2)}, u32[]{:S(2)}) %collective-permute-start.1) | collective-permute-done | bytes 196640 | tf_op jit(solution)/shard_map/ppermute | solution.py:485
  12.1 1.7 %early_near.1 = (bf16[1920,512]{1,0:T(8,128)(2,1)S(1)}, bf16[1920,512]{1,0:T(8,128)(2,1)S(1)}, f32[24,512]{1,0:T(8,128)S(1)}) custom-call(bf16[768,128]{1,0:T(8,128)(2,1)S(1)} %get-tuple-element.48.own_kv.refs_8_, bf16[128,1536]{1,0:T(8,128)(2,1)S(1)} %get-tuple-element.49.query_t, bf16[128,1536]{1,0:T(8,128)(2,1)S(1)} %get-tuple-element.50.dout_t, ...), custom_call_target="tpu_custom_call" | custom-call | tf_op jit(solution)/shard_map/early_near/pallas_call | solution.py:235
  13.9 0.0 collective-permute-done.prev1.refs_1_
  13.9 1.7 %collective-permute-done.2.prev2.refs_2_ = bf16[768,128]{1,0:T(8,128)(2,1)S(1)} collective-permute-done((bf16[768,128]{1,0:T(8,128)(2,1)S(1)}, bf16[768,128]{1,0:T(8,128)(2,1)S(1)}, u32[]{:S(2)}, u32[]{:S(2)}) %collective-permute-start.2) | collective-permute-done | bytes 196640 | tf_op jit(solution)/shard_map/ppermute | solution.py:485
  15.6 2.8 %late_far.1 = (bf16[1920,512]{1,0:T(8,128)(2,1)S(1)}, bf16[1920,512]{1,0:T(8,128)(2,1)S(1)}, bf16[768,512]{1,0:T(8,128)(2,1)S(1)}, f32[24,512]{1,0:T(8,128)S(1)}, bf16[256,384]{1,0:T(8,128)(2,1)S(1)}) custom-call(bf16[128,1536]{1,0:T(8,128)(2,1)S(1)} %get-tuple-element.56.query_t, bf16[128,1536]{1,0:T(8,128)(2,1)S(1)} %get-tuple-element.57.dout_t, ...), custom_call_target="tpu_custom_call" | custom-call | flops 2147483648 | tf_op jit(solution)/shard_map/late_far/pallas_call | solution.py:328
  18.4 0.1 collective-permute-start.3
  18.4 1.3 %collective-permute-start.4 = (bf16[256,384]{1,0:T(8,128)(2,1)S(1)}, bf16[256,384]{1,0:T(8,128)(2,1)S(1)}, u32[]{:S(2)}, u32[]{:S(2)}) collective-permute-start(bf16[256,384]{1,0:T(8,128)(2,1)S(1)} %get-tuple-element.82), channel_id=1, source_target_pairs={{2,0},{4,2},{6,4},{8,6},{10,8},{12,10},{14,12},{15,14},{13,15},{11... | collective-permute-start | bytes 589832 | tf_op jit(solution)/shard_map/ppermute | solution.py:485
  19.7 0.1 collective-permute-done.3.prev2.refs_10_
  19.9 1.3 %grads_far.1 = (bf16[1920,512]{1,0:T(8,128)(2,1)S(1)}, bf16[256,384]{1,0:T(8,128)(2,1)S(1)}, f32[256,384]{1,0:T(8,128)S(1)}) custom-call(bf16[128,1536]{1,0:T(8,128)(2,1)S(1)} %get-tuple-element.56.query_t, bf16[128,1536]{1,0:T(8,128)(2,1)S(1)} %get-tuple-element.57.dout_t, f32[24,512]{1,0:T(8,128)S(1)} %get-tuple-element.60.stats.refs_7_, ...), custom_call_target="tpu_custom_call" | custom-call | tf_op jit(solution)/shard_map/grads_far/pallas_call | solution.py:388
  21.2 3.3 %collective-permute-start.6 = (bf16[256,384]{1,0:T(8,128)(2,1)S(1)}, bf16[256,384]{1,0:T(8,128)(2,1)S(1)}, u32[]{:S(2)}, u32[]{:S(2)}) collective-permute-start(bf16[256,384]{1,0:T(8,128)(2,1)S(1)} %get-tuple-element.87), channel_id=1, source_target_pairs={{0,1},{1,0},{2,3},{3,2},{4,5},{5,4},{6,7},{7,6},{8,9},{9,8},{10,11... | collective-permute-start | bytes 589832 | tf_op jit(solution)/shard_map/ppermute | solution.py:485
  24.5 1.7 %late_near.1 = (bf16[768,512]{1,0:T(8,128)(2,1)S(1)}, bf16[768,512]{1,0:T(8,128)(2,1)S(1)}, f32[24,512]{1,0:T(8,128)S(1)}, bf16[256,384]{1,0:T(8,128)(2,1)S(1)}) custom-call(bf16[128,1536]{1,0:T(8,128)(2,1)S(1)} %get-tuple-element.49.query_t, bf16[128,1536]{1,0:T(8,128)(2,1)S(1)} %get-tuple-element.50.dout_t, s32[8,128]{1,0:T(8,128)S(1)} %get-tuple-element.51.doc_start, ...), custom_call_target="tpu_custom_call" | custom-call | flops 2147483648 | tf_op jit(solution)/shard_map/late_near/pallas_call | solution.py:328
  26.2 0.0 collective-permute-done.6
  26.2 0.1 add_convert_fusion
  26.3 3.0 %collective-permute-start.7 = (bf16[256,384]{1,0:T(8,128)(2,1)S(1)}, bf16[256,384]{1,0:T(8,128)(2,1)S(1)}, u32[]{:S(2)}, u32[]{:S(2)}) collective-permute-start(bf16[256,384]{1,0:T(8,128)(2,1)S(1)} %add_convert_fusion), channel_id=1, source_target_pairs={{3,1},{5,3},{7,5},{9,7},{11,9},{13,11},{15,13},{14,15},{12,14},{10... | collective-permute-start | bytes 589832 | tf_op jit(solution)/shard_map/ppermute | solution.py:485
  29.3 1.4 %grads_near.1 = (bf16[1920,512]{1,0:T(8,128)(2,1)S(1)}, bf16[256,384]{1,0:T(8,128)(2,1)S(1)}, f32[256,384]{1,0:T(8,128)S(1)}) custom-call(bf16[128,1536]{1,0:T(8,128)(2,1)S(1)} %get-tuple-element.49.query_t, bf16[128,1536]{1,0:T(8,128)(2,1)S(1)} %get-tuple-element.50.dout_t, f32[24,512]{1,0:T(8,128)S(1)} %get-tuple-element.73.stats.refs_15_, ...), custom_call_target="tpu_custom_call" | custom-call | flops 2147483648 | tf_op jit(solution)/shard_map/grads_near/pallas_call | solution.py:388
  30.7 0.0 collective-permute-done.4.far_2
  30.7 0.1 collective-permute-start.5
  30.8 3.1 %block_outputs.1 = (bf16[768,512]{1,0:T(8,128)(2,1)}, bf16[768,512]{1,0:T(8,128)(2,1)}) custom-call(bf16[768,128]{1,0:T(8,128)(2,1)S(1)} %get-tuple-element.47.own_kv.refs_0_, bf16[768,128]{1,0:T(8,128)(2,1)S(1)} %collective-permute-done.prev1.refs_1_, bf16[768,128]{1,0:T(8,128)(2,1)S(1)} %collective-permute-done.2.prev2.refs_2_, ...), custom_call_target="tpu_custom_call" | custom-call | tf_op jit(solution)/shard_map/block_outputs/pallas_call | solution.py:445
  33.8 0.5 %collective-permute-done.7 = bf16[256,384]{1,0:T(8,128)(2,1)S(1)} collective-permute-done((bf16[256,384]{1,0:T(8,128)(2,1)S(1)}, bf16[256,384]{1,0:T(8,128)(2,1)S(1)}, u32[]{:S(2)}, u32[]{:S(2)}) %collective-permute-start.7) | collective-permute-done | bytes 196640 | tf_op jit(solution)/shard_map/ppermute | solution.py:485
  34.3 0.0 collective-permute-done.5.far_1
  34.4 0.9 %total_grads.1 = (bf16[768,128]{1,0:T(8,128)(2,1)}, bf16[768,128]{1,0:T(8,128)(2,1)}) custom-call(f32[256,384]{1,0:T(8,128)S(1)} %get-tuple-element.80.far_own, bf16[256,384]{1,0:T(8,128)(2,1)S(1)} %collective-permute-done.5.far_1, bf16[256,384]{1,0:T(8,128)(2,1)S(1)} %collective-permute-done.4.far_2, f32[256,384]{1,0:T(8,128)S(1)} %convert_add_fusion.near), custom_call_target="tpu_custom_call" | custom-call | tf_op jit(solution)/shard_map/total_grads/pallas_call | solution.py:468
  (1 shorter events, 0.0 us)
Async XLA Ops:
  1.8 12.1 %collective-permute-start = (bf16[768,128]{1,0:T(8,128)(2,1)S(1)}, bf16[768,128]{1,0:T(8,128)(2,1)S(1)}, u32[]{:S(2)}, u32[]{:S(2)}) collective-permute-start(bf16[768,128]{1,0:T(8,128)(2,1)S(1)} %get-tuple-element.90.refs_1_), channel_id=1, source_target_pairs={{1,2},{3,4},{5,6},{7,8},{9,10},{11,12},{13,14},{15,15},{14,13},{12... | collective-permute-start | bytes 589832 | tf_op jit(solution)/shard_map/ppermute | solution.py:485
  2.5 13.1 %collective-permute-start.2 = (bf16[768,128]{1,0:T(8,128)(2,1)S(1)}, bf16[768,128]{1,0:T(8,128)(2,1)S(1)}, u32[]{:S(2)}, u32[]{:S(2)}) collective-permute-start(bf16[768,128]{1,0:T(8,128)(2,1)S(1)} %get-tuple-element.91.refs_0_), channel_id=1, source_target_pairs={{0,2},{2,4},{4,6},{6,8},{8,10},{10,12},{12,14},{14,15},{15,13},{13... | collective-permute-start | bytes 589832 | tf_op jit(solution)/shard_map/ppermute | solution.py:485
  10.6 1.5 %collective-permute-start.1 = (bf16[768,128]{1,0:T(8,128)(2,1)S(1)}, bf16[768,128]{1,0:T(8,128)(2,1)S(1)}, u32[]{:S(2)}, u32[]{:S(2)}) collective-permute-start(bf16[768,128]{1,0:T(8,128)(2,1)S(1)} %get-tuple-element.47.own_kv.refs_0_), channel_id=1, source_target_pairs={{0,1},{1,0},{2,3},{3,2},{4,5},{5,4},{6,7},{7,6},{8,9},{9,8},{10,11... | collective-permute-start | bytes 589832 | tf_op jit(solution)/shard_map/ppermute | solution.py:485
  18.4 1.5 %collective-permute-start.3 = (bf16[768,128]{1,0:T(8,128)(2,1)S(1)}, bf16[768,128]{1,0:T(8,128)(2,1)S(1)}, u32[]{:S(2)}, u32[]{:S(2)}) collective-permute-start(bf16[768,128]{1,0:T(8,128)(2,1)S(1)} %collective-permute-done.prev1.refs_1_), channel_id=1, source_target_pairs={{0,1},{1,0},{2,3},{3,2},{4,5},{5,4},{6,7},{7,6},{8,9},{9,8},{10,11... | collective-permute-start | bytes 589832 | tf_op jit(solution)/shard_map/ppermute | solution.py:485
  18.4 12.2 %collective-permute-start.4 = (bf16[256,384]{1,0:T(8,128)(2,1)S(1)}, bf16[256,384]{1,0:T(8,128)(2,1)S(1)}, u32[]{:S(2)}, u32[]{:S(2)}) collective-permute-start(bf16[256,384]{1,0:T(8,128)(2,1)S(1)} %get-tuple-element.82), channel_id=1, source_target_pairs={{2,0},{4,2},{6,4},{8,6},{10,8},{12,10},{14,12},{15,14},{13,15},{11... | collective-permute-start | bytes 589832 | tf_op jit(solution)/shard_map/ppermute | solution.py:485
  21.2 5.0 %collective-permute-start.6 = (bf16[256,384]{1,0:T(8,128)(2,1)S(1)}, bf16[256,384]{1,0:T(8,128)(2,1)S(1)}, u32[]{:S(2)}, u32[]{:S(2)}) collective-permute-start(bf16[256,384]{1,0:T(8,128)(2,1)S(1)} %get-tuple-element.87), channel_id=1, source_target_pairs={{0,1},{1,0},{2,3},{3,2},{4,5},{5,4},{6,7},{7,6},{8,9},{9,8},{10,11... | collective-permute-start | bytes 589832 | tf_op jit(solution)/shard_map/ppermute | solution.py:485
  26.3 8.0 %collective-permute-start.7 = (bf16[256,384]{1,0:T(8,128)(2,1)S(1)}, bf16[256,384]{1,0:T(8,128)(2,1)S(1)}, u32[]{:S(2)}, u32[]{:S(2)}) collective-permute-start(bf16[256,384]{1,0:T(8,128)(2,1)S(1)} %add_convert_fusion), channel_id=1, source_target_pairs={{3,1},{5,3},{7,5},{9,7},{11,9},{13,11},{15,13},{14,15},{12,14},{10... | collective-permute-start | bytes 589832 | tf_op jit(solution)/shard_map/ppermute | solution.py:485
  30.7 3.7 %collective-permute-start.5 = (bf16[256,384]{1,0:T(8,128)(2,1)S(1)}, bf16[256,384]{1,0:T(8,128)(2,1)S(1)}, u32[]{:S(2)}, u32[]{:S(2)}) collective-permute-start(bf16[256,384]{1,0:T(8,128)(2,1)S(1)} %get-tuple-element.83), channel_id=1, source_target_pairs={{0,1},{1,0},{2,3},{3,2},{4,5},{5,4},{6,7},{7,6},{8,9},{9,8},{10,11... | collective-permute-start | bytes 589832 | tf_op jit(solution)/shard_map/ppermute | solution.py:485

commit v12 on v11

--- a/solution.py
+++ b/solution.py
@@ -179,29 +179,32 @@
         following = start_max()
         ahead = len(jobs[job + 1][1]) if job + 1 < len(jobs) else 0
         done = 0
-        total = jnp.zeros((8, wide), jnp.float32)
-        delta = jnp.zeros((8, wide), jnp.float32)
+        total = [jnp.zeros((8, TQ), jnp.float32)] * heads
+        delta = [jnp.zeros((8, TQ), jnp.float32)] * heads
         for index, (chunk, keys, row, weights, dprobs, kept) in enumerate(chunks):
             product = dot_nn(keys[rows + row : rows + row + CHUNK, :], dout_t[:, tile])
             for start in range(0, CHUNK, GROUP):
                 place = chunk * CHUNK + start
                 there = slice(kept.start + start, kept.start + start + GROUP)
-                dprob = product[start : start + GROUP, :]
-                dprobs[there, :] = dprob.astype(jnp.bfloat16)
-                part = jnp.exp2(scores[job % 2, place : place + GROUP, :] * base2 - row_max)
-                weights[there, :] = part.astype(jnp.bfloat16)
-                term = part * dprob
-                for row8 in range(0, GROUP, 8):
-                    total = total + part[row8 : row8 + 8, :]
-                    delta = delta + term[row8 : row8 + 8, :]
+                for h in range(heads):
+                    lanes = slice(h * TQ, (h + 1) * TQ)
+                    dprob = product[start : start + GROUP, lanes]
+                    dprobs[there, lanes] = dprob.astype(jnp.bfloat16)
+                    part = scores[job % 2, place : place + GROUP, lanes]
+                    part = jnp.exp2(part * base2 - row_max[:, lanes])
+                    weights[there, lanes] = part.astype(jnp.bfloat16)
+                    term = part * dprob
+                    for row8 in range(0, GROUP, 8):
+                        total[h] = total[h] + part[row8 : row8 + 8, :]
+                        delta[h] = delta[h] + term[row8 : row8 + 8, :]
             while done * len(chunks) < ahead * (index + 1):
                 score(job + 1, done, following)
                 done += 1
-        end(
-            row_max,
-            jnp.sum(total, axis=0, keepdims=True),
-            jnp.sum(delta, axis=0, keepdims=True),
+        sums = (
+            jnp.concatenate([jnp.sum(part, axis=0, keepdims=True) for part in parts], axis=1)
+            for parts in (total, delta)
         )
+        end(row_max, *sums)
 
 
 def early_kernel(rows, heads, count, slot, own_kv, query_t, dout_t, doc_start, *refs):
@@ -506,9 +509,7 @@
     far_1, near_early = lax.optimization_barrier((far_1, near_early))
     far_late = late_scores(0, count, far_ready, far_early, far_1, far_2)
     from_far_2 = move(far_late[-1], far_back)
-    far_1, far_stats = lax.optimization_barrier((far_1, far_late[-2]))
     near_2 = move(far_1, swap)
-    near_2, far_early = lax.optimization_barrier((near_2, far_early))
     far_rest_d, far_g1, far_own = rest_grads(0, far_ready, far_early, far_late)
     relayed = move(far_g1, swap)
     near_late = late_scores(1, count, near_ready, near_early, near_1, near_2)

time: 35.5 us -> 35.5 us (level)
  waiting for transfers between devices: 2.98 us -> 2.02 us
  starting transfers between devices: 14.6 us -> 15.2 us
    ppermute x8, waiting for transfers between devices: 2.98 us -> 2.02 us  [move(): return lax.ppermute(array, 'ctx', pairs)]
    ppermute x8, starting transfers between devices: 14.6 us -> 15.2 us  [move(): return lax.ppermute(array, 'ctx', pairs)]
  transfers between devices with their start and end apart: 8 -> 8, of which waited for: 4 -> 3; matrix products, arithmetic and copies ran while one was open for 0% -> 0% of each run, Pallas kernels for 34% -> 43%
where the time goes in v12:
time: 35.5 us; the launch traced here: 35.3 us
  Pallas kernels  16 us (45%)
  starting transfers between devices  15.2 us (43%)
  waiting for transfers between devices  2.02 us (6%)
  local copies, waits for them, and re-layouts  1.06 us (3%)
  between operations  0.79 us (2%)
    ppermute x8, starting transfers between devices, move(): return lax.ppermute(array, 'ctx', pairs)  15.2 us
    pallas_call x2, Pallas kernels, late_scores(): pl.pallas_call(functools.partial(late_kernel, rows, heads, count, slot),...  4.58 us
    pallas_call x1, Pallas kernels, block_outputs(): pl.pallas_call(functools.partial(outputs_kernel, rows, heads), out_shape=...  3.07 us
    pallas_call x2, Pallas kernels, early_scores(): pl.pallas_call(functools.partial(early_kernel, rows, heads, count, slot),...  2.76 us
    pallas_call x2, Pallas kernels, rest_grads(): pl.pallas_call(functools.partial(grads_kernel, rows, heads, slot), out_sh...  2.71 us
    ppermute x8, waiting for transfers between devices, move(): return lax.ppermute(array, 'ctx', pairs)  2.02 us
    pallas_call x1, Pallas kernels, prepare(): pl.pallas_call(functools.partial(prepare_kernel, rows, heads, doc_lengths...  2.01 us
    slice x1, local copies, waits for them, and re-layouts, body(): upper = jnp.concatenate([key[rows:], value[rows:]], axis=0)  1.06 us
  transfers between devices with their start and end apart: 8, of which 3 were waited for; matrix products, arithmetic and copies ran while one was open for 0% of the time, Pallas kernels for 43%

profile of v12, /device:TPU:0, one launch (start us, length us, event | category | flops | bytes accessed | tf_op | source)
XLA Modules:
  0.0 35.3 jit_solution(4012516825373572565)
XLA Ops:
  0.6 1.1 %fusion = (bf16[384,128]{1,0:T(8,128)(2,1)S(1)}, bf16[384,128]{1,0:T(8,128)(2,1)S(1)}, bf16[384,128]{1,0:T(8,128)(2,1)S(1)}, bf16[384,128]{1,0:T(8,128)(2,1)S(1)}) fusion(bf16[768,128]{1,0:T(8,128)(2,1)} %param.6, bf16[768,128]{1,0:T(8,128)(2,1)} %param.7), kind=kLoop, calls=%fused_computation.6 | loop fusion | bytes 786432 | tf_op jit(solution)/shard_map/slice | solution.py:500
  1.7 0.1 broadcast_select_fusion
  1.8 0.7 %collective-permute-start = (bf16[768,128]{1,0:T(8,128)(2,1)S(1)}, bf16[768,128]{1,0:T(8,128)(2,1)S(1)}, u32[]{:S(2)}, u32[]{:S(2)}) collective-permute-start(bf16[768,128]{1,0:T(8,128)(2,1)S(1)} %get-tuple-element.82.refs_1_), channel_id=1, source_target_pairs={{1,2},{3,4},{5,6},{7,8},{9,10},{11,12},{13,14},{15,15},{14,13},{12... | collective-permute-start | bytes 589832 | tf_op jit(solution)/shard_map/ppermute | solution.py:488
  2.5 6.1 %collective-permute-start.2 = (bf16[768,128]{1,0:T(8,128)(2,1)S(1)}, bf16[768,128]{1,0:T(8,128)(2,1)S(1)}, u32[]{:S(2)}, u32[]{:S(2)}) collective-permute-start(bf16[768,128]{1,0:T(8,128)(2,1)S(1)} %get-tuple-element.83.refs_0_), channel_id=1, source_target_pairs={{0,2},{2,4},{4,6},{6,8},{8,10},{10,12},{12,14},{14,15},{15,13},{13... | collective-permute-start | bytes 589832 | tf_op jit(solution)/shard_map/ppermute | solution.py:488
  8.6 2.0 %prepare.1 = (bf16[768,128]{1,0:T(8,128)(2,1)S(1)}, bf16[128,1536]{1,0:T(8,128)(2,1)S(1)}, bf16[128,1536]{1,0:T(8,128)(2,1)S(1)}, s32[8,128]{1,0:T(8,128)S(1)}, ...) custom-call(bf16[768,128]{1,0:T(8,128)(2,1)S(1)} %get-tuple-element., ...), custom_call_target="tpu_custom_call" | custom-call | bytes 4194304 | tf_op jit(solution)/shard_map/prepare/pallas_call | solution.py:107
  10.6 0.1 collective-permute-start.1
  10.7 0.9 %early_far.1 = (bf16[768,512]{1,0:T(8,128)(2,1)S(1)}, bf16[768,512]{1,0:T(8,128)(2,1)S(1)}, f32[24,512]{1,0:T(8,128)S(1)}) custom-call(bf16[768,128]{1,0:T(8,128)(2,1)S(1)} %get-tuple-element.43.own_kv.refs_0_, bf16[128,1536]{1,0:T(8,128)(2,1)S(1)} %get-tuple-element.52.query_t, bf16[128,1536]{1,0:T(8,128)(2,1)S(1)} %get-tuple-element.53.dout_t, ...), custom_call_target="tpu_custom_call" | custom-call | flops 8589934592 | tf_op jit(solution)/shard_map/early_far/pallas_call | solution.py:238
  11.6 0.6 %collective-permute-done.1.refs_0_.prev1.refs_9_ = bf16[768,128]{1,0:T(8,128)(2,1)S(1)} collective-permute-done((bf16[768,128]{1,0:T(8,128)(2,1)S(1)}, bf16[768,128]{1,0:T(8,128)(2,1)S(1)}, u32[]{:S(2)}, u32[]{:S(2)}) %collective-permute-start.1) | collective-permute-done | bytes 196640 | tf_op jit(solution)/shard_map/ppermute | solution.py:488
  12.1 1.9 %early_near.1 = (bf16[1920,512]{1,0:T(8,128)(2,1)S(1)}, bf16[1920,512]{1,0:T(8,128)(2,1)S(1)}, f32[24,512]{1,0:T(8,128)S(1)}) custom-call(bf16[768,128]{1,0:T(8,128)(2,1)S(1)} %get-tuple-element.44.own_kv.refs_8_, bf16[128,1536]{1,0:T(8,128)(2,1)S(1)} %get-tuple-element.45.query_t, bf16[128,1536]{1,0:T(8,128)(2,1)S(1)} %get-tuple-element.46.dout_t, ...), custom_call_target="tpu_custom_call" | custom-call | tf_op jit(solution)/shard_map/early_near/pallas_call | solution.py:238
  14.1 0.0 collective-permute-done.prev1.refs_1_
  14.1 0.6 %collective-permute-start.3 = (bf16[768,128]{1,0:T(8,128)(2,1)S(1)}, bf16[768,128]{1,0:T(8,128)(2,1)S(1)}, u32[]{:S(2)}, u32[]{:S(2)}) collective-permute-start(bf16[768,128]{1,0:T(8,128)(2,1)S(1)} %collective-permute-done.prev1.refs_1_), channel_id=1, source_target_pairs={{0,1},{1,0},{2,3},{3,2},{4,5},{5,4},{6,7},{7,6},{8,9},{9,8},{10,11... | collective-permute-start | bytes 589832 | tf_op jit(solution)/shard_map/ppermute | solution.py:488
  14.6 1.0 %collective-permute-done.2.prev2.refs_2_ = bf16[768,128]{1,0:T(8,128)(2,1)S(1)} collective-permute-done((bf16[768,128]{1,0:T(8,128)(2,1)S(1)}, bf16[768,128]{1,0:T(8,128)(2,1)S(1)}, u32[]{:S(2)}, u32[]{:S(2)}) %collective-permute-start.2) | collective-permute-done | bytes 196640 | tf_op jit(solution)/shard_map/ppermute | solution.py:488
  15.6 2.9 %late_far.1 = (bf16[1920,512]{1,0:T(8,128)(2,1)S(1)}, bf16[1920,512]{1,0:T(8,128)(2,1)S(1)}, bf16[768,512]{1,0:T(8,128)(2,1)S(1)}, f32[24,512]{1,0:T(8,128)S(1)}, bf16[256,384]{1,0:T(8,128)(2,1)S(1)}) custom-call(bf16[128,1536]{1,0:T(8,128)(2,1)S(1)} %get-tuple-element.52.query_t, bf16[128,1536]{1,0:T(8,128)(2,1)S(1)} %get-tuple-element.53.dout_t, ...), custom_call_target="tpu_custom_call" | custom-call | flops 2147483648 | tf_op jit(solution)/shard_map/late_far/pallas_call | solution.py:331
  18.5 1.3 %collective-permute-start.4 = (bf16[256,384]{1,0:T(8,128)(2,1)S(1)}, bf16[256,384]{1,0:T(8,128)(2,1)S(1)}, u32[]{:S(2)}, u32[]{:S(2)}) collective-permute-start(bf16[256,384]{1,0:T(8,128)(2,1)S(1)} %get-tuple-element.74), channel_id=1, source_target_pairs={{2,0},{4,2},{6,4},{8,6},{10,8},{12,10},{14,12},{15,14},{13,15},{11... | collective-permute-start | bytes 589832 | tf_op jit(solution)/shard_map/ppermute | solution.py:488
  19.8 1.3 %grads_far.1 = (bf16[1920,512]{1,0:T(8,128)(2,1)S(1)}, bf16[256,384]{1,0:T(8,128)(2,1)S(1)}, f32[256,384]{1,0:T(8,128)S(1)}) custom-call(bf16[128,1536]{1,0:T(8,128)(2,1)S(1)} %get-tuple-element.52.query_t, bf16[128,1536]{1,0:T(8,128)(2,1)S(1)} %get-tuple-element.53.dout_t, f32[24,512]{1,0:T(8,128)S(1)} %get-tuple-element.57.stats.refs_7_, ...), custom_call_target="tpu_custom_call" | custom-call | tf_op jit(solution)/shard_map/grads_far/pallas_call | solution.py:391
  21.1 2.3 %collective-permute-start.6 = (bf16[256,384]{1,0:T(8,128)(2,1)S(1)}, bf16[256,384]{1,0:T(8,128)(2,1)S(1)}, u32[]{:S(2)}, u32[]{:S(2)}) collective-permute-start(bf16[256,384]{1,0:T(8,128)(2,1)S(1)} %get-tuple-element.79), channel_id=1, source_target_pairs={{0,1},{1,0},{2,3},{3,2},{4,5},{5,4},{6,7},{7,6},{8,9},{9,8},{10,11... | collective-permute-start | bytes 589832 | tf_op jit(solution)/shard_map/ppermute | solution.py:488
  23.4 0.0 collective-permute-done.3.prev2.refs_10_
  23.4 1.7 %late_near.1 = (bf16[768,512]{1,0:T(8,128)(2,1)S(1)}, bf16[768,512]{1,0:T(8,128)(2,1)S(1)}, f32[24,512]{1,0:T(8,128)S(1)}, bf16[256,384]{1,0:T(8,128)(2,1)S(1)}) custom-call(bf16[128,1536]{1,0:T(8,128)(2,1)S(1)} %get-tuple-element.45.query_t, bf16[128,1536]{1,0:T(8,128)(2,1)S(1)} %get-tuple-element.46.dout_t, s32[8,128]{1,0:T(8,128)S(1)} %get-tuple-element.47.doc_start, ...), custom_call_target="tpu_custom_call" | custom-call | flops 2147483648 | tf_op jit(solution)/shard_map/late_near/pallas_call | solution.py:331
  25.1 0.0 collective-permute-done.6
  25.1 0.1 add_convert_fusion
  25.2 4.1 %collective-permute-start.7 = (bf16[256,384]{1,0:T(8,128)(2,1)S(1)}, bf16[256,384]{1,0:T(8,128)(2,1)S(1)}, u32[]{:S(2)}, u32[]{:S(2)}) collective-permute-start(bf16[256,384]{1,0:T(8,128)(2,1)S(1)} %add_convert_fusion), channel_id=1, source_target_pairs={{3,1},{5,3},{7,5},{9,7},{11,9},{13,11},{15,13},{14,15},{12,14},{10... | collective-permute-start | bytes 589832 | tf_op jit(solution)/shard_map/ppermute | solution.py:488
  29.3 1.4 %grads_near.1 = (bf16[1920,512]{1,0:T(8,128)(2,1)S(1)}, bf16[256,384]{1,0:T(8,128)(2,1)S(1)}, f32[256,384]{1,0:T(8,128)S(1)}) custom-call(bf16[128,1536]{1,0:T(8,128)(2,1)S(1)} %get-tuple-element.45.query_t, bf16[128,1536]{1,0:T(8,128)(2,1)S(1)} %get-tuple-element.46.dout_t, f32[24,512]{1,0:T(8,128)S(1)} %get-tuple-element.65.stats.refs_15_, ...), custom_call_target="tpu_custom_call" | custom-call | flops 2147483648 | tf_op jit(solution)/shard_map/grads_near/pallas_call | solution.py:391
  30.7 0.0 collective-permute-done.4.far_2
  30.7 0.1 collective-permute-start.5
  30.8 3.1 %block_outputs.1 = (bf16[768,512]{1,0:T(8,128)(2,1)}, bf16[768,512]{1,0:T(8,128)(2,1)}) custom-call(bf16[768,128]{1,0:T(8,128)(2,1)S(1)} %get-tuple-element.43.own_kv.refs_0_, bf16[768,128]{1,0:T(8,128)(2,1)S(1)} %collective-permute-done.prev1.refs_1_, bf16[768,128]{1,0:T(8,128)(2,1)S(1)} %collective-permute-done.2.prev2.refs_2_, ...), custom_call_target="tpu_custom_call" | custom-call | tf_op jit(solution)/shard_map/block_outputs/pallas_call | solution.py:448
  33.9 0.5 %collective-permute-done.7 = bf16[256,384]{1,0:T(8,128)(2,1)S(1)} collective-permute-done((bf16[256,384]{1,0:T(8,128)(2,1)S(1)}, bf16[256,384]{1,0:T(8,128)(2,1)S(1)}, u32[]{:S(2)}, u32[]{:S(2)}) %collective-permute-start.7) | collective-permute-done | bytes 196640 | tf_op jit(solution)/shard_map/ppermute | solution.py:488
  34.4 0.0 collective-permute-done.5.far_1
  34.4 0.9 %total_grads.1 = (bf16[768,128]{1,0:T(8,128)(2,1)}, bf16[768,128]{1,0:T(8,128)(2,1)}) custom-call(f32[256,384]{1,0:T(8,128)S(1)} %get-tuple-element.72.far_own, bf16[256,384]{1,0:T(8,128)(2,1)S(1)} %collective-permute-done.5.far_1, bf16[256,384]{1,0:T(8,128)(2,1)S(1)} %collective-permute-done.4.far_2, f32[256,384]{1,0:T(8,128)S(1)} %convert_add_fusion.near), custom_call_target="tpu_custom_call" | custom-call | tf_op jit(solution)/shard_map/total_grads/pallas_call | solution.py:471
  (1 shorter events, 0.0 us)
Async XLA Ops:
  1.8 12.3 %collective-permute-start = (bf16[768,128]{1,0:T(8,128)(2,1)S(1)}, bf16[768,128]{1,0:T(8,128)(2,1)S(1)}, u32[]{:S(2)}, u32[]{:S(2)}) collective-permute-start(bf16[768,128]{1,0:T(8,128)(2,1)S(1)} %get-tuple-element.82.refs_1_), channel_id=1, source_target_pairs={{1,2},{3,4},{5,6},{7,8},{9,10},{11,12},{13,14},{15,15},{14,13},{12... | collective-permute-start | bytes 589832 | tf_op jit(solution)/shard_map/ppermute | solution.py:488
  2.5 13.1 %collective-permute-start.2 = (bf16[768,128]{1,0:T(8,128)(2,1)S(1)}, bf16[768,128]{1,0:T(8,128)(2,1)S(1)}, u32[]{:S(2)}, u32[]{:S(2)}) collective-permute-start(bf16[768,128]{1,0:T(8,128)(2,1)S(1)} %get-tuple-element.83.refs_0_), channel_id=1, source_target_pairs={{0,2},{2,4},{4,6},{6,8},{8,10},{10,12},{12,14},{14,15},{15,13},{13... | collective-permute-start | bytes 589832 | tf_op jit(solution)/shard_map/ppermute | solution.py:488
  10.6 1.5 %collective-permute-start.1 = (bf16[768,128]{1,0:T(8,128)(2,1)S(1)}, bf16[768,128]{1,0:T(8,128)(2,1)S(1)}, u32[]{:S(2)}, u32[]{:S(2)}) collective-permute-start(bf16[768,128]{1,0:T(8,128)(2,1)S(1)} %get-tuple-element.43.own_kv.refs_0_), channel_id=1, source_target_pairs={{0,1},{1,0},{2,3},{3,2},{4,5},{5,4},{6,7},{7,6},{8,9},{9,8},{10,11... | collective-permute-start | bytes 589832 | tf_op jit(solution)/shard_map/ppermute | solution.py:488
  14.1 9.4 %collective-permute-start.3 = (bf16[768,128]{1,0:T(8,128)(2,1)S(1)}, bf16[768,128]{1,0:T(8,128)(2,1)S(1)}, u32[]{:S(2)}, u32[]{:S(2)}) collective-permute-start(bf16[768,128]{1,0:T(8,128)(2,1)S(1)} %collective-permute-done.prev1.refs_1_), channel_id=1, source_target_pairs={{0,1},{1,0},{2,3},{3,2},{4,5},{5,4},{6,7},{7,6},{8,9},{9,8},{10,11... | collective-permute-start | bytes 589832 | tf_op jit(solution)/shard_map/ppermute | solution.py:488
  18.5 12.2 %collective-permute-start.4 = (bf16[256,384]{1,0:T(8,128)(2,1)S(1)}, bf16[256,384]{1,0:T(8,128)(2,1)S(1)}, u32[]{:S(2)}, u32[]{:S(2)}) collective-permute-start(bf16[256,384]{1,0:T(8,128)(2,1)S(1)} %get-tuple-element.74), channel_id=1, source_target_pairs={{2,0},{4,2},{6,4},{8,6},{10,8},{12,10},{14,12},{15,14},{13,15},{11... | collective-permute-start | bytes 589832 | tf_op jit(solution)/shard_map/ppermute | solution.py:488
  21.1 4.0 %collective-permute-start.6 = (bf16[256,384]{1,0:T(8,128)(2,1)S(1)}, bf16[256,384]{1,0:T(8,128)(2,1)S(1)}, u32[]{:S(2)}, u32[]{:S(2)}) collective-permute-start(bf16[256,384]{1,0:T(8,128)(2,1)S(1)} %get-tuple-element.79), channel_id=1, source_target_pairs={{0,1},{1,0},{2,3},{3,2},{4,5},{5,4},{6,7},{7,6},{8,9},{9,8},{10,11... | collective-permute-start | bytes 589832 | tf_op jit(solution)/shard_map/ppermute | solution.py:488
  25.2 9.1 %collective-permute-start.7 = (bf16[256,384]{1,0:T(8,128)(2,1)S(1)}, bf16[256,384]{1,0:T(8,128)(2,1)S(1)}, u32[]{:S(2)}, u32[]{:S(2)}) collective-permute-start(bf16[256,384]{1,0:T(8,128)(2,1)S(1)} %add_convert_fusion), channel_id=1, source_target_pairs={{3,1},{5,3},{7,5},{9,7},{11,9},{13,11},{15,13},{14,15},{12,14},{10... | collective-permute-start | bytes 589832 | tf_op jit(solution)/shard_map/ppermute | solution.py:488
  30.7 3.7 %collective-permute-start.5 = (bf16[256,384]{1,0:T(8,128)(2,1)S(1)}, bf16[256,384]{1,0:T(8,128)(2,1)S(1)}, u32[]{:S(2)}, u32[]{:S(2)}) collective-permute-start(bf16[256,384]{1,0:T(8,128)(2,1)S(1)} %get-tuple-element.75), channel_id=1, source_target_pairs={{0,1},{1,0},{2,3},{3,2},{4,5},{5,4},{6,7},{7,6},{8,9},{9,8},{10,11... | collective-permute-start | bytes 589832 | tf_op jit(solution)/shard_map/ppermute | solution.py:488

commit v13 on v11

--- a/solution.py
+++ b/solution.py
@@ -166,6 +166,7 @@
     def start_max():
         return [jnp.full((8, TQ), masked_score, jnp.float32)] * heads
 
+    pending = None
     following = start_max()
     for index in range(len(jobs[0][1])):
         score(0, index, following)
@@ -197,11 +198,11 @@
             while done * len(chunks) < ahead * (index + 1):
                 score(job + 1, done, following)
                 done += 1
-        end(
-            row_max,
-            jnp.sum(total, axis=0, keepdims=True),
-            jnp.sum(delta, axis=0, keepdims=True),
-        )
+            if index == 0 and pending is not None:
+                pending()
+        sums = [jnp.sum(part, axis=0, keepdims=True) for part in (total, delta)]
+        pending = functools.partial(end, row_max, *sums)
+    pending()
 
 
 def early_kernel(rows, heads, count, slot, own_kv, query_t, dout_t, doc_start, *refs):
@@ -506,9 +507,7 @@
     far_1, near_early = lax.optimization_barrier((far_1, near_early))
     far_late = late_scores(0, count, far_ready, far_early, far_1, far_2)
     from_far_2 = move(far_late[-1], far_back)
-    far_1, far_stats = lax.optimization_barrier((far_1, far_late[-2]))
     near_2 = move(far_1, swap)
-    near_2, far_early = lax.optimization_barrier((near_2, far_early))
     far_rest_d, far_g1, far_own = rest_grads(0, far_ready, far_early, far_late)
     relayed = move(far_g1, swap)
     near_late = late_scores(1, count, near_ready, near_early, near_1, near_2)

time: 35.5 us -> 35.2 us (level)
  waiting for transfers between devices: 2.98 us -> 2.11 us
  starting transfers between devices: 14.6 us -> 15.4 us
    ppermute x8, waiting for transfers between devices: 2.98 us -> 2.11 us  [move(): return lax.ppermute(array, 'ctx', pairs)]
    ppermute x8, starting transfers between devices: 14.6 us -> 15.4 us  [move(): return lax.ppermute(array, 'ctx', pairs)]
  transfers between devices with their start and end apart: 8 -> 8, of which waited for: 4 -> 3; matrix products, arithmetic and copies ran while one was open for 0% -> 0% of each run, Pallas kernels for 34% -> 41%
where the time goes in v13:
time: 35.2 us; the launch traced here: 34.9 us
  starting transfers between devices  15.4 us (44%)
  Pallas kernels  15.4 us (44%)
  waiting for transfers between devices  2.11 us (6%)
  local copies, waits for them, and re-layouts  1.06 us (3%)
  between operations  0.8 us (2%)
    ppermute x8, starting transfers between devices, move(): return lax.ppermute(array, 'ctx', pairs)  15.4 us
    pallas_call x2, Pallas kernels, late_scores(): pl.pallas_call(functools.partial(late_kernel, rows, heads, count, slot),...  4.2 us
    pallas_call x1, Pallas kernels, block_outputs(): pl.pallas_call(functools.partial(outputs_kernel, rows, heads), out_shape=...  3.06 us
    pallas_call x2, Pallas kernels, rest_grads(): pl.pallas_call(functools.partial(grads_kernel, rows, heads, slot), out_sh...  2.71 us
    pallas_call x2, Pallas kernels, early_scores(): pl.pallas_call(functools.partial(early_kernel, rows, heads, count, slot),...  2.48 us
    ppermute x8, waiting for transfers between devices, move(): return lax.ppermute(array, 'ctx', pairs)  2.11 us
    pallas_call x1, Pallas kernels, prepare(): pl.pallas_call(functools.partial(prepare_kernel, rows, heads, doc_lengths...  2.01 us
    slice x1, local copies, waits for them, and re-layouts, body(): upper = jnp.concatenate([key[rows:], value[rows:]], axis=0)  1.06 us
  transfers between devices with their start and end apart: 8, of which 3 were waited for; matrix products, arithmetic and copies ran while one was open for 0% of the time, Pallas kernels for 41%

profile of v13, /device:TPU:0, one launch (start us, length us, event | category | flops | bytes accessed | tf_op | source)
XLA Modules:
  0.0 34.9 jit_solution(17174165397465870188)
XLA Ops:
  0.6 1.1 %fusion = (bf16[384,128]{1,0:T(8,128)(2,1)S(1)}, bf16[384,128]{1,0:T(8,128)(2,1)S(1)}, bf16[384,128]{1,0:T(8,128)(2,1)S(1)}, bf16[384,128]{1,0:T(8,128)(2,1)S(1)}) fusion(bf16[768,128]{1,0:T(8,128)(2,1)} %param.6, bf16[768,128]{1,0:T(8,128)(2,1)} %param.7), kind=kLoop, calls=%fused_computation.6 | loop fusion | bytes 786432 | tf_op jit(solution)/shard_map/slice | solution.py:498
  1.7 0.1 broadcast_select_fusion
  1.8 0.7 %collective-permute-start = (bf16[768,128]{1,0:T(8,128)(2,1)S(1)}, bf16[768,128]{1,0:T(8,128)(2,1)S(1)}, u32[]{:S(2)}, u32[]{:S(2)}) collective-permute-start(bf16[768,128]{1,0:T(8,128)(2,1)S(1)} %get-tuple-element.82.refs_1_), channel_id=1, source_target_pairs={{1,2},{3,4},{5,6},{7,8},{9,10},{11,12},{13,14},{15,15},{14,13},{12... | collective-permute-start | bytes 589832 | tf_op jit(solution)/shard_map/ppermute | solution.py:486
  2.5 6.1 %collective-permute-start.2 = (bf16[768,128]{1,0:T(8,128)(2,1)S(1)}, bf16[768,128]{1,0:T(8,128)(2,1)S(1)}, u32[]{:S(2)}, u32[]{:S(2)}) collective-permute-start(bf16[768,128]{1,0:T(8,128)(2,1)S(1)} %get-tuple-element.83.refs_0_), channel_id=1, source_target_pairs={{0,2},{2,4},{4,6},{6,8},{8,10},{10,12},{12,14},{14,15},{15,13},{13... | collective-permute-start | bytes 589832 | tf_op jit(solution)/shard_map/ppermute | solution.py:486
  8.6 2.0 %prepare.1 = (bf16[768,128]{1,0:T(8,128)(2,1)S(1)}, bf16[128,1536]{1,0:T(8,128)(2,1)S(1)}, bf16[128,1536]{1,0:T(8,128)(2,1)S(1)}, s32[8,128]{1,0:T(8,128)S(1)}, ...) custom-call(bf16[768,128]{1,0:T(8,128)(2,1)S(1)} %get-tuple-element., ...), custom_call_target="tpu_custom_call" | custom-call | bytes 4194304 | tf_op jit(solution)/shard_map/prepare/pallas_call | solution.py:107
  10.6 0.1 collective-permute-start.1
  10.7 0.8 %early_far.1 = (bf16[768,512]{1,0:T(8,128)(2,1)S(1)}, bf16[768,512]{1,0:T(8,128)(2,1)S(1)}, f32[24,512]{1,0:T(8,128)S(1)}) custom-call(bf16[768,128]{1,0:T(8,128)(2,1)S(1)} %get-tuple-element.43.own_kv.refs_0_, bf16[128,1536]{1,0:T(8,128)(2,1)S(1)} %get-tuple-element.52.query_t, bf16[128,1536]{1,0:T(8,128)(2,1)S(1)} %get-tuple-element.53.dout_t, ...), custom_call_target="tpu_custom_call" | custom-call | flops 8589934592 | tf_op jit(solution)/shard_map/early_far/pallas_call | solution.py:236
  11.5 0.6 %collective-permute-done.1.refs_0_.prev1.refs_9_ = bf16[768,128]{1,0:T(8,128)(2,1)S(1)} collective-permute-done((bf16[768,128]{1,0:T(8,128)(2,1)S(1)}, bf16[768,128]{1,0:T(8,128)(2,1)S(1)}, u32[]{:S(2)}, u32[]{:S(2)}) %collective-permute-start.1) | collective-permute-done | bytes 196640 | tf_op jit(solution)/shard_map/ppermute | solution.py:486
  12.1 1.7 %early_near.1 = (bf16[1920,512]{1,0:T(8,128)(2,1)S(1)}, bf16[1920,512]{1,0:T(8,128)(2,1)S(1)}, f32[24,512]{1,0:T(8,128)S(1)}) custom-call(bf16[768,128]{1,0:T(8,128)(2,1)S(1)} %get-tuple-element.44.own_kv.refs_8_, bf16[128,1536]{1,0:T(8,128)(2,1)S(1)} %get-tuple-element.45.query_t, bf16[128,1536]{1,0:T(8,128)(2,1)S(1)} %get-tuple-element.46.dout_t, ...), custom_call_target="tpu_custom_call" | custom-call | tf_op jit(solution)/shard_map/early_near/pallas_call | solution.py:236
  13.9 0.0 collective-permute-done.prev1.refs_1_
  13.9 0.8 %collective-permute-start.3 = (bf16[768,128]{1,0:T(8,128)(2,1)S(1)}, bf16[768,128]{1,0:T(8,128)(2,1)S(1)}, u32[]{:S(2)}, u32[]{:S(2)}) collective-permute-start(bf16[768,128]{1,0:T(8,128)(2,1)S(1)} %collective-permute-done.prev1.refs_1_), channel_id=1, source_target_pairs={{0,1},{1,0},{2,3},{3,2},{4,5},{5,4},{6,7},{7,6},{8,9},{9,8},{10,11... | collective-permute-start | bytes 589832 | tf_op jit(solution)/shard_map/ppermute | solution.py:486
  14.6 1.0 %collective-permute-done.2.prev2.refs_2_ = bf16[768,128]{1,0:T(8,128)(2,1)S(1)} collective-permute-done((bf16[768,128]{1,0:T(8,128)(2,1)S(1)}, bf16[768,128]{1,0:T(8,128)(2,1)S(1)}, u32[]{:S(2)}, u32[]{:S(2)}) %collective-permute-start.2) | collective-permute-done | bytes 196640 | tf_op jit(solution)/shard_map/ppermute | solution.py:486
  15.6 2.7 %late_far.1 = (bf16[1920,512]{1,0:T(8,128)(2,1)S(1)}, bf16[1920,512]{1,0:T(8,128)(2,1)S(1)}, bf16[768,512]{1,0:T(8,128)(2,1)S(1)}, f32[24,512]{1,0:T(8,128)S(1)}, bf16[256,384]{1,0:T(8,128)(2,1)S(1)}) custom-call(bf16[128,1536]{1,0:T(8,128)(2,1)S(1)} %get-tuple-element.52.query_t, bf16[128,1536]{1,0:T(8,128)(2,1)S(1)} %get-tuple-element.53.dout_t, ...), custom_call_target="tpu_custom_call" | custom-call | flops 2147483648 | tf_op jit(solution)/shard_map/late_far/pallas_call | solution.py:329
  18.3 1.3 %collective-permute-start.4 = (bf16[256,384]{1,0:T(8,128)(2,1)S(1)}, bf16[256,384]{1,0:T(8,128)(2,1)S(1)}, u32[]{:S(2)}, u32[]{:S(2)}) collective-permute-start(bf16[256,384]{1,0:T(8,128)(2,1)S(1)} %get-tuple-element.74), channel_id=1, source_target_pairs={{2,0},{4,2},{6,4},{8,6},{10,8},{12,10},{14,12},{15,14},{13,15},{11... | collective-permute-start | bytes 589832 | tf_op jit(solution)/shard_map/ppermute | solution.py:486
  19.6 1.3 %grads_far.1 = (bf16[1920,512]{1,0:T(8,128)(2,1)S(1)}, bf16[256,384]{1,0:T(8,128)(2,1)S(1)}, f32[256,384]{1,0:T(8,128)S(1)}) custom-call(bf16[128,1536]{1,0:T(8,128)(2,1)S(1)} %get-tuple-element.52.query_t, bf16[128,1536]{1,0:T(8,128)(2,1)S(1)} %get-tuple-element.53.dout_t, f32[24,512]{1,0:T(8,128)S(1)} %get-tuple-element.57.stats.refs_7_, ...), custom_call_target="tpu_custom_call" | custom-call | tf_op jit(solution)/shard_map/grads_far/pallas_call | solution.py:389
  20.9 2.3 %collective-permute-start.6 = (bf16[256,384]{1,0:T(8,128)(2,1)S(1)}, bf16[256,384]{1,0:T(8,128)(2,1)S(1)}, u32[]{:S(2)}, u32[]{:S(2)}) collective-permute-start(bf16[256,384]{1,0:T(8,128)(2,1)S(1)} %get-tuple-element.79), channel_id=1, source_target_pairs={{0,1},{1,0},{2,3},{3,2},{4,5},{5,4},{6,7},{7,6},{8,9},{9,8},{10,11... | collective-permute-start | bytes 589832 | tf_op jit(solution)/shard_map/ppermute | solution.py:486
  23.2 0.0 collective-permute-done.3.prev2.refs_10_
  23.3 1.5 %late_near.1 = (bf16[768,512]{1,0:T(8,128)(2,1)S(1)}, bf16[768,512]{1,0:T(8,128)(2,1)S(1)}, f32[24,512]{1,0:T(8,128)S(1)}, bf16[256,384]{1,0:T(8,128)(2,1)S(1)}) custom-call(bf16[128,1536]{1,0:T(8,128)(2,1)S(1)} %get-tuple-element.45.query_t, bf16[128,1536]{1,0:T(8,128)(2,1)S(1)} %get-tuple-element.46.dout_t, s32[8,128]{1,0:T(8,128)S(1)} %get-tuple-element.47.doc_start, ...), custom_call_target="tpu_custom_call" | custom-call | flops 2147483648 | tf_op jit(solution)/shard_map/late_near/pallas_call | solution.py:329
  24.8 0.0 collective-permute-done.6
  24.8 0.1 add_convert_fusion
  24.8 4.1 %collective-permute-start.7 = (bf16[256,384]{1,0:T(8,128)(2,1)S(1)}, bf16[256,384]{1,0:T(8,128)(2,1)S(1)}, u32[]{:S(2)}, u32[]{:S(2)}) collective-permute-start(bf16[256,384]{1,0:T(8,128)(2,1)S(1)} %add_convert_fusion), channel_id=1, source_target_pairs={{3,1},{5,3},{7,5},{9,7},{11,9},{13,11},{15,13},{14,15},{12,14},{10... | collective-permute-start | bytes 589832 | tf_op jit(solution)/shard_map/ppermute | solution.py:486
  28.9 1.4 %grads_near.1 = (bf16[1920,512]{1,0:T(8,128)(2,1)S(1)}, bf16[256,384]{1,0:T(8,128)(2,1)S(1)}, f32[256,384]{1,0:T(8,128)S(1)}) custom-call(bf16[128,1536]{1,0:T(8,128)(2,1)S(1)} %get-tuple-element.45.query_t, bf16[128,1536]{1,0:T(8,128)(2,1)S(1)} %get-tuple-element.46.dout_t, f32[24,512]{1,0:T(8,128)S(1)} %get-tuple-element.65.stats.refs_15_, ...), custom_call_target="tpu_custom_call" | custom-call | flops 2147483648 | tf_op jit(solution)/shard_map/grads_near/pallas_call | solution.py:389
  30.3 0.0 collective-permute-done.4.far_2
  30.3 0.1 collective-permute-start.5
  30.4 3.1 %block_outputs.1 = (bf16[768,512]{1,0:T(8,128)(2,1)}, bf16[768,512]{1,0:T(8,128)(2,1)}) custom-call(bf16[768,128]{1,0:T(8,128)(2,1)S(1)} %get-tuple-element.43.own_kv.refs_0_, bf16[768,128]{1,0:T(8,128)(2,1)S(1)} %collective-permute-done.prev1.refs_1_, bf16[768,128]{1,0:T(8,128)(2,1)S(1)} %collective-permute-done.2.prev2.refs_2_, ...), custom_call_target="tpu_custom_call" | custom-call | tf_op jit(solution)/shard_map/block_outputs/pallas_call | solution.py:446
  33.5 0.5 %collective-permute-done.7 = bf16[256,384]{1,0:T(8,128)(2,1)S(1)} collective-permute-done((bf16[256,384]{1,0:T(8,128)(2,1)S(1)}, bf16[256,384]{1,0:T(8,128)(2,1)S(1)}, u32[]{:S(2)}, u32[]{:S(2)}) %collective-permute-start.7) | collective-permute-done | bytes 196640 | tf_op jit(solution)/shard_map/ppermute | solution.py:486
  34.0 0.0 collective-permute-done.5.far_1
  34.0 0.9 %total_grads.1 = (bf16[768,128]{1,0:T(8,128)(2,1)}, bf16[768,128]{1,0:T(8,128)(2,1)}) custom-call(f32[256,384]{1,0:T(8,128)S(1)} %get-tuple-element.72.far_own, bf16[256,384]{1,0:T(8,128)(2,1)S(1)} %collective-permute-done.5.far_1, bf16[256,384]{1,0:T(8,128)(2,1)S(1)} %collective-permute-done.4.far_2, f32[256,384]{1,0:T(8,128)S(1)} %convert_add_fusion.near), custom_call_target="tpu_custom_call" | custom-call | tf_op jit(solution)/shard_map/total_grads/pallas_call | solution.py:469
  (1 shorter events, 0.0 us)
Async XLA Ops:
  1.8 12.1 %collective-permute-start = (bf16[768,128]{1,0:T(8,128)(2,1)S(1)}, bf16[768,128]{1,0:T(8,128)(2,1)S(1)}, u32[]{:S(2)}, u32[]{:S(2)}) collective-permute-start(bf16[768,128]{1,0:T(8,128)(2,1)S(1)} %get-tuple-element.82.refs_1_), channel_id=1, source_target_pairs={{1,2},{3,4},{5,6},{7,8},{9,10},{11,12},{13,14},{15,15},{14,13},{12... | collective-permute-start | bytes 589832 | tf_op jit(solution)/shard_map/ppermute | solution.py:486
  2.5 13.1 %collective-permute-start.2 = (bf16[768,128]{1,0:T(8,128)(2,1)S(1)}, bf16[768,128]{1,0:T(8,128)(2,1)S(1)}, u32[]{:S(2)}, u32[]{:S(2)}) collective-permute-start(bf16[768,128]{1,0:T(8,128)(2,1)S(1)} %get-tuple-element.83.refs_0_), channel_id=1, source_target_pairs={{0,2},{2,4},{4,6},{6,8},{8,10},{10,12},{12,14},{14,15},{15,13},{13... | collective-permute-start | bytes 589832 | tf_op jit(solution)/shard_map/ppermute | solution.py:486
  10.6 1.5 %collective-permute-start.1 = (bf16[768,128]{1,0:T(8,128)(2,1)S(1)}, bf16[768,128]{1,0:T(8,128)(2,1)S(1)}, u32[]{:S(2)}, u32[]{:S(2)}) collective-permute-start(bf16[768,128]{1,0:T(8,128)(2,1)S(1)} %get-tuple-element.43.own_kv.refs_0_), channel_id=1, source_target_pairs={{0,1},{1,0},{2,3},{3,2},{4,5},{5,4},{6,7},{7,6},{8,9},{9,8},{10,11... | collective-permute-start | bytes 589832 | tf_op jit(solution)/shard_map/ppermute | solution.py:486
  13.9 9.4 %collective-permute-start.3 = (bf16[768,128]{1,0:T(8,128)(2,1)S(1)}, bf16[768,128]{1,0:T(8,128)(2,1)S(1)}, u32[]{:S(2)}, u32[]{:S(2)}) collective-permute-start(bf16[768,128]{1,0:T(8,128)(2,1)S(1)} %collective-permute-done.prev1.refs_1_), channel_id=1, source_target_pairs={{0,1},{1,0},{2,3},{3,2},{4,5},{5,4},{6,7},{7,6},{8,9},{9,8},{10,11... | collective-permute-start | bytes 589832 | tf_op jit(solution)/shard_map/ppermute | solution.py:486
  18.3 12.0 %collective-permute-start.4 = (bf16[256,384]{1,0:T(8,128)(2,1)S(1)}, bf16[256,384]{1,0:T(8,128)(2,1)S(1)}, u32[]{:S(2)}, u32[]{:S(2)}) collective-permute-start(bf16[256,384]{1,0:T(8,128)(2,1)S(1)} %get-tuple-element.74), channel_id=1, source_target_pairs={{2,0},{4,2},{6,4},{8,6},{10,8},{12,10},{14,12},{15,14},{13,15},{11... | collective-permute-start | bytes 589832 | tf_op jit(solution)/shard_map/ppermute | solution.py:486
  20.9 3.8 %collective-permute-start.6 = (bf16[256,384]{1,0:T(8,128)(2,1)S(1)}, bf16[256,384]{1,0:T(8,128)(2,1)S(1)}, u32[]{:S(2)}, u32[]{:S(2)}) collective-permute-start(bf16[256,384]{1,0:T(8,128)(2,1)S(1)} %get-tuple-element.79), channel_id=1, source_target_pairs={{0,1},{1,0},{2,3},{3,2},{4,5},{5,4},{6,7},{7,6},{8,9},{9,8},{10,11... | collective-permute-start | bytes 589832 | tf_op jit(solution)/shard_map/ppermute | solution.py:486
  24.8 9.1 %collective-permute-start.7 = (bf16[256,384]{1,0:T(8,128)(2,1)S(1)}, bf16[256,384]{1,0:T(8,128)(2,1)S(1)}, u32[]{:S(2)}, u32[]{:S(2)}) collective-permute-start(bf16[256,384]{1,0:T(8,128)(2,1)S(1)} %add_convert_fusion), channel_id=1, source_target_pairs={{3,1},{5,3},{7,5},{9,7},{11,9},{13,11},{15,13},{14,15},{12,14},{10... | collective-permute-start | bytes 589832 | tf_op jit(solution)/shard_map/ppermute | solution.py:486
  30.3 3.7 %collective-permute-start.5 = (bf16[256,384]{1,0:T(8,128)(2,1)S(1)}, bf16[256,384]{1,0:T(8,128)(2,1)S(1)}, u32[]{:S(2)}, u32[]{:S(2)}) collective-permute-start(bf16[256,384]{1,0:T(8,128)(2,1)S(1)} %get-tuple-element.75), channel_id=1, source_target_pairs={{0,1},{1,0},{2,3},{3,2},{4,5},{5,4},{6,7},{7,6},{8,9},{9,8},{10,11... | collective-permute-start | bytes 589832 | tf_op jit(solution)/shard_map/ppermute | solution.py:486

commit v14 on v13

--- a/solution.py
+++ b/solution.py
@@ -13,6 +13,7 @@
 GROUP = 32
 
 masked_score = -1e30
+other_document = -65536.0
 VMEM_LIMIT = 24 * 1024 * 1024
 SCALE = 1.0 / math.sqrt(HD)
 VMEM = pl.BlockSpec(memory_space=pltpu.VMEM)
@@ -70,8 +71,22 @@
             pltpu.make_async_copy(doc_hbm, doc_lengths, sems.at[2]),
         ]
     )
+    lane = lax.broadcasted_iota(jnp.int32, (1, HD), 1)
+
+    def one(index, carry):
+        start, starts, ends = carry
+        end = start + doc_lengths[index]
+        starts = jnp.where(lane == index, start, starts)
+        return (end, starts, jnp.where(lane == index, end, ends))
+
+    none = jnp.zeros((1, HD), jnp.int32)
+    _, starts, ends = lax.fori_loop(0, docs, one, (jnp.int32(0), none, none), unroll=8)
+    starts_t, ends_t = (
+        jnp.transpose(jnp.broadcast_to(row.astype(jnp.float32), (HD, HD))).astype(jnp.int32)
+        for row in (starts, ends)
+    )
     for slot in (0, 1):
-        own_kv, query_t, dout_t, doc_start = refs[4 * slot : 4 * slot + 4]
+        own_kv, query_t, dout_t, documents = refs[4 * slot : 4 * slot + 4]
         own_kv[...] = (far_kv, near_kv)[slot][...]
         own_rows = half_start(rows, slot)
         for step in range(rows // TQ):
@@ -79,23 +94,23 @@
             for h in range(heads):
                 place = slice(step * wide + h * TQ, step * wide + (h + 1) * TQ)
                 columns = slice(h * HD, (h + 1) * HD)
-                query_t[:, place] = jnp.transpose(query[source, columns])
+                query_t[0:HD, place] = jnp.transpose(query[source, columns])
                 dout_t[:, place] = jnp.transpose(dout[source, columns])
-        at = (
-            block_number(count, slot) * rows
-            + lax.broadcasted_iota(jnp.int32, (8, TQ), 0) * TQ
-            + lax.broadcasted_iota(jnp.int32, (8, TQ), 1)
-        )
-
-        def one(index, carry):
-            start, found = carry
-            found = jnp.where(at >= start, start, found)
-            return (start + doc_lengths[index], found)
-
-        _, found = lax.fori_loop(
-            0, docs, one, (jnp.int32(0), jnp.zeros((8, TQ), jnp.int32)), unroll=8
-        )
-        doc_start[...] = found
+        position = block_number(count, slot) * rows
+        for tile in range(3 * rows // TQ):
+            at = lax.broadcasted_iota(jnp.int32, (TQ, HD), 0) + (position - 2 * rows + tile * TQ)
+            inside = jnp.logical_and(at >= starts, at < ends)
+            inside = jnp.logical_or(inside, at < 0)
+            documents[tile * TQ : (tile + 1) * TQ, :] = jnp.where(inside, 1.0, 0.0).astype(
+                documents.dtype
+            )
+        for step in range(rows // TQ):
+            at = lax.broadcasted_iota(jnp.int32, (HD, TQ), 1) + (position + step * TQ)
+            inside = jnp.logical_and(at >= starts_t, at < ends_t)
+            other = jnp.where(inside, 0.0, other_document).astype(query_t.dtype)
+            for h in range(heads):
+                place = slice(step * wide + h * TQ, step * wide + (h + 1) * TQ)
+                query_t[HD : 2 * HD, place] = other
 
 
 def prepare(count, doc_lengths, query, dout, far_kv, near_kv):
@@ -103,10 +118,12 @@
     heads = query.shape[1] // HD
     pair = jax.ShapeDtypeStruct(far_kv.shape, far_kv.dtype)
     stacked_t = jax.ShapeDtypeStruct((HD, rows * heads), query.dtype)
-    starts = jax.ShapeDtypeStruct((8, TQ), jnp.int32)
+    query_shape = jax.ShapeDtypeStruct((2 * HD, rows * heads), query.dtype)
+    documents = jax.ShapeDtypeStruct((3 * rows, HD), query.dtype)
+    assert doc_lengths.shape[0] <= HD
     return pl.pallas_call(
         functools.partial(prepare_kernel, rows, heads, doc_lengths.shape[0], count),
-        out_shape=(pair, stacked_t, stacked_t, starts) * 2,
+        out_shape=(pair, query_shape, stacked_t, documents) * 2,
         in_specs=[VMEM] * 2 + [HBM] * 3,
         out_specs=[VMEM] * 8,
         scratch_shapes=[
@@ -127,9 +144,9 @@
         self.chunks = 2 * self.tiles + 1
         self.steps = range(self.tiles)
         self.first = [self.tiles - step for step in self.steps]
-        self.rest = [self.chunks - first for first in self.first]
         self.late = [first + (1 - slot) * self.tiles for first in self.first]
         self.early = [self.chunks - late for late in self.late]
+        self.middle = [late - first for late, first in zip(self.late, self.first)]
 
 
 def chunk_rows(counts, step, first=0, count=None):
@@ -138,27 +155,29 @@
     return slice(start * CHUNK, (start + count) * CHUNK)
 
 
-def exponentials(jobs, rows, heads, block_pos, scores):
+def exponentials(jobs, rows, heads, scores):
     back = 2 * rows
     wide = heads * TQ
     base2 = SCALE * math.log2(math.e)
 
     def score(job, index, row_max):
-        step, chunks, (query_t, _, doc_start), _, _ = jobs[job]
+        step, chunks, (query_t, _, documents), _, _ = jobs[job]
         chunk, keys, row = chunks[index][0:3]
-        low = doc_start[step : step + 1, :] - (block_pos(job) - back + step * TQ)
-        high = lax.broadcasted_iota(jnp.int32, (1, TQ), 1) + back
         tile = slice(step * wide, (step + 1) * wide)
-        product = dot_nn(keys[row : row + CHUNK, :], query_t[:, tile])
+        window = slice(step * TQ + chunk * CHUNK, step * TQ + (chunk + 1) * CHUNK)
+        product = dot_nn(
+            jnp.concatenate([keys[row : row + CHUNK, :], documents[window, :]], axis=1),
+            query_t[:, tile],
+        )
         for start in range(0, CHUNK, GROUP):
             place = chunk * CHUNK + start
-            at = lax.broadcasted_iota(jnp.int32, (GROUP, TQ), 0) + place
-            allowed = at >= low
-            if place >= back:
-                allowed = jnp.logical_and(allowed, at <= high)
             for h in range(heads):
                 lanes = slice(h * TQ, (h + 1) * TQ)
-                part = jnp.where(allowed, product[start : start + GROUP, lanes], masked_score)
+                part = product[start : start + GROUP, lanes]
+                if place >= back:
+                    key_at = lax.broadcasted_iota(jnp.int32, (GROUP, TQ), 0) + (place - back)
+                    query_at = lax.broadcasted_iota(jnp.int32, (GROUP, TQ), 1)
+                    part = jnp.where(key_at <= query_at, part, masked_score)
                 scores[job % 2, place : place + GROUP, lanes] = part
                 for row8 in range(0, GROUP, 8):
                     row_max[h] = jnp.maximum(row_max[h], part[row8 : row8 + 8, :])
@@ -205,11 +224,10 @@
     pending()
 
 
-def early_kernel(rows, heads, count, slot, own_kv, query_t, dout_t, doc_start, *refs):
+def early_kernel(rows, heads, slot, own_kv, query_t, dout_t, documents, *refs):
     (weights, dprobs, stats, scores) = refs[-4:]
     prev1 = refs[0] if slot == 1 else None
     window = Window(rows, slot)
-    position = block_number(count, slot) * rows
     jobs = []
     for step in window.steps:
         chunks = []
@@ -224,17 +242,17 @@
             for kind, value in enumerate(found):
                 stats[8 * kind + step : 8 * kind + step + 1, :] = value
 
-        jobs.append((step, chunks, (query_t, dout_t, doc_start), None, end))
-    exponentials(jobs, rows, heads, lambda job: position, scores)
-
-
-def early_scores(slot, count, ready, *prev1):
+        jobs.append((step, chunks, (query_t, dout_t, documents), None, end))
+    exponentials(jobs, rows, heads, scores)
+
+
+def early_scores(slot, ready, *prev1):
     rows = ready[0].shape[0] // 2
     heads = ready[1].shape[1] // rows
     wide = heads * TQ
     kept = jax.ShapeDtypeStruct((sum(Window(rows, slot).early) * CHUNK, wide), jnp.bfloat16)
     return pl.pallas_call(
-        functools.partial(early_kernel, rows, heads, count, slot),
+        functools.partial(early_kernel, rows, heads, slot),
         out_shape=(kept, kept, jax.ShapeDtypeStruct((24, wide), jnp.float32)),
         in_specs=[VMEM] * (4 + len(prev1)),
         out_specs=[VMEM] * 3,
@@ -246,7 +264,7 @@
 
 
 def scaled_by(array, tile, factor):
-    return (array[:, tile].astype(jnp.float32) * factor).astype(jnp.bfloat16)
+    return (array[0:HD, tile].astype(jnp.float32) * factor).astype(jnp.bfloat16)
 
 
 def dscore_rows(dscores, there, weights, dprobs, kept, delta):
@@ -269,11 +287,10 @@
 def late_kernel(
     rows,
     heads,
-    count,
     slot,
     query_t,
     dout_t,
-    doc_start,
+    documents,
     early_stats,
     prev1,
     prev2,
@@ -283,7 +300,6 @@
     (dprobs, dscores, stats, prev2_out, scores, dk, dv) = refs if slot == 0 else refs[-1:] + refs[:-1]
     wide = heads * TQ
     window = Window(rows, slot)
-    position = block_number(count, slot) * rows
     jobs = []
     for step in window.steps:
         chunks = []
@@ -314,20 +330,20 @@
             )
 
         first_max = early_stats[step : step + 1, :]
-        jobs.append((step, chunks, (query_t, dout_t, doc_start), first_max, end))
-    exponentials(jobs, rows, heads, lambda job: position, scores)
+        jobs.append((step, chunks, (query_t, dout_t, documents), first_max, end))
+    exponentials(jobs, rows, heads, scores)
     prev2_out[0:HD] = (dk[...] * SCALE).astype(prev2_out.dtype)
     prev2_out[HD : 2 * HD] = dv[...].astype(prev2_out.dtype)
 
 
-def late_scores(slot, count, ready, early, prev1, prev2):
+def late_scores(slot, ready, early, prev1, prev2):
     rows = prev2.shape[0] // 2
     heads = ready[1].shape[1] // rows
     wide = heads * TQ
     window = Window(rows, slot)
     late = jax.ShapeDtypeStruct((sum(window.late) * CHUNK, wide), jnp.bfloat16)
     return pl.pallas_call(
-        functools.partial(late_kernel, rows, heads, count, slot),
+        functools.partial(late_kernel, rows, heads, slot),
         out_shape=(
             *([late] * (2 - slot)),
             jax.ShapeDtypeStruct((sum(window.first) * CHUNK, wide), jnp.bfloat16),
@@ -348,65 +364,69 @@
     )(*ready[1:4], early[2], prev1, prev2)
 
 
-def grads_kernel(rows, heads, slot, query_t, dout_t, stats, *refs):
-    (late_w, late_dprobs, early_w, early_dprobs) = refs[0:4] if slot == 0 else (None, None) + refs[0:2]
-    (dscores, prev1_out, own_out, dk, dv) = refs[4:] if slot == 0 else refs[2:]
+def grads_kernel(rows, heads, slots, *refs):
     wide = heads * TQ
-    window = Window(rows, slot)
-    for step in reversed(window.steps):
-        tile = slice(step * wide, (step + 1) * wide)
-        late_factor, early_factor, delta = (
-            stats[8 * kind + step : 8 * kind + step + 1, :] for kind in range(3)
-        )
-        beyond = window.late[step] - window.first[step]
-        parts = [(beyond, early_w, early_dprobs, chunk_rows(window.early, step), early_factor)]
-        if beyond:
-            kept = chunk_rows(window.late, step, window.first[step])
-            parts.append((0, late_w, late_dprobs, kept, late_factor))
-        for start, weights, dprobs, kept, factor in parts:
-            length = (kept.stop - kept.start) // CHUNK
-            there = chunk_rows(window.rest, step, start, length)
+    outs = list(refs[5 * len(slots) : -2])
+    (dk, dv) = refs[-2:]
+    for part, (slot, late) in enumerate(slots):
+        (query_t, dout_t, stats, weights, dprobs) = refs[5 * part : 5 * part + 5]
+        dscores = outs.pop(0)
+        window = Window(rows, slot)
+        counts = window.middle if late else window.early
+        for step in reversed(window.steps):
+            tile = slice(step * wide, (step + 1) * wide)
+            late_factor, early_factor, delta = (
+                stats[8 * kind + step : 8 * kind + step + 1, :] for kind in range(3)
+            )
+            factor = late_factor if late else early_factor
+            there = chunk_rows(counts, step)
+            kept = chunk_rows(window.late, step, window.first[step]) if late else there
             dscore_rows(dscores, there, weights, dprobs, kept, delta.astype(jnp.bfloat16))
             add_products(
                 step == window.tiles - 1,
-                slice(start * CHUNK, (start + length) * CHUNK),
+                slice(0, counts[step] * CHUNK),
                 (
                     (dv, scaled_by(dout_t, tile, factor), weights[kept, :]),
                     (dk, scaled_by(query_t, tile, factor), dscores[there, :]),
                 ),
             )
-    prev1_out[0:HD] = (dk[:, 0:rows] * SCALE).astype(prev1_out.dtype)
-    prev1_out[HD : 2 * HD] = dv[:, 0:rows].astype(prev1_out.dtype)
-    own_out[0:HD] = dk[:, rows : 2 * rows] * SCALE
-    own_out[HD : 2 * HD] = dv[:, rows : 2 * rows]
-
-
-def rest_grads(slot, ready, early, late):
-    rows = ready[0].shape[0] // 2
-    heads = ready[1].shape[1] // rows
-    rest = (sum(Window(rows, slot).rest) * CHUNK, heads * TQ)
-    operands = (*ready[1:3], late[-2], *(late[0:2] if slot == 0 else ()), *early[0:2])
+        for block in range(counts[-1] // window.tiles):
+            out = outs.pop(0)
+            place = slice(block * rows, (block + 1) * rows)
+            out[0:HD] = (dk[:, place] * SCALE).astype(out.dtype)
+            out[HD : 2 * HD] = dv[:, place].astype(out.dtype)
+
+
+def rest_grads(name, cost, parts):
+    rows = parts[0][2][0].shape[0] // 2
+    heads = parts[0][2][1].shape[1] // rows
+    operands, out_shape = [], []
+    for slot, late, (_, query_t, dout_t, _, stats, weights, dprobs), sent in parts:
+        window = Window(rows, slot)
+        kept = (sum(window.middle if late else window.early) * CHUNK, heads * TQ)
+        operands += [query_t, dout_t, stats, weights, dprobs]
+        out_shape.append(jax.ShapeDtypeStruct(kept, jnp.bfloat16))
+        for one in sent:
+            kind = jnp.bfloat16 if one else jnp.float32
+            out_shape.append(jax.ShapeDtypeStruct((2 * HD, rows), kind))
+    slots = tuple(part[0:2] for part in parts)
     return pl.pallas_call(
-        functools.partial(grads_kernel, rows, heads, slot),
-        out_shape=(
-            jax.ShapeDtypeStruct(rest, jnp.bfloat16),
-            jax.ShapeDtypeStruct((2 * HD, rows), jnp.bfloat16),
-            jax.ShapeDtypeStruct((2 * HD, rows), jnp.float32),
-        ),
+        functools.partial(grads_kernel, rows, heads, slots),
+        out_shape=out_shape,
         in_specs=[VMEM] * len(operands),
-        out_specs=[VMEM] * 3,
+        out_specs=[VMEM] * len(out_shape),
         scratch_shapes=[pltpu.VMEM((HD, 2 * rows), jnp.float32)] * 2,
         compiler_params=pltpu.CompilerParams(vmem_limit_bytes=VMEM_LIMIT),
-        cost_estimate=pl.CostEstimate(flops=2**31 if slot else 0, bytes_accessed=0, transcendentals=0),
-        name="grads_far" if slot == 0 else "grads_near",
+        cost_estimate=pl.CostEstimate(flops=cost, bytes_accessed=0, transcendentals=0),
+        name=name,
     )(*operands)
 
 
 def outputs_kernel(rows, heads, *refs):
-    blocks = (refs[0:8], refs[8:16])
-    (attended, grad_query, keys_t, values_t) = refs[16:]
+    blocks = (refs[0:9], refs[9:17])
+    (attended, grad_query, keys_t, values_t) = refs[17:]
     for slot, block in enumerate(blocks):
-        (own_kv, prev1, prev2, early_w, rest_d, late_w, first_d, stats) = block
+        (own_kv, prev1, prev2, early_w, early_d, late_w, first_d, stats) = block[0:8]
         window = Window(rows, slot)
         own_rows = half_start(rows, slot)
         for place, source in enumerate((prev2, prev1, own_kv)):
@@ -429,8 +449,8 @@
             attended_t += product(values_t, early_w, window.early, late, 0, early) * early_factor
             late_t = product(keys_t, first_d, window.first, 0, 0, first)
             if late > first:
-                late_t += product(keys_t, rest_d, window.rest, first, 0, late - first)
-            early_t = product(keys_t, rest_d, window.rest, late, late - first, early)
+                late_t += product(keys_t, block[8], window.middle, first, 0, late - first)
+            early_t = product(keys_t, early_d, window.early, late, 0, early)
             grad_query_t = late_t * (late_factor * SCALE) + early_t * (early_factor * SCALE)
             place = pl.ds(own_rows + step * TQ, TQ)
             for out, found in ((attended, attended_t), (grad_query, grad_query_t)):
@@ -446,7 +466,7 @@
     return pl.pallas_call(
         functools.partial(outputs_kernel, rows, heads),
         out_shape=(shape, shape),
-        in_specs=[VMEM] * 16,
+        in_specs=[VMEM] * 17,
         out_specs=[VMEM] * 2,
         scratch_shapes=[pltpu.VMEM((HD, 3 * rows), jnp.bfloat16)] * 2,
         compiler_params=pltpu.CompilerParams(vmem_limit_bytes=VMEM_LIMIT),
@@ -502,24 +522,34 @@
     prepared = prepare(count, doc_lengths, query, d_out, far_kv, near_kv)
     far_ready, near_ready = prepared[0:4], prepared[4:8]
     near_1 = move(far_ready[0], swap)
-    far_early = early_scores(0, count, far_ready)
-    near_early = early_scores(1, count, near_ready, near_1)
+    far_early = early_scores(0, far_ready)
+    near_early = early_scores(1, near_ready, near_1)
     far_1, near_early = lax.optimization_barrier((far_1, near_early))
-    far_late = late_scores(0, count, far_ready, far_early, far_1, far_2)
+    far_late = late_scores(0, far_ready, far_early, far_1, far_2)
     from_far_2 = move(far_late[-1], far_back)
     near_2 = move(far_1, swap)
-    far_rest_d, far_g1, far_own = rest_grads(0, far_ready, far_early, far_late)
+    near_2, far_stats = lax.optimization_barrier((near_2, far_late[-2]))
+    far_middle_d, far_g1 = rest_grads(
+        "grads_far", 0, [(0, True, (*far_ready, far_stats, *far_late[0:2]), (True,))]
+    )
     relayed = move(far_g1, swap)
-    near_late = late_scores(1, count, near_ready, near_early, near_1, near_2)
+    near_late = late_scores(1, near_ready, near_early, near_1, near_2)
     near_sum = near_late[-1].astype(jnp.float32) + relayed.astype(jnp.float32)
     from_near_2 = move(near_sum.astype(jnp.bfloat16), near_back)
-    near_rest_d, near_g1, near_own = rest_grads(1, near_ready, near_early, near_late)
+    near_early_d, near_g1, near_own, far_early_d, far_own = rest_grads(
+        "grads_near",
+        2**31,
+        [
+            (1, False, (*near_ready, near_late[-2], *near_early[0:2]), (True, False)),
+            (0, False, (*far_ready, far_late[-2], *far_early[0:2]), (False,)),
+        ],
+    )
     near_g1, from_far_2 = lax.optimization_barrier((near_g1, from_far_2))
     from_near_1 = move(near_g1, swap)
     attended, grad_query = block_outputs(
         query,
-        (far_ready[0], far_1, far_2, far_early[0], far_rest_d, far_late[0], *far_late[-3:-1]),
-        (near_ready[0], near_1, near_2, near_early[0], near_rest_d, near_late[0], *near_late[-3:-1]),
+        (far_ready[0], far_1, far_2, far_early[0], far_early_d, far_late[0], *far_late[-3:-1], far_middle_d),
+        (near_ready[0], near_1, near_2, near_early[0], near_early_d, near_late[0], *near_late[-3:-1]),
     )
     near_total = near_own + from_near_2.astype(jnp.float32)
     grad_key, grad_value = total_grads(far_own, from_near_1, from_far_2, near_total)

time: 35.2 us -> 34.8 us (0.989)
  waiting for transfers between devices: 2.11 us -> 1.66 us
    ppermute x8, waiting for transfers between devices: 2.11 us -> 1.66 us  [move(): return lax.ppermute(array, 'ctx', pairs)]
  transfers between devices with their start and end apart: 8 -> 8, of which waited for: 3 -> 2; matrix products, arithmetic and copies ran while one was open for 0% -> 0% of each run, Pallas kernels for 41% -> 42%
where the time goes in v14:
time: 34.8 us; the launch traced here: 34.5 us
  Pallas kernels  15.5 us (45%)
  starting transfers between devices  15.4 us (44%)
  waiting for transfers between devices  1.66 us (5%)
  local copies, waits for them, and re-layouts  1.06 us (3%)
  between operations  0.8 us (2%)
    ppermute x8, starting transfers between devices, move(): return lax.ppermute(array, 'ctx', pairs)  15.4 us
    pallas_call x2, Pallas kernels, late_scores(): pl.pallas_call(functools.partial(late_kernel, rows, heads, slot), out_sha...  4.26 us
    pallas_call x1, Pallas kernels, block_outputs(): pl.pallas_call(functools.partial(outputs_kernel, rows, heads), out_shape=...  3.07 us
    pallas_call x2, Pallas kernels, rest_grads(): pl.pallas_call(functools.partial(grads_kernel, rows, heads, slots), out_s...  2.72 us
    pallas_call x2, Pallas kernels, early_scores(): pl.pallas_call(functools.partial(early_kernel, rows, heads, slot), out_sh...  2.25 us
    pallas_call x1, Pallas kernels, prepare(): pl.pallas_call(functools.partial(prepare_kernel, rows, heads, doc_lengths...  2.23 us
    ppermute x8, waiting for transfers between devices, move(): return lax.ppermute(array, 'ctx', pairs)  1.66 us
    slice x1, local copies, waits for them, and re-layouts, body(): upper = jnp.concatenate([key[rows:], value[rows:]], axis=0)  1.06 us
  transfers between devices with their start and end apart: 8, of which 2 were waited for; matrix products, arithmetic and copies ran while one was open for 0% of the time, Pallas kernels for 42%

profile of v14, /device:TPU:0, one launch (start us, length us, event | category | flops | bytes accessed | tf_op | source)
XLA Modules:
  0.0 34.5 jit_solution(9962204664191929769)
XLA Ops:
  0.6 1.1 %fusion = (bf16[384,128]{1,0:T(8,128)(2,1)S(1)}, bf16[384,128]{1,0:T(8,128)(2,1)S(1)}, bf16[384,128]{1,0:T(8,128)(2,1)S(1)}, bf16[384,128]{1,0:T(8,128)(2,1)S(1)}) fusion(bf16[768,128]{1,0:T(8,128)(2,1)} %param.6, bf16[768,128]{1,0:T(8,128)(2,1)} %param.7), kind=kLoop, calls=%fused_computation.6 | loop fusion | bytes 786432 | tf_op jit(solution)/shard_map/slice | solution.py:518
  1.7 0.1 broadcast_select_fusion
  1.8 0.7 %collective-permute-start = (bf16[768,128]{1,0:T(8,128)(2,1)S(1)}, bf16[768,128]{1,0:T(8,128)(2,1)S(1)}, u32[]{:S(2)}, u32[]{:S(2)}) collective-permute-start(bf16[768,128]{1,0:T(8,128)(2,1)S(1)} %get-tuple-element.88.refs_1_), channel_id=1, source_target_pairs={{1,2},{3,4},{5,6},{7,8},{9,10},{11,12},{13,14},{15,15},{14,13},{12... | collective-permute-start | bytes 589832 | tf_op jit(solution)/shard_map/ppermute | solution.py:506
  2.5 6.1 %collective-permute-start.2 = (bf16[768,128]{1,0:T(8,128)(2,1)S(1)}, bf16[768,128]{1,0:T(8,128)(2,1)S(1)}, u32[]{:S(2)}, u32[]{:S(2)}) collective-permute-start(bf16[768,128]{1,0:T(8,128)(2,1)S(1)} %get-tuple-element.89.refs_0_), channel_id=1, source_target_pairs={{0,2},{2,4},{4,6},{6,8},{8,10},{10,12},{12,14},{14,15},{15,13},{13... | collective-permute-start | bytes 589832 | tf_op jit(solution)/shard_map/ppermute | solution.py:506
  8.6 2.2 %prepare.1 = (bf16[768,128]{1,0:T(8,128)(2,1)S(1)}, bf16[256,1536]{1,0:T(8,128)(2,1)S(1)}, bf16[128,1536]{1,0:T(8,128)(2,1)S(1)}, bf16[1152,128]{1,0:T(8,128)(2,...) custom-call(bf16[768,128]{1,0:T(8,128)(2,1)S(1)} %get-tuple-element., ...), custom_call_target="tpu_custom_call" | custom-call | bytes 4194304 | tf_op jit(solution)/shard_map/prepare/pallas_call | solution.py:124
  10.9 0.1 collective-permute-start.1
  10.9 0.7 %early_far.1 = (bf16[768,512]{1,0:T(8,128)(2,1)S(1)}, bf16[768,512]{1,0:T(8,128)(2,1)S(1)}, f32[24,512]{1,0:T(8,128)S(1)}) custom-call(bf16[768,128]{1,0:T(8,128)(2,1)S(1)} %get-tuple-element.46.own_kv.refs_0_, bf16[256,1536]{1,0:T(8,128)(2,1)S(1)} %get-tuple-element.55.query_t.refs_5_.refs_0_, ...), custom_call_target="tpu_custom_call" | custom-call | flops 8589934592 | tf_op jit(solution)/shard_map/early_far/pallas_call | solution.py:254
  11.7 0.7 %collective-permute-done.1.refs_0_.prev1.refs_10_ = bf16[768,128]{1,0:T(8,128)(2,1)S(1)} collective-permute-done((bf16[768,128]{1,0:T(8,128)(2,1)S(1)}, bf16[768,128]{1,0:T(8,128)(2,1)S(1)}, u32[]{:S(2)}, u32[]{:S(2)}) %collective-permute-start.1) | collective-permute-done | bytes 196640 | tf_op jit(solution)/shard_map/ppermute | solution.py:506
  12.4 1.5 %early_near.1 = (bf16[1920,512]{1,0:T(8,128)(2,1)S(1)}, bf16[1920,512]{1,0:T(8,128)(2,1)S(1)}, f32[24,512]{1,0:T(8,128)S(1)}) custom-call(bf16[768,128]{1,0:T(8,128)(2,1)S(1)} %get-tuple-element.47.own_kv.refs_9_, bf16[256,1536]{1,0:T(8,128)(2,1)S(1)} %get-tuple-element.48.query_t.refs_0_, bf16[128,1536]{1,0:T(8,128)(2,1)S(1)} %get-tuple-element.49.dout_t.refs_1_, ...), custom_call_target="tpu_custom_call" | custom-call | tf_op jit(solution)/shard_map/early_near/pallas_call | solution.py:254
  13.9 0.0 collective-permute-done.prev1.refs_1_
  13.9 0.7 %collective-permute-start.3 = (bf16[768,128]{1,0:T(8,128)(2,1)S(1)}, bf16[768,128]{1,0:T(8,128)(2,1)S(1)}, u32[]{:S(2)}, u32[]{:S(2)}) collective-permute-start(bf16[768,128]{1,0:T(8,128)(2,1)S(1)} %collective-permute-done.prev1.refs_1_), channel_id=1, source_target_pairs={{0,1},{1,0},{2,3},{3,2},{4,5},{5,4},{6,7},{7,6},{8,9},{9,8},{10,11... | collective-permute-start | bytes 589832 | tf_op jit(solution)/shard_map/ppermute | solution.py:506
  14.6 1.0 %collective-permute-done.2.prev2.refs_2_ = bf16[768,128]{1,0:T(8,128)(2,1)S(1)} collective-permute-done((bf16[768,128]{1,0:T(8,128)(2,1)S(1)}, bf16[768,128]{1,0:T(8,128)(2,1)S(1)}, u32[]{:S(2)}, u32[]{:S(2)}) %collective-permute-start.2) | collective-permute-done | bytes 196640 | tf_op jit(solution)/shard_map/ppermute | solution.py:506
  15.6 2.7 %late_far.1 = (bf16[1920,512]{1,0:T(8,128)(2,1)S(1)}, bf16[1920,512]{1,0:T(8,128)(2,1)S(1)}, bf16[768,512]{1,0:T(8,128)(2,1)S(1)}, f32[24,512]{1,0:T(8,128)S(1)}, bf16[256,384]{1,0:T(8,128)(2,1)S(1)}) custom-call(bf16[256,1536]{1,0:T(8,128)(2,1)S(1)} %get-tuple-element.55.query_t.refs_5_.refs_0_, ...), custom_call_target="tpu_custom_call" | custom-call | flops 2147483648 | tf_op jit(solution)/shard_map/late_far/pallas_call | solution.py:345
  18.3 1.3 %collective-permute-start.4 = (bf16[256,384]{1,0:T(8,128)(2,1)S(1)}, bf16[256,384]{1,0:T(8,128)(2,1)S(1)}, u32[]{:S(2)}, u32[]{:S(2)}) collective-permute-start(bf16[256,384]{1,0:T(8,128)(2,1)S(1)} %get-tuple-element.80), channel_id=1, source_target_pairs={{2,0},{4,2},{6,4},{8,6},{10,8},{12,10},{14,12},{15,14},{13,15},{11... | collective-permute-start | bytes 589832 | tf_op jit(solution)/shard_map/ppermute | solution.py:506
  19.6 0.0 collective-permute-done.3.prev2.refs_11_
  19.6 0.8 %grads_far.1 = (bf16[1152,512]{1,0:T(8,128)(2,1)S(1)}, bf16[256,384]{1,0:T(8,128)(2,1)S(1)}) custom-call(bf16[256,1536]{1,0:T(8,128)(2,1)S(1)} %get-tuple-element.55.query_t.refs_5_.refs_0_, bf16[128,1536]{1,0:T(8,128)(2,1)S(1)} %get-tuple-element.56.dout_t.refs_6_.refs_1_, f32[24,512]{1,0:T(8,128)S(1)} %get-tuple-element.70.refs_7_.refs_2_, ...), custom_call_target="tpu_custom_call" | custom-call | tf_op jit(solution)/shard_map/grads_far/pallas_call | solution.py:413
  20.5 2.3 %collective-permute-start.6 = (bf16[256,384]{1,0:T(8,128)(2,1)S(1)}, bf16[256,384]{1,0:T(8,128)(2,1)S(1)}, u32[]{:S(2)}, u32[]{:S(2)}) collective-permute-start(bf16[256,384]{1,0:T(8,128)(2,1)S(1)} %get-tuple-element.85), channel_id=1, source_target_pairs={{0,1},{1,0},{2,3},{3,2},{4,5},{5,4},{6,7},{7,6},{8,9},{9,8},{10,11... | collective-permute-start | bytes 589832 | tf_op jit(solution)/shard_map/ppermute | solution.py:506
  22.8 1.5 %late_near.1 = (bf16[768,512]{1,0:T(8,128)(2,1)S(1)}, bf16[768,512]{1,0:T(8,128)(2,1)S(1)}, f32[24,512]{1,0:T(8,128)S(1)}, bf16[256,384]{1,0:T(8,128)(2,1)S(1)}) custom-call(bf16[256,1536]{1,0:T(8,128)(2,1)S(1)} %get-tuple-element.48.query_t.refs_0_, bf16[128,1536]{1,0:T(8,128)(2,1)S(1)} %get-tuple-element.49.dout_t.refs_1_, ...), custom_call_target="tpu_custom_call" | custom-call | flops 2147483648 | tf_op jit(solution)/shard_map/late_near/pallas_call | solution.py:345
  24.3 0.0 collective-permute-done.6
  24.4 0.1 add_convert_fusion
  24.4 4.1 %collective-permute-start.7 = (bf16[256,384]{1,0:T(8,128)(2,1)S(1)}, bf16[256,384]{1,0:T(8,128)(2,1)S(1)}, u32[]{:S(2)}, u32[]{:S(2)}) collective-permute-start(bf16[256,384]{1,0:T(8,128)(2,1)S(1)} %add_convert_fusion), channel_id=1, source_target_pairs={{3,1},{5,3},{7,5},{9,7},{11,9},{13,11},{15,13},{14,15},{12,14},{10... | collective-permute-start | bytes 589832 | tf_op jit(solution)/shard_map/ppermute | solution.py:506
  28.5 1.9 %grads_near.1 = (bf16[1920,512]{1,0:T(8,128)(2,1)S(1)}, bf16[256,384]{1,0:T(8,128)(2,1)S(1)}, f32[256,384]{1,0:T(8,128)S(1)}, bf16[768,512]{1,0:T(8,128)(2,1)S(1)}, f32[256,384]{1,0:T(8,128)S(1)}) custom-call(bf16[256,1536]{1,0:T(8,128)(2,1)S(1)} %get-tuple-element.48.query_t.refs_0_, bf16[128,1536]{1,0:T(8,128)(2,1)S(1)} %get-tuple-element.49.dout_t.refs_1_, ...), custom_call_target="tpu_custom_call" | custom-call | flops 2147483648 | tf_op jit(solution)/shard_map/grads_near/pallas_call | solution.py:413
  30.4 0.0 collective-permute-done.4.far_2
  30.4 0.1 collective-permute-start.5
  30.5 3.1 %block_outputs.1 = (bf16[768,512]{1,0:T(8,128)(2,1)}, bf16[768,512]{1,0:T(8,128)(2,1)}) custom-call(bf16[768,128]{1,0:T(8,128)(2,1)S(1)} %get-tuple-element.46.own_kv.refs_0_, bf16[768,128]{1,0:T(8,128)(2,1)S(1)} %collective-permute-done.prev1.refs_1_, bf16[768,128]{1,0:T(8,128)(2,1)S(1)} %collective-permute-done.2.prev2.refs_2_, ...), custom_call_target="tpu_custom_call" | custom-call | tf_op jit(solution)/shard_map/block_outputs/pallas_call | solution.py:466
  33.5 0.0 collective-permute-done.7
  33.6 0.0 collective-permute-done.5.far_1
  33.6 0.9 %total_grads.1 = (bf16[768,128]{1,0:T(8,128)(2,1)}, bf16[768,128]{1,0:T(8,128)(2,1)}) custom-call(f32[256,384]{1,0:T(8,128)S(1)} %get-tuple-element.78.far_own, bf16[256,384]{1,0:T(8,128)(2,1)S(1)} %collective-permute-done.5.far_1, bf16[256,384]{1,0:T(8,128)(2,1)S(1)} %collective-permute-done.4.far_2, f32[256,384]{1,0:T(8,128)S(1)} %convert_add_fusion.near), custom_call_target="tpu_custom_call" | custom-call | tf_op jit(solution)/shard_map/total_grads/pallas_call | solution.py:489
  (1 shorter events, 0.0 us)
Async XLA Ops:
  1.8 12.1 %collective-permute-start = (bf16[768,128]{1,0:T(8,128)(2,1)S(1)}, bf16[768,128]{1,0:T(8,128)(2,1)S(1)}, u32[]{:S(2)}, u32[]{:S(2)}) collective-permute-start(bf16[768,128]{1,0:T(8,128)(2,1)S(1)} %get-tuple-element.88.refs_1_), channel_id=1, source_target_pairs={{1,2},{3,4},{5,6},{7,8},{9,10},{11,12},{13,14},{15,15},{14,13},{12... | collective-permute-start | bytes 589832 | tf_op jit(solution)/shard_map/ppermute | solution.py:506
  2.5 13.1 %collective-permute-start.2 = (bf16[768,128]{1,0:T(8,128)(2,1)S(1)}, bf16[768,128]{1,0:T(8,128)(2,1)S(1)}, u32[]{:S(2)}, u32[]{:S(2)}) collective-permute-start(bf16[768,128]{1,0:T(8,128)(2,1)S(1)} %get-tuple-element.89.refs_0_), channel_id=1, source_target_pairs={{0,2},{2,4},{4,6},{6,8},{8,10},{10,12},{12,14},{14,15},{15,13},{13... | collective-permute-start | bytes 589832 | tf_op jit(solution)/shard_map/ppermute | solution.py:506
  10.9 1.5 %collective-permute-start.1 = (bf16[768,128]{1,0:T(8,128)(2,1)S(1)}, bf16[768,128]{1,0:T(8,128)(2,1)S(1)}, u32[]{:S(2)}, u32[]{:S(2)}) collective-permute-start(bf16[768,128]{1,0:T(8,128)(2,1)S(1)} %get-tuple-element.46.own_kv.refs_0_), channel_id=1, source_target_pairs={{0,1},{1,0},{2,3},{3,2},{4,5},{5,4},{6,7},{7,6},{8,9},{9,8},{10,11... | collective-permute-start | bytes 589832 | tf_op jit(solution)/shard_map/ppermute | solution.py:506
  13.9 5.7 %collective-permute-start.3 = (bf16[768,128]{1,0:T(8,128)(2,1)S(1)}, bf16[768,128]{1,0:T(8,128)(2,1)S(1)}, u32[]{:S(2)}, u32[]{:S(2)}) collective-permute-start(bf16[768,128]{1,0:T(8,128)(2,1)S(1)} %collective-permute-done.prev1.refs_1_), channel_id=1, source_target_pairs={{0,1},{1,0},{2,3},{3,2},{4,5},{5,4},{6,7},{7,6},{8,9},{9,8},{10,11... | collective-permute-start | bytes 589832 | tf_op jit(solution)/shard_map/ppermute | solution.py:506
  18.3 12.1 %collective-permute-start.4 = (bf16[256,384]{1,0:T(8,128)(2,1)S(1)}, bf16[256,384]{1,0:T(8,128)(2,1)S(1)}, u32[]{:S(2)}, u32[]{:S(2)}) collective-permute-start(bf16[256,384]{1,0:T(8,128)(2,1)S(1)} %get-tuple-element.80), channel_id=1, source_target_pairs={{2,0},{4,2},{6,4},{8,6},{10,8},{12,10},{14,12},{15,14},{13,15},{11... | collective-permute-start | bytes 589832 | tf_op jit(solution)/shard_map/ppermute | solution.py:506
  20.5 3.9 %collective-permute-start.6 = (bf16[256,384]{1,0:T(8,128)(2,1)S(1)}, bf16[256,384]{1,0:T(8,128)(2,1)S(1)}, u32[]{:S(2)}, u32[]{:S(2)}) collective-permute-start(bf16[256,384]{1,0:T(8,128)(2,1)S(1)} %get-tuple-element.85), channel_id=1, source_target_pairs={{0,1},{1,0},{2,3},{3,2},{4,5},{5,4},{6,7},{7,6},{8,9},{9,8},{10,11... | collective-permute-start | bytes 589832 | tf_op jit(solution)/shard_map/ppermute | solution.py:506
  24.4 9.1 %collective-permute-start.7 = (bf16[256,384]{1,0:T(8,128)(2,1)S(1)}, bf16[256,384]{1,0:T(8,128)(2,1)S(1)}, u32[]{:S(2)}, u32[]{:S(2)}) collective-permute-start(bf16[256,384]{1,0:T(8,128)(2,1)S(1)} %add_convert_fusion), channel_id=1, source_target_pairs={{3,1},{5,3},{7,5},{9,7},{11,9},{13,11},{15,13},{14,15},{12,14},{10... | collective-permute-start | bytes 589832 | tf_op jit(solution)/shard_map/ppermute | solution.py:506
  30.4 3.2 %collective-permute-start.5 = (bf16[256,384]{1,0:T(8,128)(2,1)S(1)}, bf16[256,384]{1,0:T(8,128)(2,1)S(1)}, u32[]{:S(2)}, u32[]{:S(2)}) collective-permute-start(bf16[256,384]{1,0:T(8,128)(2,1)S(1)} %get-tuple-element.81), channel_id=1, source_target_pairs={{0,1},{1,0},{2,3},{3,2},{4,5},{5,4},{6,7},{7,6},{8,9},{9,8},{10,11... | collective-permute-start | bytes 589832 | tf_op jit(solution)/shard_map/ppermute | solution.py:506

commit v15 on v14

--- a/solution.py
+++ b/solution.py
@@ -19,6 +19,7 @@
 VMEM = pl.BlockSpec(memory_space=pltpu.VMEM)
 HBM = pl.BlockSpec(memory_space=pltpu.HBM)
 CHUNK = 128
+RUN = 3
 
 
 def dot_nt(a, b):
@@ -155,6 +156,23 @@
     return slice(start * CHUNK, (start + count) * CHUNK)
 
 
+def run_length(run):
+    return run[-1].stop - run[-1].start
+
+
+def runs_of(chunks):
+    runs = []
+    for chunk in chunks:
+        if runs:
+            last = runs[-1]
+            length = run_length(last)
+            if last[1] is chunk[1] and last[2] + length == chunk[2] and length < RUN * CHUNK:
+                runs[-1] = (*last[:-1], slice(last[-1].start, chunk[-1].stop))
+                continue
+        runs.append(chunk)
+    return runs
+
+
 def exponentials(jobs, rows, heads, scores):
     back = 2 * rows
     wide = heads * TQ
@@ -164,12 +182,13 @@
         step, chunks, (query_t, _, documents), _, _ = jobs[job]
         chunk, keys, row = chunks[index][0:3]
         tile = slice(step * wide, (step + 1) * wide)
-        window = slice(step * TQ + chunk * CHUNK, step * TQ + (chunk + 1) * CHUNK)
+        length = run_length(chunks[index])
+        window = slice(step * TQ + chunk * CHUNK, step * TQ + chunk * CHUNK + length)
         product = dot_nn(
-            jnp.concatenate([keys[row : row + CHUNK, :], documents[window, :]], axis=1),
+            jnp.concatenate([keys[row : row + length, :], documents[window, :]], axis=1),
             query_t[:, tile],
         )
-        for start in range(0, CHUNK, GROUP):
+        for start in range(0, length, GROUP):
             place = chunk * CHUNK + start
             for h in range(heads):
                 lanes = slice(h * TQ, (h + 1) * TQ)
@@ -202,8 +221,9 @@
         total = jnp.zeros((8, wide), jnp.float32)
         delta = jnp.zeros((8, wide), jnp.float32)
         for index, (chunk, keys, row, weights, dprobs, kept) in enumerate(chunks):
-            product = dot_nn(keys[rows + row : rows + row + CHUNK, :], dout_t[:, tile])
-            for start in range(0, CHUNK, GROUP):
+            length = kept.stop - kept.start
+            product = dot_nn(keys[rows + row : rows + row + length, :], dout_t[:, tile])
+            for start in range(0, length, GROUP):
                 place = chunk * CHUNK + start
                 there = slice(kept.start + start, kept.start + start + GROUP)
                 dprob = product[start : start + GROUP, :]
@@ -242,7 +262,7 @@
             for kind, value in enumerate(found):
                 stats[8 * kind + step : 8 * kind + step + 1, :] = value
 
-        jobs.append((step, chunks, (query_t, dout_t, documents), None, end))
+        jobs.append((step, runs_of(chunks), (query_t, dout_t, documents), None, end))
     exponentials(jobs, rows, heads, scores)
 
 
@@ -330,7 +350,7 @@
             )
 
         first_max = early_stats[step : step + 1, :]
-        jobs.append((step, chunks, (query_t, dout_t, documents), first_max, end))
+        jobs.append((step, runs_of(chunks), (query_t, dout_t, documents), first_max, end))
     exponentials(jobs, rows, heads, scores)
     prev2_out[0:HD] = (dk[...] * SCALE).astype(prev2_out.dtype)
     prev2_out[HD : 2 * HD] = dv[...].astype(prev2_out.dtype)

time: 34.8 us -> 34.5 us (level)
  transfers between devices with their start and end apart: 8 -> 8, of which waited for: 2 -> 3; matrix products, arithmetic and copies ran while one was open for 0% -> 0% of each run, Pallas kernels for 42% -> 42%
where the time goes in v15:
time: 34.5 us; the launch traced here: 34.3 us
  starting transfers between devices  15.2 us (44%)
  Pallas kernels  15.2 us (44%)
  waiting for transfers between devices  1.85 us (5%)
  local copies, waits for them, and re-layouts  1.06 us (3%)
  between operations  0.8 us (2%)
    ppermute x8, starting transfers between devices, move(): return lax.ppermute(array, 'ctx', pairs)  15.2 us
    pallas_call x2, Pallas kernels, late_scores(): pl.pallas_call(functools.partial(late_kernel, rows, heads, slot), out_sha...  4.06 us
    pallas_call x1, Pallas kernels, block_outputs(): pl.pallas_call(functools.partial(outputs_kernel, rows, heads), out_shape=...  3.07 us
    pallas_call x2, Pallas kernels, rest_grads(): pl.pallas_call(functools.partial(grads_kernel, rows, heads, slots), out_s...  2.72 us
    pallas_call x1, Pallas kernels, prepare(): pl.pallas_call(functools.partial(prepare_kernel, rows, heads, doc_lengths...  2.23 us
    pallas_call x2, Pallas kernels, early_scores(): pl.pallas_call(functools.partial(early_kernel, rows, heads, slot), out_sh...  2.2 us
    ppermute x8, waiting for transfers between devices, move(): return lax.ppermute(array, 'ctx', pairs)  1.85 us
    slice x1, local copies, waits for them, and re-layouts, body(): upper = jnp.concatenate([key[rows:], value[rows:]], axis=0)  1.06 us
  transfers between devices with their start and end apart: 8, of which 3 were waited for; matrix products, arithmetic and copies ran while one was open for 0% of the time, Pallas kernels for 42%

profile of v15, /device:TPU:0, one launch (start us, length us, event | category | flops | bytes accessed | tf_op | source)
XLA Modules:
  0.0 34.3 jit_solution(17368721149606647064)
XLA Ops:
  0.6 1.1 %fusion = (bf16[384,128]{1,0:T(8,128)(2,1)S(1)}, bf16[384,128]{1,0:T(8,128)(2,1)S(1)}, bf16[384,128]{1,0:T(8,128)(2,1)S(1)}, bf16[384,128]{1,0:T(8,128)(2,1)S(1)}) fusion(bf16[768,128]{1,0:T(8,128)(2,1)} %param.6, bf16[768,128]{1,0:T(8,128)(2,1)} %param.7), kind=kLoop, calls=%fused_computation.6 | loop fusion | bytes 786432 | tf_op jit(solution)/shard_map/slice | solution.py:538
  1.7 0.1 broadcast_select_fusion
  1.8 0.7 %collective-permute-start = (bf16[768,128]{1,0:T(8,128)(2,1)S(1)}, bf16[768,128]{1,0:T(8,128)(2,1)S(1)}, u32[]{:S(2)}, u32[]{:S(2)}) collective-permute-start(bf16[768,128]{1,0:T(8,128)(2,1)S(1)} %get-tuple-element.88.refs_1_), channel_id=1, source_target_pairs={{1,2},{3,4},{5,6},{7,8},{9,10},{11,12},{13,14},{15,15},{14,13},{12... | collective-permute-start | bytes 589832 | tf_op jit(solution)/shard_map/ppermute | solution.py:526
  2.5 6.1 %collective-permute-start.2 = (bf16[768,128]{1,0:T(8,128)(2,1)S(1)}, bf16[768,128]{1,0:T(8,128)(2,1)S(1)}, u32[]{:S(2)}, u32[]{:S(2)}) collective-permute-start(bf16[768,128]{1,0:T(8,128)(2,1)S(1)} %get-tuple-element.89.refs_0_), channel_id=1, source_target_pairs={{0,2},{2,4},{4,6},{6,8},{8,10},{10,12},{12,14},{14,15},{15,13},{13... | collective-permute-start | bytes 589832 | tf_op jit(solution)/shard_map/ppermute | solution.py:526
  8.6 2.2 %prepare.1 = (bf16[768,128]{1,0:T(8,128)(2,1)S(1)}, bf16[256,1536]{1,0:T(8,128)(2,1)S(1)}, bf16[128,1536]{1,0:T(8,128)(2,1)S(1)}, bf16[1152,128]{1,0:T(8,128)(2,...) custom-call(bf16[768,128]{1,0:T(8,128)(2,1)S(1)} %get-tuple-element., ...), custom_call_target="tpu_custom_call" | custom-call | bytes 4194304 | tf_op jit(solution)/shard_map/prepare/pallas_call | solution.py:125
  10.9 0.1 collective-permute-start.1
  10.9 0.7 %early_far.1 = (bf16[768,512]{1,0:T(8,128)(2,1)S(1)}, bf16[768,512]{1,0:T(8,128)(2,1)S(1)}, f32[24,512]{1,0:T(8,128)S(1)}) custom-call(bf16[768,128]{1,0:T(8,128)(2,1)S(1)} %get-tuple-element.46.own_kv.refs_0_, bf16[256,1536]{1,0:T(8,128)(2,1)S(1)} %get-tuple-element.55.query_t.refs_5_.refs_0_, ...), custom_call_target="tpu_custom_call" | custom-call | flops 8589934592 | tf_op jit(solution)/shard_map/early_far/pallas_call | solution.py:274
  11.7 0.7 %collective-permute-done.1.refs_0_.prev1.refs_10_ = bf16[768,128]{1,0:T(8,128)(2,1)S(1)} collective-permute-done((bf16[768,128]{1,0:T(8,128)(2,1)S(1)}, bf16[768,128]{1,0:T(8,128)(2,1)S(1)}, u32[]{:S(2)}, u32[]{:S(2)}) %collective-permute-start.1) | collective-permute-done | bytes 196640 | tf_op jit(solution)/shard_map/ppermute | solution.py:526
  12.4 1.5 %early_near.1 = (bf16[1920,512]{1,0:T(8,128)(2,1)S(1)}, bf16[1920,512]{1,0:T(8,128)(2,1)S(1)}, f32[24,512]{1,0:T(8,128)S(1)}) custom-call(bf16[768,128]{1,0:T(8,128)(2,1)S(1)} %get-tuple-element.47.own_kv.refs_9_, bf16[256,1536]{1,0:T(8,128)(2,1)S(1)} %get-tuple-element.48.query_t.refs_0_, bf16[128,1536]{1,0:T(8,128)(2,1)S(1)} %get-tuple-element.49.dout_t.refs_1_, ...), custom_call_target="tpu_custom_call" | custom-call | tf_op jit(solution)/shard_map/early_near/pallas_call | solution.py:274
  13.9 0.0 collective-permute-done.prev1.refs_1_
  13.9 0.8 %collective-permute-start.3 = (bf16[768,128]{1,0:T(8,128)(2,1)S(1)}, bf16[768,128]{1,0:T(8,128)(2,1)S(1)}, u32[]{:S(2)}, u32[]{:S(2)}) collective-permute-start(bf16[768,128]{1,0:T(8,128)(2,1)S(1)} %collective-permute-done.prev1.refs_1_), channel_id=1, source_target_pairs={{0,1},{1,0},{2,3},{3,2},{4,5},{5,4},{6,7},{7,6},{8,9},{9,8},{10,11... | collective-permute-start | bytes 589832 | tf_op jit(solution)/shard_map/ppermute | solution.py:526
  14.6 1.0 %collective-permute-done.2.prev2.refs_2_ = bf16[768,128]{1,0:T(8,128)(2,1)S(1)} collective-permute-done((bf16[768,128]{1,0:T(8,128)(2,1)S(1)}, bf16[768,128]{1,0:T(8,128)(2,1)S(1)}, u32[]{:S(2)}, u32[]{:S(2)}) %collective-permute-start.2) | collective-permute-done | bytes 196640 | tf_op jit(solution)/shard_map/ppermute | solution.py:526
  15.6 2.6 %late_far.1 = (bf16[1920,512]{1,0:T(8,128)(2,1)S(1)}, bf16[1920,512]{1,0:T(8,128)(2,1)S(1)}, bf16[768,512]{1,0:T(8,128)(2,1)S(1)}, f32[24,512]{1,0:T(8,128)S(1)}, bf16[256,384]{1,0:T(8,128)(2,1)S(1)}) custom-call(bf16[256,1536]{1,0:T(8,128)(2,1)S(1)} %get-tuple-element.55.query_t.refs_5_.refs_0_, ...), custom_call_target="tpu_custom_call" | custom-call | flops 2147483648 | tf_op jit(solution)/shard_map/late_far/pallas_call | solution.py:365
  18.2 1.3 %collective-permute-start.4 = (bf16[256,384]{1,0:T(8,128)(2,1)S(1)}, bf16[256,384]{1,0:T(8,128)(2,1)S(1)}, u32[]{:S(2)}, u32[]{:S(2)}) collective-permute-start(bf16[256,384]{1,0:T(8,128)(2,1)S(1)} %get-tuple-element.80), channel_id=1, source_target_pairs={{2,0},{4,2},{6,4},{8,6},{10,8},{12,10},{14,12},{15,14},{13,15},{11... | collective-permute-start | bytes 589832 | tf_op jit(solution)/shard_map/ppermute | solution.py:526
  19.5 0.0 collective-permute-done.3.prev2.refs_11_
  19.5 0.8 %grads_far.1 = (bf16[1152,512]{1,0:T(8,128)(2,1)S(1)}, bf16[256,384]{1,0:T(8,128)(2,1)S(1)}) custom-call(bf16[256,1536]{1,0:T(8,128)(2,1)S(1)} %get-tuple-element.55.query_t.refs_5_.refs_0_, bf16[128,1536]{1,0:T(8,128)(2,1)S(1)} %get-tuple-element.56.dout_t.refs_6_.refs_1_, f32[24,512]{1,0:T(8,128)S(1)} %get-tuple-element.70.refs_7_.refs_2_, ...), custom_call_target="tpu_custom_call" | custom-call | tf_op jit(solution)/shard_map/grads_far/pallas_call | solution.py:433
  20.3 2.3 %collective-permute-start.6 = (bf16[256,384]{1,0:T(8,128)(2,1)S(1)}, bf16[256,384]{1,0:T(8,128)(2,1)S(1)}, u32[]{:S(2)}, u32[]{:S(2)}) collective-permute-start(bf16[256,384]{1,0:T(8,128)(2,1)S(1)} %get-tuple-element.85), channel_id=1, source_target_pairs={{0,1},{1,0},{2,3},{3,2},{4,5},{5,4},{6,7},{7,6},{8,9},{9,8},{10,11... | collective-permute-start | bytes 589832 | tf_op jit(solution)/shard_map/ppermute | solution.py:526
  22.7 1.5 %late_near.1 = (bf16[768,512]{1,0:T(8,128)(2,1)S(1)}, bf16[768,512]{1,0:T(8,128)(2,1)S(1)}, f32[24,512]{1,0:T(8,128)S(1)}, bf16[256,384]{1,0:T(8,128)(2,1)S(1)}) custom-call(bf16[256,1536]{1,0:T(8,128)(2,1)S(1)} %get-tuple-element.48.query_t.refs_0_, bf16[128,1536]{1,0:T(8,128)(2,1)S(1)} %get-tuple-element.49.dout_t.refs_1_, ...), custom_call_target="tpu_custom_call" | custom-call | flops 2147483648 | tf_op jit(solution)/shard_map/late_near/pallas_call | solution.py:365
  24.1 0.0 collective-permute-done.6
  24.1 0.1 add_convert_fusion
  24.2 3.9 %collective-permute-start.7 = (bf16[256,384]{1,0:T(8,128)(2,1)S(1)}, bf16[256,384]{1,0:T(8,128)(2,1)S(1)}, u32[]{:S(2)}, u32[]{:S(2)}) collective-permute-start(bf16[256,384]{1,0:T(8,128)(2,1)S(1)} %add_convert_fusion), channel_id=1, source_target_pairs={{3,1},{5,3},{7,5},{9,7},{11,9},{13,11},{15,13},{14,15},{12,14},{10... | collective-permute-start | bytes 589832 | tf_op jit(solution)/shard_map/ppermute | solution.py:526
  28.1 1.9 %grads_near.1 = (bf16[1920,512]{1,0:T(8,128)(2,1)S(1)}, bf16[256,384]{1,0:T(8,128)(2,1)S(1)}, f32[256,384]{1,0:T(8,128)S(1)}, bf16[768,512]{1,0:T(8,128)(2,1)S(1)}, f32[256,384]{1,0:T(8,128)S(1)}) custom-call(bf16[256,1536]{1,0:T(8,128)(2,1)S(1)} %get-tuple-element.48.query_t.refs_0_, bf16[128,1536]{1,0:T(8,128)(2,1)S(1)} %get-tuple-element.49.dout_t.refs_1_, ...), custom_call_target="tpu_custom_call" | custom-call | flops 2147483648 | tf_op jit(solution)/shard_map/grads_near/pallas_call | solution.py:433
  30.0 0.0 collective-permute-done.4.far_2
  30.0 0.1 collective-permute-start.5
  30.1 3.1 %block_outputs.1 = (bf16[768,512]{1,0:T(8,128)(2,1)}, bf16[768,512]{1,0:T(8,128)(2,1)}) custom-call(bf16[768,128]{1,0:T(8,128)(2,1)S(1)} %get-tuple-element.46.own_kv.refs_0_, bf16[768,128]{1,0:T(8,128)(2,1)S(1)} %collective-permute-done.prev1.refs_1_, bf16[768,128]{1,0:T(8,128)(2,1)S(1)} %collective-permute-done.2.prev2.refs_2_, ...), custom_call_target="tpu_custom_call" | custom-call | tf_op jit(solution)/shard_map/block_outputs/pallas_call | solution.py:486
  33.2 0.2 collective-permute-done.7
  33.4 0.0 collective-permute-done.5.far_1
  33.4 0.9 %total_grads.1 = (bf16[768,128]{1,0:T(8,128)(2,1)}, bf16[768,128]{1,0:T(8,128)(2,1)}) custom-call(f32[256,384]{1,0:T(8,128)S(1)} %get-tuple-element.78.far_own, bf16[256,384]{1,0:T(8,128)(2,1)S(1)} %collective-permute-done.5.far_1, bf16[256,384]{1,0:T(8,128)(2,1)S(1)} %collective-permute-done.4.far_2, f32[256,384]{1,0:T(8,128)S(1)} %convert_add_fusion.near), custom_call_target="tpu_custom_call" | custom-call | tf_op jit(solution)/shard_map/total_grads/pallas_call | solution.py:509
  (1 shorter events, 0.0 us)
Async XLA Ops:
  1.8 12.1 %collective-permute-start = (bf16[768,128]{1,0:T(8,128)(2,1)S(1)}, bf16[768,128]{1,0:T(8,128)(2,1)S(1)}, u32[]{:S(2)}, u32[]{:S(2)}) collective-permute-start(bf16[768,128]{1,0:T(8,128)(2,1)S(1)} %get-tuple-element.88.refs_1_), channel_id=1, source_target_pairs={{1,2},{3,4},{5,6},{7,8},{9,10},{11,12},{13,14},{15,15},{14,13},{12... | collective-permute-start | bytes 589832 | tf_op jit(solution)/shard_map/ppermute | solution.py:526
  2.5 13.1 %collective-permute-start.2 = (bf16[768,128]{1,0:T(8,128)(2,1)S(1)}, bf16[768,128]{1,0:T(8,128)(2,1)S(1)}, u32[]{:S(2)}, u32[]{:S(2)}) collective-permute-start(bf16[768,128]{1,0:T(8,128)(2,1)S(1)} %get-tuple-element.89.refs_0_), channel_id=1, source_target_pairs={{0,2},{2,4},{4,6},{6,8},{8,10},{10,12},{12,14},{14,15},{15,13},{13... | collective-permute-start | bytes 589832 | tf_op jit(solution)/shard_map/ppermute | solution.py:526
  10.9 1.5 %collective-permute-start.1 = (bf16[768,128]{1,0:T(8,128)(2,1)S(1)}, bf16[768,128]{1,0:T(8,128)(2,1)S(1)}, u32[]{:S(2)}, u32[]{:S(2)}) collective-permute-start(bf16[768,128]{1,0:T(8,128)(2,1)S(1)} %get-tuple-element.46.own_kv.refs_0_), channel_id=1, source_target_pairs={{0,1},{1,0},{2,3},{3,2},{4,5},{5,4},{6,7},{7,6},{8,9},{9,8},{10,11... | collective-permute-start | bytes 589832 | tf_op jit(solution)/shard_map/ppermute | solution.py:526
  13.9 5.6 %collective-permute-start.3 = (bf16[768,128]{1,0:T(8,128)(2,1)S(1)}, bf16[768,128]{1,0:T(8,128)(2,1)S(1)}, u32[]{:S(2)}, u32[]{:S(2)}) collective-permute-start(bf16[768,128]{1,0:T(8,128)(2,1)S(1)} %collective-permute-done.prev1.refs_1_), channel_id=1, source_target_pairs={{0,1},{1,0},{2,3},{3,2},{4,5},{5,4},{6,7},{7,6},{8,9},{9,8},{10,11... | collective-permute-start | bytes 589832 | tf_op jit(solution)/shard_map/ppermute | solution.py:526
  18.2 11.8 %collective-permute-start.4 = (bf16[256,384]{1,0:T(8,128)(2,1)S(1)}, bf16[256,384]{1,0:T(8,128)(2,1)S(1)}, u32[]{:S(2)}, u32[]{:S(2)}) collective-permute-start(bf16[256,384]{1,0:T(8,128)(2,1)S(1)} %get-tuple-element.80), channel_id=1, source_target_pairs={{2,0},{4,2},{6,4},{8,6},{10,8},{12,10},{14,12},{15,14},{13,15},{11... | collective-permute-start | bytes 589832 | tf_op jit(solution)/shard_map/ppermute | solution.py:526
  20.3 3.8 %collective-permute-start.6 = (bf16[256,384]{1,0:T(8,128)(2,1)S(1)}, bf16[256,384]{1,0:T(8,128)(2,1)S(1)}, u32[]{:S(2)}, u32[]{:S(2)}) collective-permute-start(bf16[256,384]{1,0:T(8,128)(2,1)S(1)} %get-tuple-element.85), channel_id=1, source_target_pairs={{0,1},{1,0},{2,3},{3,2},{4,5},{5,4},{6,7},{7,6},{8,9},{9,8},{10,11... | collective-permute-start | bytes 589832 | tf_op jit(solution)/shard_map/ppermute | solution.py:526
  24.2 9.1 %collective-permute-start.7 = (bf16[256,384]{1,0:T(8,128)(2,1)S(1)}, bf16[256,384]{1,0:T(8,128)(2,1)S(1)}, u32[]{:S(2)}, u32[]{:S(2)}) collective-permute-start(bf16[256,384]{1,0:T(8,128)(2,1)S(1)} %add_convert_fusion), channel_id=1, source_target_pairs={{3,1},{5,3},{7,5},{9,7},{11,9},{13,11},{15,13},{14,15},{12,14},{10... | collective-permute-start | bytes 589832 | tf_op jit(solution)/shard_map/ppermute | solution.py:526
  30.0 3.4 %collective-permute-start.5 = (bf16[256,384]{1,0:T(8,128)(2,1)S(1)}, bf16[256,384]{1,0:T(8,128)(2,1)S(1)}, u32[]{:S(2)}, u32[]{:S(2)}) collective-permute-start(bf16[256,384]{1,0:T(8,128)(2,1)S(1)} %get-tuple-element.81), channel_id=1, source_target_pairs={{0,1},{1,0},{2,3},{3,2},{4,5},{5,4},{6,7},{7,6},{8,9},{9,8},{10,11... | collective-permute-start | bytes 589832 | tf_op jit(solution)/shard_map/ppermute | solution.py:526

commit v16 on v15

--- a/solution.py
+++ b/solution.py
@@ -144,10 +144,11 @@
         self.tiles = rows // TQ
         self.chunks = 2 * self.tiles + 1
         self.steps = range(self.tiles)
-        self.first = [self.tiles - step for step in self.steps]
-        self.late = [first + (1 - slot) * self.tiles for first in self.first]
-        self.early = [self.chunks - late for late in self.late]
-        self.middle = [late - first for late, first in zip(self.late, self.first)]
+        self.late = [self.tiles - step for step in self.steps]
+        self.middle = [(1 - slot) * self.tiles for step in self.steps]
+        self.early = [
+            self.chunks - late - middle for late, middle in zip(self.late, self.middle)
+        ]
 
 
 def chunk_rows(counts, step, first=0, count=None):
@@ -244,43 +245,49 @@
     pending()
 
 
-def early_kernel(rows, heads, slot, own_kv, query_t, dout_t, documents, *refs):
+def group_kernel(rows, heads, slot, middle, query_t, dout_t, documents, *refs):
     (weights, dprobs, stats, scores) = refs[-4:]
-    prev1 = refs[0] if slot == 1 else None
+    prev1 = refs[0] if middle or slot == 1 else None
+    own_kv = None if middle else refs[slot]
     window = Window(rows, slot)
+    counts = window.middle if middle else window.early
     jobs = []
     for step in window.steps:
         chunks = []
-        for index in range(window.early[step]):
-            chunk = window.late[step] + index
+        for index in range(counts[step]):
+            chunk = window.late[step] + (0 if middle else window.middle[step]) + index
             row = step * TQ + chunk * CHUNK
             keys = own_kv if row >= 2 * rows else prev1
-            kept = chunk_rows(window.early, step, index, 1)
+            kept = chunk_rows(counts, step, index, 1)
             chunks.append((chunk, keys, row % rows, weights, dprobs, kept))
 
         def end(*found, step=step):
             for kind, value in enumerate(found):
                 stats[8 * kind + step : 8 * kind + step + 1, :] = value
 
-        jobs.append((step, runs_of(chunks), (query_t, dout_t, documents), None, end))
+        first_max = refs[1][step : step + 1, :] if middle else None
+        jobs.append((step, runs_of(chunks), (query_t, dout_t, documents), first_max, end))
     exponentials(jobs, rows, heads, scores)
 
 
-def early_scores(slot, ready, *prev1):
+def group_scores(slot, middle, ready, *operands):
     rows = ready[0].shape[0] // 2
     heads = ready[1].shape[1] // rows
     wide = heads * TQ
-    kept = jax.ShapeDtypeStruct((sum(Window(rows, slot).early) * CHUNK, wide), jnp.bfloat16)
+    window = Window(rows, slot)
+    counts = window.middle if middle else window.early
+    kept = jax.ShapeDtypeStruct((sum(counts) * CHUNK, wide), jnp.bfloat16)
+    cost = (0 if slot else 2**33) if not middle else 0
     return pl.pallas_call(
-        functools.partial(early_kernel, rows, heads, slot),
+        functools.partial(group_kernel, rows, heads, slot, middle),
         out_shape=(kept, kept, jax.ShapeDtypeStruct((24, wide), jnp.float32)),
-        in_specs=[VMEM] * (4 + len(prev1)),
+        in_specs=[VMEM] * (3 + len(operands)),
         out_specs=[VMEM] * 3,
         scratch_shapes=[pltpu.VMEM((2, 2 * rows + TQ, wide), jnp.float32)],
         compiler_params=pltpu.CompilerParams(vmem_limit_bytes=VMEM_LIMIT),
-        cost_estimate=pl.CostEstimate(flops=0 if slot else 2**33, bytes_accessed=0, transcendentals=0),
-        name="early_far" if slot == 0 else "early_near",
-    )(*ready, *prev1)
+        cost_estimate=pl.CostEstimate(flops=cost, bytes_accessed=0, transcendentals=0),
+        name="middle_far" if middle else "early_far" if slot == 0 else "early_near",
+    )(*ready[1:4], *operands)
 
 
 def scaled_by(array, tile, factor):
@@ -304,109 +311,100 @@
             total_ref[:, columns] += term
 
 
-def late_kernel(
-    rows,
-    heads,
-    slot,
-    query_t,
-    dout_t,
-    documents,
-    early_stats,
-    prev1,
-    prev2,
-    weights,
-    *refs,
-):
-    (dprobs, dscores, stats, prev2_out, scores, dk, dv) = refs if slot == 0 else refs[-1:] + refs[:-1]
+def late_kernel(rows, heads, slot, query_t, dout_t, documents, prev2, *refs):
+    groups = refs[0 : 2 - slot]
+    (weights, dscores, stats, prev2_out, scores, dprobs, dk, dv) = refs[2 - slot :]
     wide = heads * TQ
     window = Window(rows, slot)
     jobs = []
     for step in window.steps:
         chunks = []
         for chunk in range(window.late[step]):
-            row = step * TQ + chunk * CHUNK
             kept = chunk_rows(window.late, step, chunk, 1)
-            chunks.append((chunk, (prev2, prev1)[row // rows], row % rows, weights, dprobs, kept))
+            chunks.append((chunk, prev2, step * TQ + chunk * CHUNK, weights, dprobs, kept))
 
         def end(row_max, total, delta, step=step):
             tile = slice(step * wide, (step + 1) * wide)
-            early = [early_stats[8 * kind + step : 8 * kind + step + 1, :] for kind in range(3)]
-            shrink = jnp.exp2(early[0] - row_max)
-            late_factor = 1.0 / (total + early[1] * shrink)
-            early_factor = late_factor * shrink
-            delta = delta * late_factor + early[2] * early_factor
-            for kind, value in enumerate((late_factor, early_factor, delta)):
+            rows_of = [
+                [group[8 * kind + step : 8 * kind + step + 1, :] for kind in range(3)]
+                for group in groups
+            ]
+            shrinks = [jnp.exp2(found[0] - row_max) for found in rows_of]
+            for found, shrink in zip(rows_of, shrinks):
+                total = total + found[1] * shrink
+                delta = delta + found[2] * shrink
+            late_factor = 1.0 / total
+            delta = delta * late_factor
+            factors = [late_factor * shrink for shrink in shrinks]
+            for kind, value in enumerate((late_factor, factors[0], delta, factors[-1])):
                 stats[8 * kind + step : 8 * kind + step + 1, :] = value
-            kept = chunk_rows(window.late, step, 0, window.first[step])
-            there = chunk_rows(window.first, step)
-            dscore_rows(dscores, there, weights, dprobs, kept, delta.astype(jnp.bfloat16))
+            there = chunk_rows(window.late, step)
+            dscore_rows(dscores, there, weights, dprobs, there, delta.astype(jnp.bfloat16))
             add_products(
                 step == 0,
                 slice(step * TQ, rows),
                 (
-                    (dv, scaled_by(dout_t, tile, late_factor), weights[kept, :]),
+                    (dv, scaled_by(dout_t, tile, late_factor), weights[there, :]),
                     (dk, scaled_by(query_t, tile, late_factor), dscores[there, :]),
                 ),
             )
 
-        first_max = early_stats[step : step + 1, :]
+        first_max = groups[-1][step : step + 1, :]
         jobs.append((step, runs_of(chunks), (query_t, dout_t, documents), first_max, end))
     exponentials(jobs, rows, heads, scores)
     prev2_out[0:HD] = (dk[...] * SCALE).astype(prev2_out.dtype)
     prev2_out[HD : 2 * HD] = dv[...].astype(prev2_out.dtype)
 
 
-def late_scores(slot, ready, early, prev1, prev2):
+def late_scores(slot, ready, groups, prev2):
     rows = prev2.shape[0] // 2
     heads = ready[1].shape[1] // rows
     wide = heads * TQ
-    window = Window(rows, slot)
-    late = jax.ShapeDtypeStruct((sum(window.late) * CHUNK, wide), jnp.bfloat16)
+    late = jax.ShapeDtypeStruct((sum(Window(rows, slot).late) * CHUNK, wide), jnp.bfloat16)
     return pl.pallas_call(
         functools.partial(late_kernel, rows, heads, slot),
         out_shape=(
-            *([late] * (2 - slot)),
-            jax.ShapeDtypeStruct((sum(window.first) * CHUNK, wide), jnp.bfloat16),
-            jax.ShapeDtypeStruct((24, wide), jnp.float32),
+            late,
+            late,
+            jax.ShapeDtypeStruct((32, wide), jnp.float32),
             jax.ShapeDtypeStruct((2 * HD, rows), jnp.bfloat16),
         ),
-        in_specs=[VMEM] * 6,
-        out_specs=[VMEM] * (5 - slot),
+        in_specs=[VMEM] * (4 + len(groups)),
+        out_specs=[VMEM] * 4,
         scratch_shapes=[
-            pltpu.VMEM((2, max(window.late) * CHUNK, wide), jnp.float32),
+            pltpu.VMEM((2, rows, wide), jnp.float32),
+            pltpu.VMEM(late.shape, late.dtype),
             pltpu.VMEM((HD, rows), jnp.float32),
             pltpu.VMEM((HD, rows), jnp.float32),
-            *([pltpu.VMEM(late.shape, late.dtype)] * slot),
         ],
         compiler_params=pltpu.CompilerParams(vmem_limit_bytes=VMEM_LIMIT),
         cost_estimate=pl.CostEstimate(flops=2**31, bytes_accessed=0, transcendentals=0),
         name="late_far" if slot == 0 else "late_near",
-    )(*ready[1:4], early[2], prev1, prev2)
+    )(*ready[1:4], prev2, *groups)
 
 
 def grads_kernel(rows, heads, slots, *refs):
     wide = heads * TQ
     outs = list(refs[5 * len(slots) : -2])
     (dk, dv) = refs[-2:]
-    for part, (slot, late) in enumerate(slots):
+    for part, (slot, middle) in enumerate(slots):
         (query_t, dout_t, stats, weights, dprobs) = refs[5 * part : 5 * part + 5]
         dscores = outs.pop(0)
         window = Window(rows, slot)
-        counts = window.middle if late else window.early
+        counts = window.middle if middle else window.early
         for step in reversed(window.steps):
             tile = slice(step * wide, (step + 1) * wide)
-            late_factor, early_factor, delta = (
-                stats[8 * kind + step : 8 * kind + step + 1, :] for kind in range(3)
+            _, early_factor, delta, middle_factor = (
+                stats[8 * kind + step : 8 * kind + step + 1, :] for kind in range(4)
             )
-            factor = late_factor if late else early_factor
+            factor = middle_factor if middle else early_factor
             there = chunk_rows(counts, step)
-            kept = chunk_rows(window.late, step, window.first[step]) if late else there
-            dscore_rows(dscores, there, weights, dprobs, kept, delta.astype(jnp.bfloat16))
+            dscore_rows(dscores, there, weights, dprobs, there, delta.astype(jnp.bfloat16))
             add_products(
                 step == window.tiles - 1,
                 slice(0, counts[step] * CHUNK),
                 (
-                    (dv, scaled_by(dout_t, tile, factor), weights[kept, :]),
+                    (dv, scaled_by(dout_t, tile, factor), weights[there, :]),
                     (dk, scaled_by(query_t, tile, factor), dscores[there, :]),
                 ),
             )
@@ -421,9 +419,9 @@
     rows = parts[0][2][0].shape[0] // 2
     heads = parts[0][2][1].shape[1] // rows
     operands, out_shape = [], []
-    for slot, late, (_, query_t, dout_t, _, stats, weights, dprobs), sent in parts:
+    for slot, middle, (_, query_t, dout_t, _, stats, weights, dprobs), sent in parts:
         window = Window(rows, slot)
-        kept = (sum(window.middle if late else window.early) * CHUNK, heads * TQ)
+        kept = (sum(window.middle if middle else window.early) * CHUNK, heads * TQ)
         operands += [query_t, dout_t, stats, weights, dprobs]
         out_shape.append(jax.ShapeDtypeStruct(kept, jnp.bfloat16))
         for one in sent:
@@ -443,37 +441,34 @@
 
 
 def outputs_kernel(rows, heads, *refs):
-    blocks = (refs[0:9], refs[9:17])
-    (attended, grad_query, keys_t, values_t) = refs[17:]
-    for slot, block in enumerate(blocks):
-        (own_kv, prev1, prev2, early_w, early_d, late_w, first_d, stats) = block[0:8]
+    blocks = (refs[0:3], refs[3:6], refs[6:9], refs[9]), (refs[10:13], refs[13:15], refs[15:17], refs[17])
+    (attended, grad_query, keys_t, values_t) = refs[18:]
+    for slot, (sources, weights, dscores, stats) in enumerate(blocks):
         window = Window(rows, slot)
+        groups = [(window.late, 0), (window.early, 1)]
+        if slot == 0:
+            groups.insert(1, (window.middle, 3))
         own_rows = half_start(rows, slot)
-        for place, source in enumerate((prev2, prev1, own_kv)):
+        for place, source in enumerate(sources):
             for tile in range(rows // TQ):
                 part = slice(place * rows + tile * TQ, place * rows + (tile + 1) * TQ)
                 row = tile * TQ
                 keys_t[:, part] = jnp.transpose(source[row : row + TQ, :])
                 values_t[:, part] = jnp.transpose(source[rows + row : rows + row + TQ, :])
         for step in window.steps:
-            first, late = window.first[step], window.late[step]
-
-            def product(side, terms, counts, start, skip, length):
-                columns = slice(step * TQ + start * CHUNK, step * TQ + (start + length) * CHUNK)
-                return dot_nn(side[:, columns], terms[chunk_rows(counts, step, skip, length), :])
-
-            early = window.chunks - late
-            late_factor = stats[step : step + 1, :]
-            early_factor = stats[8 + step : 8 + step + 1, :]
-            attended_t = product(values_t, late_w, window.late, 0, 0, late) * late_factor
-            attended_t += product(values_t, early_w, window.early, late, 0, early) * early_factor
-            late_t = product(keys_t, first_d, window.first, 0, 0, first)
-            if late > first:
-                late_t += product(keys_t, block[8], window.middle, first, 0, late - first)
-            early_t = product(keys_t, early_d, window.early, late, 0, early)
-            grad_query_t = late_t * (late_factor * SCALE) + early_t * (early_factor * SCALE)
             place = pl.ds(own_rows + step * TQ, TQ)
-            for out, found in ((attended, attended_t), (grad_query, grad_query_t)):
+            for out, side, terms, scale in (
+                (attended, values_t, weights, 1.0),
+                (grad_query, keys_t, dscores, SCALE),
+            ):
+                found = None
+                start = step * TQ
+                for (counts, kind), term in zip(groups, terms):
+                    columns = slice(start, start + counts[step] * CHUNK)
+                    start = columns.stop
+                    factor = stats[8 * kind + step : 8 * kind + step + 1, :] * scale
+                    part = dot_nn(side[:, columns], term[chunk_rows(counts, step), :]) * factor
+                    found = part if found is None else found + part
                 for h in range(heads):
                     part = found[:, h * TQ : (h + 1) * TQ]
                     out[place, h * HD : (h + 1) * HD] = jnp.transpose(part).astype(out.dtype)
@@ -486,7 +481,7 @@
     return pl.pallas_call(
         functools.partial(outputs_kernel, rows, heads),
         out_shape=(shape, shape),
-        in_specs=[VMEM] * 17,
+        in_specs=[VMEM] * 18,
         out_specs=[VMEM] * 2,
         scratch_shapes=[pltpu.VMEM((HD, 3 * rows), jnp.bfloat16)] * 2,
         compiler_params=pltpu.CompilerParams(vmem_limit_bytes=VMEM_LIMIT),
@@ -542,34 +537,45 @@
     prepared = prepare(count, doc_lengths, query, d_out, far_kv, near_kv)
     far_ready, near_ready = prepared[0:4], prepared[4:8]
     near_1 = move(far_ready[0], swap)
-    far_early = early_scores(0, far_ready)
-    near_early = early_scores(1, near_ready, near_1)
+    far_early = group_scores(0, False, far_ready, far_ready[0])
+    near_early = group_scores(1, False, near_ready, near_1, near_ready[0])
     far_1, near_early = lax.optimization_barrier((far_1, near_early))
-    far_late = late_scores(0, far_ready, far_early, far_1, far_2)
-    from_far_2 = move(far_late[-1], far_back)
+    far_middle = group_scores(0, True, far_ready, far_1, far_early[2])
+    far_late = late_scores(0, far_ready, (far_early[2], far_middle[2]), far_2)
+    from_far_2 = move(far_late[3], far_back)
     near_2 = move(far_1, swap)
-    near_2, far_stats = lax.optimization_barrier((near_2, far_late[-2]))
+    near_2, far_stats = lax.optimization_barrier((near_2, far_late[2]))
     far_middle_d, far_g1 = rest_grads(
-        "grads_far", 0, [(0, True, (*far_ready, far_stats, *far_late[0:2]), (True,))]
+        "grads_far", 0, [(0, True, (*far_ready, far_stats, *far_middle[0:2]), (True,))]
     )
     relayed = move(far_g1, swap)
-    near_late = late_scores(1, near_ready, near_early, near_1, near_2)
-    near_sum = near_late[-1].astype(jnp.float32) + relayed.astype(jnp.float32)
+    near_late = late_scores(1, near_ready, (near_early[2],), near_2)
+    near_sum = near_late[3].astype(jnp.float32) + relayed.astype(jnp.float32)
     from_near_2 = move(near_sum.astype(jnp.bfloat16), near_back)
     near_early_d, near_g1, near_own, far_early_d, far_own = rest_grads(
         "grads_near",
         2**31,
         [
-            (1, False, (*near_ready, near_late[-2], *near_early[0:2]), (True, False)),
-            (0, False, (*far_ready, far_late[-2], *far_early[0:2]), (False,)),
+            (1, False, (*near_ready, near_late[2], *near_early[0:2]), (True, False)),
+            (0, False, (*far_ready, far_late[2], *far_early[0:2]), (False,)),
         ],
     )
     near_g1, from_far_2 = lax.optimization_barrier((near_g1, from_far_2))
     from_near_1 = move(near_g1, swap)
     attended, grad_query = block_outputs(
         query,
-        (far_ready[0], far_1, far_2, far_early[0], far_early_d, far_late[0], *far_late[-3:-1], far_middle_d),
-        (near_ready[0], near_1, near_2, near_early[0], near_early_d, near_late[0], *near_late[-3:-1]),
+        (
+            *(far_2, far_1, far_ready[0]),
+            *(far_late[0], far_middle[0], far_early[0]),
+            *(far_late[1], far_middle_d, far_early_d),
+            far_late[2],
+        ),
+        (
+            *(near_2, near_1, near_ready[0]),
+            *(near_late[0], near_early[0]),
+            *(near_late[1], near_early_d),
+            near_late[2],
+        ),
     )
     near_total = near_own + from_near_2.astype(jnp.float32)
     grad_key, grad_value = total_grads(far_own, from_near_1, from_far_2, near_total)

time: 34.5 us -> 33.5 us (0.971)
  waiting for transfers between devices: 1.85 us -> 0.84 us
    pallas_call x2, Pallas kernels: 4.06 us -> 2.99 us  [late_scores(): pl.pallas_call(functools.partial(late_kernel, rows, heads, slot), out_sha...]
    ppermute x8, waiting for transfers between devices: 1.85 us -> 0.84 us  [move(): return lax.ppermute(array, 'ctx', pairs)]
    pallas_call x2 -> x3, Pallas kernels: 2.2 us -> 3.18 us  [group_scores(): pl.pallas_call(functools.partial(group_kernel, rows, heads, slot, middle)...]
  transfers between devices with their start and end apart: 8 -> 8, of which waited for: 3 -> 2; matrix products, arithmetic and copies ran while one was open for 0% -> 0% of each run, Pallas kernels for 42% -> 43%
where the time goes in v16:
time: 33.5 us; the launch traced here: 33.2 us
  starting transfers between devices  15.2 us (45%)
  Pallas kernels  15.2 us (45%)
  local copies, waits for them, and re-layouts  1.06 us (3%)
  waiting for transfers between devices  0.84 us (3%)
  between operations  0.81 us (2%)
    ppermute x8, starting transfers between devices, move(): return lax.ppermute(array, 'ctx', pairs)  15.2 us
    pallas_call x3, Pallas kernels, group_scores(): pl.pallas_call(functools.partial(group_kernel, rows, heads, slot, middle)...  3.18 us
    pallas_call x1, Pallas kernels, block_outputs(): pl.pallas_call(functools.partial(outputs_kernel, rows, heads), out_shape=...  3.13 us
    pallas_call x2, Pallas kernels, late_scores(): pl.pallas_call(functools.partial(late_kernel, rows, heads, slot), out_sha...  2.99 us
    pallas_call x2, Pallas kernels, rest_grads(): pl.pallas_call(functools.partial(grads_kernel, rows, heads, slots), out_s...  2.71 us
    pallas_call x1, Pallas kernels, prepare(): pl.pallas_call(functools.partial(prepare_kernel, rows, heads, doc_lengths...  2.23 us
    slice x1, local copies, waits for them, and re-layouts, body(): upper = jnp.concatenate([key[rows:], value[rows:]], axis=0)  1.06 us
    pallas_call x1, Pallas kernels, total_grads(): pl.pallas_call(functools.partial(total_kernel, rows), out_shape=(shape, s...  0.92 us
  transfers between devices with their start and end apart: 8, of which 2 were waited for; matrix products, arithmetic and copies ran while one was open for 0% of the time, Pallas kernels for 43%

profile of v16, /device:TPU:0, one launch (start us, length us, event | category | flops | bytes accessed | tf_op | source)
XLA Modules:
  0.0 33.2 jit_solution(7935528647400635890)
XLA Ops:
  0.6 1.1 %fusion = (bf16[384,128]{1,0:T(8,128)(2,1)S(1)}, bf16[384,128]{1,0:T(8,128)(2,1)S(1)}, bf16[384,128]{1,0:T(8,128)(2,1)S(1)}, bf16[384,128]{1,0:T(8,128)(2,1)S(1)}) fusion(bf16[768,128]{1,0:T(8,128)(2,1)} %param.6, bf16[768,128]{1,0:T(8,128)(2,1)} %param.7), kind=kLoop, calls=%fused_computation.6 | loop fusion | bytes 786432 | tf_op jit(solution)/shard_map/slice | solution.py:533
  1.7 0.1 broadcast_select_fusion
  1.8 0.7 %collective-permute-start.1 = (bf16[768,128]{1,0:T(8,128)(2,1)S(1)}, bf16[768,128]{1,0:T(8,128)(2,1)S(1)}, u32[]{:S(2)}, u32[]{:S(2)}) collective-permute-start(bf16[768,128]{1,0:T(8,128)(2,1)S(1)} %get-tuple-element.92.refs_1_), channel_id=1, source_target_pairs={{1,2},{3,4},{5,6},{7,8},{9,10},{11,12},{13,14},{15,15},{14,13},{12... | collective-permute-start | bytes 589832 | tf_op jit(solution)/shard_map/ppermute | solution.py:521
  2.5 6.1 %collective-permute-start = (bf16[768,128]{1,0:T(8,128)(2,1)S(1)}, bf16[768,128]{1,0:T(8,128)(2,1)S(1)}, u32[]{:S(2)}, u32[]{:S(2)}) collective-permute-start(bf16[768,128]{1,0:T(8,128)(2,1)S(1)} %get-tuple-element.93.refs_0_), channel_id=1, source_target_pairs={{0,2},{2,4},{4,6},{6,8},{8,10},{10,12},{12,14},{14,15},{15,13},{13... | collective-permute-start | bytes 589832 | tf_op jit(solution)/shard_map/ppermute | solution.py:521
  8.6 2.2 %prepare.1 = (bf16[768,128]{1,0:T(8,128)(2,1)S(1)}, bf16[256,1536]{1,0:T(8,128)(2,1)S(1)}, bf16[128,1536]{1,0:T(8,128)(2,1)S(1)}, bf16[1152,128]{1,0:T(8,128)(2,...) custom-call(bf16[768,128]{1,0:T(8,128)(2,1)S(1)} %get-tuple-element., ...), custom_call_target="tpu_custom_call" | custom-call | bytes 4194304 | tf_op jit(solution)/shard_map/prepare/pallas_call | solution.py:125
  10.9 0.1 collective-permute-start.2
  10.9 0.7 %early_far.1 = (bf16[768,512]{1,0:T(8,128)(2,1)S(1)}, bf16[768,512]{1,0:T(8,128)(2,1)S(1)}, f32[24,512]{1,0:T(8,128)S(1)}) custom-call(bf16[256,1536]{1,0:T(8,128)(2,1)S(1)} %get-tuple-element.57.query_t.refs_0_.refs_5_, bf16[128,1536]{1,0:T(8,128)(2,1)S(1)} %get-tuple-element.58.dout_t.refs_1_.refs_6_, bf16[1152,128]{1,0:T(8,128)(2,1)S(1)} %get-tuple-element.59.documents, ...), custom_call_target="tpu_custom_call" | custom-call | flops 8589934592 | tf_op jit(solution)/shard_map/early_far/pallas_call | solution.py:281
  11.7 0.7 %collective-permute-done.2.refs_0_.refs_11_ = bf16[768,128]{1,0:T(8,128)(2,1)S(1)} collective-permute-done((bf16[768,128]{1,0:T(8,128)(2,1)S(1)}, bf16[768,128]{1,0:T(8,128)(2,1)S(1)}, u32[]{:S(2)}, u32[]{:S(2)}) %collective-permute-start.2) | collective-permute-done | bytes 196640 | tf_op jit(solution)/shard_map/ppermute | solution.py:521
  12.4 1.5 %early_near.1 = (bf16[1920,512]{1,0:T(8,128)(2,1)S(1)}, bf16[1920,512]{1,0:T(8,128)(2,1)S(1)}, f32[24,512]{1,0:T(8,128)S(1)}) custom-call(bf16[256,1536]{1,0:T(8,128)(2,1)S(1)} %get-tuple-element.48.query_t.refs_0_, bf16[128,1536]{1,0:T(8,128)(2,1)S(1)} %get-tuple-element.49.dout_t.refs_1_, bf16[1152,128]{1,0:T(8,128)(2,1)S(1)} %get-tuple-element.50.documents, ...), custom_call_target="tpu_custom_call" | custom-call | tf_op jit(solution)/shard_map/early_near/pallas_call | solution.py:281
  13.9 0.0 collective-permute-done.1.refs_0_.refs_1_
  13.9 0.8 %collective-permute-start.3 = (bf16[768,128]{1,0:T(8,128)(2,1)S(1)}, bf16[768,128]{1,0:T(8,128)(2,1)S(1)}, u32[]{:S(2)}, u32[]{:S(2)}) collective-permute-start(bf16[768,128]{1,0:T(8,128)(2,1)S(1)} %collective-permute-done.1.refs_0_.refs_1_), channel_id=1, source_target_pairs={{0,1},{1,0},{2,3},{3,2},{4,5},{5,4},{6,7},{7,6},{8,9},{9,8},{10,11... | collective-permute-start | bytes 589832 | tf_op jit(solution)/shard_map/ppermute | solution.py:521
  14.6 1.0 %middle_far.1 = (bf16[1152,512]{1,0:T(8,128)(2,1)S(1)}, bf16[1152,512]{1,0:T(8,128)(2,1)S(1)}, f32[24,512]{1,0:T(8,128)S(1)}) custom-call(bf16[256,1536]{1,0:T(8,128)(2,1)S(1)} %get-tuple-element.57.query_t.refs_0_.refs_5_, bf16[128,1536]{1,0:T(8,128)(2,1)S(1)} %get-tuple-element.58.dout_t.refs_1_.refs_6_, ...), custom_call_target="tpu_custom_call" | custom-call | tf_op jit(solution)/shard_map/middle_far/pallas_call | solution.py:281
  15.6 0.0 collective-permute-done.prev2.refs_0_
  15.6 1.5 %late_far.1 = (bf16[768,512]{1,0:T(8,128)(2,1)S(1)}, bf16[768,512]{1,0:T(8,128)(2,1)S(1)}, f32[32,512]{1,0:T(8,128)S(1)}, bf16[256,384]{1,0:T(8,128)(2,1)S(1)}) custom-call(bf16[256,1536]{1,0:T(8,128)(2,1)S(1)} %get-tuple-element.57.query_t.refs_0_.refs_5_, bf16[128,1536]{1,0:T(8,128)(2,1)S(1)} %get-tuple-element.58.dout_t.refs_1_.refs_6_, ...), custom_call_target="tpu_custom_call" | custom-call | flops 2147483648 | tf_op jit(solution)/shard_map/late_far/pallas_call | solution.py:364
  17.1 1.3 %collective-permute-start.4 = (bf16[256,384]{1,0:T(8,128)(2,1)S(1)}, bf16[256,384]{1,0:T(8,128)(2,1)S(1)}, u32[]{:S(2)}, u32[]{:S(2)}) collective-permute-start(bf16[256,384]{1,0:T(8,128)(2,1)S(1)} %get-tuple-element.84), channel_id=1, source_target_pairs={{2,0},{4,2},{6,4},{8,6},{10,8},{12,10},{14,12},{15,14},{13,15},{11... | collective-permute-start | bytes 589832 | tf_op jit(solution)/shard_map/ppermute | solution.py:521
  18.4 0.0 collective-permute-done.3.prev2.refs_10_
  18.5 0.8 %grads_far.1 = (bf16[1152,512]{1,0:T(8,128)(2,1)S(1)}, bf16[256,384]{1,0:T(8,128)(2,1)S(1)}) custom-call(bf16[256,1536]{1,0:T(8,128)(2,1)S(1)} %get-tuple-element.57.query_t.refs_0_.refs_5_, bf16[128,1536]{1,0:T(8,128)(2,1)S(1)} %get-tuple-element.58.dout_t.refs_1_.refs_6_, f32[32,512]{1,0:T(8,128)S(1)} %get-tuple-element.67.refs_2_.refs_7_.refs_9_, ...), custom_call_target="tpu_custom_call" | custom-call | tf_op jit(solution)/shard_map/grads_far/pallas_call | solution.py:431
  19.3 3.3 %collective-permute-start.6 = (bf16[256,384]{1,0:T(8,128)(2,1)S(1)}, bf16[256,384]{1,0:T(8,128)(2,1)S(1)}, u32[]{:S(2)}, u32[]{:S(2)}) collective-permute-start(bf16[256,384]{1,0:T(8,128)(2,1)S(1)} %get-tuple-element.89), channel_id=1, source_target_pairs={{0,1},{1,0},{2,3},{3,2},{4,5},{5,4},{6,7},{7,6},{8,9},{9,8},{10,11... | collective-permute-start | bytes 589832 | tf_op jit(solution)/shard_map/ppermute | solution.py:521
  22.6 1.5 %late_near.1 = (bf16[768,512]{1,0:T(8,128)(2,1)S(1)}, bf16[768,512]{1,0:T(8,128)(2,1)S(1)}, f32[32,512]{1,0:T(8,128)S(1)}, bf16[256,384]{1,0:T(8,128)(2,1)S(1)}) custom-call(bf16[256,1536]{1,0:T(8,128)(2,1)S(1)} %get-tuple-element.48.query_t.refs_0_, bf16[128,1536]{1,0:T(8,128)(2,1)S(1)} %get-tuple-element.49.dout_t.refs_1_, ...), custom_call_target="tpu_custom_call" | custom-call | flops 2147483648 | tf_op jit(solution)/shard_map/late_near/pallas_call | solution.py:364
  24.1 0.0 collective-permute-done.6
  24.1 0.1 add_convert_fusion
  24.1 2.9 %collective-permute-start.7 = (bf16[256,384]{1,0:T(8,128)(2,1)S(1)}, bf16[256,384]{1,0:T(8,128)(2,1)S(1)}, u32[]{:S(2)}, u32[]{:S(2)}) collective-permute-start(bf16[256,384]{1,0:T(8,128)(2,1)S(1)} %add_convert_fusion), channel_id=1, source_target_pairs={{3,1},{5,3},{7,5},{9,7},{11,9},{13,11},{15,13},{14,15},{12,14},{10... | collective-permute-start | bytes 589832 | tf_op jit(solution)/shard_map/ppermute | solution.py:521
  27.0 1.9 %grads_near.1 = (bf16[1920,512]{1,0:T(8,128)(2,1)S(1)}, bf16[256,384]{1,0:T(8,128)(2,1)S(1)}, f32[256,384]{1,0:T(8,128)S(1)}, bf16[768,512]{1,0:T(8,128)(2,1)S(1)}, f32[256,384]{1,0:T(8,128)S(1)}) custom-call(bf16[256,1536]{1,0:T(8,128)(2,1)S(1)} %get-tuple-element.48.query_t.refs_0_, bf16[128,1536]{1,0:T(8,128)(2,1)S(1)} %get-tuple-element.49.dout_t.refs_1_, ...), custom_call_target="tpu_custom_call" | custom-call | flops 2147483648 | tf_op jit(solution)/shard_map/grads_near/pallas_call | solution.py:431
  28.9 0.0 collective-permute-done.4.far_2
  28.9 0.1 collective-permute-start.5
  29.0 3.1 %block_outputs.1 = (bf16[768,512]{1,0:T(8,128)(2,1)}, bf16[768,512]{1,0:T(8,128)(2,1)}) custom-call(bf16[768,128]{1,0:T(8,128)(2,1)S(1)} %collective-permute-done.prev2.refs_0_, bf16[768,128]{1,0:T(8,128)(2,1)S(1)} %collective-permute-done.1.refs_0_.refs_1_, bf16[768,128]{1,0:T(8,128)(2,1)S(1)} %get-tuple-element.51.refs_0_.refs_2_, ...), custom_call_target="tpu_custom_call" | custom-call | tf_op jit(solution)/shard_map/block_outputs/pallas_call | solution.py:481
  32.1 0.1 collective-permute-done.7
  32.3 0.0 collective-permute-done.5.far_1
  32.3 0.9 %total_grads.1 = (bf16[768,128]{1,0:T(8,128)(2,1)}, bf16[768,128]{1,0:T(8,128)(2,1)}) custom-call(f32[256,384]{1,0:T(8,128)S(1)} %get-tuple-element.82.far_own, bf16[256,384]{1,0:T(8,128)(2,1)S(1)} %collective-permute-done.5.far_1, bf16[256,384]{1,0:T(8,128)(2,1)S(1)} %collective-permute-done.4.far_2, f32[256,384]{1,0:T(8,128)S(1)} %convert_add_fusion.near), custom_call_target="tpu_custom_call" | custom-call | tf_op jit(solution)/shard_map/total_grads/pallas_call | solution.py:504
  (1 shorter events, 0.0 us)
Async XLA Ops:
  1.8 12.1 %collective-permute-start.1 = (bf16[768,128]{1,0:T(8,128)(2,1)S(1)}, bf16[768,128]{1,0:T(8,128)(2,1)S(1)}, u32[]{:S(2)}, u32[]{:S(2)}) collective-permute-start(bf16[768,128]{1,0:T(8,128)(2,1)S(1)} %get-tuple-element.92.refs_1_), channel_id=1, source_target_pairs={{1,2},{3,4},{5,6},{7,8},{9,10},{11,12},{13,14},{15,15},{14,13},{12... | collective-permute-start | bytes 589832 | tf_op jit(solution)/shard_map/ppermute | solution.py:521
  2.5 13.1 %collective-permute-start = (bf16[768,128]{1,0:T(8,128)(2,1)S(1)}, bf16[768,128]{1,0:T(8,128)(2,1)S(1)}, u32[]{:S(2)}, u32[]{:S(2)}) collective-permute-start(bf16[768,128]{1,0:T(8,128)(2,1)S(1)} %get-tuple-element.93.refs_0_), channel_id=1, source_target_pairs={{0,2},{2,4},{4,6},{6,8},{8,10},{10,12},{12,14},{14,15},{15,13},{13... | collective-permute-start | bytes 589832 | tf_op jit(solution)/shard_map/ppermute | solution.py:521
  10.9 1.5 %collective-permute-start.2 = (bf16[768,128]{1,0:T(8,128)(2,1)S(1)}, bf16[768,128]{1,0:T(8,128)(2,1)S(1)}, u32[]{:S(2)}, u32[]{:S(2)}) collective-permute-start(bf16[768,128]{1,0:T(8,128)(2,1)S(1)} %get-tuple-element.51.refs_0_.refs_2_), channel_id=1, source_target_pairs={{0,1},{1,0},{2,3},{3,2},{4,5},{5,4},{6,7},{7,6},{8,9},{9,8},{10,11... | collective-permute-start | bytes 589832 | tf_op jit(solution)/shard_map/ppermute | solution.py:521
  13.9 4.6 %collective-permute-start.3 = (bf16[768,128]{1,0:T(8,128)(2,1)S(1)}, bf16[768,128]{1,0:T(8,128)(2,1)S(1)}, u32[]{:S(2)}, u32[]{:S(2)}) collective-permute-start(bf16[768,128]{1,0:T(8,128)(2,1)S(1)} %collective-permute-done.1.refs_0_.refs_1_), channel_id=1, source_target_pairs={{0,1},{1,0},{2,3},{3,2},{4,5},{5,4},{6,7},{7,6},{8,9},{9,8},{10,11... | collective-permute-start | bytes 589832 | tf_op jit(solution)/shard_map/ppermute | solution.py:521
  17.1 11.8 %collective-permute-start.4 = (bf16[256,384]{1,0:T(8,128)(2,1)S(1)}, bf16[256,384]{1,0:T(8,128)(2,1)S(1)}, u32[]{:S(2)}, u32[]{:S(2)}) collective-permute-start(bf16[256,384]{1,0:T(8,128)(2,1)S(1)} %get-tuple-element.84), channel_id=1, source_target_pairs={{2,0},{4,2},{6,4},{8,6},{10,8},{12,10},{14,12},{15,14},{13,15},{11... | collective-permute-start | bytes 589832 | tf_op jit(solution)/shard_map/ppermute | solution.py:521
  19.3 4.8 %collective-permute-start.6 = (bf16[256,384]{1,0:T(8,128)(2,1)S(1)}, bf16[256,384]{1,0:T(8,128)(2,1)S(1)}, u32[]{:S(2)}, u32[]{:S(2)}) collective-permute-start(bf16[256,384]{1,0:T(8,128)(2,1)S(1)} %get-tuple-element.89), channel_id=1, source_target_pairs={{0,1},{1,0},{2,3},{3,2},{4,5},{5,4},{6,7},{7,6},{8,9},{9,8},{10,11... | collective-permute-start | bytes 589832 | tf_op jit(solution)/shard_map/ppermute | solution.py:521
  24.1 8.1 %collective-permute-start.7 = (bf16[256,384]{1,0:T(8,128)(2,1)S(1)}, bf16[256,384]{1,0:T(8,128)(2,1)S(1)}, u32[]{:S(2)}, u32[]{:S(2)}) collective-permute-start(bf16[256,384]{1,0:T(8,128)(2,1)S(1)} %add_convert_fusion), channel_id=1, source_target_pairs={{3,1},{5,3},{7,5},{9,7},{11,9},{13,11},{15,13},{14,15},{12,14},{10... | collective-permute-start | bytes 589832 | tf_op jit(solution)/shard_map/ppermute | solution.py:521
  28.9 3.4 %collective-permute-start.5 = (bf16[256,384]{1,0:T(8,128)(2,1)S(1)}, bf16[256,384]{1,0:T(8,128)(2,1)S(1)}, u32[]{:S(2)}, u32[]{:S(2)}) collective-permute-start(bf16[256,384]{1,0:T(8,128)(2,1)S(1)} %get-tuple-element.85), channel_id=1, source_target_pairs={{0,1},{1,0},{2,3},{3,2},{4,5},{5,4},{6,7},{7,6},{8,9},{9,8},{10,11... | collective-permute-start | bytes 589832 | tf_op jit(solution)/shard_map/ppermute | solution.py:521

commit v17 on v16

--- a/solution.py
+++ b/solution.py
@@ -383,6 +383,20 @@
     )(*ready[1:4], prev2, *groups)
 
 
+def gated_kernel(rows, heads, slots, core, *refs):
+    here = lax.axis_index("ctx") % 2 == core
+    count = 5 * len(slots)
+    given = len(refs) - count - 2 - 2 * len(slots)
+    pl.when(here)(lambda: grads_kernel(rows, heads, slots, *refs[0:count], *refs[count + given :]))
+
+    if given:
+
+        @pl.when(jnp.logical_not(here))
+        def _():
+            for source, out in zip(refs[count : count + given], refs[count + given :]):
+                out[...] = source[...]
+
+
 def grads_kernel(rows, heads, slots, *refs):
     wide = heads * TQ
     outs = list(refs[5 * len(slots) : -2])
@@ -415,7 +429,7 @@
             out[HD : 2 * HD] = dv[:, place].astype(out.dtype)
 
 
-def rest_grads(name, cost, parts):
+def rest_grads(name, cost, parts, core=None, given=()):
     rows = parts[0][2][0].shape[0] // 2
     heads = parts[0][2][1].shape[1] // rows
     operands, out_shape = [], []
@@ -428,8 +442,12 @@
             kind = jnp.bfloat16 if one else jnp.float32
             out_shape.append(jax.ShapeDtypeStruct((2 * HD, rows), kind))
     slots = tuple(part[0:2] for part in parts)
+    operands += given
+    kernel = functools.partial(grads_kernel, rows, heads, slots)
+    if core is not None:
+        kernel = functools.partial(gated_kernel, rows, heads, slots, core)
     return pl.pallas_call(
-        functools.partial(grads_kernel, rows, heads, slots),
+        kernel,
         out_shape=out_shape,
         in_specs=[VMEM] * len(operands),
         out_specs=[VMEM] * len(out_shape),
@@ -542,12 +560,13 @@
     far_1, near_early = lax.optimization_barrier((far_1, near_early))
     far_middle = group_scores(0, True, far_ready, far_1, far_early[2])
     far_late = late_scores(0, far_ready, (far_early[2], far_middle[2]), far_2)
-    from_far_2 = move(far_late[3], far_back)
     near_2 = move(far_1, swap)
-    near_2, far_stats = lax.optimization_barrier((near_2, far_late[2]))
-    far_middle_d, far_g1 = rest_grads(
-        "grads_far", 0, [(0, True, (*far_ready, far_stats, *far_middle[0:2]), (True,))]
-    )
+    middle = [(0, True, (*far_ready, far_late[2], *far_middle[0:2]), (True,))]
+    odd_grads = rest_grads("grads_far_odd", 0, middle, 1)
+    far_g2, odd_grads = lax.optimization_barrier((far_late[3], odd_grads))
+    from_far_2 = move(far_g2, far_back)
+    near_2, odd_grads = lax.optimization_barrier((near_2, odd_grads))
+    far_middle_d, far_g1 = rest_grads("grads_far", 0, middle, 0, odd_grads)
     relayed = move(far_g1, swap)
     near_late = late_scores(1, near_ready, (near_early[2],), near_2)
     near_sum = near_late[3].astype(jnp.float32) + relayed.astype(jnp.float32)

time: 33.5 us -> 33.7 us (level)
    pallas_call x2 -> x3, Pallas kernels: 2.71 us -> 2.75 us  [rest_grads(): pl.pallas_call(kernel, out_shape=out_shape, in_specs=[VMEM] * len(operand...]
  transfers between devices with their start and end apart: 8 -> 8, of which waited for: 2 -> 1; matrix products, arithmetic and copies ran while one was open for 0% -> 0% of each run, Pallas kernels for 43% -> 43%
where the time goes in v17:
time: 33.7 us; the launch traced here: 33.4 us
  starting transfers between devices  15.4 us (46%)
  Pallas kernels  15.2 us (45%)
  local copies, waits for them, and re-layouts  1.06 us (3%)
  between operations  0.82 us (2%)
  waiting for transfers between devices  0.72 us (2%)
    ppermute x8, starting transfers between devices, move(): return lax.ppermute(array, 'ctx', pairs)  15.4 us
    pallas_call x3, Pallas kernels, group_scores(): pl.pallas_call(functools.partial(group_kernel, rows, heads, slot, middle)...  3.19 us
    pallas_call x1, Pallas kernels, block_outputs(): pl.pallas_call(functools.partial(outputs_kernel, rows, heads), out_shape=...  3.13 us
    pallas_call x2, Pallas kernels, late_scores(): pl.pallas_call(functools.partial(late_kernel, rows, heads, slot), out_sha...  2.99 us
    pallas_call x3, Pallas kernels, rest_grads(): pl.pallas_call(kernel, out_shape=out_shape, in_specs=[VMEM] * len(operand...  2.75 us
    pallas_call x1, Pallas kernels, prepare(): pl.pallas_call(functools.partial(prepare_kernel, rows, heads, doc_lengths...  2.23 us
    slice x1, local copies, waits for them, and re-layouts, body(): upper = jnp.concatenate([key[rows:], value[rows:]], axis=0)  1.06 us
    pallas_call x1, Pallas kernels, total_grads(): pl.pallas_call(functools.partial(total_kernel, rows), out_shape=(shape, s...  0.92 us
  transfers between devices with their start and end apart: 8, of which 1 were waited for; matrix products, arithmetic and copies ran while one was open for 0% of the time, Pallas kernels for 43%

profile of v17, /device:TPU:0, one launch (start us, length us, event | category | flops | bytes accessed | tf_op | source)
XLA Modules:
  0.0 33.4 jit_solution(2171936514955895487)
XLA Ops:
  0.6 1.1 %fusion = (bf16[384,128]{1,0:T(8,128)(2,1)S(1)}, bf16[384,128]{1,0:T(8,128)(2,1)S(1)}, bf16[384,128]{1,0:T(8,128)(2,1)S(1)}, bf16[384,128]{1,0:T(8,128)(2,1)S(1)}) fusion(bf16[768,128]{1,0:T(8,128)(2,1)} %param.6, bf16[768,128]{1,0:T(8,128)(2,1)} %param.7), kind=kLoop, calls=%fused_computation.6 | loop fusion | bytes 786432 | tf_op jit(solution)/shard_map/slice | solution.py:551
  1.7 0.1 broadcast_select_fusion
  1.8 0.7 %collective-permute-start.1 = (bf16[768,128]{1,0:T(8,128)(2,1)S(1)}, bf16[768,128]{1,0:T(8,128)(2,1)S(1)}, u32[]{:S(2)}, u32[]{:S(2)}) collective-permute-start(bf16[768,128]{1,0:T(8,128)(2,1)S(1)} %get-tuple-element.104.refs_1_), channel_id=1, source_target_pairs={{1,2},{3,4},{5,6},{7,8},{9,10},{11,12},{13,14},{15,15},{14,13},{12... | collective-permute-start | bytes 589832 | tf_op jit(solution)/shard_map/ppermute | solution.py:539
  2.5 6.1 %collective-permute-start = (bf16[768,128]{1,0:T(8,128)(2,1)S(1)}, bf16[768,128]{1,0:T(8,128)(2,1)S(1)}, u32[]{:S(2)}, u32[]{:S(2)}) collective-permute-start(bf16[768,128]{1,0:T(8,128)(2,1)S(1)} %get-tuple-element.105.refs_0_), channel_id=1, source_target_pairs={{0,2},{2,4},{4,6},{6,8},{8,10},{10,12},{12,14},{14,15},{15,13},{13... | collective-permute-start | bytes 589832 | tf_op jit(solution)/shard_map/ppermute | solution.py:539
  8.6 2.2 %prepare.1 = (bf16[768,128]{1,0:T(8,128)(2,1)S(1)}, bf16[256,1536]{1,0:T(8,128)(2,1)S(1)}, bf16[128,1536]{1,0:T(8,128)(2,1)S(1)}, bf16[1152,128]{1,0:T(8,128)(2,...) custom-call(bf16[768,128]{1,0:T(8,128)(2,1)S(1)} %get-tuple-element., ...), custom_call_target="tpu_custom_call" | custom-call | bytes 4194304 | tf_op jit(solution)/shard_map/prepare/pallas_call | solution.py:125
  10.9 0.1 collective-permute-start.2
  10.9 0.7 %early_far.1 = (bf16[768,512]{1,0:T(8,128)(2,1)S(1)}, bf16[768,512]{1,0:T(8,128)(2,1)S(1)}, f32[24,512]{1,0:T(8,128)S(1)}) custom-call(bf16[256,1536]{1,0:T(8,128)(2,1)S(1)} %get-tuple-element.63.query_t.refs_0_.refs_5_, bf16[128,1536]{1,0:T(8,128)(2,1)S(1)} %get-tuple-element.64.dout_t.refs_1_.refs_6_, bf16[1152,128]{1,0:T(8,128)(2,1)S(1)} %get-tuple-element.65.documents, ...), custom_call_target="tpu_custom_call" | custom-call | flops 8589934592 | tf_op jit(solution)/shard_map/early_far/pallas_call | solution.py:281
  11.7 0.7 %collective-permute-done.2.refs_0_.refs_11_ = bf16[768,128]{1,0:T(8,128)(2,1)S(1)} collective-permute-done((bf16[768,128]{1,0:T(8,128)(2,1)S(1)}, bf16[768,128]{1,0:T(8,128)(2,1)S(1)}, u32[]{:S(2)}, u32[]{:S(2)}) %collective-permute-start.2) | collective-permute-done | bytes 196640 | tf_op jit(solution)/shard_map/ppermute | solution.py:539
  12.4 1.5 %early_near.1 = (bf16[1920,512]{1,0:T(8,128)(2,1)S(1)}, bf16[1920,512]{1,0:T(8,128)(2,1)S(1)}, f32[24,512]{1,0:T(8,128)S(1)}) custom-call(bf16[256,1536]{1,0:T(8,128)(2,1)S(1)} %get-tuple-element.54.query_t.refs_0_, bf16[128,1536]{1,0:T(8,128)(2,1)S(1)} %get-tuple-element.55.dout_t.refs_1_, bf16[1152,128]{1,0:T(8,128)(2,1)S(1)} %get-tuple-element.56.documents, ...), custom_call_target="tpu_custom_call" | custom-call | tf_op jit(solution)/shard_map/early_near/pallas_call | solution.py:281
  13.9 0.0 collective-permute-done.1.refs_0_.refs_1_
  13.9 0.8 %collective-permute-start.3 = (bf16[768,128]{1,0:T(8,128)(2,1)S(1)}, bf16[768,128]{1,0:T(8,128)(2,1)S(1)}, u32[]{:S(2)}, u32[]{:S(2)}) collective-permute-start(bf16[768,128]{1,0:T(8,128)(2,1)S(1)} %collective-permute-done.1.refs_0_.refs_1_), channel_id=1, source_target_pairs={{0,1},{1,0},{2,3},{3,2},{4,5},{5,4},{6,7},{7,6},{8,9},{9,8},{10,11... | collective-permute-start | bytes 589832 | tf_op jit(solution)/shard_map/ppermute | solution.py:539
  14.6 1.0 %middle_far.1 = (bf16[1152,512]{1,0:T(8,128)(2,1)S(1)}, bf16[1152,512]{1,0:T(8,128)(2,1)S(1)}, f32[24,512]{1,0:T(8,128)S(1)}) custom-call(bf16[256,1536]{1,0:T(8,128)(2,1)S(1)} %get-tuple-element.63.query_t.refs_0_.refs_5_, bf16[128,1536]{1,0:T(8,128)(2,1)S(1)} %get-tuple-element.64.dout_t.refs_1_.refs_6_, ...), custom_call_target="tpu_custom_call" | custom-call | tf_op jit(solution)/shard_map/middle_far/pallas_call | solution.py:281
  15.6 0.0 collective-permute-done.prev2.refs_0_
  15.6 1.5 %late_far.1 = (bf16[768,512]{1,0:T(8,128)(2,1)S(1)}, bf16[768,512]{1,0:T(8,128)(2,1)S(1)}, f32[32,512]{1,0:T(8,128)S(1)}, bf16[256,384]{1,0:T(8,128)(2,1)S(1)}) custom-call(bf16[256,1536]{1,0:T(8,128)(2,1)S(1)} %get-tuple-element.63.query_t.refs_0_.refs_5_, bf16[128,1536]{1,0:T(8,128)(2,1)S(1)} %get-tuple-element.64.dout_t.refs_1_.refs_6_, ...), custom_call_target="tpu_custom_call" | custom-call | flops 2147483648 | tf_op jit(solution)/shard_map/late_far/pallas_call | solution.py:364
  17.2 1.3 %collective-permute-start.4 = (bf16[256,384]{1,0:T(8,128)(2,1)S(1)}, bf16[256,384]{1,0:T(8,128)(2,1)S(1)}, u32[]{:S(2)}, u32[]{:S(2)}) collective-permute-start(bf16[256,384]{1,0:T(8,128)(2,1)S(1)} %get-tuple-element.96), channel_id=1, source_target_pairs={{2,0},{4,2},{6,4},{8,6},{10,8},{12,10},{14,12},{15,14},{13,15},{11... | collective-permute-start | bytes 589832 | tf_op jit(solution)/shard_map/ppermute | solution.py:539
  18.5 0.0 collective-permute-done.3.prev2.refs_10_
  18.5 0.9 %grads_far.1 = (bf16[1152,512]{1,0:T(8,128)(2,1)S(1)}, bf16[256,384]{1,0:T(8,128)(2,1)S(1)}) custom-call(bf16[256,1536]{1,0:T(8,128)(2,1)S(1)} %get-tuple-element.63.query_t.refs_0_.refs_5_, bf16[128,1536]{1,0:T(8,128)(2,1)S(1)} %get-tuple-element.64.dout_t.refs_1_.refs_6_, f32[32,512]{1,0:T(8,128)S(1)} %get-tuple-element.72.refs_2_.refs_7_.refs_9_, ...), custom_call_target="tpu_custom_call" | custom-call | tf_op jit(solution)/shard_map/grads_far/pallas_call | solution.py:449
  19.3 3.4 %collective-permute-start.6 = (bf16[256,384]{1,0:T(8,128)(2,1)S(1)}, bf16[256,384]{1,0:T(8,128)(2,1)S(1)}, u32[]{:S(2)}, u32[]{:S(2)}) collective-permute-start(bf16[256,384]{1,0:T(8,128)(2,1)S(1)} %get-tuple-element.101), channel_id=1, source_target_pairs={{0,1},{1,0},{2,3},{3,2},{4,5},{5,4},{6,7},{7,6},{8,9},{9,8},{10,11... | collective-permute-start | bytes 589832 | tf_op jit(solution)/shard_map/ppermute | solution.py:539
  22.7 1.5 %late_near.1 = (bf16[768,512]{1,0:T(8,128)(2,1)S(1)}, bf16[768,512]{1,0:T(8,128)(2,1)S(1)}, f32[32,512]{1,0:T(8,128)S(1)}, bf16[256,384]{1,0:T(8,128)(2,1)S(1)}) custom-call(bf16[256,1536]{1,0:T(8,128)(2,1)S(1)} %get-tuple-element.54.query_t.refs_0_, bf16[128,1536]{1,0:T(8,128)(2,1)S(1)} %get-tuple-element.55.dout_t.refs_1_, ...), custom_call_target="tpu_custom_call" | custom-call | flops 2147483648 | tf_op jit(solution)/shard_map/late_near/pallas_call | solution.py:364
  24.2 0.0 collective-permute-done.6
  24.2 0.1 add_convert_fusion
  24.3 3.1 %collective-permute-start.7 = (bf16[256,384]{1,0:T(8,128)(2,1)S(1)}, bf16[256,384]{1,0:T(8,128)(2,1)S(1)}, u32[]{:S(2)}, u32[]{:S(2)}) collective-permute-start(bf16[256,384]{1,0:T(8,128)(2,1)S(1)} %add_convert_fusion), channel_id=1, source_target_pairs={{3,1},{5,3},{7,5},{9,7},{11,9},{13,11},{15,13},{14,15},{12,14},{10... | collective-permute-start | bytes 589832 | tf_op jit(solution)/shard_map/ppermute | solution.py:539
  27.4 1.9 %grads_near.1 = (bf16[1920,512]{1,0:T(8,128)(2,1)S(1)}, bf16[256,384]{1,0:T(8,128)(2,1)S(1)}, f32[256,384]{1,0:T(8,128)S(1)}, bf16[768,512]{1,0:T(8,128)(2,1)S(1)}, f32[256,384]{1,0:T(8,128)S(1)}) custom-call(bf16[256,1536]{1,0:T(8,128)(2,1)S(1)} %get-tuple-element.54.query_t.refs_0_, bf16[128,1536]{1,0:T(8,128)(2,1)S(1)} %get-tuple-element.55.dout_t.refs_1_, ...), custom_call_target="tpu_custom_call" | custom-call | flops 2147483648 | tf_op jit(solution)/shard_map/grads_near/pallas_call | solution.py:449
  29.2 0.0 collective-permute-done.4.far_2
  29.3 0.1 collective-permute-start.5
  29.3 3.1 %block_outputs.1 = (bf16[768,512]{1,0:T(8,128)(2,1)}, bf16[768,512]{1,0:T(8,128)(2,1)}) custom-call(bf16[768,128]{1,0:T(8,128)(2,1)S(1)} %collective-permute-done.prev2.refs_0_, bf16[768,128]{1,0:T(8,128)(2,1)S(1)} %collective-permute-done.1.refs_0_.refs_1_, bf16[768,128]{1,0:T(8,128)(2,1)S(1)} %get-tuple-element.57.refs_0_.refs_2_, ...), custom_call_target="tpu_custom_call" | custom-call | tf_op jit(solution)/shard_map/block_outputs/pallas_call | solution.py:499
  32.5 0.0 collective-permute-done.7
  32.5 0.0 collective-permute-done.5.far_1
  32.5 0.9 %total_grads.1 = (bf16[768,128]{1,0:T(8,128)(2,1)}, bf16[768,128]{1,0:T(8,128)(2,1)}) custom-call(f32[256,384]{1,0:T(8,128)S(1)} %get-tuple-element.94.far_own, bf16[256,384]{1,0:T(8,128)(2,1)S(1)} %collective-permute-done.5.far_1, bf16[256,384]{1,0:T(8,128)(2,1)S(1)} %collective-permute-done.4.far_2, f32[256,384]{1,0:T(8,128)S(1)} %convert_add_fusion.near), custom_call_target="tpu_custom_call" | custom-call | tf_op jit(solution)/shard_map/total_grads/pallas_call | solution.py:522
  (2 shorter events, 0.1 us)
Async XLA Ops:
  1.8 12.1 %collective-permute-start.1 = (bf16[768,128]{1,0:T(8,128)(2,1)S(1)}, bf16[768,128]{1,0:T(8,128)(2,1)S(1)}, u32[]{:S(2)}, u32[]{:S(2)}) collective-permute-start(bf16[768,128]{1,0:T(8,128)(2,1)S(1)} %get-tuple-element.104.refs_1_), channel_id=1, source_target_pairs={{1,2},{3,4},{5,6},{7,8},{9,10},{11,12},{13,14},{15,15},{14,13},{12... | collective-permute-start | bytes 589832 | tf_op jit(solution)/shard_map/ppermute | solution.py:539
  2.5 13.1 %collective-permute-start = (bf16[768,128]{1,0:T(8,128)(2,1)S(1)}, bf16[768,128]{1,0:T(8,128)(2,1)S(1)}, u32[]{:S(2)}, u32[]{:S(2)}) collective-permute-start(bf16[768,128]{1,0:T(8,128)(2,1)S(1)} %get-tuple-element.105.refs_0_), channel_id=1, source_target_pairs={{0,2},{2,4},{4,6},{6,8},{8,10},{10,12},{12,14},{14,15},{15,13},{13... | collective-permute-start | bytes 589832 | tf_op jit(solution)/shard_map/ppermute | solution.py:539
  10.9 1.5 %collective-permute-start.2 = (bf16[768,128]{1,0:T(8,128)(2,1)S(1)}, bf16[768,128]{1,0:T(8,128)(2,1)S(1)}, u32[]{:S(2)}, u32[]{:S(2)}) collective-permute-start(bf16[768,128]{1,0:T(8,128)(2,1)S(1)} %get-tuple-element.57.refs_0_.refs_2_), channel_id=1, source_target_pairs={{0,1},{1,0},{2,3},{3,2},{4,5},{5,4},{6,7},{7,6},{8,9},{9,8},{10,11... | collective-permute-start | bytes 589832 | tf_op jit(solution)/shard_map/ppermute | solution.py:539
  13.9 4.6 %collective-permute-start.3 = (bf16[768,128]{1,0:T(8,128)(2,1)S(1)}, bf16[768,128]{1,0:T(8,128)(2,1)S(1)}, u32[]{:S(2)}, u32[]{:S(2)}) collective-permute-start(bf16[768,128]{1,0:T(8,128)(2,1)S(1)} %collective-permute-done.1.refs_0_.refs_1_), channel_id=1, source_target_pairs={{0,1},{1,0},{2,3},{3,2},{4,5},{5,4},{6,7},{7,6},{8,9},{9,8},{10,11... | collective-permute-start | bytes 589832 | tf_op jit(solution)/shard_map/ppermute | solution.py:539
  17.2 12.1 %collective-permute-start.4 = (bf16[256,384]{1,0:T(8,128)(2,1)S(1)}, bf16[256,384]{1,0:T(8,128)(2,1)S(1)}, u32[]{:S(2)}, u32[]{:S(2)}) collective-permute-start(bf16[256,384]{1,0:T(8,128)(2,1)S(1)} %get-tuple-element.96), channel_id=1, source_target_pairs={{2,0},{4,2},{6,4},{8,6},{10,8},{12,10},{14,12},{15,14},{13,15},{11... | collective-permute-start | bytes 589832 | tf_op jit(solution)/shard_map/ppermute | solution.py:539
  19.3 4.9 %collective-permute-start.6 = (bf16[256,384]{1,0:T(8,128)(2,1)S(1)}, bf16[256,384]{1,0:T(8,128)(2,1)S(1)}, u32[]{:S(2)}, u32[]{:S(2)}) collective-permute-start(bf16[256,384]{1,0:T(8,128)(2,1)S(1)} %get-tuple-element.101), channel_id=1, source_target_pairs={{0,1},{1,0},{2,3},{3,2},{4,5},{5,4},{6,7},{7,6},{8,9},{9,8},{10,11... | collective-permute-start | bytes 589832 | tf_op jit(solution)/shard_map/ppermute | solution.py:539
  24.3 8.2 %collective-permute-start.7 = (bf16[256,384]{1,0:T(8,128)(2,1)S(1)}, bf16[256,384]{1,0:T(8,128)(2,1)S(1)}, u32[]{:S(2)}, u32[]{:S(2)}) collective-permute-start(bf16[256,384]{1,0:T(8,128)(2,1)S(1)} %add_convert_fusion), channel_id=1, source_target_pairs={{3,1},{5,3},{7,5},{9,7},{11,9},{13,11},{15,13},{14,15},{12,14},{10... | collective-permute-start | bytes 589832 | tf_op jit(solution)/shard_map/ppermute | solution.py:539
  29.3 3.3 %collective-permute-start.5 = (bf16[256,384]{1,0:T(8,128)(2,1)S(1)}, bf16[256,384]{1,0:T(8,128)(2,1)S(1)}, u32[]{:S(2)}, u32[]{:S(2)}) collective-permute-start(bf16[256,384]{1,0:T(8,128)(2,1)S(1)} %get-tuple-element.97), channel_id=1, source_target_pairs={{0,1},{1,0},{2,3},{3,2},{4,5},{5,4},{6,7},{7,6},{8,9},{9,8},{10,11... | collective-permute-start | bytes 589832 | tf_op jit(solution)/shard_map/ppermute | solution.py:539

commit v18 on v16

--- a/solution.py
+++ b/solution.py
@@ -174,7 +174,7 @@
     return runs
 
 
-def exponentials(jobs, rows, heads, scores):
+def exponentials(jobs, rows, heads, scores, scores_first=False):
     back = 2 * rows
     wide = heads * TQ
     base2 = SCALE * math.log2(math.e)
@@ -198,7 +198,7 @@
                     key_at = lax.broadcasted_iota(jnp.int32, (GROUP, TQ), 0) + (place - back)
                     query_at = lax.broadcasted_iota(jnp.int32, (GROUP, TQ), 1)
                     part = jnp.where(key_at <= query_at, part, masked_score)
-                scores[job % 2, place : place + GROUP, lanes] = part
+                scores[job % scores.shape[0], place : place + GROUP, lanes] = part
                 for row8 in range(0, GROUP, 8):
                     row_max[h] = jnp.maximum(row_max[h], part[row8 : row8 + 8, :])
 
@@ -206,18 +206,18 @@
         return [jnp.full((8, TQ), masked_score, jnp.float32)] * heads
 
     pending = None
-    following = start_max()
-    for index in range(len(jobs[0][1])):
-        score(0, index, following)
+    every = [start_max() for _ in jobs]
+    for job in range(len(jobs) if scores_first else 1):
+        for index in range(len(jobs[job][1])):
+            score(job, index, every[job])
     for job, (step, chunks, (_, dout_t, _), first_max, end) in enumerate(jobs):
         tile = slice(step * wide, (step + 1) * wide)
         row_max = jnp.concatenate(
-            [jnp.max(part, axis=0, keepdims=True) * base2 for part in following], axis=1
+            [jnp.max(part, axis=0, keepdims=True) * base2 for part in every[job]], axis=1
         )
         if first_max is not None:
             row_max = jnp.maximum(row_max, first_max)
-        following = start_max()
-        ahead = len(jobs[job + 1][1]) if job + 1 < len(jobs) else 0
+        ahead = len(jobs[job + 1][1]) if job + 1 < len(jobs) and not scores_first else 0
         done = 0
         total = jnp.zeros((8, wide), jnp.float32)
         delta = jnp.zeros((8, wide), jnp.float32)
@@ -229,14 +229,14 @@
                 there = slice(kept.start + start, kept.start + start + GROUP)
                 dprob = product[start : start + GROUP, :]
                 dprobs[there, :] = dprob.astype(jnp.bfloat16)
-                part = jnp.exp2(scores[job % 2, place : place + GROUP, :] * base2 - row_max)
+                part = jnp.exp2(scores[job % scores.shape[0], place : place + GROUP, :] * base2 - row_max)
                 weights[there, :] = part.astype(jnp.bfloat16)
                 term = part * dprob
                 for row8 in range(0, GROUP, 8):
                     total = total + part[row8 : row8 + 8, :]
                     delta = delta + term[row8 : row8 + 8, :]
             while done * len(chunks) < ahead * (index + 1):
-                score(job + 1, done, following)
+                score(job + 1, done, every[job + 1])
                 done += 1
             if index == 0 and pending is not None:
                 pending()
@@ -351,7 +351,7 @@
 
         first_max = groups[-1][step : step + 1, :]
         jobs.append((step, runs_of(chunks), (query_t, dout_t, documents), first_max, end))
-    exponentials(jobs, rows, heads, scores)
+    exponentials(jobs, rows, heads, scores, True)
     prev2_out[0:HD] = (dk[...] * SCALE).astype(prev2_out.dtype)
     prev2_out[HD : 2 * HD] = dv[...].astype(prev2_out.dtype)
 
@@ -372,7 +372,7 @@
         in_specs=[VMEM] * (4 + len(groups)),
         out_specs=[VMEM] * 4,
         scratch_shapes=[
-            pltpu.VMEM((2, rows, wide), jnp.float32),
+            pltpu.VMEM((rows // TQ, rows, wide), jnp.float32),
             pltpu.VMEM(late.shape, late.dtype),
             pltpu.VMEM((HD, rows), jnp.float32),
             pltpu.VMEM((HD, rows), jnp.float32),
@@ -442,7 +442,8 @@
 
 def outputs_kernel(rows, heads, *refs):
     blocks = (refs[0:3], refs[3:6], refs[6:9], refs[9]), (refs[10:13], refs[13:15], refs[15:17], refs[17])
-    (attended, grad_query, keys_t, values_t) = refs[18:]
+    (attended_hbm, grad_query_hbm, attended, grad_query, keys_t, values_t, sems) = refs[18:]
+    copies = []
     for slot, (sources, weights, dscores, stats) in enumerate(blocks):
         window = Window(rows, slot)
         groups = [(window.late, 0), (window.early, 1)]
@@ -458,8 +459,8 @@
         for step in window.steps:
             place = pl.ds(own_rows + step * TQ, TQ)
             for out, side, terms, scale in (
-                (attended, values_t, weights, 1.0),
-                (grad_query, keys_t, dscores, SCALE),
+                (0, values_t, weights, 1.0),
+                (1, keys_t, dscores, SCALE),
             ):
                 found = None
                 start = step * TQ
@@ -469,9 +470,18 @@
                     factor = stats[8 * kind + step : 8 * kind + step + 1, :] * scale
                     part = dot_nn(side[:, columns], term[chunk_rows(counts, step), :]) * factor
                     found = part if found is None else found + part
+                target = (attended_hbm, grad_query_hbm)[out]
+                source = (attended, grad_query)[out]
                 for h in range(heads):
-                    part = found[:, h * TQ : (h + 1) * TQ]
-                    out[place, h * HD : (h + 1) * HD] = jnp.transpose(part).astype(out.dtype)
+                    part = jnp.transpose(found[:, h * TQ : (h + 1) * TQ])
+                    source[place, h * HD : (h + 1) * HD] = part.astype(source.dtype)
+                copy = pltpu.make_async_copy(
+                    source.at[place], target.at[place], sems.at[slot, step, out]
+                )
+                copy.start()
+                copies.append(copy)
+    for copy in copies:
+        copy.wait()
 
 
 def block_outputs(query, far, near):
@@ -482,8 +492,10 @@
         functools.partial(outputs_kernel, rows, heads),
         out_shape=(shape, shape),
         in_specs=[VMEM] * 18,
-        out_specs=[VMEM] * 2,
-        scratch_shapes=[pltpu.VMEM((HD, 3 * rows), jnp.bfloat16)] * 2,
+        out_specs=[HBM] * 2,
+        scratch_shapes=[pltpu.VMEM(query.shape, query.dtype)] * 2
+        + [pltpu.VMEM((HD, 3 * rows), jnp.bfloat16)] * 2
+        + [pltpu.SemaphoreType.DMA((2, rows // TQ, 2))],
         compiler_params=pltpu.CompilerParams(vmem_limit_bytes=VMEM_LIMIT),
         cost_estimate=pl.CostEstimate(flops=0, bytes_accessed=0, transcendentals=0),
         name="block_outputs",

time: 33.5 us -> 33.4 us (level)
  transfers between devices with their start and end apart: 8 -> 8, of which waited for: 2 -> 2; matrix products, arithmetic and copies ran while one was open for 0% -> 0% of each run, Pallas kernels for 43% -> 42%
where the time goes in v18:
time: 33.4 us; the launch traced here: 33.2 us
  starting transfers between devices  15.2 us (46%)
  Pallas kernels  15 us (45%)
  local copies, waits for them, and re-layouts  1.06 us (3%)
  waiting for transfers between devices  1 us (3%)
  between operations  0.81 us (2%)
    ppermute x8, starting transfers between devices, move(): return lax.ppermute(array, 'ctx', pairs)  15.2 us
    pallas_call x3, Pallas kernels, group_scores(): pl.pallas_call(functools.partial(group_kernel, rows, heads, slot, middle)...  3.18 us
    pallas_call x1, Pallas kernels, block_outputs(): pl.pallas_call(functools.partial(outputs_kernel, rows, heads), out_shape=...  2.95 us
    pallas_call x2, Pallas kernels, late_scores(): pl.pallas_call(functools.partial(late_kernel, rows, heads, slot), out_sha...  2.95 us
    pallas_call x2, Pallas kernels, rest_grads(): pl.pallas_call(functools.partial(grads_kernel, rows, heads, slots), out_s...  2.72 us
    pallas_call x1, Pallas kernels, prepare(): pl.pallas_call(functools.partial(prepare_kernel, rows, heads, doc_lengths...  2.23 us
    slice x1, local copies, waits for them, and re-layouts, body(): upper = jnp.concatenate([key[rows:], value[rows:]], axis=0)  1.06 us
    ppermute x8, waiting for transfers between devices, move(): return lax.ppermute(array, 'ctx', pairs)  1 us
  transfers between devices with their start and end apart: 8, of which 2 were waited for; matrix products, arithmetic and copies ran while one was open for 0% of the time, Pallas kernels for 42%

profile of v18, /device:TPU:0, one launch (start us, length us, event | category | flops | bytes accessed | tf_op | source)
XLA Modules:
  0.0 33.2 jit_solution(2633739190248191636)
XLA Ops:
  0.6 1.1 %fusion = (bf16[384,128]{1,0:T(8,128)(2,1)S(1)}, bf16[384,128]{1,0:T(8,128)(2,1)S(1)}, bf16[384,128]{1,0:T(8,128)(2,1)S(1)}, bf16[384,128]{1,0:T(8,128)(2,1)S(1)}) fusion(bf16[768,128]{1,0:T(8,128)(2,1)} %param.6, bf16[768,128]{1,0:T(8,128)(2,1)} %param.7), kind=kLoop, calls=%fused_computation.6 | loop fusion | bytes 786432 | tf_op jit(solution)/shard_map/slice | solution.py:545
  1.7 0.1 broadcast_select_fusion
  1.8 0.7 %collective-permute-start.1 = (bf16[768,128]{1,0:T(8,128)(2,1)S(1)}, bf16[768,128]{1,0:T(8,128)(2,1)S(1)}, u32[]{:S(2)}, u32[]{:S(2)}) collective-permute-start(bf16[768,128]{1,0:T(8,128)(2,1)S(1)} %get-tuple-element.92.refs_1_), channel_id=1, source_target_pairs={{1,2},{3,4},{5,6},{7,8},{9,10},{11,12},{13,14},{15,15},{14,13},{12... | collective-permute-start | bytes 589832 | tf_op jit(solution)/shard_map/ppermute | solution.py:533
  2.5 6.1 %collective-permute-start = (bf16[768,128]{1,0:T(8,128)(2,1)S(1)}, bf16[768,128]{1,0:T(8,128)(2,1)S(1)}, u32[]{:S(2)}, u32[]{:S(2)}) collective-permute-start(bf16[768,128]{1,0:T(8,128)(2,1)S(1)} %get-tuple-element.93.refs_0_), channel_id=1, source_target_pairs={{0,2},{2,4},{4,6},{6,8},{8,10},{10,12},{12,14},{14,15},{15,13},{13... | collective-permute-start | bytes 589832 | tf_op jit(solution)/shard_map/ppermute | solution.py:533
  8.6 2.2 %prepare.1 = (bf16[768,128]{1,0:T(8,128)(2,1)S(1)}, bf16[256,1536]{1,0:T(8,128)(2,1)S(1)}, bf16[128,1536]{1,0:T(8,128)(2,1)S(1)}, bf16[1152,128]{1,0:T(8,128)(2,...) custom-call(bf16[768,128]{1,0:T(8,128)(2,1)S(1)} %get-tuple-element., ...), custom_call_target="tpu_custom_call" | custom-call | bytes 4194304 | tf_op jit(solution)/shard_map/prepare/pallas_call | solution.py:125
  10.9 0.1 collective-permute-start.2
  10.9 0.7 %early_far.1 = (bf16[768,512]{1,0:T(8,128)(2,1)S(1)}, bf16[768,512]{1,0:T(8,128)(2,1)S(1)}, f32[24,512]{1,0:T(8,128)S(1)}) custom-call(bf16[256,1536]{1,0:T(8,128)(2,1)S(1)} %get-tuple-element.57.query_t.refs_0_.refs_5_, bf16[128,1536]{1,0:T(8,128)(2,1)S(1)} %get-tuple-element.58.dout_t.refs_1_.refs_6_, bf16[1152,128]{1,0:T(8,128)(2,1)S(1)} %get-tuple-element.59.documents, ...), custom_call_target="tpu_custom_call" | custom-call | flops 8589934592 | tf_op jit(solution)/shard_map/early_far/pallas_call | solution.py:281
  11.7 0.7 %collective-permute-done.2.refs_0_.refs_11_ = bf16[768,128]{1,0:T(8,128)(2,1)S(1)} collective-permute-done((bf16[768,128]{1,0:T(8,128)(2,1)S(1)}, bf16[768,128]{1,0:T(8,128)(2,1)S(1)}, u32[]{:S(2)}, u32[]{:S(2)}) %collective-permute-start.2) | collective-permute-done | bytes 196640 | tf_op jit(solution)/shard_map/ppermute | solution.py:533
  12.4 1.5 %early_near.1 = (bf16[1920,512]{1,0:T(8,128)(2,1)S(1)}, bf16[1920,512]{1,0:T(8,128)(2,1)S(1)}, f32[24,512]{1,0:T(8,128)S(1)}) custom-call(bf16[256,1536]{1,0:T(8,128)(2,1)S(1)} %get-tuple-element.48.query_t.refs_0_, bf16[128,1536]{1,0:T(8,128)(2,1)S(1)} %get-tuple-element.49.dout_t.refs_1_, bf16[1152,128]{1,0:T(8,128)(2,1)S(1)} %get-tuple-element.50.documents, ...), custom_call_target="tpu_custom_call" | custom-call | tf_op jit(solution)/shard_map/early_near/pallas_call | solution.py:281
  13.9 0.0 collective-permute-done.1.refs_0_.refs_1_
  13.9 0.8 %collective-permute-start.3 = (bf16[768,128]{1,0:T(8,128)(2,1)S(1)}, bf16[768,128]{1,0:T(8,128)(2,1)S(1)}, u32[]{:S(2)}, u32[]{:S(2)}) collective-permute-start(bf16[768,128]{1,0:T(8,128)(2,1)S(1)} %collective-permute-done.1.refs_0_.refs_1_), channel_id=1, source_target_pairs={{0,1},{1,0},{2,3},{3,2},{4,5},{5,4},{6,7},{7,6},{8,9},{9,8},{10,11... | collective-permute-start | bytes 589832 | tf_op jit(solution)/shard_map/ppermute | solution.py:533
  14.6 1.0 %middle_far.1 = (bf16[1152,512]{1,0:T(8,128)(2,1)S(1)}, bf16[1152,512]{1,0:T(8,128)(2,1)S(1)}, f32[24,512]{1,0:T(8,128)S(1)}) custom-call(bf16[256,1536]{1,0:T(8,128)(2,1)S(1)} %get-tuple-element.57.query_t.refs_0_.refs_5_, bf16[128,1536]{1,0:T(8,128)(2,1)S(1)} %get-tuple-element.58.dout_t.refs_1_.refs_6_, ...), custom_call_target="tpu_custom_call" | custom-call | tf_op jit(solution)/shard_map/middle_far/pallas_call | solution.py:281
  15.6 0.0 collective-permute-done.prev2.refs_0_
  15.6 1.5 %late_far.1 = (bf16[768,512]{1,0:T(8,128)(2,1)S(1)}, bf16[768,512]{1,0:T(8,128)(2,1)S(1)}, f32[32,512]{1,0:T(8,128)S(1)}, bf16[256,384]{1,0:T(8,128)(2,1)S(1)}) custom-call(bf16[256,1536]{1,0:T(8,128)(2,1)S(1)} %get-tuple-element.57.query_t.refs_0_.refs_5_, bf16[128,1536]{1,0:T(8,128)(2,1)S(1)} %get-tuple-element.58.dout_t.refs_1_.refs_6_, ...), custom_call_target="tpu_custom_call" | custom-call | flops 2147483648 | tf_op jit(solution)/shard_map/late_far/pallas_call | solution.py:364
  17.1 1.3 %collective-permute-start.4 = (bf16[256,384]{1,0:T(8,128)(2,1)S(1)}, bf16[256,384]{1,0:T(8,128)(2,1)S(1)}, u32[]{:S(2)}, u32[]{:S(2)}) collective-permute-start(bf16[256,384]{1,0:T(8,128)(2,1)S(1)} %get-tuple-element.84), channel_id=1, source_target_pairs={{2,0},{4,2},{6,4},{8,6},{10,8},{12,10},{14,12},{15,14},{13,15},{11... | collective-permute-start | bytes 589832 | tf_op jit(solution)/shard_map/ppermute | solution.py:533
  18.4 0.0 collective-permute-done.3.prev2.refs_10_
  18.4 0.8 %grads_far.1 = (bf16[1152,512]{1,0:T(8,128)(2,1)S(1)}, bf16[256,384]{1,0:T(8,128)(2,1)S(1)}) custom-call(bf16[256,1536]{1,0:T(8,128)(2,1)S(1)} %get-tuple-element.57.query_t.refs_0_.refs_5_, bf16[128,1536]{1,0:T(8,128)(2,1)S(1)} %get-tuple-element.58.dout_t.refs_1_.refs_6_, f32[32,512]{1,0:T(8,128)S(1)} %get-tuple-element.67.refs_2_.refs_7_.refs_9_, ...), custom_call_target="tpu_custom_call" | custom-call | tf_op jit(solution)/shard_map/grads_far/pallas_call | solution.py:431
  19.3 3.3 %collective-permute-start.6 = (bf16[256,384]{1,0:T(8,128)(2,1)S(1)}, bf16[256,384]{1,0:T(8,128)(2,1)S(1)}, u32[]{:S(2)}, u32[]{:S(2)}) collective-permute-start(bf16[256,384]{1,0:T(8,128)(2,1)S(1)} %get-tuple-element.89), channel_id=1, source_target_pairs={{0,1},{1,0},{2,3},{3,2},{4,5},{5,4},{6,7},{7,6},{8,9},{9,8},{10,11... | collective-permute-start | bytes 589832 | tf_op jit(solution)/shard_map/ppermute | solution.py:533
  22.6 1.5 %late_near.1 = (bf16[768,512]{1,0:T(8,128)(2,1)S(1)}, bf16[768,512]{1,0:T(8,128)(2,1)S(1)}, f32[32,512]{1,0:T(8,128)S(1)}, bf16[256,384]{1,0:T(8,128)(2,1)S(1)}) custom-call(bf16[256,1536]{1,0:T(8,128)(2,1)S(1)} %get-tuple-element.48.query_t.refs_0_, bf16[128,1536]{1,0:T(8,128)(2,1)S(1)} %get-tuple-element.49.dout_t.refs_1_, ...), custom_call_target="tpu_custom_call" | custom-call | flops 2147483648 | tf_op jit(solution)/shard_map/late_near/pallas_call | solution.py:364
  24.0 0.0 collective-permute-done.6
  24.0 0.1 add_convert_fusion
  24.1 2.9 %collective-permute-start.7 = (bf16[256,384]{1,0:T(8,128)(2,1)S(1)}, bf16[256,384]{1,0:T(8,128)(2,1)S(1)}, u32[]{:S(2)}, u32[]{:S(2)}) collective-permute-start(bf16[256,384]{1,0:T(8,128)(2,1)S(1)} %add_convert_fusion), channel_id=1, source_target_pairs={{3,1},{5,3},{7,5},{9,7},{11,9},{13,11},{15,13},{14,15},{12,14},{10... | collective-permute-start | bytes 589832 | tf_op jit(solution)/shard_map/ppermute | solution.py:533
  27.0 1.9 %grads_near.1 = (bf16[1920,512]{1,0:T(8,128)(2,1)S(1)}, bf16[256,384]{1,0:T(8,128)(2,1)S(1)}, f32[256,384]{1,0:T(8,128)S(1)}, bf16[768,512]{1,0:T(8,128)(2,1)S(1)}, f32[256,384]{1,0:T(8,128)S(1)}) custom-call(bf16[256,1536]{1,0:T(8,128)(2,1)S(1)} %get-tuple-element.48.query_t.refs_0_, bf16[128,1536]{1,0:T(8,128)(2,1)S(1)} %get-tuple-element.49.dout_t.refs_1_, ...), custom_call_target="tpu_custom_call" | custom-call | flops 2147483648 | tf_op jit(solution)/shard_map/grads_near/pallas_call | solution.py:431
  28.9 0.0 collective-permute-done.4.far_2
  28.9 0.1 collective-permute-start.5
  29.0 2.9 %block_outputs.1 = (bf16[768,512]{1,0:T(8,128)(2,1)}, bf16[768,512]{1,0:T(8,128)(2,1)}) custom-call(bf16[768,128]{1,0:T(8,128)(2,1)S(1)} %collective-permute-done.prev2.refs_0_, bf16[768,128]{1,0:T(8,128)(2,1)S(1)} %collective-permute-done.1.refs_0_.refs_1_, bf16[768,128]{1,0:T(8,128)(2,1)S(1)} %get-tuple-element.51.refs_0_.refs_2_, ...), custom_call_target="tpu_custom_call" | custom-call | tf_op jit(solution)/shard_map/block_outputs/pallas_call | solution.py:491
  31.9 0.3 collective-permute-done.7
  32.2 0.0 collective-permute-done.5.far_1
  32.3 0.9 %total_grads.1 = (bf16[768,128]{1,0:T(8,128)(2,1)}, bf16[768,128]{1,0:T(8,128)(2,1)}) custom-call(f32[256,384]{1,0:T(8,128)S(1)} %get-tuple-element.82.far_own, bf16[256,384]{1,0:T(8,128)(2,1)S(1)} %collective-permute-done.5.far_1, bf16[256,384]{1,0:T(8,128)(2,1)S(1)} %collective-permute-done.4.far_2, f32[256,384]{1,0:T(8,128)S(1)} %convert_add_fusion.near), custom_call_target="tpu_custom_call" | custom-call | tf_op jit(solution)/shard_map/total_grads/pallas_call | solution.py:516
  (1 shorter events, 0.0 us)
Async XLA Ops:
  1.8 12.1 %collective-permute-start.1 = (bf16[768,128]{1,0:T(8,128)(2,1)S(1)}, bf16[768,128]{1,0:T(8,128)(2,1)S(1)}, u32[]{:S(2)}, u32[]{:S(2)}) collective-permute-start(bf16[768,128]{1,0:T(8,128)(2,1)S(1)} %get-tuple-element.92.refs_1_), channel_id=1, source_target_pairs={{1,2},{3,4},{5,6},{7,8},{9,10},{11,12},{13,14},{15,15},{14,13},{12... | collective-permute-start | bytes 589832 | tf_op jit(solution)/shard_map/ppermute | solution.py:533
  2.5 13.1 %collective-permute-start = (bf16[768,128]{1,0:T(8,128)(2,1)S(1)}, bf16[768,128]{1,0:T(8,128)(2,1)S(1)}, u32[]{:S(2)}, u32[]{:S(2)}) collective-permute-start(bf16[768,128]{1,0:T(8,128)(2,1)S(1)} %get-tuple-element.93.refs_0_), channel_id=1, source_target_pairs={{0,2},{2,4},{4,6},{6,8},{8,10},{10,12},{12,14},{14,15},{15,13},{13... | collective-permute-start | bytes 589832 | tf_op jit(solution)/shard_map/ppermute | solution.py:533
  10.9 1.5 %collective-permute-start.2 = (bf16[768,128]{1,0:T(8,128)(2,1)S(1)}, bf16[768,128]{1,0:T(8,128)(2,1)S(1)}, u32[]{:S(2)}, u32[]{:S(2)}) collective-permute-start(bf16[768,128]{1,0:T(8,128)(2,1)S(1)} %get-tuple-element.51.refs_0_.refs_2_), channel_id=1, source_target_pairs={{0,1},{1,0},{2,3},{3,2},{4,5},{5,4},{6,7},{7,6},{8,9},{9,8},{10,11... | collective-permute-start | bytes 589832 | tf_op jit(solution)/shard_map/ppermute | solution.py:533
  13.9 4.5 %collective-permute-start.3 = (bf16[768,128]{1,0:T(8,128)(2,1)S(1)}, bf16[768,128]{1,0:T(8,128)(2,1)S(1)}, u32[]{:S(2)}, u32[]{:S(2)}) collective-permute-start(bf16[768,128]{1,0:T(8,128)(2,1)S(1)} %collective-permute-done.1.refs_0_.refs_1_), channel_id=1, source_target_pairs={{0,1},{1,0},{2,3},{3,2},{4,5},{5,4},{6,7},{7,6},{8,9},{9,8},{10,11... | collective-permute-start | bytes 589832 | tf_op jit(solution)/shard_map/ppermute | solution.py:533
  17.1 11.8 %collective-permute-start.4 = (bf16[256,384]{1,0:T(8,128)(2,1)S(1)}, bf16[256,384]{1,0:T(8,128)(2,1)S(1)}, u32[]{:S(2)}, u32[]{:S(2)}) collective-permute-start(bf16[256,384]{1,0:T(8,128)(2,1)S(1)} %get-tuple-element.84), channel_id=1, source_target_pairs={{2,0},{4,2},{6,4},{8,6},{10,8},{12,10},{14,12},{15,14},{13,15},{11... | collective-permute-start | bytes 589832 | tf_op jit(solution)/shard_map/ppermute | solution.py:533
  19.3 4.8 %collective-permute-start.6 = (bf16[256,384]{1,0:T(8,128)(2,1)S(1)}, bf16[256,384]{1,0:T(8,128)(2,1)S(1)}, u32[]{:S(2)}, u32[]{:S(2)}) collective-permute-start(bf16[256,384]{1,0:T(8,128)(2,1)S(1)} %get-tuple-element.89), channel_id=1, source_target_pairs={{0,1},{1,0},{2,3},{3,2},{4,5},{5,4},{6,7},{7,6},{8,9},{9,8},{10,11... | collective-permute-start | bytes 589832 | tf_op jit(solution)/shard_map/ppermute | solution.py:533
  24.1 8.1 %collective-permute-start.7 = (bf16[256,384]{1,0:T(8,128)(2,1)S(1)}, bf16[256,384]{1,0:T(8,128)(2,1)S(1)}, u32[]{:S(2)}, u32[]{:S(2)}) collective-permute-start(bf16[256,384]{1,0:T(8,128)(2,1)S(1)} %add_convert_fusion), channel_id=1, source_target_pairs={{3,1},{5,3},{7,5},{9,7},{11,9},{13,11},{15,13},{14,15},{12,14},{10... | collective-permute-start | bytes 589832 | tf_op jit(solution)/shard_map/ppermute | solution.py:533
  28.9 3.3 %collective-permute-start.5 = (bf16[256,384]{1,0:T(8,128)(2,1)S(1)}, bf16[256,384]{1,0:T(8,128)(2,1)S(1)}, u32[]{:S(2)}, u32[]{:S(2)}) collective-permute-start(bf16[256,384]{1,0:T(8,128)(2,1)S(1)} %get-tuple-element.85), channel_id=1, source_target_pairs={{0,1},{1,0},{2,3},{3,2},{4,5},{5,4},{6,7},{7,6},{8,9},{9,8},{10,11... | collective-permute-start | bytes 589832 | tf_op jit(solution)/shard_map/ppermute | solution.py:533

commit v19 on v18

--- a/solution.py
+++ b/solution.py
@@ -10,7 +10,7 @@
 
 HD = 128
 TQ = 128
-GROUP = 32
+GROUP = 16
 
 masked_score = -1e30
 other_document = -65536.0

time: 33.4 us -> 33.4 us (level)
  no operation moved by 1% of the time
where the time goes in v19:
time: 33.4 us; the launch traced here: 33.2 us
  starting transfers between devices  15.2 us (46%)
  Pallas kernels  15 us (45%)
  local copies, waits for them, and re-layouts  1.06 us (3%)
  waiting for transfers between devices  0.99 us (3%)
  between operations  0.81 us (2%)
    ppermute x8, starting transfers between devices, move(): return lax.ppermute(array, 'ctx', pairs)  15.2 us
    pallas_call x3, Pallas kernels, group_scores(): pl.pallas_call(functools.partial(group_kernel, rows, heads, slot, middle)...  3.19 us
    pallas_call x1, Pallas kernels, block_outputs(): pl.pallas_call(functools.partial(outputs_kernel, rows, heads), out_shape=...  2.95 us
    pallas_call x2, Pallas kernels, late_scores(): pl.pallas_call(functools.partial(late_kernel, rows, heads, slot), out_sha...  2.95 us
    pallas_call x2, Pallas kernels, rest_grads(): pl.pallas_call(functools.partial(grads_kernel, rows, heads, slots), out_s...  2.72 us
    pallas_call x1, Pallas kernels, prepare(): pl.pallas_call(functools.partial(prepare_kernel, rows, heads, doc_lengths...  2.23 us
    slice x1, local copies, waits for them, and re-layouts, body(): upper = jnp.concatenate([key[rows:], value[rows:]], axis=0)  1.06 us
    ppermute x8, waiting for transfers between devices, move(): return lax.ppermute(array, 'ctx', pairs)  0.99 us
  transfers between devices with their start and end apart: 8, of which 2 were waited for; matrix products, arithmetic and copies ran while one was open for 0% of the time, Pallas kernels for 42%

profile of v19, /device:TPU:0, one launch (start us, length us, event | category | flops | bytes accessed | tf_op | source)
XLA Modules:
  0.0 33.2 jit_solution(17214199139304580567)
XLA Ops:
  0.6 1.1 %fusion = (bf16[384,128]{1,0:T(8,128)(2,1)S(1)}, bf16[384,128]{1,0:T(8,128)(2,1)S(1)}, bf16[384,128]{1,0:T(8,128)(2,1)S(1)}, bf16[384,128]{1,0:T(8,128)(2,1)S(1)}) fusion(bf16[768,128]{1,0:T(8,128)(2,1)} %param.6, bf16[768,128]{1,0:T(8,128)(2,1)} %param.7), kind=kLoop, calls=%fused_computation.6 | loop fusion | bytes 786432 | tf_op jit(solution)/shard_map/slice | solution.py:545
  1.7 0.1 broadcast_select_fusion
  1.8 0.7 %collective-permute-start.1 = (bf16[768,128]{1,0:T(8,128)(2,1)S(1)}, bf16[768,128]{1,0:T(8,128)(2,1)S(1)}, u32[]{:S(2)}, u32[]{:S(2)}) collective-permute-start(bf16[768,128]{1,0:T(8,128)(2,1)S(1)} %get-tuple-element.92.refs_1_), channel_id=1, source_target_pairs={{1,2},{3,4},{5,6},{7,8},{9,10},{11,12},{13,14},{15,15},{14,13},{12... | collective-permute-start | bytes 589832 | tf_op jit(solution)/shard_map/ppermute | solution.py:533
  2.5 6.1 %collective-permute-start = (bf16[768,128]{1,0:T(8,128)(2,1)S(1)}, bf16[768,128]{1,0:T(8,128)(2,1)S(1)}, u32[]{:S(2)}, u32[]{:S(2)}) collective-permute-start(bf16[768,128]{1,0:T(8,128)(2,1)S(1)} %get-tuple-element.93.refs_0_), channel_id=1, source_target_pairs={{0,2},{2,4},{4,6},{6,8},{8,10},{10,12},{12,14},{14,15},{15,13},{13... | collective-permute-start | bytes 589832 | tf_op jit(solution)/shard_map/ppermute | solution.py:533
  8.6 2.2 %prepare.1 = (bf16[768,128]{1,0:T(8,128)(2,1)S(1)}, bf16[256,1536]{1,0:T(8,128)(2,1)S(1)}, bf16[128,1536]{1,0:T(8,128)(2,1)S(1)}, bf16[1152,128]{1,0:T(8,128)(2,...) custom-call(bf16[768,128]{1,0:T(8,128)(2,1)S(1)} %get-tuple-element., ...), custom_call_target="tpu_custom_call" | custom-call | bytes 4194304 | tf_op jit(solution)/shard_map/prepare/pallas_call | solution.py:125
  10.9 0.1 collective-permute-start.2
  10.9 0.7 %early_far.1 = (bf16[768,512]{1,0:T(8,128)(2,1)S(1)}, bf16[768,512]{1,0:T(8,128)(2,1)S(1)}, f32[24,512]{1,0:T(8,128)S(1)}) custom-call(bf16[256,1536]{1,0:T(8,128)(2,1)S(1)} %get-tuple-element.57.query_t.refs_0_.refs_5_, bf16[128,1536]{1,0:T(8,128)(2,1)S(1)} %get-tuple-element.58.dout_t.refs_1_.refs_6_, bf16[1152,128]{1,0:T(8,128)(2,1)S(1)} %get-tuple-element.59.documents, ...), custom_call_target="tpu_custom_call" | custom-call | flops 8589934592 | tf_op jit(solution)/shard_map/early_far/pallas_call | solution.py:281
  11.7 0.7 %collective-permute-done.2.refs_0_.refs_11_ = bf16[768,128]{1,0:T(8,128)(2,1)S(1)} collective-permute-done((bf16[768,128]{1,0:T(8,128)(2,1)S(1)}, bf16[768,128]{1,0:T(8,128)(2,1)S(1)}, u32[]{:S(2)}, u32[]{:S(2)}) %collective-permute-start.2) | collective-permute-done | bytes 196640 | tf_op jit(solution)/shard_map/ppermute | solution.py:533
  12.4 1.5 %early_near.1 = (bf16[1920,512]{1,0:T(8,128)(2,1)S(1)}, bf16[1920,512]{1,0:T(8,128)(2,1)S(1)}, f32[24,512]{1,0:T(8,128)S(1)}) custom-call(bf16[256,1536]{1,0:T(8,128)(2,1)S(1)} %get-tuple-element.48.query_t.refs_0_, bf16[128,1536]{1,0:T(8,128)(2,1)S(1)} %get-tuple-element.49.dout_t.refs_1_, bf16[1152,128]{1,0:T(8,128)(2,1)S(1)} %get-tuple-element.50.documents, ...), custom_call_target="tpu_custom_call" | custom-call | tf_op jit(solution)/shard_map/early_near/pallas_call | solution.py:281
  13.9 0.0 collective-permute-done.1.refs_0_.refs_1_
  13.9 0.8 %collective-permute-start.3 = (bf16[768,128]{1,0:T(8,128)(2,1)S(1)}, bf16[768,128]{1,0:T(8,128)(2,1)S(1)}, u32[]{:S(2)}, u32[]{:S(2)}) collective-permute-start(bf16[768,128]{1,0:T(8,128)(2,1)S(1)} %collective-permute-done.1.refs_0_.refs_1_), channel_id=1, source_target_pairs={{0,1},{1,0},{2,3},{3,2},{4,5},{5,4},{6,7},{7,6},{8,9},{9,8},{10,11... | collective-permute-start | bytes 589832 | tf_op jit(solution)/shard_map/ppermute | solution.py:533
  14.6 1.0 %middle_far.1 = (bf16[1152,512]{1,0:T(8,128)(2,1)S(1)}, bf16[1152,512]{1,0:T(8,128)(2,1)S(1)}, f32[24,512]{1,0:T(8,128)S(1)}) custom-call(bf16[256,1536]{1,0:T(8,128)(2,1)S(1)} %get-tuple-element.57.query_t.refs_0_.refs_5_, bf16[128,1536]{1,0:T(8,128)(2,1)S(1)} %get-tuple-element.58.dout_t.refs_1_.refs_6_, ...), custom_call_target="tpu_custom_call" | custom-call | tf_op jit(solution)/shard_map/middle_far/pallas_call | solution.py:281
  15.6 0.0 collective-permute-done.prev2.refs_0_
  15.6 1.5 %late_far.1 = (bf16[768,512]{1,0:T(8,128)(2,1)S(1)}, bf16[768,512]{1,0:T(8,128)(2,1)S(1)}, f32[32,512]{1,0:T(8,128)S(1)}, bf16[256,384]{1,0:T(8,128)(2,1)S(1)}) custom-call(bf16[256,1536]{1,0:T(8,128)(2,1)S(1)} %get-tuple-element.57.query_t.refs_0_.refs_5_, bf16[128,1536]{1,0:T(8,128)(2,1)S(1)} %get-tuple-element.58.dout_t.refs_1_.refs_6_, ...), custom_call_target="tpu_custom_call" | custom-call | flops 2147483648 | tf_op jit(solution)/shard_map/late_far/pallas_call | solution.py:364
  17.1 1.3 %collective-permute-start.4 = (bf16[256,384]{1,0:T(8,128)(2,1)S(1)}, bf16[256,384]{1,0:T(8,128)(2,1)S(1)}, u32[]{:S(2)}, u32[]{:S(2)}) collective-permute-start(bf16[256,384]{1,0:T(8,128)(2,1)S(1)} %get-tuple-element.84), channel_id=1, source_target_pairs={{2,0},{4,2},{6,4},{8,6},{10,8},{12,10},{14,12},{15,14},{13,15},{11... | collective-permute-start | bytes 589832 | tf_op jit(solution)/shard_map/ppermute | solution.py:533
  18.4 0.0 collective-permute-done.3.prev2.refs_10_
  18.4 0.8 %grads_far.1 = (bf16[1152,512]{1,0:T(8,128)(2,1)S(1)}, bf16[256,384]{1,0:T(8,128)(2,1)S(1)}) custom-call(bf16[256,1536]{1,0:T(8,128)(2,1)S(1)} %get-tuple-element.57.query_t.refs_0_.refs_5_, bf16[128,1536]{1,0:T(8,128)(2,1)S(1)} %get-tuple-element.58.dout_t.refs_1_.refs_6_, f32[32,512]{1,0:T(8,128)S(1)} %get-tuple-element.67.refs_2_.refs_7_.refs_9_, ...), custom_call_target="tpu_custom_call" | custom-call | tf_op jit(solution)/shard_map/grads_far/pallas_call | solution.py:431
  19.3 3.3 %collective-permute-start.6 = (bf16[256,384]{1,0:T(8,128)(2,1)S(1)}, bf16[256,384]{1,0:T(8,128)(2,1)S(1)}, u32[]{:S(2)}, u32[]{:S(2)}) collective-permute-start(bf16[256,384]{1,0:T(8,128)(2,1)S(1)} %get-tuple-element.89), channel_id=1, source_target_pairs={{0,1},{1,0},{2,3},{3,2},{4,5},{5,4},{6,7},{7,6},{8,9},{9,8},{10,11... | collective-permute-start | bytes 589832 | tf_op jit(solution)/shard_map/ppermute | solution.py:533
  22.6 1.5 %late_near.1 = (bf16[768,512]{1,0:T(8,128)(2,1)S(1)}, bf16[768,512]{1,0:T(8,128)(2,1)S(1)}, f32[32,512]{1,0:T(8,128)S(1)}, bf16[256,384]{1,0:T(8,128)(2,1)S(1)}) custom-call(bf16[256,1536]{1,0:T(8,128)(2,1)S(1)} %get-tuple-element.48.query_t.refs_0_, bf16[128,1536]{1,0:T(8,128)(2,1)S(1)} %get-tuple-element.49.dout_t.refs_1_, ...), custom_call_target="tpu_custom_call" | custom-call | flops 2147483648 | tf_op jit(solution)/shard_map/late_near/pallas_call | solution.py:364
  24.0 0.0 collective-permute-done.6
  24.0 0.1 add_convert_fusion
  24.1 2.9 %collective-permute-start.7 = (bf16[256,384]{1,0:T(8,128)(2,1)S(1)}, bf16[256,384]{1,0:T(8,128)(2,1)S(1)}, u32[]{:S(2)}, u32[]{:S(2)}) collective-permute-start(bf16[256,384]{1,0:T(8,128)(2,1)S(1)} %add_convert_fusion), channel_id=1, source_target_pairs={{3,1},{5,3},{7,5},{9,7},{11,9},{13,11},{15,13},{14,15},{12,14},{10... | collective-permute-start | bytes 589832 | tf_op jit(solution)/shard_map/ppermute | solution.py:533
  27.0 1.9 %grads_near.1 = (bf16[1920,512]{1,0:T(8,128)(2,1)S(1)}, bf16[256,384]{1,0:T(8,128)(2,1)S(1)}, f32[256,384]{1,0:T(8,128)S(1)}, bf16[768,512]{1,0:T(8,128)(2,1)S(1)}, f32[256,384]{1,0:T(8,128)S(1)}) custom-call(bf16[256,1536]{1,0:T(8,128)(2,1)S(1)} %get-tuple-element.48.query_t.refs_0_, bf16[128,1536]{1,0:T(8,128)(2,1)S(1)} %get-tuple-element.49.dout_t.refs_1_, ...), custom_call_target="tpu_custom_call" | custom-call | flops 2147483648 | tf_op jit(solution)/shard_map/grads_near/pallas_call | solution.py:431
  28.9 0.0 collective-permute-done.4.far_2
  28.9 0.1 collective-permute-start.5
  29.0 2.9 %block_outputs.1 = (bf16[768,512]{1,0:T(8,128)(2,1)}, bf16[768,512]{1,0:T(8,128)(2,1)}) custom-call(bf16[768,128]{1,0:T(8,128)(2,1)S(1)} %collective-permute-done.prev2.refs_0_, bf16[768,128]{1,0:T(8,128)(2,1)S(1)} %collective-permute-done.1.refs_0_.refs_1_, bf16[768,128]{1,0:T(8,128)(2,1)S(1)} %get-tuple-element.51.refs_0_.refs_2_, ...), custom_call_target="tpu_custom_call" | custom-call | tf_op jit(solution)/shard_map/block_outputs/pallas_call | solution.py:491
  31.9 0.3 collective-permute-done.7
  32.2 0.0 collective-permute-done.5.far_1
  32.3 0.9 %total_grads.1 = (bf16[768,128]{1,0:T(8,128)(2,1)}, bf16[768,128]{1,0:T(8,128)(2,1)}) custom-call(f32[256,384]{1,0:T(8,128)S(1)} %get-tuple-element.82.far_own, bf16[256,384]{1,0:T(8,128)(2,1)S(1)} %collective-permute-done.5.far_1, bf16[256,384]{1,0:T(8,128)(2,1)S(1)} %collective-permute-done.4.far_2, f32[256,384]{1,0:T(8,128)S(1)} %convert_add_fusion.near), custom_call_target="tpu_custom_call" | custom-call | tf_op jit(solution)/shard_map/total_grads/pallas_call | solution.py:516
  (1 shorter events, 0.0 us)
Async XLA Ops:
  1.8 12.1 %collective-permute-start.1 = (bf16[768,128]{1,0:T(8,128)(2,1)S(1)}, bf16[768,128]{1,0:T(8,128)(2,1)S(1)}, u32[]{:S(2)}, u32[]{:S(2)}) collective-permute-start(bf16[768,128]{1,0:T(8,128)(2,1)S(1)} %get-tuple-element.92.refs_1_), channel_id=1, source_target_pairs={{1,2},{3,4},{5,6},{7,8},{9,10},{11,12},{13,14},{15,15},{14,13},{12... | collective-permute-start | bytes 589832 | tf_op jit(solution)/shard_map/ppermute | solution.py:533
  2.5 13.1 %collective-permute-start = (bf16[768,128]{1,0:T(8,128)(2,1)S(1)}, bf16[768,128]{1,0:T(8,128)(2,1)S(1)}, u32[]{:S(2)}, u32[]{:S(2)}) collective-permute-start(bf16[768,128]{1,0:T(8,128)(2,1)S(1)} %get-tuple-element.93.refs_0_), channel_id=1, source_target_pairs={{0,2},{2,4},{4,6},{6,8},{8,10},{10,12},{12,14},{14,15},{15,13},{13... | collective-permute-start | bytes 589832 | tf_op jit(solution)/shard_map/ppermute | solution.py:533
  10.9 1.5 %collective-permute-start.2 = (bf16[768,128]{1,0:T(8,128)(2,1)S(1)}, bf16[768,128]{1,0:T(8,128)(2,1)S(1)}, u32[]{:S(2)}, u32[]{:S(2)}) collective-permute-start(bf16[768,128]{1,0:T(8,128)(2,1)S(1)} %get-tuple-element.51.refs_0_.refs_2_), channel_id=1, source_target_pairs={{0,1},{1,0},{2,3},{3,2},{4,5},{5,4},{6,7},{7,6},{8,9},{9,8},{10,11... | collective-permute-start | bytes 589832 | tf_op jit(solution)/shard_map/ppermute | solution.py:533
  13.9 4.5 %collective-permute-start.3 = (bf16[768,128]{1,0:T(8,128)(2,1)S(1)}, bf16[768,128]{1,0:T(8,128)(2,1)S(1)}, u32[]{:S(2)}, u32[]{:S(2)}) collective-permute-start(bf16[768,128]{1,0:T(8,128)(2,1)S(1)} %collective-permute-done.1.refs_0_.refs_1_), channel_id=1, source_target_pairs={{0,1},{1,0},{2,3},{3,2},{4,5},{5,4},{6,7},{7,6},{8,9},{9,8},{10,11... | collective-permute-start | bytes 589832 | tf_op jit(solution)/shard_map/ppermute | solution.py:533
  17.1 11.8 %collective-permute-start.4 = (bf16[256,384]{1,0:T(8,128)(2,1)S(1)}, bf16[256,384]{1,0:T(8,128)(2,1)S(1)}, u32[]{:S(2)}, u32[]{:S(2)}) collective-permute-start(bf16[256,384]{1,0:T(8,128)(2,1)S(1)} %get-tuple-element.84), channel_id=1, source_target_pairs={{2,0},{4,2},{6,4},{8,6},{10,8},{12,10},{14,12},{15,14},{13,15},{11... | collective-permute-start | bytes 589832 | tf_op jit(solution)/shard_map/ppermute | solution.py:533
  19.3 4.8 %collective-permute-start.6 = (bf16[256,384]{1,0:T(8,128)(2,1)S(1)}, bf16[256,384]{1,0:T(8,128)(2,1)S(1)}, u32[]{:S(2)}, u32[]{:S(2)}) collective-permute-start(bf16[256,384]{1,0:T(8,128)(2,1)S(1)} %get-tuple-element.89), channel_id=1, source_target_pairs={{0,1},{1,0},{2,3},{3,2},{4,5},{5,4},{6,7},{7,6},{8,9},{9,8},{10,11... | collective-permute-start | bytes 589832 | tf_op jit(solution)/shard_map/ppermute | solution.py:533
  24.1 8.1 %collective-permute-start.7 = (bf16[256,384]{1,0:T(8,128)(2,1)S(1)}, bf16[256,384]{1,0:T(8,128)(2,1)S(1)}, u32[]{:S(2)}, u32[]{:S(2)}) collective-permute-start(bf16[256,384]{1,0:T(8,128)(2,1)S(1)} %add_convert_fusion), channel_id=1, source_target_pairs={{3,1},{5,3},{7,5},{9,7},{11,9},{13,11},{15,13},{14,15},{12,14},{10... | collective-permute-start | bytes 589832 | tf_op jit(solution)/shard_map/ppermute | solution.py:533
  28.9 3.3 %collective-permute-start.5 = (bf16[256,384]{1,0:T(8,128)(2,1)S(1)}, bf16[256,384]{1,0:T(8,128)(2,1)S(1)}, u32[]{:S(2)}, u32[]{:S(2)}) collective-permute-start(bf16[256,384]{1,0:T(8,128)(2,1)S(1)} %get-tuple-element.85), channel_id=1, source_target_pairs={{0,1},{1,0},{2,3},{3,2},{4,5},{5,4},{6,7},{7,6},{8,9},{9,8},{10,11... | collective-permute-start | bytes 589832 | tf_op jit(solution)/shard_map/ppermute | solution.py:533

commit v20 on v19

--- a/solution.py
+++ b/solution.py
@@ -43,14 +43,6 @@
 
 def in_hbm(array):
     return pltpu.with_memory_space_constraint(array, pltpu.HBM)
-
-
-def load_block(rows, slot, key, value, out, sems):
-    place = pl.ds(half_start(rows, slot), rows)
-    return [
-        pltpu.make_async_copy(key.at[place], out.at[0:rows], sems.at[2 * slot]),
-        pltpu.make_async_copy(value.at[place], out.at[rows : 2 * rows], sems.at[2 * slot + 1]),
-    ]
 
 
 def run_copies(copies):
@@ -313,10 +305,11 @@
 
 def late_kernel(rows, heads, slot, query_t, dout_t, documents, prev2, *refs):
     groups = refs[0 : 2 - slot]
-    (weights, dscores, stats, prev2_out, scores, dprobs, dk, dv) = refs[2 - slot :]
+    (weights, dscores, stats, prev2_out, scores, dprobs) = refs[2 - slot :]
     wide = heads * TQ
     window = Window(rows, slot)
     jobs = []
+    key_terms, value_terms = [], []
     for step in window.steps:
         chunks = []
         for chunk in range(window.late[step]):
@@ -340,20 +333,21 @@
                 stats[8 * kind + step : 8 * kind + step + 1, :] = value
             there = chunk_rows(window.late, step)
             dscore_rows(dscores, there, weights, dprobs, there, delta.astype(jnp.bfloat16))
-            add_products(
-                step == 0,
-                slice(step * TQ, rows),
-                (
-                    (dv, scaled_by(dout_t, tile, late_factor), weights[there, :]),
-                    (dk, scaled_by(query_t, tile, late_factor), dscores[there, :]),
-                ),
-            )
+            value_terms.append(dot_nt(scaled_by(dout_t, tile, late_factor), weights[there, :]))
+            key_terms.append(dot_nt(scaled_by(query_t, tile, late_factor), dscores[there, :]))
 
         first_max = groups[-1][step : step + 1, :]
         jobs.append((step, runs_of(chunks), (query_t, dout_t, documents), first_max, end))
     exponentials(jobs, rows, heads, scores, True)
-    prev2_out[0:HD] = (dk[...] * SCALE).astype(prev2_out.dtype)
-    prev2_out[HD : 2 * HD] = dv[...].astype(prev2_out.dtype)
+    for first, terms, scale in ((0, key_terms, SCALE), (HD, value_terms, 1.0)):
+        for tile in range(window.tiles):
+            parts = [
+                terms[step][:, (tile - step) * TQ : (tile - step + 1) * TQ]
+                for step in range(tile + 1)
+            ]
+            prev2_out[first : first + HD, tile * TQ : (tile + 1) * TQ] = (
+                sum(parts[1:], parts[0]) * scale
+            ).astype(prev2_out.dtype)
 
 
 def late_scores(slot, ready, groups, prev2):
@@ -374,8 +368,6 @@
         scratch_shapes=[
             pltpu.VMEM((rows // TQ, rows, wide), jnp.float32),
             pltpu.VMEM(late.shape, late.dtype),
-            pltpu.VMEM((HD, rows), jnp.float32),
-            pltpu.VMEM((HD, rows), jnp.float32),
         ],
         compiler_params=pltpu.CompilerParams(vmem_limit_bytes=VMEM_LIMIT),
         cost_estimate=pl.CostEstimate(flops=2**31, bytes_accessed=0, transcendentals=0),

time: 33.4 us -> 33.4 us (level)
  no operation moved by 1% of the time
where the time goes in v20:
time: 33.4 us; the launch traced here: 33.2 us
  starting transfers between devices  15.2 us (46%)
  Pallas kernels  15 us (45%)
  local copies, waits for them, and re-layouts  1.06 us (3%)
  waiting for transfers between devices  0.99 us (3%)
  between operations  0.82 us (2%)
    ppermute x8, starting transfers between devices, move(): return lax.ppermute(array, 'ctx', pairs)  15.2 us
    pallas_call x3, Pallas kernels, group_scores(): pl.pallas_call(functools.partial(group_kernel, rows, heads, slot, middle)...  3.19 us
    pallas_call x1, Pallas kernels, block_outputs(): pl.pallas_call(functools.partial(outputs_kernel, rows, heads), out_shape=...  2.95 us
    pallas_call x2, Pallas kernels, late_scores(): pl.pallas_call(functools.partial(late_kernel, rows, heads, slot), out_sha...  2.95 us
    pallas_call x2, Pallas kernels, rest_grads(): pl.pallas_call(functools.partial(grads_kernel, rows, heads, slots), out_s...  2.72 us
    pallas_call x1, Pallas kernels, prepare(): pl.pallas_call(functools.partial(prepare_kernel, rows, heads, doc_lengths...  2.23 us
    slice x1, local copies, waits for them, and re-layouts, body(): upper = jnp.concatenate([key[rows:], value[rows:]], axis=0)  1.06 us
    ppermute x8, waiting for transfers between devices, move(): return lax.ppermute(array, 'ctx', pairs)  0.99 us
  transfers between devices with their start and end apart: 8, of which 2 were waited for; matrix products, arithmetic and copies ran while one was open for 0% of the time, Pallas kernels for 42%

profile of v20, /device:TPU:0, one launch (start us, length us, event | category | flops | bytes accessed | tf_op | source)
XLA Modules:
  0.0 33.2 jit_solution(14298213866902084085)
XLA Ops:
  0.6 1.1 %fusion = (bf16[384,128]{1,0:T(8,128)(2,1)S(1)}, bf16[384,128]{1,0:T(8,128)(2,1)S(1)}, bf16[384,128]{1,0:T(8,128)(2,1)S(1)}, bf16[384,128]{1,0:T(8,128)(2,1)S(1)}) fusion(bf16[768,128]{1,0:T(8,128)(2,1)} %param.6, bf16[768,128]{1,0:T(8,128)(2,1)} %param.7), kind=kLoop, calls=%fused_computation.6 | loop fusion | bytes 786432 | tf_op jit(solution)/shard_map/slice | solution.py:537
  1.7 0.1 broadcast_select_fusion
  1.8 0.7 %collective-permute-start.1 = (bf16[768,128]{1,0:T(8,128)(2,1)S(1)}, bf16[768,128]{1,0:T(8,128)(2,1)S(1)}, u32[]{:S(2)}, u32[]{:S(2)}) collective-permute-start(bf16[768,128]{1,0:T(8,128)(2,1)S(1)} %get-tuple-element.92.refs_1_), channel_id=1, source_target_pairs={{1,2},{3,4},{5,6},{7,8},{9,10},{11,12},{13,14},{15,15},{14,13},{12... | collective-permute-start | bytes 589832 | tf_op jit(solution)/shard_map/ppermute | solution.py:525
  2.5 6.1 %collective-permute-start = (bf16[768,128]{1,0:T(8,128)(2,1)S(1)}, bf16[768,128]{1,0:T(8,128)(2,1)S(1)}, u32[]{:S(2)}, u32[]{:S(2)}) collective-permute-start(bf16[768,128]{1,0:T(8,128)(2,1)S(1)} %get-tuple-element.93.refs_0_), channel_id=1, source_target_pairs={{0,2},{2,4},{4,6},{6,8},{8,10},{10,12},{12,14},{14,15},{15,13},{13... | collective-permute-start | bytes 589832 | tf_op jit(solution)/shard_map/ppermute | solution.py:525
  8.6 2.2 %prepare.1 = (bf16[768,128]{1,0:T(8,128)(2,1)S(1)}, bf16[256,1536]{1,0:T(8,128)(2,1)S(1)}, bf16[128,1536]{1,0:T(8,128)(2,1)S(1)}, bf16[1152,128]{1,0:T(8,128)(2,...) custom-call(bf16[768,128]{1,0:T(8,128)(2,1)S(1)} %get-tuple-element., ...), custom_call_target="tpu_custom_call" | custom-call | bytes 4194304 | tf_op jit(solution)/shard_map/prepare/pallas_call | solution.py:117
  10.9 0.1 collective-permute-start.2
  10.9 0.7 %early_far.1 = (bf16[768,512]{1,0:T(8,128)(2,1)S(1)}, bf16[768,512]{1,0:T(8,128)(2,1)S(1)}, f32[24,512]{1,0:T(8,128)S(1)}) custom-call(bf16[256,1536]{1,0:T(8,128)(2,1)S(1)} %get-tuple-element.57.query_t.refs_0_.refs_5_, bf16[128,1536]{1,0:T(8,128)(2,1)S(1)} %get-tuple-element.58.dout_t.refs_1_.refs_6_, bf16[1152,128]{1,0:T(8,128)(2,1)S(1)} %get-tuple-element.59.documents, ...), custom_call_target="tpu_custom_call" | custom-call | flops 8589934592 | tf_op jit(solution)/shard_map/early_far/pallas_call | solution.py:273
  11.7 0.7 %collective-permute-done.2.refs_0_.refs_11_ = bf16[768,128]{1,0:T(8,128)(2,1)S(1)} collective-permute-done((bf16[768,128]{1,0:T(8,128)(2,1)S(1)}, bf16[768,128]{1,0:T(8,128)(2,1)S(1)}, u32[]{:S(2)}, u32[]{:S(2)}) %collective-permute-start.2) | collective-permute-done | bytes 196640 | tf_op jit(solution)/shard_map/ppermute | solution.py:525
  12.4 1.5 %early_near.1 = (bf16[1920,512]{1,0:T(8,128)(2,1)S(1)}, bf16[1920,512]{1,0:T(8,128)(2,1)S(1)}, f32[24,512]{1,0:T(8,128)S(1)}) custom-call(bf16[256,1536]{1,0:T(8,128)(2,1)S(1)} %get-tuple-element.48.query_t.refs_0_, bf16[128,1536]{1,0:T(8,128)(2,1)S(1)} %get-tuple-element.49.dout_t.refs_1_, bf16[1152,128]{1,0:T(8,128)(2,1)S(1)} %get-tuple-element.50.documents, ...), custom_call_target="tpu_custom_call" | custom-call | tf_op jit(solution)/shard_map/early_near/pallas_call | solution.py:273
  13.9 0.0 collective-permute-done.1.refs_0_.refs_1_
  13.9 0.8 %collective-permute-start.3 = (bf16[768,128]{1,0:T(8,128)(2,1)S(1)}, bf16[768,128]{1,0:T(8,128)(2,1)S(1)}, u32[]{:S(2)}, u32[]{:S(2)}) collective-permute-start(bf16[768,128]{1,0:T(8,128)(2,1)S(1)} %collective-permute-done.1.refs_0_.refs_1_), channel_id=1, source_target_pairs={{0,1},{1,0},{2,3},{3,2},{4,5},{5,4},{6,7},{7,6},{8,9},{9,8},{10,11... | collective-permute-start | bytes 589832 | tf_op jit(solution)/shard_map/ppermute | solution.py:525
  14.6 1.0 %middle_far.1 = (bf16[1152,512]{1,0:T(8,128)(2,1)S(1)}, bf16[1152,512]{1,0:T(8,128)(2,1)S(1)}, f32[24,512]{1,0:T(8,128)S(1)}) custom-call(bf16[256,1536]{1,0:T(8,128)(2,1)S(1)} %get-tuple-element.57.query_t.refs_0_.refs_5_, bf16[128,1536]{1,0:T(8,128)(2,1)S(1)} %get-tuple-element.58.dout_t.refs_1_.refs_6_, ...), custom_call_target="tpu_custom_call" | custom-call | tf_op jit(solution)/shard_map/middle_far/pallas_call | solution.py:273
  15.6 0.0 collective-permute-done.prev2.refs_0_
  15.6 1.5 %late_far.1 = (bf16[768,512]{1,0:T(8,128)(2,1)S(1)}, bf16[768,512]{1,0:T(8,128)(2,1)S(1)}, f32[32,512]{1,0:T(8,128)S(1)}, bf16[256,384]{1,0:T(8,128)(2,1)S(1)}) custom-call(bf16[256,1536]{1,0:T(8,128)(2,1)S(1)} %get-tuple-element.57.query_t.refs_0_.refs_5_, bf16[128,1536]{1,0:T(8,128)(2,1)S(1)} %get-tuple-element.58.dout_t.refs_1_.refs_6_, ...), custom_call_target="tpu_custom_call" | custom-call | flops 2147483648 | tf_op jit(solution)/shard_map/late_far/pallas_call | solution.py:358
  17.1 1.3 %collective-permute-start.4 = (bf16[256,384]{1,0:T(8,128)(2,1)S(1)}, bf16[256,384]{1,0:T(8,128)(2,1)S(1)}, u32[]{:S(2)}, u32[]{:S(2)}) collective-permute-start(bf16[256,384]{1,0:T(8,128)(2,1)S(1)} %get-tuple-element.84), channel_id=1, source_target_pairs={{2,0},{4,2},{6,4},{8,6},{10,8},{12,10},{14,12},{15,14},{13,15},{11... | collective-permute-start | bytes 589832 | tf_op jit(solution)/shard_map/ppermute | solution.py:525
  18.4 0.0 collective-permute-done.3.prev2.refs_10_
  18.4 0.8 %grads_far.1 = (bf16[1152,512]{1,0:T(8,128)(2,1)S(1)}, bf16[256,384]{1,0:T(8,128)(2,1)S(1)}) custom-call(bf16[256,1536]{1,0:T(8,128)(2,1)S(1)} %get-tuple-element.57.query_t.refs_0_.refs_5_, bf16[128,1536]{1,0:T(8,128)(2,1)S(1)} %get-tuple-element.58.dout_t.refs_1_.refs_6_, f32[32,512]{1,0:T(8,128)S(1)} %get-tuple-element.67.refs_2_.refs_7_.refs_9_, ...), custom_call_target="tpu_custom_call" | custom-call | tf_op jit(solution)/shard_map/grads_far/pallas_call | solution.py:423
  19.3 3.3 %collective-permute-start.6 = (bf16[256,384]{1,0:T(8,128)(2,1)S(1)}, bf16[256,384]{1,0:T(8,128)(2,1)S(1)}, u32[]{:S(2)}, u32[]{:S(2)}) collective-permute-start(bf16[256,384]{1,0:T(8,128)(2,1)S(1)} %get-tuple-element.89), channel_id=1, source_target_pairs={{0,1},{1,0},{2,3},{3,2},{4,5},{5,4},{6,7},{7,6},{8,9},{9,8},{10,11... | collective-permute-start | bytes 589832 | tf_op jit(solution)/shard_map/ppermute | solution.py:525
  22.6 1.5 %late_near.1 = (bf16[768,512]{1,0:T(8,128)(2,1)S(1)}, bf16[768,512]{1,0:T(8,128)(2,1)S(1)}, f32[32,512]{1,0:T(8,128)S(1)}, bf16[256,384]{1,0:T(8,128)(2,1)S(1)}) custom-call(bf16[256,1536]{1,0:T(8,128)(2,1)S(1)} %get-tuple-element.48.query_t.refs_0_, bf16[128,1536]{1,0:T(8,128)(2,1)S(1)} %get-tuple-element.49.dout_t.refs_1_, ...), custom_call_target="tpu_custom_call" | custom-call | flops 2147483648 | tf_op jit(solution)/shard_map/late_near/pallas_call | solution.py:358
  24.0 0.0 collective-permute-done.6
  24.0 0.1 add_convert_fusion
  24.1 2.9 %collective-permute-start.7 = (bf16[256,384]{1,0:T(8,128)(2,1)S(1)}, bf16[256,384]{1,0:T(8,128)(2,1)S(1)}, u32[]{:S(2)}, u32[]{:S(2)}) collective-permute-start(bf16[256,384]{1,0:T(8,128)(2,1)S(1)} %add_convert_fusion), channel_id=1, source_target_pairs={{3,1},{5,3},{7,5},{9,7},{11,9},{13,11},{15,13},{14,15},{12,14},{10... | collective-permute-start | bytes 589832 | tf_op jit(solution)/shard_map/ppermute | solution.py:525
  27.0 1.9 %grads_near.1 = (bf16[1920,512]{1,0:T(8,128)(2,1)S(1)}, bf16[256,384]{1,0:T(8,128)(2,1)S(1)}, f32[256,384]{1,0:T(8,128)S(1)}, bf16[768,512]{1,0:T(8,128)(2,1)S(1)}, f32[256,384]{1,0:T(8,128)S(1)}) custom-call(bf16[256,1536]{1,0:T(8,128)(2,1)S(1)} %get-tuple-element.48.query_t.refs_0_, bf16[128,1536]{1,0:T(8,128)(2,1)S(1)} %get-tuple-element.49.dout_t.refs_1_, ...), custom_call_target="tpu_custom_call" | custom-call | flops 2147483648 | tf_op jit(solution)/shard_map/grads_near/pallas_call | solution.py:423
  28.9 0.0 collective-permute-done.4.far_2
  28.9 0.1 collective-permute-start.5
  29.0 3.0 %block_outputs.1 = (bf16[768,512]{1,0:T(8,128)(2,1)}, bf16[768,512]{1,0:T(8,128)(2,1)}) custom-call(bf16[768,128]{1,0:T(8,128)(2,1)S(1)} %collective-permute-done.prev2.refs_0_, bf16[768,128]{1,0:T(8,128)(2,1)S(1)} %collective-permute-done.1.refs_0_.refs_1_, bf16[768,128]{1,0:T(8,128)(2,1)S(1)} %get-tuple-element.51.refs_0_.refs_2_, ...), custom_call_target="tpu_custom_call" | custom-call | tf_op jit(solution)/shard_map/block_outputs/pallas_call | solution.py:483
  31.9 0.3 collective-permute-done.7
  32.2 0.0 collective-permute-done.5.far_1
  32.3 0.9 %total_grads.1 = (bf16[768,128]{1,0:T(8,128)(2,1)}, bf16[768,128]{1,0:T(8,128)(2,1)}) custom-call(f32[256,384]{1,0:T(8,128)S(1)} %get-tuple-element.82.far_own, bf16[256,384]{1,0:T(8,128)(2,1)S(1)} %collective-permute-done.5.far_1, bf16[256,384]{1,0:T(8,128)(2,1)S(1)} %collective-permute-done.4.far_2, f32[256,384]{1,0:T(8,128)S(1)} %convert_add_fusion.near), custom_call_target="tpu_custom_call" | custom-call | tf_op jit(solution)/shard_map/total_grads/pallas_call | solution.py:508
  (1 shorter events, 0.0 us)
Async XLA Ops:
  1.8 12.1 %collective-permute-start.1 = (bf16[768,128]{1,0:T(8,128)(2,1)S(1)}, bf16[768,128]{1,0:T(8,128)(2,1)S(1)}, u32[]{:S(2)}, u32[]{:S(2)}) collective-permute-start(bf16[768,128]{1,0:T(8,128)(2,1)S(1)} %get-tuple-element.92.refs_1_), channel_id=1, source_target_pairs={{1,2},{3,4},{5,6},{7,8},{9,10},{11,12},{13,14},{15,15},{14,13},{12... | collective-permute-start | bytes 589832 | tf_op jit(solution)/shard_map/ppermute | solution.py:525
  2.5 13.1 %collective-permute-start = (bf16[768,128]{1,0:T(8,128)(2,1)S(1)}, bf16[768,128]{1,0:T(8,128)(2,1)S(1)}, u32[]{:S(2)}, u32[]{:S(2)}) collective-permute-start(bf16[768,128]{1,0:T(8,128)(2,1)S(1)} %get-tuple-element.93.refs_0_), channel_id=1, source_target_pairs={{0,2},{2,4},{4,6},{6,8},{8,10},{10,12},{12,14},{14,15},{15,13},{13... | collective-permute-start | bytes 589832 | tf_op jit(solution)/shard_map/ppermute | solution.py:525
  10.9 1.5 %collective-permute-start.2 = (bf16[768,128]{1,0:T(8,128)(2,1)S(1)}, bf16[768,128]{1,0:T(8,128)(2,1)S(1)}, u32[]{:S(2)}, u32[]{:S(2)}) collective-permute-start(bf16[768,128]{1,0:T(8,128)(2,1)S(1)} %get-tuple-element.51.refs_0_.refs_2_), channel_id=1, source_target_pairs={{0,1},{1,0},{2,3},{3,2},{4,5},{5,4},{6,7},{7,6},{8,9},{9,8},{10,11... | collective-permute-start | bytes 589832 | tf_op jit(solution)/shard_map/ppermute | solution.py:525
  13.9 4.5 %collective-permute-start.3 = (bf16[768,128]{1,0:T(8,128)(2,1)S(1)}, bf16[768,128]{1,0:T(8,128)(2,1)S(1)}, u32[]{:S(2)}, u32[]{:S(2)}) collective-permute-start(bf16[768,128]{1,0:T(8,128)(2,1)S(1)} %collective-permute-done.1.refs_0_.refs_1_), channel_id=1, source_target_pairs={{0,1},{1,0},{2,3},{3,2},{4,5},{5,4},{6,7},{7,6},{8,9},{9,8},{10,11... | collective-permute-start | bytes 589832 | tf_op jit(solution)/shard_map/ppermute | solution.py:525
  17.1 11.8 %collective-permute-start.4 = (bf16[256,384]{1,0:T(8,128)(2,1)S(1)}, bf16[256,384]{1,0:T(8,128)(2,1)S(1)}, u32[]{:S(2)}, u32[]{:S(2)}) collective-permute-start(bf16[256,384]{1,0:T(8,128)(2,1)S(1)} %get-tuple-element.84), channel_id=1, source_target_pairs={{2,0},{4,2},{6,4},{8,6},{10,8},{12,10},{14,12},{15,14},{13,15},{11... | collective-permute-start | bytes 589832 | tf_op jit(solution)/shard_map/ppermute | solution.py:525
  19.3 4.8 %collective-permute-start.6 = (bf16[256,384]{1,0:T(8,128)(2,1)S(1)}, bf16[256,384]{1,0:T(8,128)(2,1)S(1)}, u32[]{:S(2)}, u32[]{:S(2)}) collective-permute-start(bf16[256,384]{1,0:T(8,128)(2,1)S(1)} %get-tuple-element.89), channel_id=1, source_target_pairs={{0,1},{1,0},{2,3},{3,2},{4,5},{5,4},{6,7},{7,6},{8,9},{9,8},{10,11... | collective-permute-start | bytes 589832 | tf_op jit(solution)/shard_map/ppermute | solution.py:525
  24.1 8.1 %collective-permute-start.7 = (bf16[256,384]{1,0:T(8,128)(2,1)S(1)}, bf16[256,384]{1,0:T(8,128)(2,1)S(1)}, u32[]{:S(2)}, u32[]{:S(2)}) collective-permute-start(bf16[256,384]{1,0:T(8,128)(2,1)S(1)} %add_convert_fusion), channel_id=1, source_target_pairs={{3,1},{5,3},{7,5},{9,7},{11,9},{13,11},{15,13},{14,15},{12,14},{10... | collective-permute-start | bytes 589832 | tf_op jit(solution)/shard_map/ppermute | solution.py:525
  28.9 3.3 %collective-permute-start.5 = (bf16[256,384]{1,0:T(8,128)(2,1)S(1)}, bf16[256,384]{1,0:T(8,128)(2,1)S(1)}, u32[]{:S(2)}, u32[]{:S(2)}) collective-permute-start(bf16[256,384]{1,0:T(8,128)(2,1)S(1)} %get-tuple-element.85), channel_id=1, source_target_pairs={{0,1},{1,0},{2,3},{3,2},{4,5},{5,4},{6,7},{7,6},{8,9},{9,8},{10,11... | collective-permute-start | bytes 589832 | tf_op jit(solution)/shard_map/ppermute | solution.py:525

commit v21 on v20

--- a/solution.py
+++ b/solution.py
@@ -533,9 +533,10 @@
 
     rows = key.shape[0] // 2
     odd = lax.axis_index("ctx") % 2 == 1
-    lower = jnp.concatenate([key[:rows], value[:rows]], axis=0)
-    upper = jnp.concatenate([key[rows:], value[rows:]], axis=0)
-    near_kv, far_kv = jnp.where(odd, lower, upper), jnp.where(odd, upper, lower)
+    near_kv, far_kv = (
+        jnp.concatenate([jnp.where(first, part[:rows], part[rows:]) for part in (key, value)], axis=0)
+        for first in (odd, jnp.logical_not(odd))
+    )
     far_1 = move(near_kv, near_to_far)
     far_2 = move(far_kv, far_on)
     prepared = prepare(count, doc_lengths, query, d_out, far_kv, near_kv)

time: 33.4 us -> 33.4 us (level)
  local copies, waits for them, and re-layouts: 1.06 us -> 0 us
  other arithmetic: 0.17 us -> 1.19 us
    slice x1 -> x0, local copies, waits for them, and re-layouts: 1.06 us -> none  [body(): upper = jnp.concatenate([key[rows:], value[rows:]], axis=0)]
    select_n x1, other arithmetic: 0.08 us -> 1.07 us  [body(): jnp.where(first, part[:rows], part[rows:])]
where the time goes in v21:
time: 33.4 us; the launch traced here: 33.1 us
  starting transfers between devices  15.1 us (45%)
  Pallas kernels  15 us (45%)
  other arithmetic  1.19 us (4%)
  waiting for transfers between devices  0.98 us (3%)
  between operations  0.82 us (2%)
    ppermute x8, starting transfers between devices, move(): return lax.ppermute(array, 'ctx', pairs)  15.1 us
    pallas_call x3, Pallas kernels, group_scores(): pl.pallas_call(functools.partial(group_kernel, rows, heads, slot, middle)...  3.2 us
    pallas_call x2, Pallas kernels, late_scores(): pl.pallas_call(functools.partial(late_kernel, rows, heads, slot), out_sha...  2.95 us
    pallas_call x1, Pallas kernels, block_outputs(): pl.pallas_call(functools.partial(outputs_kernel, rows, heads), out_shape=...  2.95 us
    pallas_call x2, Pallas kernels, rest_grads(): pl.pallas_call(functools.partial(grads_kernel, rows, heads, slots), out_s...  2.73 us
    pallas_call x1, Pallas kernels, prepare(): pl.pallas_call(functools.partial(prepare_kernel, rows, heads, doc_lengths...  2.23 us
    select_n x1, other arithmetic, body(): jnp.where(first, part[:rows], part[rows:])  1.07 us
    ppermute x8, waiting for transfers between devices, move(): return lax.ppermute(array, 'ctx', pairs)  0.98 us
  transfers between devices with their start and end apart: 8, of which 2 were waited for; matrix products, arithmetic and copies ran while one was open for 0% of the time, Pallas kernels for 42%

profile of v21, /device:TPU:0, one launch (start us, length us, event | category | flops | bytes accessed | tf_op | source)
XLA Modules:
  0.0 33.1 jit_solution(1685215752343688207)
XLA Ops:
  0.6 1.1 %broadcast_select_fusion = (bf16[384,128]{1,0:T(8,128)(2,1)S(1)}, bf16[384,128]{1,0:T(8,128)(2,1)S(1)}, bf16[384,128]{1,0:T(8,128)(2,1)S(1)}, bf16[384,128]{1,0:T(8,128)(2,1)S(1)}) fusion(pred[]{:T(512)S(6)} %eq.5, bf16[768,128]{1,0:T(8,128)(2,1)} %param.7, pred[]{:T(512)S(6)} %not.3, bf16[768,128]{1,0:T(8,128)(2,1)} %param.6), kind=kLoop, calls=%fused_computation.4 | loop fusion | flops 196608 | bytes 786434 | tf_op jit(solution)/shard_map/jit(_where)/select_n | solution.py:537
  1.7 0.7 %collective-permute-start.1 = (bf16[768,128]{1,0:T(8,128)(2,1)S(1)}, bf16[768,128]{1,0:T(8,128)(2,1)S(1)}, u32[]{:S(2)}, u32[]{:S(2)}) collective-permute-start(bf16[768,128]{1,0:T(8,128)(2,1)S(1)} %pad_maximum_fusion.1.refs_1_), channel_id=1, source_target_pairs={{1,2},{3,4},{5,6},{7,8},{9,10},{11,12},{13,14},{15,15},{14,13},{12... | collective-permute-start | bytes 589832 | tf_op jit(solution)/shard_map/ppermute | solution.py:525
  2.4 6.1 %collective-permute-start = (bf16[768,128]{1,0:T(8,128)(2,1)S(1)}, bf16[768,128]{1,0:T(8,128)(2,1)S(1)}, u32[]{:S(2)}, u32[]{:S(2)}) collective-permute-start(bf16[768,128]{1,0:T(8,128)(2,1)S(1)} %pad_maximum_fusion.refs_0_), channel_id=1, source_target_pairs={{0,2},{2,4},{4,6},{6,8},{8,10},{10,12},{12,14},{14,15},{15,13},{13... | collective-permute-start | bytes 589832 | tf_op jit(solution)/shard_map/ppermute | solution.py:525
  8.6 2.2 %prepare.1 = (bf16[768,128]{1,0:T(8,128)(2,1)S(1)}, bf16[256,1536]{1,0:T(8,128)(2,1)S(1)}, bf16[128,1536]{1,0:T(8,128)(2,1)S(1)}, bf16[1152,128]{1,0:T(8,128)(2,...) custom-call(bf16[768,128]{1,0:T(8,128)(2,1)S(1)} %pad_maximum_fusion, ...), custom_call_target="tpu_custom_call" | custom-call | bytes 4194304 | tf_op jit(solution)/shard_map/prepare/pallas_call | solution.py:117
  10.8 0.1 collective-permute-start.2
  10.9 0.7 %early_far.1 = (bf16[768,512]{1,0:T(8,128)(2,1)S(1)}, bf16[768,512]{1,0:T(8,128)(2,1)S(1)}, f32[24,512]{1,0:T(8,128)S(1)}) custom-call(bf16[256,1536]{1,0:T(8,128)(2,1)S(1)} %get-tuple-element.57.query_t.refs_0_.refs_5_, bf16[128,1536]{1,0:T(8,128)(2,1)S(1)} %get-tuple-element.58.dout_t.refs_1_.refs_6_, bf16[1152,128]{1,0:T(8,128)(2,1)S(1)} %get-tuple-element.59.documents, ...), custom_call_target="tpu_custom_call" | custom-call | flops 8589934592 | tf_op jit(solution)/shard_map/early_far/pallas_call | solution.py:273
  11.6 0.7 %collective-permute-done.2.refs_0_.refs_11_ = bf16[768,128]{1,0:T(8,128)(2,1)S(1)} collective-permute-done((bf16[768,128]{1,0:T(8,128)(2,1)S(1)}, bf16[768,128]{1,0:T(8,128)(2,1)S(1)}, u32[]{:S(2)}, u32[]{:S(2)}) %collective-permute-start.2) | collective-permute-done | bytes 196640 | tf_op jit(solution)/shard_map/ppermute | solution.py:525
  12.3 1.5 %early_near.1 = (bf16[1920,512]{1,0:T(8,128)(2,1)S(1)}, bf16[1920,512]{1,0:T(8,128)(2,1)S(1)}, f32[24,512]{1,0:T(8,128)S(1)}) custom-call(bf16[256,1536]{1,0:T(8,128)(2,1)S(1)} %get-tuple-element.48.query_t.refs_0_, bf16[128,1536]{1,0:T(8,128)(2,1)S(1)} %get-tuple-element.49.dout_t.refs_1_, bf16[1152,128]{1,0:T(8,128)(2,1)S(1)} %get-tuple-element.50.documents, ...), custom_call_target="tpu_custom_call" | custom-call | tf_op jit(solution)/shard_map/early_near/pallas_call | solution.py:273
  13.8 0.0 collective-permute-done.1.refs_0_.refs_1_
  13.8 0.7 %collective-permute-start.3 = (bf16[768,128]{1,0:T(8,128)(2,1)S(1)}, bf16[768,128]{1,0:T(8,128)(2,1)S(1)}, u32[]{:S(2)}, u32[]{:S(2)}) collective-permute-start(bf16[768,128]{1,0:T(8,128)(2,1)S(1)} %collective-permute-done.1.refs_0_.refs_1_), channel_id=1, source_target_pairs={{0,1},{1,0},{2,3},{3,2},{4,5},{5,4},{6,7},{7,6},{8,9},{9,8},{10,11... | collective-permute-start | bytes 589832 | tf_op jit(solution)/shard_map/ppermute | solution.py:525
  14.6 1.0 %middle_far.1 = (bf16[1152,512]{1,0:T(8,128)(2,1)S(1)}, bf16[1152,512]{1,0:T(8,128)(2,1)S(1)}, f32[24,512]{1,0:T(8,128)S(1)}) custom-call(bf16[256,1536]{1,0:T(8,128)(2,1)S(1)} %get-tuple-element.57.query_t.refs_0_.refs_5_, bf16[128,1536]{1,0:T(8,128)(2,1)S(1)} %get-tuple-element.58.dout_t.refs_1_.refs_6_, ...), custom_call_target="tpu_custom_call" | custom-call | tf_op jit(solution)/shard_map/middle_far/pallas_call | solution.py:273
  15.6 0.0 collective-permute-done.prev2.refs_0_
  15.6 1.5 %late_far.1 = (bf16[768,512]{1,0:T(8,128)(2,1)S(1)}, bf16[768,512]{1,0:T(8,128)(2,1)S(1)}, f32[32,512]{1,0:T(8,128)S(1)}, bf16[256,384]{1,0:T(8,128)(2,1)S(1)}) custom-call(bf16[256,1536]{1,0:T(8,128)(2,1)S(1)} %get-tuple-element.57.query_t.refs_0_.refs_5_, bf16[128,1536]{1,0:T(8,128)(2,1)S(1)} %get-tuple-element.58.dout_t.refs_1_.refs_6_, ...), custom_call_target="tpu_custom_call" | custom-call | flops 2147483648 | tf_op jit(solution)/shard_map/late_far/pallas_call | solution.py:358
  17.0 1.3 %collective-permute-start.4 = (bf16[256,384]{1,0:T(8,128)(2,1)S(1)}, bf16[256,384]{1,0:T(8,128)(2,1)S(1)}, u32[]{:S(2)}, u32[]{:S(2)}) collective-permute-start(bf16[256,384]{1,0:T(8,128)(2,1)S(1)} %get-tuple-element.84), channel_id=1, source_target_pairs={{2,0},{4,2},{6,4},{8,6},{10,8},{12,10},{14,12},{15,14},{13,15},{11... | collective-permute-start | bytes 589832 | tf_op jit(solution)/shard_map/ppermute | solution.py:525
  18.3 0.0 collective-permute-done.3.prev2.refs_10_
  18.4 0.8 %grads_far.1 = (bf16[1152,512]{1,0:T(8,128)(2,1)S(1)}, bf16[256,384]{1,0:T(8,128)(2,1)S(1)}) custom-call(bf16[256,1536]{1,0:T(8,128)(2,1)S(1)} %get-tuple-element.57.query_t.refs_0_.refs_5_, bf16[128,1536]{1,0:T(8,128)(2,1)S(1)} %get-tuple-element.58.dout_t.refs_1_.refs_6_, f32[32,512]{1,0:T(8,128)S(1)} %get-tuple-element.67.refs_2_.refs_7_.refs_9_, ...), custom_call_target="tpu_custom_call" | custom-call | tf_op jit(solution)/shard_map/grads_far/pallas_call | solution.py:423
  19.2 3.3 %collective-permute-start.6 = (bf16[256,384]{1,0:T(8,128)(2,1)S(1)}, bf16[256,384]{1,0:T(8,128)(2,1)S(1)}, u32[]{:S(2)}, u32[]{:S(2)}) collective-permute-start(bf16[256,384]{1,0:T(8,128)(2,1)S(1)} %get-tuple-element.89), channel_id=1, source_target_pairs={{0,1},{1,0},{2,3},{3,2},{4,5},{5,4},{6,7},{7,6},{8,9},{9,8},{10,11... | collective-permute-start | bytes 589832 | tf_op jit(solution)/shard_map/ppermute | solution.py:525
  22.5 1.5 %late_near.1 = (bf16[768,512]{1,0:T(8,128)(2,1)S(1)}, bf16[768,512]{1,0:T(8,128)(2,1)S(1)}, f32[32,512]{1,0:T(8,128)S(1)}, bf16[256,384]{1,0:T(8,128)(2,1)S(1)}) custom-call(bf16[256,1536]{1,0:T(8,128)(2,1)S(1)} %get-tuple-element.48.query_t.refs_0_, bf16[128,1536]{1,0:T(8,128)(2,1)S(1)} %get-tuple-element.49.dout_t.refs_1_, ...), custom_call_target="tpu_custom_call" | custom-call | flops 2147483648 | tf_op jit(solution)/shard_map/late_near/pallas_call | solution.py:358
  24.0 0.0 collective-permute-done.6
  24.0 0.1 add_convert_fusion
  24.0 2.9 %collective-permute-start.7 = (bf16[256,384]{1,0:T(8,128)(2,1)S(1)}, bf16[256,384]{1,0:T(8,128)(2,1)S(1)}, u32[]{:S(2)}, u32[]{:S(2)}) collective-permute-start(bf16[256,384]{1,0:T(8,128)(2,1)S(1)} %add_convert_fusion), channel_id=1, source_target_pairs={{3,1},{5,3},{7,5},{9,7},{11,9},{13,11},{15,13},{14,15},{12,14},{10... | collective-permute-start | bytes 589832 | tf_op jit(solution)/shard_map/ppermute | solution.py:525
  26.9 1.9 %grads_near.1 = (bf16[1920,512]{1,0:T(8,128)(2,1)S(1)}, bf16[256,384]{1,0:T(8,128)(2,1)S(1)}, f32[256,384]{1,0:T(8,128)S(1)}, bf16[768,512]{1,0:T(8,128)(2,1)S(1)}, f32[256,384]{1,0:T(8,128)S(1)}) custom-call(bf16[256,1536]{1,0:T(8,128)(2,1)S(1)} %get-tuple-element.48.query_t.refs_0_, bf16[128,1536]{1,0:T(8,128)(2,1)S(1)} %get-tuple-element.49.dout_t.refs_1_, ...), custom_call_target="tpu_custom_call" | custom-call | flops 2147483648 | tf_op jit(solution)/shard_map/grads_near/pallas_call | solution.py:423
  28.8 0.0 collective-permute-done.4.far_2
  28.8 0.1 collective-permute-start.5
  28.9 2.9 %block_outputs.1 = (bf16[768,512]{1,0:T(8,128)(2,1)}, bf16[768,512]{1,0:T(8,128)(2,1)}) custom-call(bf16[768,128]{1,0:T(8,128)(2,1)S(1)} %collective-permute-done.prev2.refs_0_, bf16[768,128]{1,0:T(8,128)(2,1)S(1)} %collective-permute-done.1.refs_0_.refs_1_, bf16[768,128]{1,0:T(8,128)(2,1)S(1)} %get-tuple-element.51.refs_0_.refs_2_, ...), custom_call_target="tpu_custom_call" | custom-call | tf_op jit(solution)/shard_map/block_outputs/pallas_call | solution.py:483
  31.9 0.3 collective-permute-done.7
  32.2 0.0 collective-permute-done.5.far_1
  32.2 0.9 %total_grads.1 = (bf16[768,128]{1,0:T(8,128)(2,1)}, bf16[768,128]{1,0:T(8,128)(2,1)}) custom-call(f32[256,384]{1,0:T(8,128)S(1)} %get-tuple-element.82.far_own, bf16[256,384]{1,0:T(8,128)(2,1)S(1)} %collective-permute-done.5.far_1, bf16[256,384]{1,0:T(8,128)(2,1)S(1)} %collective-permute-done.4.far_2, f32[256,384]{1,0:T(8,128)S(1)} %convert_add_fusion.near), custom_call_target="tpu_custom_call" | custom-call | tf_op jit(solution)/shard_map/total_grads/pallas_call | solution.py:508
  (3 shorter events, 0.1 us)
Async XLA Ops:
  1.7 12.1 %collective-permute-start.1 = (bf16[768,128]{1,0:T(8,128)(2,1)S(1)}, bf16[768,128]{1,0:T(8,128)(2,1)S(1)}, u32[]{:S(2)}, u32[]{:S(2)}) collective-permute-start(bf16[768,128]{1,0:T(8,128)(2,1)S(1)} %pad_maximum_fusion.1.refs_1_), channel_id=1, source_target_pairs={{1,2},{3,4},{5,6},{7,8},{9,10},{11,12},{13,14},{15,15},{14,13},{12... | collective-permute-start | bytes 589832 | tf_op jit(solution)/shard_map/ppermute | solution.py:525
  2.4 13.1 %collective-permute-start = (bf16[768,128]{1,0:T(8,128)(2,1)S(1)}, bf16[768,128]{1,0:T(8,128)(2,1)S(1)}, u32[]{:S(2)}, u32[]{:S(2)}) collective-permute-start(bf16[768,128]{1,0:T(8,128)(2,1)S(1)} %pad_maximum_fusion.refs_0_), channel_id=1, source_target_pairs={{0,2},{2,4},{4,6},{6,8},{8,10},{10,12},{12,14},{14,15},{15,13},{13... | collective-permute-start | bytes 589832 | tf_op jit(solution)/shard_map/ppermute | solution.py:525
  10.8 1.5 %collective-permute-start.2 = (bf16[768,128]{1,0:T(8,128)(2,1)S(1)}, bf16[768,128]{1,0:T(8,128)(2,1)S(1)}, u32[]{:S(2)}, u32[]{:S(2)}) collective-permute-start(bf16[768,128]{1,0:T(8,128)(2,1)S(1)} %get-tuple-element.51.refs_0_.refs_2_), channel_id=1, source_target_pairs={{0,1},{1,0},{2,3},{3,2},{4,5},{5,4},{6,7},{7,6},{8,9},{9,8},{10,11... | collective-permute-start | bytes 589832 | tf_op jit(solution)/shard_map/ppermute | solution.py:525
  13.8 4.5 %collective-permute-start.3 = (bf16[768,128]{1,0:T(8,128)(2,1)S(1)}, bf16[768,128]{1,0:T(8,128)(2,1)S(1)}, u32[]{:S(2)}, u32[]{:S(2)}) collective-permute-start(bf16[768,128]{1,0:T(8,128)(2,1)S(1)} %collective-permute-done.1.refs_0_.refs_1_), channel_id=1, source_target_pairs={{0,1},{1,0},{2,3},{3,2},{4,5},{5,4},{6,7},{7,6},{8,9},{9,8},{10,11... | collective-permute-start | bytes 589832 | tf_op jit(solution)/shard_map/ppermute | solution.py:525
  17.0 11.8 %collective-permute-start.4 = (bf16[256,384]{1,0:T(8,128)(2,1)S(1)}, bf16[256,384]{1,0:T(8,128)(2,1)S(1)}, u32[]{:S(2)}, u32[]{:S(2)}) collective-permute-start(bf16[256,384]{1,0:T(8,128)(2,1)S(1)} %get-tuple-element.84), channel_id=1, source_target_pairs={{2,0},{4,2},{6,4},{8,6},{10,8},{12,10},{14,12},{15,14},{13,15},{11... | collective-permute-start | bytes 589832 | tf_op jit(solution)/shard_map/ppermute | solution.py:525
  19.2 4.8 %collective-permute-start.6 = (bf16[256,384]{1,0:T(8,128)(2,1)S(1)}, bf16[256,384]{1,0:T(8,128)(2,1)S(1)}, u32[]{:S(2)}, u32[]{:S(2)}) collective-permute-start(bf16[256,384]{1,0:T(8,128)(2,1)S(1)} %get-tuple-element.89), channel_id=1, source_target_pairs={{0,1},{1,0},{2,3},{3,2},{4,5},{5,4},{6,7},{7,6},{8,9},{9,8},{10,11... | collective-permute-start | bytes 589832 | tf_op jit(solution)/shard_map/ppermute | solution.py:525
  24.0 8.1 %collective-permute-start.7 = (bf16[256,384]{1,0:T(8,128)(2,1)S(1)}, bf16[256,384]{1,0:T(8,128)(2,1)S(1)}, u32[]{:S(2)}, u32[]{:S(2)}) collective-permute-start(bf16[256,384]{1,0:T(8,128)(2,1)S(1)} %add_convert_fusion), channel_id=1, source_target_pairs={{3,1},{5,3},{7,5},{9,7},{11,9},{13,11},{15,13},{14,15},{12,14},{10... | collective-permute-start | bytes 589832 | tf_op jit(solution)/shard_map/ppermute | solution.py:525
  28.8 3.3 %collective-permute-start.5 = (bf16[256,384]{1,0:T(8,128)(2,1)S(1)}, bf16[256,384]{1,0:T(8,128)(2,1)S(1)}, u32[]{:S(2)}, u32[]{:S(2)}) collective-permute-start(bf16[256,384]{1,0:T(8,128)(2,1)S(1)} %get-tuple-element.85), channel_id=1, source_target_pairs={{0,1},{1,0},{2,3},{3,2},{4,5},{5,4},{6,7},{7,6},{8,9},{9,8},{10,11... | collective-permute-start | bytes 589832 | tf_op jit(solution)/shard_map/ppermute | solution.py:525

commit v22 on v21

--- a/solution.py
+++ b/solution.py
@@ -494,12 +494,22 @@
     )(*far, *near)
 
 
-def total_kernel(rows, far_own, far_1, far_2, near, grad_key, grad_value):
-    far = far_own[...] + far_1[...].astype(jnp.float32) + far_2[...].astype(jnp.float32)
-    for slot, total in ((0, far), (1, near[...])):
+def total_kernel(rows, far_own, far_1, far_2, near, *refs):
+    (key_hbm, value_hbm, grad_key, grad_value, sems) = refs
+    copies = []
+    for slot in (0, 1):
+        total = near[...]
+        if slot == 0:
+            total = far_own[...] + far_1[...].astype(jnp.float32) + far_2[...].astype(jnp.float32)
         place = pl.ds(half_start(rows, slot), rows)
-        grad_key[place, :] = jnp.transpose(total[0:HD]).astype(grad_key.dtype)
-        grad_value[place, :] = jnp.transpose(total[HD : 2 * HD]).astype(grad_value.dtype)
+        for side, (source, out) in enumerate(((grad_key, key_hbm), (grad_value, value_hbm))):
+            part = jnp.transpose(total[side * HD : (side + 1) * HD])
+            source[place, :] = part.astype(source.dtype)
+            copy = pltpu.make_async_copy(source.at[place], out.at[place], sems.at[slot, side])
+            copy.start()
+            copies.append(copy)
+    for copy in copies:
+        copy.wait()
 
 
 def total_grads(*parts):
@@ -509,7 +519,9 @@
         functools.partial(total_kernel, rows),
         out_shape=(shape, shape),
         in_specs=[VMEM] * 4,
-        out_specs=[VMEM] * 2,
+        out_specs=[HBM] * 2,
+        scratch_shapes=[pltpu.VMEM(shape.shape, shape.dtype)] * 2
+        + [pltpu.SemaphoreType.DMA((2, 2))],
         compiler_params=pltpu.CompilerParams(vmem_limit_bytes=VMEM_LIMIT),
         name="total_grads",
     )(*parts)

time: 33.4 us -> 33.3 us (level)
  no operation moved by 1% of the time
where the time goes in v22:
time: 33.3 us; the launch traced here: 33.1 us
  starting transfers between devices  15.1 us (45%)
  Pallas kernels  14.9 us (45%)
  other arithmetic  1.19 us (4%)
  waiting for transfers between devices  0.98 us (3%)
  between operations  0.82 us (2%)
    ppermute x8, starting transfers between devices, move(): return lax.ppermute(array, 'ctx', pairs)  15.1 us
    pallas_call x3, Pallas kernels, group_scores(): pl.pallas_call(functools.partial(group_kernel, rows, heads, slot, middle)...  3.2 us
    pallas_call x2, Pallas kernels, late_scores(): pl.pallas_call(functools.partial(late_kernel, rows, heads, slot), out_sha...  2.95 us
    pallas_call x1, Pallas kernels, block_outputs(): pl.pallas_call(functools.partial(outputs_kernel, rows, heads), out_shape=...  2.95 us
    pallas_call x2, Pallas kernels, rest_grads(): pl.pallas_call(functools.partial(grads_kernel, rows, heads, slots), out_s...  2.73 us
    pallas_call x1, Pallas kernels, prepare(): pl.pallas_call(functools.partial(prepare_kernel, rows, heads, doc_lengths...  2.23 us
    select_n x1, other arithmetic, body(): jnp.where(first, part[:rows], part[rows:])  1.07 us
    ppermute x8, waiting for transfers between devices, move(): return lax.ppermute(array, 'ctx', pairs)  0.98 us
  transfers between devices with their start and end apart: 8, of which 2 were waited for; matrix products, arithmetic and copies ran while one was open for 0% of the time, Pallas kernels for 42%

profile of v22, /device:TPU:0, one launch (start us, length us, event | category | flops | bytes accessed | tf_op | source)
XLA Modules:
  0.0 33.1 jit_solution(5897289671596528847)
XLA Ops:
  0.6 1.1 %broadcast_select_fusion = (bf16[384,128]{1,0:T(8,128)(2,1)S(1)}, bf16[384,128]{1,0:T(8,128)(2,1)S(1)}, bf16[384,128]{1,0:T(8,128)(2,1)S(1)}, bf16[384,128]{1,0:T(8,128)(2,1)S(1)}) fusion(pred[]{:T(512)S(6)} %eq.5, bf16[768,128]{1,0:T(8,128)(2,1)} %param.7, pred[]{:T(512)S(6)} %not.3, bf16[768,128]{1,0:T(8,128)(2,1)} %param.6), kind=kLoop, calls=%fused_computation.4 | loop fusion | flops 196608 | bytes 786434 | tf_op jit(solution)/shard_map/jit(_where)/select_n | solution.py:549
  1.7 0.7 %collective-permute-start.1 = (bf16[768,128]{1,0:T(8,128)(2,1)S(1)}, bf16[768,128]{1,0:T(8,128)(2,1)S(1)}, u32[]{:S(2)}, u32[]{:S(2)}) collective-permute-start(bf16[768,128]{1,0:T(8,128)(2,1)S(1)} %pad_maximum_fusion.1.refs_1_), channel_id=1, source_target_pairs={{1,2},{3,4},{5,6},{7,8},{9,10},{11,12},{13,14},{15,15},{14,13},{12... | collective-permute-start | bytes 589832 | tf_op jit(solution)/shard_map/ppermute | solution.py:537
  2.4 6.1 %collective-permute-start = (bf16[768,128]{1,0:T(8,128)(2,1)S(1)}, bf16[768,128]{1,0:T(8,128)(2,1)S(1)}, u32[]{:S(2)}, u32[]{:S(2)}) collective-permute-start(bf16[768,128]{1,0:T(8,128)(2,1)S(1)} %pad_maximum_fusion.refs_0_), channel_id=1, source_target_pairs={{0,2},{2,4},{4,6},{6,8},{8,10},{10,12},{12,14},{14,15},{15,13},{13... | collective-permute-start | bytes 589832 | tf_op jit(solution)/shard_map/ppermute | solution.py:537
  8.6 2.2 %prepare.1 = (bf16[768,128]{1,0:T(8,128)(2,1)S(1)}, bf16[256,1536]{1,0:T(8,128)(2,1)S(1)}, bf16[128,1536]{1,0:T(8,128)(2,1)S(1)}, bf16[1152,128]{1,0:T(8,128)(2,...) custom-call(bf16[768,128]{1,0:T(8,128)(2,1)S(1)} %pad_maximum_fusion, ...), custom_call_target="tpu_custom_call" | custom-call | bytes 4194304 | tf_op jit(solution)/shard_map/prepare/pallas_call | solution.py:117
  10.8 0.1 collective-permute-start.2
  10.9 0.7 %early_far.1 = (bf16[768,512]{1,0:T(8,128)(2,1)S(1)}, bf16[768,512]{1,0:T(8,128)(2,1)S(1)}, f32[24,512]{1,0:T(8,128)S(1)}) custom-call(bf16[256,1536]{1,0:T(8,128)(2,1)S(1)} %get-tuple-element.57.query_t.refs_0_.refs_5_, bf16[128,1536]{1,0:T(8,128)(2,1)S(1)} %get-tuple-element.58.dout_t.refs_1_.refs_6_, bf16[1152,128]{1,0:T(8,128)(2,1)S(1)} %get-tuple-element.59.documents, ...), custom_call_target="tpu_custom_call" | custom-call | flops 8589934592 | tf_op jit(solution)/shard_map/early_far/pallas_call | solution.py:273
  11.6 0.7 %collective-permute-done.2.refs_0_.refs_11_ = bf16[768,128]{1,0:T(8,128)(2,1)S(1)} collective-permute-done((bf16[768,128]{1,0:T(8,128)(2,1)S(1)}, bf16[768,128]{1,0:T(8,128)(2,1)S(1)}, u32[]{:S(2)}, u32[]{:S(2)}) %collective-permute-start.2) | collective-permute-done | bytes 196640 | tf_op jit(solution)/shard_map/ppermute | solution.py:537
  12.3 1.5 %early_near.1 = (bf16[1920,512]{1,0:T(8,128)(2,1)S(1)}, bf16[1920,512]{1,0:T(8,128)(2,1)S(1)}, f32[24,512]{1,0:T(8,128)S(1)}) custom-call(bf16[256,1536]{1,0:T(8,128)(2,1)S(1)} %get-tuple-element.48.query_t.refs_0_, bf16[128,1536]{1,0:T(8,128)(2,1)S(1)} %get-tuple-element.49.dout_t.refs_1_, bf16[1152,128]{1,0:T(8,128)(2,1)S(1)} %get-tuple-element.50.documents, ...), custom_call_target="tpu_custom_call" | custom-call | tf_op jit(solution)/shard_map/early_near/pallas_call | solution.py:273
  13.8 0.0 collective-permute-done.1.refs_0_.refs_1_
  13.8 0.7 %collective-permute-start.3 = (bf16[768,128]{1,0:T(8,128)(2,1)S(1)}, bf16[768,128]{1,0:T(8,128)(2,1)S(1)}, u32[]{:S(2)}, u32[]{:S(2)}) collective-permute-start(bf16[768,128]{1,0:T(8,128)(2,1)S(1)} %collective-permute-done.1.refs_0_.refs_1_), channel_id=1, source_target_pairs={{0,1},{1,0},{2,3},{3,2},{4,5},{5,4},{6,7},{7,6},{8,9},{9,8},{10,11... | collective-permute-start | bytes 589832 | tf_op jit(solution)/shard_map/ppermute | solution.py:537
  14.6 1.0 %middle_far.1 = (bf16[1152,512]{1,0:T(8,128)(2,1)S(1)}, bf16[1152,512]{1,0:T(8,128)(2,1)S(1)}, f32[24,512]{1,0:T(8,128)S(1)}) custom-call(bf16[256,1536]{1,0:T(8,128)(2,1)S(1)} %get-tuple-element.57.query_t.refs_0_.refs_5_, bf16[128,1536]{1,0:T(8,128)(2,1)S(1)} %get-tuple-element.58.dout_t.refs_1_.refs_6_, ...), custom_call_target="tpu_custom_call" | custom-call | tf_op jit(solution)/shard_map/middle_far/pallas_call | solution.py:273
  15.6 0.0 collective-permute-done.prev2.refs_0_
  15.6 1.5 %late_far.1 = (bf16[768,512]{1,0:T(8,128)(2,1)S(1)}, bf16[768,512]{1,0:T(8,128)(2,1)S(1)}, f32[32,512]{1,0:T(8,128)S(1)}, bf16[256,384]{1,0:T(8,128)(2,1)S(1)}) custom-call(bf16[256,1536]{1,0:T(8,128)(2,1)S(1)} %get-tuple-element.57.query_t.refs_0_.refs_5_, bf16[128,1536]{1,0:T(8,128)(2,1)S(1)} %get-tuple-element.58.dout_t.refs_1_.refs_6_, ...), custom_call_target="tpu_custom_call" | custom-call | flops 2147483648 | tf_op jit(solution)/shard_map/late_far/pallas_call | solution.py:358
  17.0 1.3 %collective-permute-start.4 = (bf16[256,384]{1,0:T(8,128)(2,1)S(1)}, bf16[256,384]{1,0:T(8,128)(2,1)S(1)}, u32[]{:S(2)}, u32[]{:S(2)}) collective-permute-start(bf16[256,384]{1,0:T(8,128)(2,1)S(1)} %get-tuple-element.84), channel_id=1, source_target_pairs={{2,0},{4,2},{6,4},{8,6},{10,8},{12,10},{14,12},{15,14},{13,15},{11... | collective-permute-start | bytes 589832 | tf_op jit(solution)/shard_map/ppermute | solution.py:537
  18.3 0.0 collective-permute-done.3.prev2.refs_10_
  18.4 0.8 %grads_far.1 = (bf16[1152,512]{1,0:T(8,128)(2,1)S(1)}, bf16[256,384]{1,0:T(8,128)(2,1)S(1)}) custom-call(bf16[256,1536]{1,0:T(8,128)(2,1)S(1)} %get-tuple-element.57.query_t.refs_0_.refs_5_, bf16[128,1536]{1,0:T(8,128)(2,1)S(1)} %get-tuple-element.58.dout_t.refs_1_.refs_6_, f32[32,512]{1,0:T(8,128)S(1)} %get-tuple-element.67.refs_2_.refs_7_.refs_9_, ...), custom_call_target="tpu_custom_call" | custom-call | tf_op jit(solution)/shard_map/grads_far/pallas_call | solution.py:423
  19.2 3.3 %collective-permute-start.6 = (bf16[256,384]{1,0:T(8,128)(2,1)S(1)}, bf16[256,384]{1,0:T(8,128)(2,1)S(1)}, u32[]{:S(2)}, u32[]{:S(2)}) collective-permute-start(bf16[256,384]{1,0:T(8,128)(2,1)S(1)} %get-tuple-element.89), channel_id=1, source_target_pairs={{0,1},{1,0},{2,3},{3,2},{4,5},{5,4},{6,7},{7,6},{8,9},{9,8},{10,11... | collective-permute-start | bytes 589832 | tf_op jit(solution)/shard_map/ppermute | solution.py:537
  22.5 1.5 %late_near.1 = (bf16[768,512]{1,0:T(8,128)(2,1)S(1)}, bf16[768,512]{1,0:T(8,128)(2,1)S(1)}, f32[32,512]{1,0:T(8,128)S(1)}, bf16[256,384]{1,0:T(8,128)(2,1)S(1)}) custom-call(bf16[256,1536]{1,0:T(8,128)(2,1)S(1)} %get-tuple-element.48.query_t.refs_0_, bf16[128,1536]{1,0:T(8,128)(2,1)S(1)} %get-tuple-element.49.dout_t.refs_1_, ...), custom_call_target="tpu_custom_call" | custom-call | flops 2147483648 | tf_op jit(solution)/shard_map/late_near/pallas_call | solution.py:358
  24.0 0.0 collective-permute-done.6
  24.0 0.1 add_convert_fusion
  24.0 2.9 %collective-permute-start.7 = (bf16[256,384]{1,0:T(8,128)(2,1)S(1)}, bf16[256,384]{1,0:T(8,128)(2,1)S(1)}, u32[]{:S(2)}, u32[]{:S(2)}) collective-permute-start(bf16[256,384]{1,0:T(8,128)(2,1)S(1)} %add_convert_fusion), channel_id=1, source_target_pairs={{3,1},{5,3},{7,5},{9,7},{11,9},{13,11},{15,13},{14,15},{12,14},{10... | collective-permute-start | bytes 589832 | tf_op jit(solution)/shard_map/ppermute | solution.py:537
  26.9 1.9 %grads_near.1 = (bf16[1920,512]{1,0:T(8,128)(2,1)S(1)}, bf16[256,384]{1,0:T(8,128)(2,1)S(1)}, f32[256,384]{1,0:T(8,128)S(1)}, bf16[768,512]{1,0:T(8,128)(2,1)S(1)}, f32[256,384]{1,0:T(8,128)S(1)}) custom-call(bf16[256,1536]{1,0:T(8,128)(2,1)S(1)} %get-tuple-element.48.query_t.refs_0_, bf16[128,1536]{1,0:T(8,128)(2,1)S(1)} %get-tuple-element.49.dout_t.refs_1_, ...), custom_call_target="tpu_custom_call" | custom-call | flops 2147483648 | tf_op jit(solution)/shard_map/grads_near/pallas_call | solution.py:423
  28.8 0.0 collective-permute-done.4.far_2
  28.8 0.1 collective-permute-start.5
  28.9 2.9 %block_outputs.1 = (bf16[768,512]{1,0:T(8,128)(2,1)}, bf16[768,512]{1,0:T(8,128)(2,1)}) custom-call(bf16[768,128]{1,0:T(8,128)(2,1)S(1)} %collective-permute-done.prev2.refs_0_, bf16[768,128]{1,0:T(8,128)(2,1)S(1)} %collective-permute-done.1.refs_0_.refs_1_, bf16[768,128]{1,0:T(8,128)(2,1)S(1)} %get-tuple-element.51.refs_0_.refs_2_, ...), custom_call_target="tpu_custom_call" | custom-call | tf_op jit(solution)/shard_map/block_outputs/pallas_call | solution.py:483
  31.9 0.3 collective-permute-done.7
  32.2 0.0 collective-permute-done.5.far_1
  32.2 0.9 %total_grads.1 = (bf16[768,128]{1,0:T(8,128)(2,1)}, bf16[768,128]{1,0:T(8,128)(2,1)}) custom-call(f32[256,384]{1,0:T(8,128)S(1)} %get-tuple-element.82.far_own, bf16[256,384]{1,0:T(8,128)(2,1)S(1)} %collective-permute-done.5.far_1, bf16[256,384]{1,0:T(8,128)(2,1)S(1)} %collective-permute-done.4.far_2, f32[256,384]{1,0:T(8,128)S(1)} %convert_add_fusion.near), custom_call_target="tpu_custom_call" | custom-call | tf_op jit(solution)/shard_map/total_grads/pallas_call | solution.py:518
  (3 shorter events, 0.1 us)
Async XLA Ops:
  1.7 12.1 %collective-permute-start.1 = (bf16[768,128]{1,0:T(8,128)(2,1)S(1)}, bf16[768,128]{1,0:T(8,128)(2,1)S(1)}, u32[]{:S(2)}, u32[]{:S(2)}) collective-permute-start(bf16[768,128]{1,0:T(8,128)(2,1)S(1)} %pad_maximum_fusion.1.refs_1_), channel_id=1, source_target_pairs={{1,2},{3,4},{5,6},{7,8},{9,10},{11,12},{13,14},{15,15},{14,13},{12... | collective-permute-start | bytes 589832 | tf_op jit(solution)/shard_map/ppermute | solution.py:537
  2.4 13.1 %collective-permute-start = (bf16[768,128]{1,0:T(8,128)(2,1)S(1)}, bf16[768,128]{1,0:T(8,128)(2,1)S(1)}, u32[]{:S(2)}, u32[]{:S(2)}) collective-permute-start(bf16[768,128]{1,0:T(8,128)(2,1)S(1)} %pad_maximum_fusion.refs_0_), channel_id=1, source_target_pairs={{0,2},{2,4},{4,6},{6,8},{8,10},{10,12},{12,14},{14,15},{15,13},{13... | collective-permute-start | bytes 589832 | tf_op jit(solution)/shard_map/ppermute | solution.py:537
  10.8 1.5 %collective-permute-start.2 = (bf16[768,128]{1,0:T(8,128)(2,1)S(1)}, bf16[768,128]{1,0:T(8,128)(2,1)S(1)}, u32[]{:S(2)}, u32[]{:S(2)}) collective-permute-start(bf16[768,128]{1,0:T(8,128)(2,1)S(1)} %get-tuple-element.51.refs_0_.refs_2_), channel_id=1, source_target_pairs={{0,1},{1,0},{2,3},{3,2},{4,5},{5,4},{6,7},{7,6},{8,9},{9,8},{10,11... | collective-permute-start | bytes 589832 | tf_op jit(solution)/shard_map/ppermute | solution.py:537
  13.8 4.5 %collective-permute-start.3 = (bf16[768,128]{1,0:T(8,128)(2,1)S(1)}, bf16[768,128]{1,0:T(8,128)(2,1)S(1)}, u32[]{:S(2)}, u32[]{:S(2)}) collective-permute-start(bf16[768,128]{1,0:T(8,128)(2,1)S(1)} %collective-permute-done.1.refs_0_.refs_1_), channel_id=1, source_target_pairs={{0,1},{1,0},{2,3},{3,2},{4,5},{5,4},{6,7},{7,6},{8,9},{9,8},{10,11... | collective-permute-start | bytes 589832 | tf_op jit(solution)/shard_map/ppermute | solution.py:537
  17.0 11.8 %collective-permute-start.4 = (bf16[256,384]{1,0:T(8,128)(2,1)S(1)}, bf16[256,384]{1,0:T(8,128)(2,1)S(1)}, u32[]{:S(2)}, u32[]{:S(2)}) collective-permute-start(bf16[256,384]{1,0:T(8,128)(2,1)S(1)} %get-tuple-element.84), channel_id=1, source_target_pairs={{2,0},{4,2},{6,4},{8,6},{10,8},{12,10},{14,12},{15,14},{13,15},{11... | collective-permute-start | bytes 589832 | tf_op jit(solution)/shard_map/ppermute | solution.py:537
  19.2 4.8 %collective-permute-start.6 = (bf16[256,384]{1,0:T(8,128)(2,1)S(1)}, bf16[256,384]{1,0:T(8,128)(2,1)S(1)}, u32[]{:S(2)}, u32[]{:S(2)}) collective-permute-start(bf16[256,384]{1,0:T(8,128)(2,1)S(1)} %get-tuple-element.89), channel_id=1, source_target_pairs={{0,1},{1,0},{2,3},{3,2},{4,5},{5,4},{6,7},{7,6},{8,9},{9,8},{10,11... | collective-permute-start | bytes 589832 | tf_op jit(solution)/shard_map/ppermute | solution.py:537
  24.0 8.1 %collective-permute-start.7 = (bf16[256,384]{1,0:T(8,128)(2,1)S(1)}, bf16[256,384]{1,0:T(8,128)(2,1)S(1)}, u32[]{:S(2)}, u32[]{:S(2)}) collective-permute-start(bf16[256,384]{1,0:T(8,128)(2,1)S(1)} %add_convert_fusion), channel_id=1, source_target_pairs={{3,1},{5,3},{7,5},{9,7},{11,9},{13,11},{15,13},{14,15},{12,14},{10... | collective-permute-start | bytes 589832 | tf_op jit(solution)/shard_map/ppermute | solution.py:537
  28.8 3.3 %collective-permute-start.5 = (bf16[256,384]{1,0:T(8,128)(2,1)S(1)}, bf16[256,384]{1,0:T(8,128)(2,1)S(1)}, u32[]{:S(2)}, u32[]{:S(2)}) collective-permute-start(bf16[256,384]{1,0:T(8,128)(2,1)S(1)} %get-tuple-element.85), channel_id=1, source_target_pairs={{0,1},{1,0},{2,3},{3,2},{4,5},{5,4},{6,7},{7,6},{8,9},{9,8},{10,11... | collective-permute-start | bytes 589832 | tf_op jit(solution)/shard_map/ppermute | solution.py:537
